TPU v7x, 32 devices: a whole 2x2x4 slice. The times are simulated.
32 devices in a mesh: dp: 8 (over z, core), comp: 4 (over y, x).
Axes of the slice: x: 2, y: 2, z: 4, core: 2. Of those that a mesh axis runs over, the one named last changes fastest.
Arguments:
- points: bfloat16 [65536, 768], P(('dp', 'comp')), may hold values from -6 to 6
- candidates: int32 [512, 4], P(('dp', 'comp')), may hold values from 0 to 127, as said below
- means: bfloat16 [16384, 768], P(('dp', 'comp')), may hold values from -0.59765625 to 0.59765625
- inv_var: bfloat16 [16384, 768], P(('dp', 'comp')), may hold values from 0.5 to 1.5
- log_weight: bfloat16 [16384], P(('dp', 'comp')), may hold values from -12 to -9
Outputs:
- counts: float32 [16384], P(('dp', 'comp'))
- first_moment: float32 [16384, 768], P(('dp', 'comp'))
- second_moment: float32 [16384, 768], P(('dp', 'comp'))
- loglik: float32 [65536], P(('dp', 'comp'))
Inputs may be any that keep to these rules, and one draw needn't show every extreme that they name: `candidates`: each row block names 4 different component blocks; all blocks b named by the row blocks of device index i along dp+comp satisfy (b // 4) % 4 == i % 4, that is, one owner group serves each device's rows.
All inputs are finite; a program needn't handle non-finite values.
Results may differ from a plain program's by a relative error of at most 0.028.
Values may be sent and summed in bfloat16 or wider, within the bound.
No kernel may reach another device: no remote copies, remote signals or barrier semaphores. Data moves between devices by JAX's collectives and lax.ppermute only.
A program may use at most 128 MiB of HBM per device.

v0:
```python
import math

import jax
import jax.numpy as jnp
from jax import lax
from jax.sharding import PartitionSpec as P

CB = 128
RB = 128
CANDS = 4


def component_consts(mean_values, inv_values, log_values):
    feature_count = mean_values.shape[1]
    mean_f = mean_values.astype(jnp.float32)
    inv_f = inv_values.astype(jnp.float32)
    return (
        log_values.astype(jnp.float32)
        + 0.5 * jnp.sum(jnp.log(inv_f), axis=1)
        - 0.5 * jnp.sum(inv_f * mean_f * mean_f, axis=1)
        - 0.5 * feature_count * math.log(2.0 * math.pi)
    )


def block_terms(row_block, selector, scaled_flat, inverse_flat, constants):
    group_rows, slot_count, block_total = selector.shape
    feature_count = row_block.shape[2]
    row_f = row_block.astype(jnp.float32)
    squares = (row_f * row_f).astype(jnp.bfloat16)
    pick = selector.reshape(group_rows * slot_count, block_total)
    pick_bf = pick.astype(jnp.bfloat16)
    chosen_scaled = jnp.dot(pick_bf, scaled_flat, preferred_element_type=jnp.float32).astype(
        jnp.bfloat16
    )
    chosen_inverse = jnp.dot(pick_bf, inverse_flat, preferred_element_type=jnp.float32).astype(
        jnp.bfloat16
    )
    chosen_scaled = chosen_scaled.reshape(group_rows, slot_count, CB, feature_count)
    chosen_inverse = chosen_inverse.reshape(group_rows, slot_count, CB, feature_count)
    chosen_consts = jnp.dot(pick, constants, precision=lax.Precision.HIGHEST).reshape(
        group_rows, slot_count, CB
    )
    linear = jnp.einsum(
        "grd,gskd->grsk", row_block, chosen_scaled, preferred_element_type=jnp.float32
    )
    quadratic = jnp.einsum(
        "grd,gskd->grsk", squares, chosen_inverse, preferred_element_type=jnp.float32
    )
    densities = chosen_consts[:, None] + linear - 0.5 * quadratic
    row_peak = jnp.max(densities, axis=(2, 3))
    normalizer = row_peak + jnp.log(
        jnp.sum(jnp.exp(densities - row_peak[:, :, None, None]), axis=(2, 3))
    )
    responsibility = jnp.exp(densities - normalizer[:, :, None, None]).astype(jnp.bfloat16)
    counts = jnp.sum(responsibility.astype(jnp.float32), axis=1)
    first_moment = jnp.einsum(
        "grsk,grd->gskd", responsibility, row_block, preferred_element_type=jnp.float32
    )
    second_moment = jnp.einsum(
        "grsk,grd->gskd", responsibility, squares, preferred_element_type=jnp.float32
    )
    return (normalizer, counts, first_moment, second_moment)


def on_device(points, candidates, means, inv_var, log_weight):
    feature_count = points.shape[1]
    owner_count = lax.axis_size("comp")
    held_blocks = means.shape[0] // CB
    all_means, all_inverse, all_logs = (
        lax.all_gather(means, "dp", axis=0, tiled=True),
        lax.all_gather(inv_var, "dp", axis=0, tiled=True),
        lax.all_gather(log_weight, "dp", axis=0, tiled=True),
    )
    all_scaled = (all_inverse.astype(jnp.float32) * all_means.astype(jnp.float32)).astype(
        jnp.bfloat16
    )
    all_consts = component_consts(all_means, all_inverse, all_logs)
    group_blocks = all_scaled.shape[0] // CB
    scaled_flat = all_scaled.reshape(group_blocks, CB * feature_count)
    inverse_flat = all_inverse.reshape(group_blocks, CB * feature_count)
    constants = all_consts.reshape(group_blocks, CB)
    local_ids = candidates // (owner_count * held_blocks) * held_blocks + candidates % held_blocks
    block_count = candidates.shape[0]
    row_groups = points.reshape(block_count // 4, 4, RB, feature_count)
    id_groups = local_ids.reshape(block_count // 4, 4, CANDS)
    block_iota = jnp.arange(group_blocks, dtype=jnp.int32)

    def accumulate(running, inputs):
        row_block, chosen_ids = inputs
        selector = (chosen_ids[:, :, None] == block_iota[None, None, :]).astype(jnp.float32)
        normalizer, counts, first_part, second_part = block_terms(
            row_block, selector, scaled_flat, inverse_flat, constants
        )
        spread = selector.reshape(-1, group_blocks).T
        slot_total = spread.shape[1]
        new_counts = jnp.dot(
            spread, counts.reshape(slot_total, CB), precision=lax.Precision.HIGHEST
        )
        new_first = jnp.dot(
            spread,
            first_part.reshape(slot_total, CB * feature_count),
            precision=lax.Precision.HIGHEST,
        )
        new_second = jnp.dot(
            spread,
            second_part.reshape(slot_total, CB * feature_count),
            precision=lax.Precision.HIGHEST,
        )
        running = (running[0] + new_counts, running[1] + new_first, running[2] + new_second)
        return (running, normalizer)

    initial = (
        jnp.zeros((group_blocks, CB), jnp.float32),
        jnp.zeros((group_blocks, CB * feature_count), jnp.float32),
        jnp.zeros((group_blocks, CB * feature_count), jnp.float32),
    )
    partials, normalizers = lax.scan(accumulate, initial, (row_groups, id_groups))
    count_sum, first_sum, second_sum = (
        lax.psum_scatter(
            partials[0].astype(jnp.bfloat16), "dp", scatter_dimension=0, tiled=True
        ).astype(jnp.float32),
        lax.psum_scatter(
            partials[1].astype(jnp.bfloat16), "dp", scatter_dimension=0, tiled=True
        ).astype(jnp.float32),
        lax.psum_scatter(
            partials[2].astype(jnp.bfloat16), "dp", scatter_dimension=0, tiled=True
        ).astype(jnp.float32),
    )
    loglik = normalizers.reshape(-1) / feature_count
    return (
        count_sum.reshape(-1),
        first_sum.reshape(-1, feature_count),
        second_sum.reshape(-1, feature_count),
        loglik,
    )


def solution(mesh):
    return jax.shard_map(
        on_device,
        mesh=mesh,
        in_specs=(
            P(("dp", "comp"), None),
            P(("dp", "comp"), None),
            P(("dp", "comp"), None),
            P(("dp", "comp"), None),
            P(("dp", "comp")),
        ),
        out_specs=(
            P(("dp", "comp")),
            P(("dp", "comp"), None),
            P(("dp", "comp"), None),
            P(("dp", "comp")),
        ),
        check_vma=False,
    )
```

profile of v0, /device:TPU:0, one launch (start us, length us, event | category | flops | bytes accessed | tf_op | source)
XLA Modules:
  0.0 654.7 jit_solution(7923150392438582720)
XLA Ops:
  9.4 14.4 %all-gather = bf16[8,1,512]{2,1,0:T(2,128)(2,1)S(1)} all-gather(bf16[1,1,512]{2,1,0:T(2,128)(2,1)S(1)} %reshape.127), channel_id=1, replica_groups=mesh['dp'=8,'comp'=4] {'dp'}, dimensions={0}, use_global_device_ids=true | all-gather | bytes 9216 | tf_op jit(solution)/shard_map/all_gather | solution.py:72
  24.6 52.5 %all-gather.4.cloned.1.call-done = bf16[4096,768]{1,0:T(8,128)(2,1)} async-done(((bf16[512,768]{1,0:T(8,128)(2,1)}), bf16[4096,768]{1,0:T(8,128)(2,1)}) %all-gather.4.cloned.1.call-update) | async-done | bytes 6291472 | tf_op jit(solution)/shard_map/all_gather | solution.py:71
  77.1 65.1 %all-gather.6.cloned.1.call-done = bf16[4096,768]{1,0:T(8,128)(2,1)} async-done(((bf16[512,768]{1,0:T(8,128)(2,1)}), bf16[4096,768]{1,0:T(8,128)(2,1)}) %all-gather.6.cloned.1.call-update) | async-done | bytes 6291472 | tf_op jit(solution)/shard_map/all_gather | solution.py:70
  142.2 10.6 %fusion.32 = (f32[4096]{0:T(1024)S(1)}, f32[4096]{0:T(1024)S(1)}, bf16[4096,768]{1,0:T(8,128)(2,1)}) fusion(bf16[4096,768]{1,0:T(8,128)(2,1)} %all-gather.4.cloned.1.call-done, bf16[4096,768]{1,0:T(8,128)(2,1)} %all-gather.6.cloned.1.call-done), kind=kLoop, calls=%fused_computation.46 | loop fusion | flops 22011904 | bytes 18907136 | tf_op jit(solution)/shard_map/reduce_sum | solution.py:19
  152.8 7.2 %reshape.109 = bf16[32,98304]{1,0:T(8,128)(2,1)} reshape(bf16[4096,768]{1,0:T(8,128)(2,1)} %get-tuple-element.182) | data formatting | bytes 12582912 | tf_op jit(solution)/shard_map/reshape | solution.py:79
  160.0 7.3 %reshape.110 = bf16[32,98304]{1,0:T(8,128)(2,1)} reshape(bf16[4096,768]{1,0:T(8,128)(2,1)} %all-gather.4.cloned.1.call-done) | data formatting | bytes 12582912 | tf_op jit(solution)/shard_map/reshape | solution.py:80
  167.3 203.8 %while.18 = (s32[]{:T(128)}, f32[32,128]{1,0:T(8,128)S(1)}, f32[32,98304]{1,0:T(8,128)}, f32[32,98304]{1,0:T(8,128)}, f32[4,4,128]{2,1,0:T(4,128)S(1)}, /*index=...) while((s32[]{:T(128)}, f32[32,128]{1,0:T(8,128)S(1)}, ...), condition=%wide.region_6.7_spmd.clone.clone, body=%wide.region_2.6_spmd.clone.clone.sunk | while | flops 3042191872 | bytes 255429680 | solution.py:117
  167.4 4.0 convolution_convert_fusion.4
  181.0 6.3 copy.24
  187.3 10.6 %convolution_add_fusion.7 = f32[32,98304]{1,0:T(8,128)} fusion(f32[16,98304]{1,0:T(8,128)} %bitcast.117, f32[32,98304]{1,0:T(8,128)} %get-tuple-element.272, pred[]{:T(512)S(6)} %compare.6, s32[16]{0:T(128)S(1)} %eq.108), kind=kOutput, calls=%fused_computation.2.clone.1 | convolution fusion | flops 610271744 | bytes 31457344 | tf_op jit(solution)/shard_map/while/body/eval_jaxpr/dot_general | solution.py:99
  200.2 3.6 copy.25
  203.9 8.2 %convolution_add_fusion.8 = f32[32,98304]{1,0:T(8,128)S(1)} fusion(f32[16,98304]{1,0:T(8,128)S(1)} %bitcast.118, f32[32,98304]{1,0:T(8,128)S(1)} %bitcast.124, pred[]{:T(512)S(6)} %compare.6, s32[16]{0:T(128)S(1)} %eq.108), kind=kOutput, calls=%fused_computation.1.clone.1 | convolution fusion | flops 610271744 | bytes 31457344 | tf_op jit(solution)/shard_map/while/body/eval_jaxpr/dot_general | solution.py:104
  212.1 4.5 copy-done
  217.0 4.0 convolution_convert_fusion.4
  230.5 6.3 copy.24
  236.8 12.5 %convolution_add_fusion.7 = f32[32,98304]{1,0:T(8,128)} fusion(f32[16,98304]{1,0:T(8,128)} %bitcast.117, f32[32,98304]{1,0:T(8,128)} %get-tuple-element.272, pred[]{:T(512)S(6)} %compare.6, s32[16]{0:T(128)S(1)} %eq.108), kind=kOutput, calls=%fused_computation.2.clone.1 | convolution fusion | flops 610271744 | bytes 31457344 | tf_op jit(solution)/shard_map/while/body/eval_jaxpr/dot_general | solution.py:99
  255.2 8.2 %convolution_add_fusion.8 = f32[32,98304]{1,0:T(8,128)S(1)} fusion(f32[16,98304]{1,0:T(8,128)S(1)} %bitcast.118, f32[32,98304]{1,0:T(8,128)S(1)} %bitcast.124, pred[]{:T(512)S(6)} %compare.6, s32[16]{0:T(128)S(1)} %eq.108), kind=kOutput, calls=%fused_computation.1.clone.1 | convolution fusion | flops 610271744 | bytes 31457344 | tf_op jit(solution)/shard_map/while/body/eval_jaxpr/dot_general | solution.py:104
  263.5 4.5 copy-done
  268.3 4.0 convolution_convert_fusion.4
  281.9 6.3 copy.24
  288.2 12.5 %convolution_add_fusion.7 = f32[32,98304]{1,0:T(8,128)} fusion(f32[16,98304]{1,0:T(8,128)} %bitcast.117, f32[32,98304]{1,0:T(8,128)} %get-tuple-element.272, pred[]{:T(512)S(6)} %compare.6, s32[16]{0:T(128)S(1)} %eq.108), kind=kOutput, calls=%fused_computation.2.clone.1 | convolution fusion | flops 610271744 | bytes 31457344 | tf_op jit(solution)/shard_map/while/body/eval_jaxpr/dot_general | solution.py:99
  306.6 8.2 %convolution_add_fusion.8 = f32[32,98304]{1,0:T(8,128)S(1)} fusion(f32[16,98304]{1,0:T(8,128)S(1)} %bitcast.118, f32[32,98304]{1,0:T(8,128)S(1)} %bitcast.124, pred[]{:T(512)S(6)} %compare.6, s32[16]{0:T(128)S(1)} %eq.108), kind=kOutput, calls=%fused_computation.1.clone.1 | convolution fusion | flops 610271744 | bytes 31457344 | tf_op jit(solution)/shard_map/while/body/eval_jaxpr/dot_general | solution.py:104
  314.8 4.5 copy-done
  319.7 4.0 convolution_convert_fusion.4
  333.2 6.3 copy.24
  339.5 12.5 %convolution_add_fusion.7 = f32[32,98304]{1,0:T(8,128)} fusion(f32[16,98304]{1,0:T(8,128)} %bitcast.117, f32[32,98304]{1,0:T(8,128)} %get-tuple-element.272, pred[]{:T(512)S(6)} %compare.6, s32[16]{0:T(128)S(1)} %eq.108), kind=kOutput, calls=%fused_computation.2.clone.1 | convolution fusion | flops 610271744 | bytes 31457344 | tf_op jit(solution)/shard_map/while/body/eval_jaxpr/dot_general | solution.py:99
  358.0 8.2 %convolution_add_fusion.8 = f32[32,98304]{1,0:T(8,128)S(1)} fusion(f32[16,98304]{1,0:T(8,128)S(1)} %bitcast.118, f32[32,98304]{1,0:T(8,128)S(1)} %bitcast.124, pred[]{:T(512)S(6)} %compare.6, s32[16]{0:T(128)S(1)} %eq.108), kind=kOutput, calls=%fused_computation.1.clone.1 | convolution fusion | flops 610271744 | bytes 31457344 | tf_op jit(solution)/shard_map/while/body/eval_jaxpr/dot_general | solution.py:104
  366.2 4.5 copy-done
  371.2 7.9 %convert_element_type.56 = bf16[32,98304]{1,0:T(8,128)(2,1)} convert(f32[32,98304]{1,0:T(8,128)} %get-tuple-element.68) | non-fusion elementwise | flops 3145728 | bytes 18874368 | tf_op jit(solution)/shard_map/convert_element_type | solution.py:123
  379.0 7.9 %convert_element_type.57 = bf16[32,98304]{1,0:T(8,128)(2,1)} convert(f32[32,98304]{1,0:T(8,128)} %get-tuple-element.69) | non-fusion elementwise | flops 3145728 | bytes 18874368 | tf_op jit(solution)/shard_map/convert_element_type | solution.py:126
  388.8 15.0 %all-reduce = bf16[32,128]{1,0:T(8,128)(2,1)S(1)} all-reduce(bf16[32,128]{1,0:T(8,128)(2,1)S(1)} %convert_element_type.55), channel_id=2, replica_groups=mesh['dp'=8,'comp'=4] {'dp'}, use_global_device_ids=true, to_apply=%region_7.8.clone | all-reduce | flops 4096 | bytes 16384
  404.9 236.3 %all-reduce.6.cloned.1.call-done = (bf16[32,98304]{1,0:T(8,128)(2,1)}, bf16[32,98304]{1,0:T(8,128)(2,1)}) async-done(((bf16[32,98304]{1,0:T(8,128)(2,1)}, bf16[32,98304]{1,0:T(8,128)(2,1)}), (bf16[32,98304]{1,0:T(8,128)(2,1)}, bf16[32,98304]{1,0:T(8,128)(2,1)})) %all-reduce.6.cloned.1.call-update) | async-done | bytes 12582928
  (139 shorter events, 71.8 us)
Async XLA Ops:
  7.2 70.0 %all-gather.4.cloned.1.call-start = ((), (), s32[]{:S(2)}) async-start(), calls=%async_computation | async-start | bytes 7077888 | tf_op jit(solution)/shard_map/all_gather | solution.py:71
  7.9 134.3 %all-gather.6.cloned.1.call-start = ((), (), s32[]{:S(2)}) async-start(), calls=%async_computation.1 | async-start | bytes 7077888 | tf_op jit(solution)/shard_map/all_gather | solution.py:70
  8.6 632.6 %all-reduce.6.cloned.1.call-start = ((), (), s32[]{:S(2)}) async-start(), calls=%async_computation.2 | async-start | bytes 25165824
  167.4 7.0 %slice-start.3 = ((s8[6291456]{0:T(1024)(128)(4,1)}), s8[4194304]{0:T(1024)(128)(4,1)S(1)}, s32[]{:S(2)}) async-start(s8[6291456]{0:T(1024)(128)(4,1)} %bitcast.127), calls=%async_computation.6 | async-start | bytes 8388608 | tf_op jit(solution)/shard_map/while
  171.4 3.1 slice-start.4
  187.3 16.6 %slice-start = ((s8[12582912]{0:T(1024)(128)(4,1)}), s8[4194304]{0:T(1024)(128)(4,1)S(1)}, s32[]{:S(2)}) async-start(s8[12582912]{0:T(1024)(128)(4,1)} %bitcast.123), calls=%async_computation.3 | async-start | bytes 8388608 | tf_op jit(solution)/shard_map/while
  187.3 16.6 %slice-start.1 = ((s8[12582912]{0:T(1024)(128)(4,1)}), s8[4194304]{0:T(1024)(128)(4,1)S(1)}, s32[]{:S(2)}) async-start(s8[12582912]{0:T(1024)(128)(4,1)} %bitcast.123), calls=%async_computation.4 | async-start | bytes 8388608 | tf_op jit(solution)/shard_map/while
  197.9 5.9 slice-start.2
  212.1 4.5 copy-start
  217.0 7.0 %slice-start.3 = ((s8[6291456]{0:T(1024)(128)(4,1)}), s8[4194304]{0:T(1024)(128)(4,1)S(1)}, s32[]{:S(2)}) async-start(s8[6291456]{0:T(1024)(128)(4,1)} %bitcast.127), calls=%async_computation.6 | async-start | bytes 8388608 | tf_op jit(solution)/shard_map/while
  220.9 3.1 slice-start.4
  236.8 18.4 %slice-start = ((s8[12582912]{0:T(1024)(128)(4,1)}), s8[4194304]{0:T(1024)(128)(4,1)S(1)}, s32[]{:S(2)}) async-start(s8[12582912]{0:T(1024)(128)(4,1)} %bitcast.123), calls=%async_computation.3 | async-start | bytes 8388608 | tf_op jit(solution)/shard_map/while
  236.8 18.4 %slice-start.1 = ((s8[12582912]{0:T(1024)(128)(4,1)}), s8[4194304]{0:T(1024)(128)(4,1)S(1)}, s32[]{:S(2)}) async-start(s8[12582912]{0:T(1024)(128)(4,1)} %bitcast.123), calls=%async_computation.4 | async-start | bytes 8388608 | tf_op jit(solution)/shard_map/while
  249.3 5.9 slice-start.2
  263.4 4.5 copy-start
  268.3 7.0 %slice-start.3 = ((s8[6291456]{0:T(1024)(128)(4,1)}), s8[4194304]{0:T(1024)(128)(4,1)S(1)}, s32[]{:S(2)}) async-start(s8[6291456]{0:T(1024)(128)(4,1)} %bitcast.127), calls=%async_computation.6 | async-start | bytes 8388608 | tf_op jit(solution)/shard_map/while
  272.3 3.1 slice-start.4
  288.2 18.4 %slice-start = ((s8[12582912]{0:T(1024)(128)(4,1)}), s8[4194304]{0:T(1024)(128)(4,1)S(1)}, s32[]{:S(2)}) async-start(s8[12582912]{0:T(1024)(128)(4,1)} %bitcast.123), calls=%async_computation.3 | async-start | bytes 8388608 | tf_op jit(solution)/shard_map/while
  288.2 18.4 %slice-start.1 = ((s8[12582912]{0:T(1024)(128)(4,1)}), s8[4194304]{0:T(1024)(128)(4,1)S(1)}, s32[]{:S(2)}) async-start(s8[12582912]{0:T(1024)(128)(4,1)} %bitcast.123), calls=%async_computation.4 | async-start | bytes 8388608 | tf_op jit(solution)/shard_map/while
  300.7 5.9 slice-start.2
  314.8 4.5 copy-start
  319.7 7.0 %slice-start.3 = ((s8[6291456]{0:T(1024)(128)(4,1)}), s8[4194304]{0:T(1024)(128)(4,1)S(1)}, s32[]{:S(2)}) async-start(s8[6291456]{0:T(1024)(128)(4,1)} %bitcast.127), calls=%async_computation.6 | async-start | bytes 8388608 | tf_op jit(solution)/shard_map/while
  323.7 3.1 slice-start.4
  339.5 18.4 %slice-start = ((s8[12582912]{0:T(1024)(128)(4,1)}), s8[4194304]{0:T(1024)(128)(4,1)S(1)}, s32[]{:S(2)}) async-start(s8[12582912]{0:T(1024)(128)(4,1)} %bitcast.123), calls=%async_computation.3 | async-start | bytes 8388608 | tf_op jit(solution)/shard_map/while
  339.5 18.4 %slice-start.1 = ((s8[12582912]{0:T(1024)(128)(4,1)}), s8[4194304]{0:T(1024)(128)(4,1)S(1)}, s32[]{:S(2)}) async-start(s8[12582912]{0:T(1024)(128)(4,1)} %bitcast.123), calls=%async_computation.4 | async-start | bytes 8388608 | tf_op jit(solution)/shard_map/while
  352.0 5.9 slice-start.2
  366.2 4.5 copy-start
  386.9 0.7 copy-start.1
Sparse Core Ops, SparseCore 0:
  9.6 67.4 all-gather.3
  78.8 63.3 all-gather.5
  387.0 254.1 all-reduce.5
where the time goes:
time: 655 us
  waiting for transfers between devices  355 us (54%)
  matrix products  137 us (21%)
  local copies, waits for them, and re-layouts  84.5 us (13%)
  other arithmetic  32.9 us (5%)
  blocking collectives  29.3 us (4%)
  between operations  14.5 us (2%)
    unnamed x4, waiting for transfers between devices  238 us
    all_gather x1, waiting for transfers between devices, on_device(): lax.all_gather(means, 'dp', axis=0, tiled=True)  65.1 us
    while x64, local copies, waits for them, and re-layouts  63.1 us
    all_gather x1, waiting for transfers between devices, on_device(): lax.all_gather(inv_var, 'dp', axis=0, tiled=True)  52.5 us
    dot_general x4, matrix products, accumulate(): jnp.dot(spread, first_part.reshape(slot_total, CB * feature_count), preci...  48.1 us
    dot_general x4, matrix products, accumulate(): jnp.dot(spread, second_part.reshape(slot_total, CB * feature_count), prec...  32.8 us
    dot_general x4, matrix products, block_terms(): jnp.dot(pick_bf, scaled_flat, preferred_element_type=jnp.float32)  15.9 us
    unnamed x1, blocking collectives  15 us
  transfers between devices with their start and end apart: 3, of which 3 were waited for; matrix products, arithmetic and copies ran while one was open for 0% of the time, Pallas kernels for 0%

commit v1 on v0

v1 whole, which is shorter than its diff:
```python
import functools
import math

import jax
import jax.numpy as jnp
from jax import lax
from jax.experimental import pallas as pl
from jax.experimental.pallas import tpu as pltpu
from jax.sharding import PartitionSpec as P

CB = 128
RB = 128
CANDS = 4
VMEM_LIMIT = 56 * 1024 * 1024
NT = (((1,), (1,)), ((), ()))


def component_consts(mean_values, inv_values, log_values):
    feature_count = mean_values.shape[1]
    mean_f = mean_values.astype(jnp.float32)
    inv_f = inv_values.astype(jnp.float32)
    return (
        log_values.astype(jnp.float32)
        + 0.5 * jnp.sum(jnp.log(inv_f), axis=1)
        - 0.5 * jnp.sum(inv_f * mean_f * mean_f, axis=1)
        - 0.5 * feature_count * math.log(2.0 * math.pi)
    )


def square_of(x):
    x_f = x.astype(jnp.float32)
    return (x_f * x_f).astype(jnp.bfloat16)


def density_body(shards, held, pos_ref, nat_ref, x_ref, const_ref, *rest):
    weight_refs = rest[:shards]
    resp_ref, norm_ref, count_ref, weights, sems = rest[shards:]
    step = pl.program_id(0)

    @pl.when(step == 0)
    def _():
        copies = [
            pltpu.make_async_copy(weight_refs[j], weights.at[j], sems.at[j]) for j in range(shards)
        ]
        for copy in copies:
            copy.start()
        for copy in copies:
            copy.wait()

    x = x_ref[...]
    half = (square_of(x).astype(jnp.float32) * -0.5).astype(jnp.bfloat16)
    densities = []
    for slot in range(CANDS):
        pos = pos_ref[step, slot]
        shard, block = lax.div(pos, held), lax.rem(pos, held)
        linear = lax.dot_general(
            weights[shard, 0, block], x, NT, preferred_element_type=jnp.float32
        )
        quadratic = lax.dot_general(
            weights[shard, 1, block], half, NT, preferred_element_type=jnp.float32
        )
        densities.append(linear + quadratic + const_ref[nat_ref[step, slot]])
    peak = functools.reduce(jnp.maximum, [jnp.max(d, axis=0, keepdims=True) for d in densities])
    terms = [jnp.exp(d - peak) for d in densities]
    total = functools.reduce(jnp.add, [jnp.sum(t, axis=0, keepdims=True) for t in terms])
    norm_ref[0] = peak + jnp.log(total)
    inverse_total = 1.0 / total
    ones = jnp.ones((8, RB), jnp.bfloat16)
    for slot in range(CANDS):
        resp = (terms[slot] * inverse_total).astype(jnp.bfloat16)
        resp_ref[0, slot] = resp
        counts = lax.dot_general(ones, resp, NT, preferred_element_type=jnp.float32)
        count_ref[0, slot : slot + 1] = counts[0:1]


def responsibilities(rows, pos, nat, consts, weights):
    count = rows.shape[0] // RB
    feature_count = rows.shape[1]
    shards, held = len(weights), weights[0].shape[1]
    pairs = count * CANDS
    grid_spec = pltpu.PrefetchScalarGridSpec(
        num_scalar_prefetch=2,
        grid=(count,),
        in_specs=[
            pl.BlockSpec((RB, feature_count), lambda i, *_: (i, 0)),
            pl.BlockSpec(consts.shape, lambda i, *_: (0, 0, 0)),
        ]
        + [pl.BlockSpec(memory_space=pl.ANY)] * shards,
        out_specs=[
            pl.BlockSpec((1, CANDS, CB, RB), lambda i, *_: (i, 0, 0, 0)),
            pl.BlockSpec((1, 1, RB), lambda i, *_: (i, 0, 0)),
            pl.BlockSpec((1, CANDS, CB), lambda i, *_: (i, 0, 0)),
        ],
        scratch_shapes=[
            pltpu.VMEM((shards,) + weights[0].shape, jnp.bfloat16),
            pltpu.SemaphoreType.DMA((shards,)),
        ],
    )
    return pl.pallas_call(
        functools.partial(density_body, shards, held),
        grid_spec=grid_spec,
        out_shape=[
            jax.ShapeDtypeStruct((count, CANDS, CB, RB), jnp.bfloat16),
            jax.ShapeDtypeStruct((count, 1, RB), jnp.float32),
            jax.ShapeDtypeStruct((count, CANDS, CB), jnp.float32),
        ],
        compiler_params=pltpu.CompilerParams(
            dimension_semantics=("arbitrary",), vmem_limit_bytes=VMEM_LIMIT
        ),
        cost_estimate=pl.CostEstimate(
            flops=pairs * 4 * CB * RB * feature_count,
            bytes_accessed=shards * weights[0].size * 2 + rows.size * 4,
            transcendentals=pairs * CB * RB,
        ),
        name="responsibilities",
    )(pos, nat, rows, consts, *weights)


def moment_body(first, shards, held, counts, pos_ref, *rest):
    parts = len(counts)
    row_refs, resp_refs = rest[:parts], rest[parts : 2 * parts]
    out_refs = rest[2 * parts : 2 * parts + shards]
    rows, resp, sums, sems = rest[2 * parts + shards :]
    copies = []
    start = 0
    for j in range(parts):
        here = pl.ds(start, counts[j])
        copies.append(
            (
                pltpu.make_async_copy(row_refs[j], rows.at[here], sems.at[0, j]),
                pltpu.make_async_copy(resp_refs[j], resp.at[here], sems.at[1, j]),
            )
        )
        start += counts[j]
    for pair in copies:
        for copy in pair:
            copy.start()
    sums[...] = jnp.zeros_like(sums)
    start = 0
    for j in range(parts):
        for copy in copies[j]:
            copy.wait()

        @pl.loop(start, start + counts[j])
        def _(i):
            for slot in range(CANDS):
                local = pos_ref[i, slot] - first * held

                @pl.when(jnp.logical_and(local >= 0, local < shards * held))
                def _():
                    x = rows[i]
                    weight = resp[i, slot]
                    sums[local, 0] += jnp.dot(weight, x, preferred_element_type=jnp.float32)
                    sums[local, 1] += jnp.dot(
                        weight, square_of(x), preferred_element_type=jnp.float32
                    )

        start += counts[j]
    for j in range(shards):
        for b in range(held):
            for m in range(2):
                out_refs[j][m, b] = sums[j * held + b, m].astype(jnp.bfloat16)


def moments(rows, resp, pos, held, first, shards):
    counts = tuple(r.shape[0] for r in rows)
    feature_count = rows[0].shape[2]
    total = sum(counts)
    any_spec = pl.BlockSpec(memory_space=pl.ANY)
    pairs = total * shards * held // 8
    return pl.pallas_call(
        functools.partial(moment_body, first, shards, held, counts),
        in_specs=[pl.BlockSpec(memory_space=pltpu.SMEM)] + [any_spec] * (2 * len(counts)),
        out_specs=[pl.BlockSpec(memory_space=pltpu.VMEM)] * shards,
        out_shape=[jax.ShapeDtypeStruct((2, held, CB, feature_count), jnp.bfloat16)] * shards,
        scratch_shapes=[
            pltpu.VMEM((total, RB, feature_count), jnp.bfloat16),
            pltpu.VMEM((total, CANDS, CB, RB), jnp.bfloat16),
            pltpu.VMEM((shards * held, 2, CB, feature_count), jnp.float32),
            pltpu.SemaphoreType.DMA((2, len(counts))),
        ],
        compiler_params=pltpu.CompilerParams(vmem_limit_bytes=VMEM_LIMIT),
        cost_estimate=pl.CostEstimate(
            flops=pairs * 4 * CB * RB * feature_count,
            bytes_accessed=total * RB * (feature_count + CANDS * CB) * 2,
            transcendentals=0,
        ),
        name="moments",
    )(pos, *rows, *resp)


def in_blocks(rows):
    return rows.reshape(rows.shape[0] // RB, RB, rows.shape[1])


def summed_counts(counts, ids, group_blocks):
    spread = (jnp.arange(group_blocks, dtype=jnp.int32)[:, None] == ids.reshape(1, -1)).astype(
        jnp.float32
    )
    return jnp.dot(spread, counts.reshape(-1, CB), precision=lax.Precision.HIGHEST)


def plain_plan(points, ids, weights, consts):
    dp_size = lax.axis_size("dp")
    held, feature_count = weights.shape[1], weights.shape[3]
    group_blocks = dp_size * held
    all_weights = lax.all_gather(weights, "dp", axis=0)
    all_consts = lax.all_gather(consts, "dp", axis=0, tiled=True)
    const_columns = all_consts.reshape(group_blocks, CB, 1)
    resp, norm, counts = responsibilities(
        points, ids, ids, const_columns, [all_weights[j] for j in range(dp_size)]
    )
    sums = []
    for j in range(dp_size):
        sums += moments([in_blocks(points)], [resp], ids, held, j, 1)
    total = lax.psum_scatter(jnp.stack(sums), "dp", scatter_dimension=0).astype(jnp.float32)
    count_sum = lax.psum_scatter(
        summed_counts(counts, ids, group_blocks), "dp", scatter_dimension=0, tiled=True
    )
    total = total.reshape(2, held * CB, feature_count)
    return count_sum.reshape(-1), total[0], total[1], norm.reshape(-1)


def line_pairs(links):
    return [(2 * a + c, 2 * b + c) for a, b in links for c in (0, 1)]


INWARD = line_pairs(((0, 1), (3, 2)))
OUTWARD = line_pairs(((1, 0), (2, 3)))
MIDDLE = line_pairs(((1, 2), (2, 1)))
CORES = [(2, 3), (3, 2), (4, 5), (5, 4)]


def move(value, pairs):
    return lax.ppermute(value, "dp", pairs)


def after(value, *others):
    return lax.optimization_barrier((value,) + others)[0]


def line_plan(points, ids, weights, consts):
    held, feature_count = weights.shape[1], weights.shape[3]
    group_blocks = 8 * held
    index = lax.axis_index("dp")
    chip, core = index // 2, index % 2
    row_blocks = points.shape[0] // RB
    late_blocks = row_blocks // 4
    cut = (row_blocks - late_blocks) * RB

    outer = move(weights, INWARD)
    across = move(weights, MIDDLE)
    early_rows = move(after(points[:cut], outer), INWARD)
    far = move(outer, MIDDLE)
    late_rows = move(after(points[cut:], early_rows), INWARD)
    shared = [move(w, CORES) for w in (weights, outer, across, far)]
    near = [weights, outer, across, far]
    shards = [w for pair in zip(near, shared) for w in pair]

    small = jnp.concatenate([consts, ids.reshape(-1).astype(jnp.float32)])
    all_small = lax.all_gather(small, "dp", axis=0)
    const_columns = all_small[:, : consts.shape[0]].reshape(group_blocks, CB, 1)
    all_ids = all_small[:, consts.shape[0] :].astype(jnp.int32)
    end_chip = jnp.where(chip < 2, 0, 3)
    end_ids = lax.dynamic_index_in_dim(all_ids, 2 * end_chip + core, 0, keepdims=False)
    end_ids = end_ids.reshape(row_blocks, CANDS)

    def place(nat):
        holder = nat // held
        z = jnp.where(chip < 2, holder // 2, 3 - holder // 2)
        z = jnp.where(z == 0, 1, jnp.where(z == 1, 0, z))
        other = (holder % 2 + core) % 2
        return (z * 2 + other) * held + nat % held

    early_ids, late_ids = end_ids[: row_blocks - late_blocks], end_ids[row_blocks - late_blocks :]
    runs = [(points, ids), (early_rows, early_ids), (late_rows, late_ids)]
    results = [responsibilities(r, place(i), i, const_columns, shards) for r, i in runs]
    rows = [in_blocks(r) for r, _ in runs]
    resp = [r[0] for r in results]
    all_nat = jnp.concatenate([i for _, i in runs])
    all_pos = place(all_nat)

    def both_cores(place_of):
        other = moments(rows, resp, all_pos, held, 2 * place_of + 1, 1)[0]
        received = move(other, CORES)
        own = moments(rows, resp, all_pos, held, 2 * place_of, 1)[0]
        return own.astype(jnp.float32) + received.astype(jnp.float32)

    far_sum = move(both_cores(3).astype(jnp.bfloat16), MIDDLE)
    across_sum = move(both_cores(2).astype(jnp.bfloat16), MIDDLE)
    outer_sum = (both_cores(1) + far_sum.astype(jnp.float32)).astype(jnp.bfloat16)
    end_sum = move(outer_sum, OUTWARD)
    own_sum = both_cores(0) + across_sum.astype(jnp.float32)
    is_end = jnp.logical_or(chip == 0, chip == 3)
    total = jnp.where(is_end, end_sum.astype(jnp.float32), own_sum)
    total = total.reshape(2, held * CB, feature_count)

    counts = jnp.concatenate([r[2] for r in results])
    counts = jnp.where(is_end, 0.0, summed_counts(counts, all_nat, group_blocks))
    counts = lax.psum(counts, "dp")
    counts = lax.dynamic_slice_in_dim(counts, index * held, held, 0)

    end_norm = jnp.concatenate([results[1][1], results[2][1]]).reshape(-1)
    norm = jnp.where(is_end, move(end_norm, OUTWARD), results[0][1].reshape(-1))
    return counts.reshape(-1), total[0], total[1], norm


def on_device(points, candidates, means, inv_var, log_weight):
    feature_count = points.shape[1]
    owner_count = lax.axis_size("comp")
    held = means.shape[0] // CB
    scaled = (inv_var.astype(jnp.float32) * means.astype(jnp.float32)).astype(jnp.bfloat16)
    weights = jnp.stack([scaled, inv_var]).reshape(2, held, CB, feature_count)
    consts = component_consts(means, inv_var, log_weight)
    ids = candidates // (owner_count * held) * held + candidates % held
    plan = line_plan if lax.axis_size("dp") == 8 else plain_plan
    counts, first, second, norm = plan(points, ids, weights, consts)
    return counts, first, second, norm / feature_count


def solution(mesh):
    return jax.shard_map(
        on_device,
        mesh=mesh,
        in_specs=(
            P(("dp", "comp"), None),
            P(("dp", "comp"), None),
            P(("dp", "comp"), None),
            P(("dp", "comp"), None),
            P(("dp", "comp")),
        ),
        out_specs=(
            P(("dp", "comp")),
            P(("dp", "comp"), None),
            P(("dp", "comp"), None),
            P(("dp", "comp")),
        ),
        check_vma=False,
    )
```

time: 655 us -> 351 us (0.54)
  waiting for transfers between devices: 355 us -> 31 us
  matrix products: 137 us -> 0.14 us
  Pallas kernels: 0 us -> 133 us
  blocking collectives: 29.3 us -> 124 us
  local copies, waits for them, and re-layouts: 84.5 us -> 10.6 us
  starting transfers between devices: 0.11 us -> 33.8 us
  other arithmetic: 32.9 us -> 14.4 us
  between operations: 14.5 us -> 1.75 us
    unnamed x4 -> x0, waiting for transfers between devices: 238 us -> none
    dot_general x40 -> x1, matrix products: 137 us -> 0.14 us  [summed_counts(): jnp.dot(spread, counts.reshape(-1, CB), precision=lax.Precision.HIGHEST)]
    pallas_call x0 -> x11, Pallas kernels: none -> 133 us  [the longest x8 81.2 us: moments(): pl.pallas_call(functools.partial(moment_body, first, shards, held, counts...]
    all_gather x2 -> x0, waiting for transfers between devices: 118 us -> none  [the longest x1 65.1 us: on_device(): lax.all_gather(means, 'dp', axis=0, tiled=True)]
    while x64 -> x0, local copies, waits for them, and re-layouts: 63.1 us -> none
    psum x0 -> x1, blocking collectives: none -> 63 us  [line_plan(): counts = lax.psum(counts, 'dp')]
    unnamed x1, blocking collectives: 15 us -> 61.1 us
    ppermute x0 -> x17, starting transfers between devices: none -> 33.8 us  [move(): return lax.ppermute(value, 'dp', pairs)]
  transfers between devices with their start and end apart: 3 -> 17, of which waited for: 3 -> 1; matrix products, arithmetic and copies ran while one was open for 0% -> 5% of each run, Pallas kernels for 0% -> 31%
where the time goes in v1:
time: 351 us; the launch traced here: 349 us
  Pallas kernels  133 us (38%)
  blocking collectives  124 us (35%)
  starting transfers between devices  33.8 us (10%)
  waiting for transfers between devices  31 us (9%)
  other arithmetic  14.4 us (4%)
  local copies, waits for them, and re-layouts  10.6 us (3%)
    pallas_call x8, Pallas kernels, moments(): pl.pallas_call(functools.partial(moment_body, first, shards, held, counts...  81.2 us
    psum x1, blocking collectives, line_plan(): counts = lax.psum(counts, 'dp')  63 us
    unnamed x1, blocking collectives  61.1 us
    pallas_call x3, Pallas kernels, responsibilities(): pl.pallas_call(functools.partial(density_body, shards, held), grid_spec=g...  52 us
    ppermute x17, starting transfers between devices, move(): return lax.ppermute(value, 'dp', pairs)  33.8 us
    ppermute x17, waiting for transfers between devices, move(): return lax.ppermute(value, 'dp', pairs)  31 us
  transfers between devices with their start and end apart: 17, of which 1 were waited for; matrix products, arithmetic and copies ran while one was open for 5% of the time, Pallas kernels for 31%

profile of v1, /device:TPU:0, one launch (start us, length us, event | category | flops | bytes accessed | tf_op | source)
XLA Modules:
  0.0 349.0 jit_solution(14517962561633250786)
XLA Ops:
  0.6 2.1 fusion.1
  2.7 1.3 pad_maximum_fusion.rest_0_
  4.0 6.2 %collective-permute-start.1 = (bf16[2,4,128,768]{3,2,1,0:T(8,128)(2,1)}, bf16[2,4,128,768]{3,2,1,0:T(8,128)(2,1)}, u32[]{:S(2)}, u32[]{:S(2)}) collective-permute-start(bf16[2,4,128,768]{3,2,1,0:T(8,128)(2,1)} %pad_maximum_fusion.rest_0_), channel_id=1, source_target_pairs={{0,8},{4,12},{24,16},{28,20},{1,9},{5,13},{25,17},{29,21},{2,10},{... | collective-permute-start | bytes 4718600 | tf_op jit(solution)/shard_map/ppermute | solution.py:235
  10.2 1.9 collective-permute-start.3
  12.1 30.9 %collective-permute-done.1.rest_2_ = bf16[2,4,128,768]{3,2,1,0:T(8,128)(2,1)} collective-permute-done((bf16[2,4,128,768]{3,2,1,0:T(8,128)(2,1)}, bf16[2,4,128,768]{3,2,1,0:T(8,128)(2,1)}, u32[]{:S(2)}, u32[]{:S(2)}) %collective-permute-start.1) | collective-permute-done | bytes 1572896 | tf_op jit(solution)/shard_map/ppermute | solution.py:235
  43.0 1.8 collective-permute-start.5
  44.8 1.6 slice.38
  46.4 7.6 %collective-permute-start.7 = (bf16[1536,768]{1,0:T(8,128)(2,1)}, bf16[1536,768]{1,0:T(8,128)(2,1)}, u32[]{:S(2)}, u32[]{:S(2)}) collective-permute-start(bf16[1536,768]{1,0:T(8,128)(2,1)} %slice.38), channel_id=1, source_target_pairs={{0,8},{4,12},{24,16},{28,20},{1,9},{5,13},{25,17},{29,21},{2,10},{... | collective-permute-start | bytes 7077896 | tf_op jit(solution)/shard_map/ppermute | solution.py:235
  54.1 1.9 collective-permute-start
  56.0 1.8 collective-permute-start.2
  57.8 1.8 collective-permute-start.4
  59.6 1.8 collective-permute-start.6
  64.5 61.1 %all-reduce = f32[4608]{0:T(1024)S(1)} all-reduce(f32[4608]{0:T(1024)S(1)} %maximum_dynamic-update-slice_fusion), channel_id=2, replica_groups=mesh['dp'=8,'comp'=4] {'dp'}, use_global_device_ids=true, to_apply=%add | all-reduce | flops 4608 | bytes 36864
  126.6 1.3 collective-permute-start.8
  128.6 3.3 reshape.64.const_ref
  132.7 18.6 %responsibilities.4 = (bf16[12,4,128,128]{3,2,1,0:T(8,128)(2,1)}, f32[12,1,128]{2,1,0:T(1,128)}, f32[12,4,128]{2,1,0:T(4,128)}) custom-call(s32[12,4]{1,0:T(8,128)} %fusion.24.pos_ref, s32[12,4]{1,0:T(8,128)} %copy-done.6, bf16[1536,768]{1,0:T(8,128)(2,1)} %collective-permute-done.7.x_ref, f32[32,128,1]{2,1,0:T(8,128)} %reshape.64.const_ref, ...), custom_call_target="tpu_custom_call" | custom-call | flops 2415919104 | bytes 17301504 | tf_op jit(solution)/shard_map/responsibilities/pallas_call | solution.py:99
  151.3 22.2 %responsibilities.3 = (bf16[16,4,128,128]{3,2,1,0:T(8,128)(2,1)}, f32[16,1,128]{2,1,0:T(1,128)}, f32[16,4,128]{2,1,0:T(4,128)}) custom-call(s32[16,4]{1,0:T(8,128)} %get-tuple-element.30.pos_ref, s32[16,4]{1,0:T(8,128)} %copy-done.5, bf16[2048,768]{1,0:T(8,128)(2,1)} %x_ref.1, f32[32,128,1]{2,1,0:T(8,128)} %reshape.64.const_ref, ...), custom_call_target="tpu_custom_call" | custom-call | flops 3221225472 | bytes 18874368 | tf_op jit(solution)/shard_map/responsibilities/pallas_call | solution.py:99
  174.4 11.2 %responsibilities.5 = (bf16[4,4,128,128]{3,2,1,0:T(8,128)(2,1)}, f32[4,1,128]{2,1,0:T(1,128)}, f32[4,4,128]{2,1,0:T(4,128)}) custom-call(s32[4,4]{1,0:T(4,128)} %fusion.40.pos_ref, s32[4,4]{1,0:T(4,128)} %copy-done.7, bf16[512,768]{1,0:T(8,128)(2,1)} %copy-done.1, f32[32,128,1]{2,1,0:T(8,128)} %reshape.64.const_ref, ...), custom_call_target="tpu_custom_call" | custom-call | flops 805306368 | bytes 14155776 | tf_op jit(solution)/shard_map/responsibilities/pallas_call | solution.py:99
  185.6 12.1 %moments.11 = bf16[2,4,128,768]{3,2,1,0:T(8,128)(2,1)} custom-call(s32[32,4]{1,0:T(8,128)} %get-tuple-element.28.pos_ref, bf16[16,128,768]{2,1,0:T(8,128)(2,1)} %bitcast.14, bf16[12,128,768]{2,1,0:T(8,128)(2,1)} %bitcast.6.rest_1_, bf16[4,128,768]{2,1,0:T(8,128)(2,1)} %bitcast.22, bf16[16,4,128,128]{3,2,1,0:T(8,128)(2,1)} %get-tuple-element.20.rest_3_, ...), custom_call_target="tpu_custom_call" | custom-call | flops 805306368 | bytes 10485760 | tf_op jit(solution)/shard_map/moments/pallas_call | solution.py:171
  198.7 6.6 %moments.9 = bf16[2,4,128,768]{3,2,1,0:T(8,128)(2,1)} custom-call(s32[32,4]{1,0:T(8,128)} %get-tuple-element.28.pos_ref, bf16[16,128,768]{2,1,0:T(8,128)(2,1)} %bitcast.15, bf16[12,128,768]{2,1,0:T(8,128)(2,1)} %bitcast.6.rest_1_, bf16[4,128,768]{2,1,0:T(8,128)(2,1)} %bitcast.23, bf16[16,4,128,128]{3,2,1,0:T(8,128)(2,1)} %get-tuple-element.20.rest_3_, ...), custom_call_target="tpu_custom_call" | custom-call | flops 805306368 | bytes 10485760 | tf_op jit(solution)/shard_map/moments/pallas_call | solution.py:171
  205.3 9.1 %moments.10 = bf16[2,4,128,768]{3,2,1,0:T(8,128)(2,1)} custom-call(s32[32,4]{1,0:T(8,128)} %get-tuple-element.28.pos_ref, bf16[16,128,768]{2,1,0:T(8,128)(2,1)} %bitcast.16, bf16[12,128,768]{2,1,0:T(8,128)(2,1)} %bitcast.6.rest_1_, bf16[4,128,768]{2,1,0:T(8,128)(2,1)} %bitcast.24, bf16[16,4,128,128]{3,2,1,0:T(8,128)(2,1)} %get-tuple-element.20.rest_3_, ...), custom_call_target="tpu_custom_call" | custom-call | flops 805306368 | bytes 10485760 | tf_op jit(solution)/shard_map/moments/pallas_call | solution.py:171
  214.5 10.7 %moments.15 = bf16[2,4,128,768]{3,2,1,0:T(8,128)(2,1)} custom-call(s32[32,4]{1,0:T(8,128)} %get-tuple-element.28.pos_ref, bf16[16,128,768]{2,1,0:T(8,128)(2,1)} %bitcast.17, bf16[12,128,768]{2,1,0:T(8,128)(2,1)} %bitcast.6.rest_1_, bf16[4,128,768]{2,1,0:T(8,128)(2,1)} %bitcast.25, bf16[16,4,128,128]{3,2,1,0:T(8,128)(2,1)} %get-tuple-element.20.rest_3_, ...), custom_call_target="tpu_custom_call" | custom-call | flops 805306368 | bytes 10485760 | tf_op jit(solution)/shard_map/moments/pallas_call | solution.py:171
  228.2 10.7 %moments.13 = bf16[2,4,128,768]{3,2,1,0:T(8,128)(2,1)} custom-call(s32[32,4]{1,0:T(8,128)} %get-tuple-element.28.pos_ref, bf16[16,128,768]{2,1,0:T(8,128)(2,1)} %bitcast.18, bf16[12,128,768]{2,1,0:T(8,128)(2,1)} %bitcast.6.rest_1_, bf16[4,128,768]{2,1,0:T(8,128)(2,1)} %bitcast.26, bf16[16,4,128,128]{3,2,1,0:T(8,128)(2,1)} %get-tuple-element.20.rest_3_, ...), custom_call_target="tpu_custom_call" | custom-call | flops 805306368 | bytes 10485760 | tf_op jit(solution)/shard_map/moments/pallas_call | solution.py:171
  239.6 11.2 %moments.8 = bf16[2,4,128,768]{3,2,1,0:T(8,128)(2,1)} custom-call(s32[32,4]{1,0:T(8,128)} %get-tuple-element.28.pos_ref, bf16[16,128,768]{2,1,0:T(8,128)(2,1)} %bitcast.19, bf16[12,128,768]{2,1,0:T(8,128)(2,1)} %bitcast.6.rest_1_, bf16[4,128,768]{2,1,0:T(8,128)(2,1)} %bitcast.27, bf16[16,4,128,128]{3,2,1,0:T(8,128)(2,1)} %get-tuple-element.20.rest_3_, ...), custom_call_target="tpu_custom_call" | custom-call | flops 805306368 | bytes 10485760 | tf_op jit(solution)/shard_map/moments/pallas_call | solution.py:171
  250.8 10.1 %moments.14 = bf16[2,4,128,768]{3,2,1,0:T(8,128)(2,1)} custom-call(s32[32,4]{1,0:T(8,128)} %get-tuple-element.28.pos_ref, bf16[16,128,768]{2,1,0:T(8,128)(2,1)} %bitcast.20, bf16[12,128,768]{2,1,0:T(8,128)(2,1)} %bitcast.6.rest_1_, bf16[4,128,768]{2,1,0:T(8,128)(2,1)} %bitcast.28, bf16[16,4,128,128]{3,2,1,0:T(8,128)(2,1)} %get-tuple-element.20.rest_3_, ...), custom_call_target="tpu_custom_call" | custom-call | flops 805306368 | bytes 10485760 | tf_op jit(solution)/shard_map/moments/pallas_call | solution.py:171
  260.9 3.0 add_convert_fusion
  264.9 1.8 add_convert_fusion.1
  268.1 1.3 collective-permute-start.16
  269.6 63.0 %psum.7 = f32[32,128]{1,0:T(8,128)S(1)} all-reduce(f32[32,128]{1,0:T(8,128)S(1)} %convolution_select_fusion), channel_id=1, replica_groups=mesh['dp'=8,'comp'=4] {'dp'}, use_global_device_ids=true, to_apply=%region_2.3 | all-reduce | flops 4096 | bytes 32768 | tf_op jit(solution)/shard_map/psum | solution.py:300
  333.2 10.7 %moments.12 = bf16[2,4,128,768]{3,2,1,0:T(8,128)(2,1)} custom-call(s32[32,4]{1,0:T(8,128)} %get-tuple-element.28.pos_ref, bf16[16,128,768]{2,1,0:T(8,128)(2,1)} %bitcast.21, bf16[12,128,768]{2,1,0:T(8,128)(2,1)} %bitcast.6.rest_1_, bf16[4,128,768]{2,1,0:T(8,128)(2,1)} %bitcast.29, bf16[16,4,128,128]{3,2,1,0:T(8,128)(2,1)} %get-tuple-element.20.rest_3_, ...), custom_call_target="tpu_custom_call" | custom-call | flops 805306368 | bytes 10485760 | tf_op jit(solution)/shard_map/moments/pallas_call | solution.py:171
  344.5 2.6 add_select_fusion
  347.1 1.9 fusion.46
  (84 shorter events, 14.0 us)
Async XLA Ops:
  2.7 42.1 %copy-start = (bf16[2048,768]{1,0:T(8,128)(2,1)S(1)}, bf16[2048,768]{1,0:T(8,128)(2,1)}, u32[]{:S(2)}) copy-start(bf16[2048,768]{1,0:T(8,128)(2,1)} %x_ref.1) | copy-start | bytes 9437188
  4.0 51.9 %copy-start.13 = (s32[16,4]{0,1:T(4,128)S(1)}, s32[16,4]{0,1:T(4,128)}, u32[]{:S(2)}) copy-start(s32[16,4]{0,1:T(4,128)} %param.6) | copy-start | bytes 772
  4.0 39.0 %collective-permute-start.1 = (bf16[2,4,128,768]{3,2,1,0:T(8,128)(2,1)}, bf16[2,4,128,768]{3,2,1,0:T(8,128)(2,1)}, u32[]{:S(2)}, u32[]{:S(2)}) collective-permute-start(bf16[2,4,128,768]{3,2,1,0:T(8,128)(2,1)} %pad_maximum_fusion.rest_0_), channel_id=1, source_target_pairs={{0,8},{4,12},{24,16},{28,20},{1,9},{5,13},{25,17},{29,21},{2,10},{... | collective-permute-start | bytes 4718600 | tf_op jit(solution)/shard_map/ppermute | solution.py:235
  10.2 47.6 %collective-permute-start.3 = (bf16[2,4,128,768]{3,2,1,0:T(8,128)(2,1)}, bf16[2,4,128,768]{3,2,1,0:T(8,128)(2,1)}, u32[]{:S(2)}, u32[]{:S(2)}) collective-permute-start(bf16[2,4,128,768]{3,2,1,0:T(8,128)(2,1)} %pad_maximum_fusion.rest_0_), channel_id=1, source_target_pairs={{8,16},{12,20},{16,8},{20,12},{9,17},{13,21},{17,9},{21,13},{10,18... | collective-permute-start | bytes 4718600 | tf_op jit(solution)/shard_map/ppermute | solution.py:235
  43.0 16.6 %collective-permute-start.5 = (bf16[2,4,128,768]{3,2,1,0:T(8,128)(2,1)}, bf16[2,4,128,768]{3,2,1,0:T(8,128)(2,1)}, u32[]{:S(2)}, u32[]{:S(2)}) collective-permute-start(bf16[2,4,128,768]{3,2,1,0:T(8,128)(2,1)} %collective-permute-done.1.rest_2_), channel_id=1, source_target_pairs={{8,16},{12,20},{16,8},{20,12},{9,17},{13,21},{17,9},{21,13},{10,18... | collective-permute-start | bytes 4718600 | tf_op jit(solution)/shard_map/ppermute | solution.py:235
  46.4 16.7 %copy-start.16 = (u32[32]{0:T(128)S(1)}, u32[32]{0:T(128)}, u32[]{:S(2)}) copy-start(u32[32]{0:T(128)} %constant.239) | copy-start | bytes 388
  46.4 18.0 %copy-start.15 = (bf16[512]{0:T(512)(128)(2,1)S(1)}, bf16[512]{0:T(512)(128)(2,1)}, u32[]{:S(2)}) copy-start(bf16[512]{0:T(512)(128)(2,1)} %param.9) | copy-start | bytes 3076
  46.4 80.2 %collective-permute-start.7 = (bf16[1536,768]{1,0:T(8,128)(2,1)}, bf16[1536,768]{1,0:T(8,128)(2,1)}, u32[]{:S(2)}, u32[]{:S(2)}) collective-permute-start(bf16[1536,768]{1,0:T(8,128)(2,1)} %slice.38), channel_id=1, source_target_pairs={{0,8},{4,12},{24,16},{28,20},{1,9},{5,13},{25,17},{29,21},{2,10},{... | collective-permute-start | bytes 7077896 | tf_op jit(solution)/shard_map/ppermute | solution.py:235
  54.1 78.6 %collective-permute-start = (bf16[2,4,128,768]{3,2,1,0:T(8,128)(2,1)}, bf16[2,4,128,768]{3,2,1,0:T(8,128)(2,1)}, u32[]{:S(2)}, u32[]{:S(2)}) collective-permute-start(bf16[2,4,128,768]{3,2,1,0:T(8,128)(2,1)} %pad_maximum_fusion.rest_0_), channel_id=1, source_target_pairs={{8,12},{12,8},{16,20},{20,16},{9,13},{13,9},{17,21},{21,17},{10,14... | collective-permute-start | bytes 4718600 | tf_op jit(solution)/shard_map/ppermute | solution.py:235
  56.0 76.6 %collective-permute-start.2 = (bf16[2,4,128,768]{3,2,1,0:T(8,128)(2,1)}, bf16[2,4,128,768]{3,2,1,0:T(8,128)(2,1)}, u32[]{:S(2)}, u32[]{:S(2)}) collective-permute-start(bf16[2,4,128,768]{3,2,1,0:T(8,128)(2,1)} %collective-permute-done.1.rest_2_), channel_id=1, source_target_pairs={{8,12},{12,8},{16,20},{20,16},{9,13},{13,9},{17,21},{21,17},{10,14... | collective-permute-start | bytes 4718600 | tf_op jit(solution)/shard_map/ppermute | solution.py:235
  57.8 74.8 %collective-permute-start.4 = (bf16[2,4,128,768]{3,2,1,0:T(8,128)(2,1)}, bf16[2,4,128,768]{3,2,1,0:T(8,128)(2,1)}, u32[]{:S(2)}, u32[]{:S(2)}) collective-permute-start(bf16[2,4,128,768]{3,2,1,0:T(8,128)(2,1)} %collective-permute-done.3.rest_4_), channel_id=1, source_target_pairs={{8,12},{12,8},{16,20},{20,16},{9,13},{13,9},{17,21},{21,17},{10,14... | collective-permute-start | bytes 4718600 | tf_op jit(solution)/shard_map/ppermute | solution.py:235
  59.6 73.0 %collective-permute-start.6 = (bf16[2,4,128,768]{3,2,1,0:T(8,128)(2,1)}, bf16[2,4,128,768]{3,2,1,0:T(8,128)(2,1)}, u32[]{:S(2)}, u32[]{:S(2)}) collective-permute-start(bf16[2,4,128,768]{3,2,1,0:T(8,128)(2,1)} %collective-permute-done.5.rest_6_), channel_id=1, source_target_pairs={{8,12},{12,8},{16,20},{20,16},{9,13},{13,9},{17,21},{21,17},{10,14... | collective-permute-start | bytes 4718600 | tf_op jit(solution)/shard_map/ppermute | solution.py:235
  62.1 69.9 %copy-start.5 = (s32[16,4]{1,0:T(8,128)}, s32[16,4]{1,0:T(8,128)S(1)}, u32[]{:S(2)}) copy-start(s32[16,4]{1,0:T(8,128)S(1)} %get-tuple-element.31.nat_ref) | copy-start | bytes 772
  125.8 6.8 %copy-start.6 = (s32[12,4]{1,0:T(8,128)}, s32[12,4]{1,0:T(8,128)S(1)}, u32[]{:S(2)}) copy-start(s32[12,4]{1,0:T(8,128)S(1)} %slice.34.nat_ref) | copy-start | bytes 580
  126.0 25.2 %copy-start.7 = (s32[4,4]{1,0:T(4,128)}, s32[4,4]{1,0:T(4,128)S(1)}, u32[]{:S(2)}) copy-start(s32[4,4]{1,0:T(4,128)S(1)} %slice.36.nat_ref) | copy-start | bytes 196
  126.6 46.8 %collective-permute-start.8 = (bf16[512,768]{1,0:T(8,128)(2,1)}, bf16[512,768]{1,0:T(8,128)(2,1)S(1)}, u32[]{:S(2)}, u32[]{:S(2)}) collective-permute-start(bf16[512,768]{1,0:T(8,128)(2,1)} %slice.39), channel_id=1, source_target_pairs={{0,8},{4,12},{24,16},{28,20},{1,9},{5,13},{25,17},{29,21},{2,10},{... | collective-permute-start | bytes 2359304 | tf_op jit(solution)/shard_map/ppermute | solution.py:235
  197.7 29.0 %collective-permute-start.10 = (bf16[2,4,128,768]{3,2,1,0:T(8,128)(2,1)}, bf16[2,4,128,768]{3,2,1,0:T(8,128)(2,1)S(1)}, u32[]{:S(2)}, u32[]{:S(2)}) collective-permute-start(bf16[2,4,128,768]{3,2,1,0:T(8,128)(2,1)} %moments.11), channel_id=1, source_target_pairs={{8,12},{12,8},{16,20},{20,16},{9,13},{13,9},{17,21},{21,17},{10,14... | collective-permute-start | bytes 4718600 | tf_op jit(solution)/shard_map/ppermute | solution.py:235
  214.5 12.3 %copy-start.3 = (bf16[2,4,128,768]{3,2,1,0:T(8,128)(2,1)S(1)}, bf16[2,4,128,768]{3,2,1,0:T(8,128)(2,1)}, u32[]{:S(2)}) copy-start(bf16[2,4,128,768]{3,2,1,0:T(8,128)(2,1)} %moments.10) | copy-start | bytes 4718596
  225.2 35.7 %collective-permute-start.14 = (bf16[2,4,128,768]{3,2,1,0:T(8,128)(2,1)}, bf16[2,4,128,768]{3,2,1,0:T(8,128)(2,1)S(1)}, u32[]{:S(2)}, u32[]{:S(2)}) collective-permute-start(bf16[2,4,128,768]{3,2,1,0:T(8,128)(2,1)} %moments.15), channel_id=1, source_target_pairs={{8,12},{12,8},{16,20},{20,16},{9,13},{13,9},{17,21},{21,17},{10,14... | collective-permute-start | bytes 4718600 | tf_op jit(solution)/shard_map/ppermute | solution.py:235
  226.0 38.9 %collective-permute-start.9 = (bf16[2,4,128,768]{3,2,1,0:T(8,128)(2,1)}, bf16[2,4,128,768]{3,2,1,0:T(8,128)(2,1)S(1)}, u32[]{:S(2)}, u32[]{:S(2)}) collective-permute-start(bf16[2,4,128,768]{3,2,1,0:T(8,128)(2,1)} %moments.9), channel_id=1, source_target_pairs={{8,12},{12,8},{16,20},{20,16},{9,13},{13,9},{17,21},{21,17},{10,14... | collective-permute-start | bytes 4718600 | tf_op jit(solution)/shard_map/ppermute | solution.py:235
  227.2 37.7 %collective-permute-start.11 = (bf16[2,4,128,768]{3,2,1,0:T(8,128)(2,1)S(1)}, bf16[2,4,128,768]{3,2,1,0:T(8,128)(2,1)S(1)}, u32[]{:S(2)}, u32[]{:S(2)}) collective-permute-start(bf16[2,4,128,768]{3,2,1,0:T(8,128)(2,1)S(1)} %add_convert_fusion.2), channel_id=1, source_target_pairs={{8,16},{12,20},{16,8},{20,12},{9,17},{13,21},{17,9},{21,13},{10,18... | collective-permute-start | bytes 4718600 | tf_op jit(solution)/shard_map/ppermute | solution.py:235
  238.8 105.6 %collective-permute-start.13 = (bf16[2,4,128,768]{3,2,1,0:T(8,128)(2,1)}, bf16[2,4,128,768]{3,2,1,0:T(8,128)(2,1)S(1)}, u32[]{:S(2)}, u32[]{:S(2)}) collective-permute-start(bf16[2,4,128,768]{3,2,1,0:T(8,128)(2,1)} %moments.13), channel_id=1, source_target_pairs={{8,12},{12,8},{16,20},{20,16},{9,13},{13,9},{17,21},{21,17},{10,14... | collective-permute-start | bytes 4718600 | tf_op jit(solution)/shard_map/ppermute | solution.py:235
  260.9 4.0 %copy-start.2 = (bf16[2,4,128,768]{3,2,1,0:T(8,128)(2,1)S(1)}, bf16[2,4,128,768]{3,2,1,0:T(8,128)(2,1)}, u32[]{:S(2)}) copy-start(bf16[2,4,128,768]{3,2,1,0:T(8,128)(2,1)} %moments.8) | copy-start | bytes 4718596
  264.0 4.1 %copy-start.12 = (f32[12,1,128]{2,1,0:T(1,128)S(1)}, f32[12,1,128]{2,1,0:T(1,128)}, u32[]{:S(2)}) copy-start(f32[12,1,128]{2,1,0:T(1,128)} %get-tuple-element.23) | copy-start | bytes 18436
  264.0 4.1 %copy-start.14 = (f32[4,1,128]{2,1,0:T(1,128)S(1)}, f32[4,1,128]{2,1,0:T(1,128)}, u32[]{:S(2)}) copy-start(f32[4,1,128]{2,1,0:T(1,128)} %get-tuple-element.24) | copy-start | bytes 6148
  264.0 5.5 %copy-start.8 = (f32[16,4,128]{2,1,0:T(4,128)S(1)}, f32[16,4,128]{2,1,0:T(4,128)}, u32[]{:S(2)}) copy-start(f32[16,4,128]{2,1,0:T(4,128)} %get-tuple-element.15) | copy-start | bytes 98308
  264.0 5.5 %copy-start.9 = (f32[12,4,128]{2,1,0:T(4,128)S(1)}, f32[12,4,128]{2,1,0:T(4,128)}, u32[]{:S(2)}) copy-start(f32[12,4,128]{2,1,0:T(4,128)} %get-tuple-element.17) | copy-start | bytes 73732
  264.0 5.5 %copy-start.11 = (f32[4,4,128]{2,1,0:T(4,128)S(1)}, f32[4,4,128]{2,1,0:T(4,128)}, u32[]{:S(2)}) copy-start(f32[4,4,128]{2,1,0:T(4,128)} %get-tuple-element.19) | copy-start | bytes 24580
  264.0 80.5 %collective-permute-start.15 = (bf16[2,4,128,768]{3,2,1,0:T(8,128)(2,1)}, bf16[2,4,128,768]{3,2,1,0:T(8,128)(2,1)S(1)}, u32[]{:S(2)}, u32[]{:S(2)}) collective-permute-start(bf16[2,4,128,768]{3,2,1,0:T(8,128)(2,1)} %add_convert_fusion), channel_id=1, source_target_pairs={{8,16},{12,20},{16,8},{20,12},{9,17},{13,21},{17,9},{21,13},{10,18... | collective-permute-start | bytes 4718600 | tf_op jit(solution)/shard_map/ppermute | solution.py:235
  266.7 77.8 %collective-permute-start.12 = (bf16[2,4,128,768]{3,2,1,0:T(8,128)(2,1)}, bf16[2,4,128,768]{3,2,1,0:T(8,128)(2,1)}, u32[]{:S(2)}, u32[]{:S(2)}) collective-permute-start(bf16[2,4,128,768]{3,2,1,0:T(8,128)(2,1)} %add_convert_fusion.1), channel_id=1, source_target_pairs={{8,0},{12,4},{16,24},{20,28},{9,1},{13,5},{17,25},{21,29},{10,2},{... | collective-permute-start | bytes 4718600 | tf_op jit(solution)/shard_map/ppermute | solution.py:235
  268.1 75.7 %collective-permute-start.16 = (f32[2048]{0:T(1024)S(1)}, f32[2048]{0:T(1024)S(1)}, u32[]{:S(2)}, u32[]{:S(2)}) collective-permute-start(f32[2048]{0:T(1024)S(1)} %bitcast.36), channel_id=1, source_target_pairs={{8,0},{12,4},{16,24},{20,28},{9,1},{13,5},{17,25},{21,29},{10,2},{... | collective-permute-start | bytes 24584 | tf_op jit(solution)/shard_map/ppermute | solution.py:235
  333.2 10.7 %copy-start.10 = (f32[16,1,128]{2,1,0:T(1,128)S(1)}, f32[16,1,128]{2,1,0:T(1,128)}, u32[]{:S(2)}) copy-start(f32[16,1,128]{2,1,0:T(1,128)} %get-tuple-element.25) | copy-start | bytes 24580
  (2 other events, 3.0 us)

commit v2 on v0

v2 whole, which is shorter than its diff:
```python
import functools
import math

import jax
import jax.numpy as jnp
from jax import lax
from jax.experimental import pallas as pl
from jax.experimental.pallas import tpu as pltpu
from jax.sharding import PartitionSpec as P

CB = 128
RB = 128
CANDS = 4
META = 16
VMEM_LIMIT = 12 * 1024 * 1024
NT = (((1,), (1,)), ((), ()))
TN = (((0,), (0,)), ((), ()))


def square_of(x):
    x_f = x.astype(jnp.float32)
    return (x_f * x_f).astype(jnp.bfloat16)


def in_vmem(value):
    return pltpu.with_memory_space_constraint(value, pltpu.VMEM)


def shard_body(means_ref, inv_ref, log_ref, out_ref):
    owned, feature_count = means_ref.shape
    ones = jnp.ones((META, feature_count), jnp.float32)
    row = lax.broadcasted_iota(jnp.int32, (META, CB), 0)
    out_ref[2 * owned : 2 * owned + META, :] = jnp.zeros((META, feature_count), jnp.bfloat16)
    for block in range(owned // CB):
        here = slice(block * CB, (block + 1) * CB)
        inverse = inv_ref[here, :]
        mean_f = means_ref[here, :].astype(jnp.float32)
        inv_f = inverse.astype(jnp.float32)
        scaled = inv_f * mean_f
        out_ref[here, :] = scaled.astype(jnp.bfloat16)
        out_ref[owned + block * CB : owned + (block + 1) * CB, :] = inverse
        terms = 0.5 * jnp.log(inv_f) - 0.5 * (scaled * mean_f)
        rest = lax.dot_general(
            ones, terms, NT, precision=lax.Precision.HIGHEST, preferred_element_type=jnp.float32
        )
        rest += log_ref[:, here].astype(jnp.float32)
        rest -= 0.5 * feature_count * math.log(2.0 * math.pi)
        high = rest.astype(jnp.bfloat16).astype(jnp.float32)
        rest -= high
        middle = rest.astype(jnp.bfloat16).astype(jnp.float32)
        low = rest - middle
        pieces = jnp.where(row == 0, high, jnp.where(row == 1, middle, low))
        out_ref[2 * owned : 2 * owned + META, here] = pieces.astype(jnp.bfloat16)


def parameter_shard(means, inv_var, log_weight):
    owned, feature_count = means.shape
    vmem = pl.BlockSpec(memory_space=pltpu.VMEM)
    return pl.pallas_call(
        shard_body,
        in_specs=[vmem, vmem, vmem],
        out_specs=vmem,
        out_shape=pltpu.VMEM((2 * owned + META, feature_count), jnp.bfloat16),
        compiler_params=pltpu.CompilerParams(vmem_limit_bytes=VMEM_LIMIT),
        cost_estimate=pl.CostEstimate(
            flops=owned * feature_count * 40,
            bytes_accessed=owned * feature_count * 8,
            transcendentals=owned * feature_count,
        ),
        name="parameter_shard",
    )(in_vmem(means), in_vmem(inv_var), log_weight.reshape(1, owned))


def density_body(count, held, pos_ref, x_ref, weight_ref, resp_ref, norm_ref):
    owned = held * CB
    row_index = lax.broadcasted_iota(jnp.int32, (META, RB), 0)
    pieces = jnp.where(row_index < 3, 1.0, 0.0).astype(jnp.bfloat16)

    @pl.loop(0, count)
    def _(i):
        x = x_ref[pl.ds(pl.multiple_of(i * RB, RB), RB), :]
        half = (square_of(x).astype(jnp.float32) * -0.5).astype(jnp.bfloat16)
        densities = []
        for slot in range(CANDS):
            pos = pos_ref[i, slot]
            shard, start = lax.div(pos, held), lax.rem(pos, held) * CB
            start = pl.multiple_of(start, CB)
            linear = lax.dot_general(
                weight_ref[shard, pl.ds(start, CB), :], x, NT, preferred_element_type=jnp.float32
            )
            quadratic = lax.dot_general(
                weight_ref[shard, pl.ds(owned + start, CB), :],
                half,
                NT,
                preferred_element_type=jnp.float32,
            )
            constant = lax.dot_general(
                weight_ref[shard, 2 * owned : 2 * owned + META, pl.ds(start, CB)],
                pieces,
                TN,
                preferred_element_type=jnp.float32,
            )
            densities.append(linear + quadratic + constant)
        peak = functools.reduce(
            jnp.maximum, [jnp.max(d, axis=0, keepdims=True) for d in densities]
        )
        terms = [jnp.exp(d - peak) for d in densities]
        total = functools.reduce(jnp.add, [jnp.sum(t, axis=0, keepdims=True) for t in terms])
        norm_ref[i] = peak + jnp.log(total)
        inverse_total = 1.0 / total
        for slot in range(CANDS):
            resp_ref[i, slot] = (terms[slot] * inverse_total).astype(jnp.bfloat16)


def responsibilities(rows, pos, weights, held):
    count = rows.shape[0] // RB
    feature_count = rows.shape[1]
    vmem = pl.BlockSpec(memory_space=pltpu.VMEM)
    pairs = count * CANDS
    return pl.pallas_call(
        functools.partial(density_body, count, held),
        in_specs=[pl.BlockSpec(memory_space=pltpu.SMEM), vmem, vmem],
        out_specs=[vmem, vmem],
        out_shape=[
            pltpu.VMEM((count, CANDS, CB, RB), jnp.bfloat16),
            pltpu.VMEM((count, 1, RB), jnp.float32),
        ],
        compiler_params=pltpu.CompilerParams(vmem_limit_bytes=VMEM_LIMIT),
        cost_estimate=pl.CostEstimate(
            flops=pairs * 4 * CB * RB * feature_count,
            bytes_accessed=pairs * CB * feature_count * 4 + rows.size * 2,
            transcendentals=pairs * CB * RB,
        ),
        name="responsibilities",
    )(pos, in_vmem(rows), in_vmem(weights))


def pair_lists(pos, runs, group_blocks):
    run_of = []
    for index, count in enumerate(runs):
        run_of += [index] * (count * CANDS)
    run_of = jnp.array(run_of, jnp.int32)
    key = pos.reshape(-1) * len(runs) + run_of
    number = jnp.arange(key.shape[0], dtype=jnp.int32)
    before = jnp.logical_or(
        key[None, :] < key[:, None],
        jnp.logical_and(key[None, :] == key[:, None], number[None, :] < number[:, None]),
    )
    rank = jnp.sum(before.astype(jnp.int32), axis=1)
    order = jnp.sum(jnp.where(rank[None, :] == number[:, None], number[None, :], 0), axis=1)
    bounds = jnp.arange(group_blocks * len(runs) + 1, dtype=jnp.int32)
    starts = jnp.sum((key[None, :] < bounds[:, None]).astype(jnp.int32), axis=1)
    return order, starts


def moment_body(shards, held, runs, order_ref, start_ref, *rest):
    parts, outs = len(runs), len(shards)
    row_refs, resp_refs = rest[:parts], rest[parts : 2 * parts]
    out_refs = rest[2 * parts : 2 * parts + outs]
    sums, count_sum = rest[2 * parts + outs :]
    owned = held * CB
    meta = slice(2 * owned, 2 * owned + META)
    ones = jnp.ones((META, 2 * RB), jnp.bfloat16)

    def block_sums(pos):
        sums[...] = jnp.zeros_like(sums)
        count_sum[...] = jnp.zeros_like(count_sum)
        base = 0
        for run in range(parts):
            entry = pos * parts + run
            low, high = start_ref[entry], start_ref[entry + 1]

            @pl.loop(0, lax.div(high - low + 1, 2))
            def _(step, base=base, run=run, low=low, high=high):
                one = low + 2 * step
                two = jnp.minimum(one + 1, high - 1)
                valid = (one + 1 < high).astype(jnp.float32)
                pair_a, pair_b = order_ref[one] - base, order_ref[two] - base
                row_a, row_b = lax.div(pair_a, CANDS), lax.div(pair_b, CANDS)
                weight_a = resp_refs[run][row_a, lax.rem(pair_a, CANDS)]
                weight_b = resp_refs[run][row_b, lax.rem(pair_b, CANDS)]
                weight_b = (weight_b.astype(jnp.float32) * valid).astype(jnp.bfloat16)
                weight = jnp.concatenate([weight_a, weight_b], axis=1)
                x = jnp.concatenate(
                    [
                        row_refs[run][pl.ds(pl.multiple_of(row_a * RB, RB), RB), :],
                        row_refs[run][pl.ds(pl.multiple_of(row_b * RB, RB), RB), :],
                    ],
                    axis=0,
                )
                sums[0] += jnp.dot(weight, x, preferred_element_type=jnp.float32)
                sums[1] += jnp.dot(weight, square_of(x), preferred_element_type=jnp.float32)
                count_sum[...] += lax.dot_general(
                    ones, weight, NT, preferred_element_type=jnp.float32
                )

            base += runs[run] * CANDS

    for shard, out_ref in zip(shards, out_refs):
        out_ref[meta, :] = jnp.zeros((META, out_ref.shape[1]), jnp.bfloat16)

        @pl.loop(0, held)
        def _(block, shard=shard, out_ref=out_ref):
            block_sums(shard * held + block)
            start = pl.multiple_of(block * CB, CB)
            out_ref[pl.ds(start, CB), :] = sums[0].astype(jnp.bfloat16)
            out_ref[pl.ds(owned + start, CB), :] = sums[1].astype(jnp.bfloat16)
            out_ref[meta, pl.ds(start, CB)] = count_sum[...].astype(jnp.bfloat16)


def moments(rows, resp, order, starts, held, shards):
    runs = tuple(r.shape[0] // RB for r in rows)
    feature_count = rows[0].shape[1]
    smem = pl.BlockSpec(memory_space=pltpu.SMEM)
    vmem = pl.BlockSpec(memory_space=pltpu.VMEM)
    pairs = sum(runs) * held * len(shards) // 8
    out_shape = pltpu.VMEM((2 * held * CB + META, feature_count), jnp.bfloat16)
    return pl.pallas_call(
        functools.partial(moment_body, tuple(shards), held, runs),
        in_specs=[smem, smem] + [vmem] * (2 * len(runs)),
        out_specs=[vmem] * len(shards),
        out_shape=[out_shape] * len(shards),
        scratch_shapes=[
            pltpu.VMEM((2, CB, feature_count), jnp.float32),
            pltpu.VMEM((META, CB), jnp.float32),
        ],
        compiler_params=pltpu.CompilerParams(vmem_limit_bytes=VMEM_LIMIT),
        cost_estimate=pl.CostEstimate(
            flops=pairs * 4 * CB * RB * feature_count,
            bytes_accessed=pairs * RB * (feature_count + CB) * 2,
            transcendentals=0,
        ),
        name="moments",
    )(order, starts, *[in_vmem(r) for r in rows], *[in_vmem(r) for r in resp])


def plain_plan(points, ids, weights, held):
    dp_size = lax.axis_size("dp")
    all_weights = lax.all_gather(weights, "dp", axis=0)
    resp, norm = responsibilities(points, ids, all_weights, held)
    order, starts = pair_lists(ids, (points.shape[0] // RB,), dp_size * held)
    sums = []
    for j in range(dp_size):
        sums += moments([points], [resp], order, starts, held, [j])
    total = lax.psum_scatter(jnp.concatenate(sums), "dp", scatter_dimension=0, tiled=True)
    return (lambda a, b: total[a, b].astype(jnp.float32)), norm.reshape(-1)


def line_pairs(links):
    return [(2 * a + c, 2 * b + c) for a, b in links for c in (0, 1)]


INWARD = line_pairs(((0, 1), (3, 2)))
OUTWARD = line_pairs(((1, 0), (2, 3)))
MIDDLE = line_pairs(((1, 2), (2, 1)))
CORES = [(2, 3), (3, 2), (4, 5), (5, 4)]


def move(value, pairs):
    return lax.ppermute(value, "dp", pairs)


def after(value, *others):
    return lax.optimization_barrier((value,) + others)[0]


def line_plan(points, ids, weights, held):
    group_blocks = 8 * held
    index = lax.axis_index("dp")
    chip, core = index // 2, index % 2
    row_blocks = points.shape[0] // RB
    cuts = (0, row_blocks // 2, row_blocks - row_blocks // 8, row_blocks)
    pieces = [points[a * RB : b * RB] for a, b in zip(cuts[:-1], cuts[1:])]

    outer = move(weights, INWARD)
    weights_then, *pieces = lax.optimization_barrier((weights, *pieces))
    across = move(weights_then, MIDDLE)
    moved = [move(after(pieces[0], outer), INWARD)]
    far = move(outer, MIDDLE)
    moved.append(move(after(pieces[1], moved[0]), INWARD))
    moved.append(move(after(pieces[2], moved[0], far), INWARD))
    near = [weights_then, outer, across, far]
    shards = [w for pair in ((w, move(w, CORES)) for w in near) for w in pair]
    all_weights = jnp.stack(shards)

    def place(nat):
        holder = nat // held
        z = jnp.where(chip < 2, holder // 2, 3 - holder // 2)
        z = jnp.where(z == 0, 1, jnp.where(z == 1, 0, z))
        other = (holder % 2 + core) % 2
        return (z * 2 + other) * held + nat % held

    end_pos = place(move(ids, INWARD))
    own_pos = place(ids)
    rows = [points] + moved
    runs = (row_blocks,) + tuple(b - a for a, b in zip(cuts[:-1], cuts[1:]))
    order, starts = pair_lists(jnp.concatenate([own_pos, end_pos]), runs, group_blocks)
    run_pos = [own_pos] + [end_pos[a:b] for a, b in zip(cuts[:-1], cuts[1:])]
    results = []
    for run_rows, pos in zip(rows, run_pos):
        if results:
            pos = after(pos, results[-1][1])
        results.append(responsibilities(run_rows, pos, all_weights, held))
    resp = [r[0] for r in results]

    def both_cores(own, other):
        return own.astype(jnp.float32) + move(other, CORES).astype(jnp.float32)

    def sums_of(position, *earlier):
        return moments(rows, resp, after(order, *earlier), starts, held, [position])[0]

    far_other = sums_of(7)
    far_own = sums_of(6, far_other)
    far_part = both_cores(far_own, far_other).astype(jnp.bfloat16)
    far_sum = move(far_part, MIDDLE)
    across_other = sums_of(5, far_part)
    across_own = sums_of(4, across_other)
    across_part = both_cores(across_own, across_other).astype(jnp.bfloat16)
    across_sum = move(across_part, MIDDLE)
    outer_other = sums_of(3, across_part)
    own_other = sums_of(1, outer_other)
    outer_own = sums_of(2, own_other)
    own_own = sums_of(0, outer_own)
    outer_part = both_cores(outer_own, outer_other)
    own_part = both_cores(own_own, own_other)
    outer_sum = (outer_part + far_sum.astype(jnp.float32)).astype(jnp.bfloat16)
    end_sum = move(outer_sum, OUTWARD)
    is_end = jnp.logical_or(chip == 0, chip == 3)

    def total(rows_of, columns):
        own = own_part[rows_of, columns] + across_sum[rows_of, columns].astype(jnp.float32)
        return jnp.where(is_end, end_sum[rows_of, columns].astype(jnp.float32), own)

    end_norm = jnp.concatenate([r[1].reshape(-1) for r in results[1:]])
    norm = jnp.where(is_end, move(end_norm, OUTWARD), results[0][1].reshape(-1))
    return total, norm


def on_device(points, candidates, means, inv_var, log_weight):
    feature_count = points.shape[1]
    owner_count = lax.axis_size("comp")
    owned = means.shape[0]
    held = owned // CB
    ids = candidates // (owner_count * held) * held + candidates % held
    weights = parameter_shard(means, inv_var, log_weight)
    plan = line_plan if lax.axis_size("dp") == 8 else plain_plan
    total, norm = plan(points, ids, weights, held)
    every = slice(0, feature_count)
    counts = total(2 * owned, slice(0, owned))
    first, second = total(slice(0, owned), every), total(slice(owned, 2 * owned), every)
    return counts, first, second, norm / feature_count


def solution(mesh):
    return jax.shard_map(
        on_device,
        mesh=mesh,
        in_specs=(
            P(("dp", "comp"), None),
            P(("dp", "comp"), None),
            P(("dp", "comp"), None),
            P(("dp", "comp"), None),
            P(("dp", "comp")),
        ),
        out_specs=(
            P(("dp", "comp")),
            P(("dp", "comp"), None),
            P(("dp", "comp"), None),
            P(("dp", "comp")),
        ),
        check_vma=False,
    )
```

time: 655 us -> 259 us (0.40)
  waiting for transfers between devices: 355 us -> 91 us
  matrix products: 137 us -> 0 us
  Pallas kernels: 0 us -> 68.8 us
  local copies, waits for them, and re-layouts: 84.5 us -> 39.5 us
  starting transfers between devices: 0.11 us -> 41.4 us
  blocking collectives: 29.3 us -> 0 us
  other arithmetic: 32.9 us -> 15.4 us
  between operations: 14.5 us -> 1.12 us
    unnamed x4 -> x0, waiting for transfers between devices: 238 us -> none
    dot_general x40 -> x0, matrix products: 137 us -> none  [the longest x4 48.1 us: accumulate(): jnp.dot(spread, first_part.reshape(slot_total, CB * feature_count), preci...]
    all_gather x2 -> x0, waiting for transfers between devices: 118 us -> none  [the longest x1 65.1 us: on_device(): lax.all_gather(means, 'dp', axis=0, tiled=True)]
    ppermute x0 -> x19, waiting for transfers between devices: none -> 91 us  [move(): return lax.ppermute(value, 'dp', pairs)]
    pallas_call x0 -> x13, Pallas kernels: none -> 68.8 us  [the longest x8 37.7 us: moments(): pl.pallas_call(functools.partial(moment_body, tuple(shards), held, runs),...]
    while x64 -> x0, local copies, waits for them, and re-layouts: 63.1 us -> none
    ppermute x0 -> x19, starting transfers between devices: none -> 41.4 us  [move(): return lax.ppermute(value, 'dp', pairs)]
    unnamed x5 -> x60, local copies, waits for them, and re-layouts: 1.98 us -> 32.1 us
  transfers between devices with their start and end apart: 3 -> 19, of which waited for: 3 -> 3; matrix products, arithmetic and copies ran while one was open for 0% -> 13% of each run, Pallas kernels for 0% -> 22%
where the time goes in v2:
time: 259 us; the launch traced here: 257 us
  waiting for transfers between devices  91 us (35%)
  Pallas kernels  68.8 us (27%)
  starting transfers between devices  41.4 us (16%)
  local copies, waits for them, and re-layouts  39.5 us (15%)
  other arithmetic  15.4 us (6%)
    ppermute x19, waiting for transfers between devices, move(): return lax.ppermute(value, 'dp', pairs)  91 us
    ppermute x19, starting transfers between devices, move(): return lax.ppermute(value, 'dp', pairs)  41.4 us
    pallas_call x8, Pallas kernels, moments(): pl.pallas_call(functools.partial(moment_body, tuple(shards), held, runs),...  37.7 us
    unnamed x60, local copies, waits for them, and re-layouts  32.1 us
    pallas_call x4, Pallas kernels, responsibilities(): pl.pallas_call(functools.partial(density_body, count, held), in_specs=[pl...  28.5 us
    select_n x2, other arithmetic, total(): return jnp.where(is_end, end_sum[rows_of, columns].astype(jnp.float32), own)  5.22 us
  transfers between devices with their start and end apart: 19, of which 3 were waited for; matrix products, arithmetic and copies ran while one was open for 13% of the time, Pallas kernels for 22%

profile of v2, /device:TPU:0, one launch (start us, length us, event | category | flops | bytes accessed | tf_op | source)
XLA Modules:
  0.0 257.2 jit_solution(7298109087060241330)
XLA Ops:
  3.9 2.6 %parameter_shard.1 = bf16[1040,768]{1,0:T(8,128)(2,1)} custom-call(bf16[512,768]{1,0:T(8,128)(2,1)S(1)} %copy-done.12, bf16[512,768]{1,0:T(8,128)(2,1)S(1)} %copy-done.13, bf16[1,512]{1,0:T(2,128)(2,1)S(1)} %reshape.34.log_ref), custom_call_target="tpu_custom_call" | custom-call | flops 15728640 | bytes 3145728 | tf_op jit(solution)/shard_map/parameter_shard/pallas_call | solution.py:59
  6.5 6.1 %collective-permute-start.1 = (bf16[1040,768]{1,0:T(8,128)(2,1)}, bf16[1040,768]{1,0:T(8,128)(2,1)}, u32[]{:S(2)}, u32[]{:S(2)}) collective-permute-start(bf16[1040,768]{1,0:T(8,128)(2,1)} %parameter_shard.1), channel_id=1, source_target_pairs={{0,8},{4,12},{24,16},{28,20},{1,9},{5,13},{25,17},{29,21},{2,10},{... | collective-permute-start | bytes 4792328 | tf_op jit(solution)/shard_map/ppermute | solution.py:260
  15.7 1.8 collective-permute-start.6
  19.5 1.9 collective-permute-start
  21.4 2.7 %bitcast_dynamic-update-slice_fusion.7 = bf16[8,1040,768]{2,1,0:T(8,128)(2,1)} fusion(bf16[1040,768]{1,0:T(8,128)(2,1)} %parameter_shard.1), kind=kLoop, calls=%fused_computation.11 | loop fusion | bytes 3194880
  24.2 21.8 %collective-permute-done = s32[16,4]{1,0:T(8,128)S(1)} collective-permute-done((s32[16,4]{1,0:T(8,128)S(1)}, s32[16,4]{1,0:T(8,128)S(1)}, u32[]{:S(2)}, u32[]{:S(2)}) %collective-permute-start) | collective-permute-done | bytes 288 | tf_op jit(solution)/shard_map/ppermute | solution.py:260
  46.1 5.5 %collective-permute-start.2 = (bf16[1024,768]{1,0:T(8,128)(2,1)}, bf16[1024,768]{1,0:T(8,128)(2,1)}, u32[]{:S(2)}, u32[]{:S(2)}) collective-permute-start(bf16[1024,768]{1,0:T(8,128)(2,1)} %slice.45), channel_id=1, source_target_pairs={{0,8},{4,12},{24,16},{28,20},{1,9},{5,13},{25,17},{29,21},{2,10},{... | collective-permute-start | bytes 4718600 | tf_op jit(solution)/shard_map/ppermute | solution.py:260
  58.5 2.7 %bitcast_dynamic-update-slice_fusion.6 = bf16[8,1040,768]{2,1,0:T(8,128)(2,1)} fusion(bf16[8,1040,768]{2,1,0:T(8,128)(2,1)} %bitcast_dynamic-update-slice_fusion.7, bf16[1040,768]{1,0:T(8,128)(2,1)} %collective-permute-done.6), kind=kLoop, calls=%fused_computation.10 | loop fusion | bytes 3194880
  61.2 2.8 %bitcast_dynamic-update-slice_fusion.5 = bf16[8,1040,768]{2,1,0:T(8,128)(2,1)} fusion(bf16[8,1040,768]{2,1,0:T(8,128)(2,1)} %bitcast_dynamic-update-slice_fusion.6, bf16[1040,768]{1,0:T(8,128)(2,1)} %collective-permute-done.1), kind=kLoop, calls=%fused_computation.9 | loop fusion | bytes 3194880
  64.0 19.6 %collective-permute-done.2.x_ref.rest_1_ = bf16[1024,768]{1,0:T(8,128)(2,1)} collective-permute-done((bf16[1024,768]{1,0:T(8,128)(2,1)}, bf16[1024,768]{1,0:T(8,128)(2,1)}, u32[]{:S(2)}, u32[]{:S(2)}) %collective-permute-start.2) | collective-permute-done | bytes 1572896 | tf_op jit(solution)/shard_map/ppermute | solution.py:260
  83.6 4.4 %collective-permute-start.3 = (bf16[768,768]{1,0:T(8,128)(2,1)S(1)}, bf16[768,768]{1,0:T(8,128)(2,1)S(1)}, u32[]{:S(2)}, u32[]{:S(2)}) collective-permute-start(bf16[768,768]{1,0:T(8,128)(2,1)S(1)} %copy-done.22), channel_id=1, source_target_pairs={{0,8},{4,12},{24,16},{28,20},{1,9},{5,13},{25,17},{29,21},{2,10},{... | collective-permute-start | bytes 3538952 | tf_op jit(solution)/shard_map/ppermute | solution.py:260
  88.1 5.1 %collective-permute-start.5 = (bf16[256,768]{1,0:T(8,128)(2,1)S(1)}, bf16[256,768]{1,0:T(8,128)(2,1)S(1)}, u32[]{:S(2)}, u32[]{:S(2)}) collective-permute-start(bf16[256,768]{1,0:T(8,128)(2,1)S(1)} %copy-done.23), channel_id=1, source_target_pairs={{0,8},{4,12},{24,16},{28,20},{1,9},{5,13},{25,17},{29,21},{2,10},{... | collective-permute-start | bytes 1179656 | tf_op jit(solution)/shard_map/ppermute | solution.py:260
  94.0 2.7 %bitcast_dynamic-update-slice_fusion.4 = bf16[8,1040,768]{2,1,0:T(8,128)(2,1)} fusion(bf16[8,1040,768]{2,1,0:T(8,128)(2,1)} %bitcast_dynamic-update-slice_fusion.5, bf16[1040,768]{1,0:T(8,128)(2,1)} %collective-permute-done.7), kind=kLoop, calls=%fused_computation.8 | loop fusion | bytes 3194880
  96.7 2.7 %bitcast_dynamic-update-slice_fusion.3 = bf16[8,1040,768]{2,1,0:T(8,128)(2,1)} fusion(bf16[8,1040,768]{2,1,0:T(8,128)(2,1)} %bitcast_dynamic-update-slice_fusion.4, bf16[1040,768]{1,0:T(8,128)(2,1)} %collective-permute-done.8), kind=kLoop, calls=%fused_computation.7 | loop fusion | bytes 3194880
  100.8 2.7 %bitcast_dynamic-update-slice_fusion.1 = bf16[8,1040,768]{2,1,0:T(8,128)(2,1)} fusion(bf16[8,1040,768]{2,1,0:T(8,128)(2,1)} %bitcast_dynamic-update-slice_fusion.2, bf16[1040,768]{1,0:T(8,128)(2,1)} %collective-permute-done.4), kind=kLoop, calls=%fused_computation.5 | loop fusion | bytes 3194880
  104.8 4.6 %copy-done.1 = bf16[8,1040,768]{2,1,0:T(8,128)(2,1)S(1)} copy-done((bf16[8,1040,768]{2,1,0:T(8,128)(2,1)S(1)}, bf16[8,1040,768]{2,1,0:T(8,128)(2,1)}, u32[]{:S(2)}) %copy-start.1) | copy-done | bytes 12779544
  109.5 12.9 %responsibilities.4 = (bf16[16,4,128,128]{3,2,1,0:T(8,128)(2,1)S(1)}, f32[16,1,128]{2,1,0:T(1,128)S(1)}) custom-call(s32[16,4]{1,0:T(8,128)S(1)} %get-tuple-element.54.pos_ref, bf16[2048,768]{1,0:T(8,128)(2,1)S(1)} %copy-done, bf16[8,1040,768]{2,1,0:T(8,128)(2,1)S(1)} %copy-done.1), custom_call_target="tpu_custom_call" | custom-call | flops 3221225472 | bytes 28311552 | tf_op jit(solution)/shard_map/responsibilities/pallas_call | solution.py:120
  122.4 8.3 %responsibilities.5 = (bf16[8,4,128,128]{3,2,1,0:T(8,128)(2,1)S(1)}, f32[8,1,128]{2,1,0:T(1,128)S(1)}) custom-call(s32[8,4]{1,0:T(8,128)S(1)} %copy-done.15, bf16[1024,768]{1,0:T(8,128)(2,1)} %collective-permute-done.2.x_ref.rest_1_, bf16[8,1040,768]{2,1,0:T(8,128)(2,1)S(1)} %copy-done.1), custom_call_target="tpu_custom_call" | custom-call | flops 1610612736 | bytes 14155776 | tf_op jit(solution)/shard_map/responsibilities/pallas_call | solution.py:120
  130.8 5.2 %responsibilities.6 = (bf16[6,4,128,128]{3,2,1,0:T(8,128)(2,1)S(1)}, f32[6,1,128]{2,1,0:T(1,128)S(1)}) custom-call(s32[6,4]{1,0:T(8,128)S(1)} %copy-done.14, bf16[768,768]{1,0:T(8,128)(2,1)S(1)} %collective-permute-done.3.x_ref.rest_2_, bf16[8,1040,768]{2,1,0:T(8,128)(2,1)S(1)} %copy-done.1), custom_call_target="tpu_custom_call" | custom-call | flops 1207959552 | bytes 10616832 | tf_op jit(solution)/shard_map/responsibilities/pallas_call | solution.py:120
  136.6 2.1 responsibilities.7
  139.2 3.2 %moments.8 = bf16[1040,768]{1,0:T(8,128)(2,1)S(1)} custom-call(s32[128]{0:T(128)S(1)} %select_reduce_fusion.order_ref, s32[129]{0:T(256)S(1)} %convert_reduce_fusion.start_ref, bf16[2048,768]{1,0:T(8,128)(2,1)S(1)} %copy-done, bf16[1024,768]{1,0:T(8,128)(2,1)} %collective-permute-done.2.x_ref.rest_1_, ...), custom_call_target="tpu_custom_call" | custom-call | flops 805306368 | bytes 3670016 | tf_op jit(solution)/shard_map/moments/pallas_call | solution.py:218
  143.2 3.4 %moments.9 = bf16[1040,768]{1,0:T(8,128)(2,1)S(1)} custom-call(s32[128]{0:T(128)S(1)} %select_reduce_fusion.order_ref, s32[129]{0:T(256)S(1)} %convert_reduce_fusion.start_ref, bf16[2048,768]{1,0:T(8,128)(2,1)S(1)} %copy-done, bf16[1024,768]{1,0:T(8,128)(2,1)} %collective-permute-done.2.x_ref.rest_1_, ...), custom_call_target="tpu_custom_call" | custom-call | flops 805306368 | bytes 3670016 | tf_op jit(solution)/shard_map/moments/pallas_call | solution.py:218
  147.0 3.4 %moments.10 = bf16[1040,768]{1,0:T(8,128)(2,1)S(1)} custom-call(s32[128]{0:T(128)S(1)} %select_reduce_fusion.order_ref, s32[129]{0:T(256)S(1)} %convert_reduce_fusion.start_ref, bf16[2048,768]{1,0:T(8,128)(2,1)S(1)} %copy-done, bf16[1024,768]{1,0:T(8,128)(2,1)} %collective-permute-done.2.x_ref.rest_1_, ...), custom_call_target="tpu_custom_call" | custom-call | flops 805306368 | bytes 3670016 | tf_op jit(solution)/shard_map/moments/pallas_call | solution.py:218
  152.1 3.6 %moments.11 = bf16[1040,768]{1,0:T(8,128)(2,1)S(1)} custom-call(s32[128]{0:T(128)S(1)} %select_reduce_fusion.order_ref, s32[129]{0:T(256)S(1)} %convert_reduce_fusion.start_ref, bf16[2048,768]{1,0:T(8,128)(2,1)S(1)} %copy-done, bf16[1024,768]{1,0:T(8,128)(2,1)} %collective-permute-done.2.x_ref.rest_1_, ...), custom_call_target="tpu_custom_call" | custom-call | flops 805306368 | bytes 3670016 | tf_op jit(solution)/shard_map/moments/pallas_call | solution.py:218
  157.4 3.1 %moments.12 = bf16[1040,768]{1,0:T(8,128)(2,1)S(1)} custom-call(s32[128]{0:T(128)S(1)} %select_reduce_fusion.order_ref, s32[129]{0:T(256)S(1)} %convert_reduce_fusion.start_ref, bf16[2048,768]{1,0:T(8,128)(2,1)S(1)} %copy-done, bf16[1024,768]{1,0:T(8,128)(2,1)} %collective-permute-done.2.x_ref.rest_1_, ...), custom_call_target="tpu_custom_call" | custom-call | flops 805306368 | bytes 3670016 | tf_op jit(solution)/shard_map/moments/pallas_call | solution.py:218
  161.3 4.3 %moments.13 = bf16[1040,768]{1,0:T(8,128)(2,1)} custom-call(s32[128]{0:T(128)S(1)} %select_reduce_fusion.order_ref, s32[129]{0:T(256)S(1)} %convert_reduce_fusion.start_ref, bf16[2048,768]{1,0:T(8,128)(2,1)S(1)} %copy-done, bf16[1024,768]{1,0:T(8,128)(2,1)} %collective-permute-done.2.x_ref.rest_1_, ...), custom_call_target="tpu_custom_call" | custom-call | flops 805306368 | bytes 3670016 | tf_op jit(solution)/shard_map/moments/pallas_call | solution.py:218
  167.4 1.8 collective-permute-start.17
  169.3 13.1 %moments.14 = bf16[1040,768]{1,0:T(8,128)(2,1)S(1)} custom-call(s32[128]{0:T(128)S(1)} %select_reduce_fusion.order_ref, s32[129]{0:T(256)S(1)} %convert_reduce_fusion.start_ref, bf16[2048,768]{1,0:T(8,128)(2,1)S(1)} %copy-done, bf16[1024,768]{1,0:T(8,128)(2,1)} %collective-permute-done.2.x_ref.rest_1_, ...), custom_call_target="tpu_custom_call" | custom-call | flops 805306368 | bytes 3670016 | tf_op jit(solution)/shard_map/moments/pallas_call | solution.py:218
  182.4 1.8 add_convert_fusion
  189.4 49.5 %collective-permute-done.18 = f32[2048]{0:T(1024)} collective-permute-done((f32[2048]{0:T(1024)}, f32[2048]{0:T(1024)}, u32[]{:S(2)}, u32[]{:S(2)}) %collective-permute-start.18) | collective-permute-done | bytes 8224 | tf_op jit(solution)/shard_map/ppermute | solution.py:260
  246.4 3.6 %moments.15 = bf16[1040,768]{1,0:T(8,128)(2,1)S(1)} custom-call(s32[128]{0:T(128)S(1)} %select_reduce_fusion.order_ref, s32[129]{0:T(256)S(1)} %convert_reduce_fusion.start_ref, bf16[2048,768]{1,0:T(8,128)(2,1)S(1)} %copy-done, bf16[1024,768]{1,0:T(8,128)(2,1)} %collective-permute-done.2.x_ref.rest_1_, bf16[768,768]{1,0:T(8,128)(2,1)S(1)} %copy-done.5, ...), custom_call_target="tpu_custom_call" | custom-call | flops 805306368 | bytes 3670016 | tf_op jit(solution)/shard_map/moments/pallas_call | solution.py:218
  251.9 3.9 %fusion = (f32[512,768]{1,0:T(8,128)}, f32[512,768]{1,0:T(8,128)}) fusion(f32[1040,768]{1,0:T(8,128)S(1)} %convert_add_fusion, bf16[1040,768]{1,0:T(8,128)(2,1)} %collective-permute-done.17, bf16[1040,768]{1,0:T(8,128)(2,1)} %collective-permute-done.15, pred[]{:T(512)S(6)} %or.6), kind=kLoop, calls=%fused_computation.13 | loop fusion | flops 3145728 | bytes 9437185 | tf_op jit(solution)/shard_map/jit(_where)/select_n | solution.py:332
  (106 shorter events, 42.8 us)
Async XLA Ops:
  0.6 11.9 %copy-start = (bf16[2048,768]{1,0:T(8,128)(2,1)S(1)}, bf16[2048,768]{1,0:T(8,128)(2,1)}, u32[]{:S(2)}) copy-start(bf16[2048,768]{1,0:T(8,128)(2,1)} %rest_0_.15) | copy-start | bytes 9437188
  6.5 39.6 %collective-permute-start.1 = (bf16[1040,768]{1,0:T(8,128)(2,1)}, bf16[1040,768]{1,0:T(8,128)(2,1)}, u32[]{:S(2)}, u32[]{:S(2)}) collective-permute-start(bf16[1040,768]{1,0:T(8,128)(2,1)} %parameter_shard.1), channel_id=1, source_target_pairs={{0,8},{4,12},{24,16},{28,20},{1,9},{5,13},{25,17},{29,21},{2,10},{... | collective-permute-start | bytes 4792328 | tf_op jit(solution)/shard_map/ppermute | solution.py:260
  15.7 42.8 %collective-permute-start.6 = (bf16[1040,768]{1,0:T(8,128)(2,1)}, bf16[1040,768]{1,0:T(8,128)(2,1)}, u32[]{:S(2)}, u32[]{:S(2)}) collective-permute-start(bf16[1040,768]{1,0:T(8,128)(2,1)} %parameter_shard.1), channel_id=1, source_target_pairs={{8,12},{12,8},{16,20},{20,16},{9,13},{13,9},{17,21},{21,17},{10,14... | collective-permute-start | bytes 4792328 | tf_op jit(solution)/shard_map/ppermute | solution.py:260
  17.5 40.2 %collective-permute-start.8 = (bf16[1040,768]{1,0:T(8,128)(2,1)}, bf16[1040,768]{1,0:T(8,128)(2,1)}, u32[]{:S(2)}, u32[]{:S(2)}) collective-permute-start(bf16[1040,768]{1,0:T(8,128)(2,1)} %parameter_shard.1), channel_id=1, source_target_pairs={{8,16},{12,20},{16,8},{20,12},{9,17},{13,21},{17,9},{21,13},{10,18... | collective-permute-start | bytes 4792328 | tf_op jit(solution)/shard_map/ppermute | solution.py:260
  19.4 35.8 %copy-start.25 = (s32[32,4]{0,1:T(4,128)S(1)}, s32[32,4]{0,1:T(4,128)}, u32[]{:S(2)}) copy-start(s32[32,4]{0,1:T(4,128)} %constant.135) | copy-start | bytes 1540
  19.5 26.5 %collective-permute-start = (s32[16,4]{1,0:T(8,128)S(1)}, s32[16,4]{1,0:T(8,128)S(1)}, u32[]{:S(2)}, u32[]{:S(2)}) collective-permute-start(s32[16,4]{1,0:T(8,128)S(1)} %get-tuple-element.55), channel_id=1, source_target_pairs={{0,8},{4,12},{24,16},{28,20},{1,9},{5,13},{25,17},{29,21},{2,10},{... | collective-permute-start | bytes 776 | tf_op jit(solution)/shard_map/ppermute | solution.py:260
  46.1 37.6 %collective-permute-start.2 = (bf16[1024,768]{1,0:T(8,128)(2,1)}, bf16[1024,768]{1,0:T(8,128)(2,1)}, u32[]{:S(2)}, u32[]{:S(2)}) collective-permute-start(bf16[1024,768]{1,0:T(8,128)(2,1)} %slice.45), channel_id=1, source_target_pairs={{0,8},{4,12},{24,16},{28,20},{1,9},{5,13},{25,17},{29,21},{2,10},{... | collective-permute-start | bytes 4718600 | tf_op jit(solution)/shard_map/ppermute | solution.py:260
  51.6 42.4 %collective-permute-start.7 = (bf16[1040,768]{1,0:T(8,128)(2,1)}, bf16[1040,768]{1,0:T(8,128)(2,1)}, u32[]{:S(2)}, u32[]{:S(2)}) collective-permute-start(bf16[1040,768]{1,0:T(8,128)(2,1)} %collective-permute-done.1), channel_id=1, source_target_pairs={{8,12},{12,8},{16,20},{20,16},{9,13},{13,9},{17,21},{21,17},{10,14... | collective-permute-start | bytes 4792328 | tf_op jit(solution)/shard_map/ppermute | solution.py:260
  53.4 34.7 %collective-permute-start.4 = (bf16[1040,768]{1,0:T(8,128)(2,1)}, bf16[1040,768]{1,0:T(8,128)(2,1)}, u32[]{:S(2)}, u32[]{:S(2)}) collective-permute-start(bf16[1040,768]{1,0:T(8,128)(2,1)} %collective-permute-done.1), channel_id=1, source_target_pairs={{8,16},{12,20},{16,8},{20,12},{9,17},{13,21},{17,9},{21,13},{10,18... | collective-permute-start | bytes 4792328 | tf_op jit(solution)/shard_map/ppermute | solution.py:260
  57.7 41.8 %collective-permute-start.9 = (bf16[1040,768]{1,0:T(8,128)(2,1)}, bf16[1040,768]{1,0:T(8,128)(2,1)S(1)}, u32[]{:S(2)}, u32[]{:S(2)}) collective-permute-start(bf16[1040,768]{1,0:T(8,128)(2,1)} %collective-permute-done.8), channel_id=1, source_target_pairs={{8,12},{12,8},{16,20},{20,16},{9,13},{13,9},{17,21},{21,17},{10,14... | collective-permute-start | bytes 4792328 | tf_op jit(solution)/shard_map/ppermute | solution.py:260
  61.2 22.5 %copy-start.22 = (bf16[768,768]{1,0:T(8,128)(2,1)S(1)}, bf16[768,768]{1,0:T(8,128)(2,1)}, u32[]{:S(2)}) copy-start(bf16[768,768]{1,0:T(8,128)(2,1)} %slice.46) | copy-start | bytes 3538948
  61.2 26.9 %copy-start.23 = (bf16[256,768]{1,0:T(8,128)(2,1)S(1)}, bf16[256,768]{1,0:T(8,128)(2,1)}, u32[]{:S(2)}) copy-start(bf16[256,768]{1,0:T(8,128)(2,1)} %slice.47) | copy-start | bytes 1179652
  83.6 47.1 %collective-permute-start.3 = (bf16[768,768]{1,0:T(8,128)(2,1)S(1)}, bf16[768,768]{1,0:T(8,128)(2,1)S(1)}, u32[]{:S(2)}, u32[]{:S(2)}) collective-permute-start(bf16[768,768]{1,0:T(8,128)(2,1)S(1)} %copy-done.22), channel_id=1, source_target_pairs={{0,8},{4,12},{24,16},{28,20},{1,9},{5,13},{25,17},{29,21},{2,10},{... | collective-permute-start | bytes 3538952 | tf_op jit(solution)/shard_map/ppermute | solution.py:260
  88.1 48.5 %collective-permute-start.5 = (bf16[256,768]{1,0:T(8,128)(2,1)S(1)}, bf16[256,768]{1,0:T(8,128)(2,1)S(1)}, u32[]{:S(2)}, u32[]{:S(2)}) collective-permute-start(bf16[256,768]{1,0:T(8,128)(2,1)S(1)} %copy-done.23), channel_id=1, source_target_pairs={{0,8},{4,12},{24,16},{28,20},{1,9},{5,13},{25,17},{29,21},{2,10},{... | collective-permute-start | bytes 1179656 | tf_op jit(solution)/shard_map/ppermute | solution.py:260
  93.2 10.2 %collective-permute-start.10 = (bf16[1040,768]{1,0:T(8,128)(2,1)}, bf16[1040,768]{1,0:T(8,128)(2,1)S(1)}, u32[]{:S(2)}, u32[]{:S(2)}) collective-permute-start(bf16[1040,768]{1,0:T(8,128)(2,1)} %collective-permute-done.4), channel_id=1, source_target_pairs={{8,12},{12,8},{16,20},{20,16},{9,13},{13,9},{17,21},{21,17},{10,14... | collective-permute-start | bytes 4792328 | tf_op jit(solution)/shard_map/ppermute | solution.py:260
  109.4 13.0 %copy-start.15 = (s32[8,4]{1,0:T(8,128)S(1)}, s32[8,4]{1,0:T(8,128)}, u32[]{:S(2)}) copy-start(s32[8,4]{1,0:T(8,128)} %slice.60.pos_ref) | copy-start | bytes 388
  122.4 8.3 %copy-start.16 = (f32[16,1,128]{2,1,0:T(1,128)}, f32[16,1,128]{2,1,0:T(1,128)S(1)}, u32[]{:S(2)}) copy-start(f32[16,1,128]{2,1,0:T(1,128)S(1)} %get-tuple-element.37) | copy-start | bytes 24580
  122.4 46.9 %copy-start.2 = (bf16[16,4,128,128]{3,2,1,0:T(8,128)(2,1)}, bf16[16,4,128,128]{3,2,1,0:T(8,128)(2,1)S(1)}, u32[]{:S(2)}) copy-start(bf16[16,4,128,128]{3,2,1,0:T(8,128)(2,1)S(1)} %get-tuple-element.36.rest_4_) | copy-start | bytes 6291460
  122.4 8.3 %copy-start.14 = (s32[6,4]{1,0:T(8,128)S(1)}, s32[6,4]{1,0:T(8,128)}, u32[]{:S(2)}) copy-start(s32[6,4]{1,0:T(8,128)} %slice.61.pos_ref) | copy-start | bytes 292
  130.7 38.6 %copy-start.6 = (bf16[8,4,128,128]{3,2,1,0:T(8,128)(2,1)}, bf16[8,4,128,128]{3,2,1,0:T(8,128)(2,1)S(1)}, u32[]{:S(2)}) copy-start(bf16[8,4,128,128]{3,2,1,0:T(8,128)(2,1)S(1)} %get-tuple-element.39.rest_5_) | copy-start | bytes 3145732
  130.8 38.5 %copy-start.4 = (bf16[768,768]{1,0:T(8,128)(2,1)}, bf16[768,768]{1,0:T(8,128)(2,1)S(1)}, u32[]{:S(2)}) copy-start(bf16[768,768]{1,0:T(8,128)(2,1)S(1)} %collective-permute-done.3.x_ref.rest_2_) | copy-start | bytes 3538948
  136.6 32.7 %copy-start.8 = (bf16[6,4,128,128]{3,2,1,0:T(8,128)(2,1)}, bf16[6,4,128,128]{3,2,1,0:T(8,128)(2,1)S(1)}, u32[]{:S(2)}) copy-start(bf16[6,4,128,128]{3,2,1,0:T(8,128)(2,1)S(1)} %get-tuple-element.42.rest_6_) | copy-start | bytes 2359300
  139.2 30.1 %copy-start.10 = (bf16[2,4,128,128]{3,2,1,0:T(8,128)(2,1)}, bf16[2,4,128,128]{3,2,1,0:T(8,128)(2,1)S(1)}, u32[]{:S(2)}) copy-start(bf16[2,4,128,128]{3,2,1,0:T(8,128)(2,1)S(1)} %get-tuple-element.45.rest_7_) | copy-start | bytes 786436
  142.4 4.1 %collective-permute-start.11 = (bf16[1040,768]{1,0:T(8,128)(2,1)S(1)}, bf16[1040,768]{1,0:T(8,128)(2,1)S(1)}, u32[]{:S(2)}, u32[]{:S(2)}) collective-permute-start(bf16[1040,768]{1,0:T(8,128)(2,1)S(1)} %moments.8), channel_id=1, source_target_pairs={{8,12},{12,8},{16,20},{20,16},{9,13},{13,9},{17,21},{21,17},{10,14... | collective-permute-start | bytes 4792328 | tf_op jit(solution)/shard_map/ppermute | solution.py:260
  150.4 5.4 %collective-permute-start.12 = (bf16[1040,768]{1,0:T(8,128)(2,1)S(1)}, bf16[1040,768]{1,0:T(8,128)(2,1)S(1)}, u32[]{:S(2)}, u32[]{:S(2)}) collective-permute-start(bf16[1040,768]{1,0:T(8,128)(2,1)S(1)} %moments.10), channel_id=1, source_target_pairs={{8,12},{12,8},{16,20},{20,16},{9,13},{13,9},{17,21},{21,17},{10,14... | collective-permute-start | bytes 4792328 | tf_op jit(solution)/shard_map/ppermute | solution.py:260
  151.2 31.2 %collective-permute-start.14 = (bf16[1040,768]{1,0:T(8,128)(2,1)S(1)}, bf16[1040,768]{1,0:T(8,128)(2,1)S(1)}, u32[]{:S(2)}, u32[]{:S(2)}) collective-permute-start(bf16[1040,768]{1,0:T(8,128)(2,1)S(1)} %add_convert_fusion.2), channel_id=1, source_target_pairs={{8,16},{12,20},{16,8},{20,12},{9,17},{13,21},{17,9},{21,13},{10,18... | collective-permute-start | bytes 4792328 | tf_op jit(solution)/shard_map/ppermute | solution.py:260
  160.5 21.9 %collective-permute-start.13 = (bf16[1040,768]{1,0:T(8,128)(2,1)S(1)}, bf16[1040,768]{1,0:T(8,128)(2,1)S(1)}, u32[]{:S(2)}, u32[]{:S(2)}) collective-permute-start(bf16[1040,768]{1,0:T(8,128)(2,1)S(1)} %moments.12), channel_id=1, source_target_pairs={{8,12},{12,8},{16,20},{20,16},{9,13},{13,9},{17,21},{21,17},{10,14... | collective-permute-start | bytes 4792328 | tf_op jit(solution)/shard_map/ppermute | solution.py:260
  165.6 84.5 %collective-permute-start.16 = (bf16[1040,768]{1,0:T(8,128)(2,1)}, bf16[1040,768]{1,0:T(8,128)(2,1)}, u32[]{:S(2)}, u32[]{:S(2)}) collective-permute-start(bf16[1040,768]{1,0:T(8,128)(2,1)} %moments.13), channel_id=1, source_target_pairs={{8,12},{12,8},{16,20},{20,16},{9,13},{13,9},{17,21},{21,17},{10,14... | collective-permute-start | bytes 4792328 | tf_op jit(solution)/shard_map/ppermute | solution.py:260
  167.4 84.5 %collective-permute-start.17 = (bf16[1040,768]{1,0:T(8,128)(2,1)}, bf16[1040,768]{1,0:T(8,128)(2,1)}, u32[]{:S(2)}, u32[]{:S(2)}) collective-permute-start(bf16[1040,768]{1,0:T(8,128)(2,1)} %add_convert_fusion.1), channel_id=1, source_target_pairs={{8,16},{12,20},{16,8},{20,12},{9,17},{13,21},{17,9},{21,13},{10,18... | collective-permute-start | bytes 4792328 | tf_op jit(solution)/shard_map/ppermute | solution.py:260
  182.4 56.6 %copy-start.17 = (f32[16,1,128]{2,1,0:T(1,128)S(1)}, f32[16,1,128]{2,1,0:T(1,128)}, u32[]{:S(2)}) copy-start(f32[16,1,128]{2,1,0:T(1,128)} %copy-done.16) | copy-start | bytes 24580
  184.3 67.7 %collective-permute-start.15 = (bf16[1040,768]{1,0:T(8,128)(2,1)}, bf16[1040,768]{1,0:T(8,128)(2,1)}, u32[]{:S(2)}, u32[]{:S(2)}) collective-permute-start(bf16[1040,768]{1,0:T(8,128)(2,1)} %add_convert_fusion), channel_id=1, source_target_pairs={{8,0},{12,4},{16,24},{20,28},{9,1},{13,5},{17,25},{21,29},{10,2},{... | collective-permute-start | bytes 4792328 | tf_op jit(solution)/shard_map/ppermute | solution.py:260
  188.1 50.8 %collective-permute-start.18 = (f32[2048]{0:T(1024)}, f32[2048]{0:T(1024)}, u32[]{:S(2)}, u32[]{:S(2)}) collective-permute-start(f32[2048]{0:T(1024)} %pad_maximum_fusion), channel_id=1, source_target_pairs={{8,0},{12,4},{16,24},{20,28},{9,1},{13,5},{17,25},{21,29},{10,2},{... | collective-permute-start | bytes 24584 | tf_op jit(solution)/shard_map/ppermute | solution.py:260
  (13 other events, 31.0 us)

commit v3 on v2

v3 whole, which is shorter than its diff:
```python
import functools
import math

import jax
import jax.numpy as jnp
from jax import lax
from jax.experimental import pallas as pl
from jax.experimental.pallas import tpu as pltpu
from jax.sharding import PartitionSpec as P

CB = 128
RB = 128
CANDS = 4
META = 16
VMEM_LIMIT = 8 * 1024 * 1024
NT = (((1,), (1,)), ((), ()))
TN = (((0,), (0,)), ((), ()))


def in_vmem(value):
    return pltpu.with_memory_space_constraint(value, pltpu.VMEM)


def shard_body(cuts, means_ref, inv_ref, log_ref, points_ref, out_ref, *rest):
    piece_refs, sems = rest[:-1], rest[-1]
    copies = [
        pltpu.make_async_copy(points_ref.at[pl.ds(cuts[j], piece.shape[0])], piece, sems.at[j])
        for j, piece in enumerate(piece_refs)
    ]
    for copy in copies:
        copy.start()
    owned, feature_count = means_ref.shape
    ones = jnp.ones((META, feature_count), jnp.float32)
    row = lax.broadcasted_iota(jnp.int32, (META, CB), 0)
    for half in range(2):
        out_ref[0, half, owned:, :] = jnp.zeros((META, feature_count), jnp.bfloat16)
    for block in range(owned // CB):
        here = slice(block * CB, (block + 1) * CB)
        inverse = inv_ref[here, :]
        mean_f = means_ref[here, :].astype(jnp.float32)
        inv_f = inverse.astype(jnp.float32)
        scaled = inv_f * mean_f
        out_ref[0, 0, here, :] = scaled.astype(jnp.bfloat16)
        out_ref[0, 1, here, :] = inverse
        terms = 0.5 * jnp.log(inv_f) - 0.5 * (scaled * mean_f)
        rest = lax.dot_general(
            ones, terms, NT, precision=lax.Precision.HIGHEST, preferred_element_type=jnp.float32
        )
        rest += log_ref[:, here].astype(jnp.float32)
        rest -= 0.5 * feature_count * math.log(2.0 * math.pi)
        high = rest.astype(jnp.bfloat16).astype(jnp.float32)
        rest -= high
        middle = rest.astype(jnp.bfloat16).astype(jnp.float32)
        low = rest - middle
        pieces = jnp.where(row == 0, high, jnp.where(row == 1, middle, low))
        out_ref[0, 0, owned:, here] = pieces.astype(jnp.bfloat16)
    for copy in copies:
        copy.wait()


def parameter_shard(means, inv_var, log_weight, points, cuts):
    owned, feature_count = means.shape
    vmem = pl.BlockSpec(memory_space=pltpu.VMEM)
    anywhere = pl.BlockSpec(memory_space=pl.ANY)
    lengths = [b - a for a, b in zip(cuts[:-1], cuts[1:])]
    return pl.pallas_call(
        functools.partial(shard_body, cuts),
        in_specs=[vmem, vmem, vmem, anywhere],
        out_specs=[vmem] + [anywhere] * len(lengths),
        out_shape=[pltpu.VMEM((1, 2, owned + META, feature_count), jnp.bfloat16)]
        + [jax.ShapeDtypeStruct((length, feature_count), points.dtype) for length in lengths],
        scratch_shapes=[pltpu.SemaphoreType.DMA((max(len(lengths), 1),))],
        compiler_params=pltpu.CompilerParams(vmem_limit_bytes=VMEM_LIMIT),
        cost_estimate=pl.CostEstimate(
            flops=owned * feature_count * 40,
            bytes_accessed=owned * feature_count * 8,
            transcendentals=owned * feature_count,
        ),
        name="parameter_shard",
    )(in_vmem(means), in_vmem(inv_var), log_weight.reshape(1, owned), points)


def density_body(count, held, shards, arrays, pos_ref, x_ref, *rest):
    weight_refs = rest[:arrays]
    resp_ref, norm_ref, chosen, metas, sems, meta_sems = rest[arrays:]
    owned = held * CB
    per_array = shards // arrays
    row_index = lax.broadcasted_iota(jnp.int32, (META, RB), 0)
    pieces = jnp.where(row_index < 3, 1.0, 0.0).astype(jnp.bfloat16)

    def block_copy(array, entry, start, half, slot):
        return pltpu.make_async_copy(
            weight_refs[array].at[entry, :, pl.ds(start, CB), :],
            chosen.at[half, :, pl.ds(slot * CB, CB), :],
            sems.at[half, slot],
        )

    def fetch(i, half):
        for slot in range(CANDS):
            pos = pos_ref[i, slot]
            shard = lax.div(pos, held)
            start = pl.multiple_of(lax.rem(pos, held) * CB, CB)
            if arrays == 1:
                block_copy(0, shard, start, half, slot).start()
            for array in range(arrays if arrays > 1 else 0):

                @pl.when(shard == array)
                def _(array=array, start=start, slot=slot):
                    block_copy(array, 0, start, half, slot).start()

    fetch(0, 0)
    meta_copies = [
        pltpu.make_async_copy(
            weight_refs[shard // per_array].at[shard % per_array, 0, pl.ds(owned, META), :],
            metas.at[shard],
            meta_sems.at[shard],
        )
        for shard in range(shards)
    ]
    for copy in meta_copies:
        copy.start()
    for copy in meta_copies:
        copy.wait()

    @pl.loop(0, count)
    def _(i):
        half = lax.rem(i, 2)

        @pl.when(i + 1 < count)
        def _():
            fetch(i + 1, 1 - half)

        x = x_ref[pl.ds(pl.multiple_of(i * RB, RB), RB), :]
        constants = []
        for slot in range(CANDS):
            pos = pos_ref[i, slot]
            start = pl.multiple_of(lax.rem(pos, held) * CB, CB)
            constants.append(metas[lax.div(pos, held), :, pl.ds(start, CB)])
        densities = lax.dot_general(
            jnp.concatenate(constants, axis=1), pieces, TN, preferred_element_type=jnp.float32
        )
        for slot in range(CANDS):
            block_copy(0, 0, 0, half, slot).wait()
        densities += lax.dot_general(chosen[half, 0], x, NT, preferred_element_type=jnp.float32)
        densities += lax.dot_general(
            chosen[half, 1], x * x * -0.5, NT, preferred_element_type=jnp.float32
        )
        peak = jnp.max(densities, axis=0, keepdims=True)
        terms = jnp.exp(densities - peak)
        total = jnp.sum(terms, axis=0, keepdims=True)
        norm_ref[pl.ds(i, 1), :] = peak + jnp.log(total)
        resp = (terms * (1.0 / total)).astype(jnp.bfloat16)
        for slot in range(CANDS):
            resp_ref[i, slot] = resp[slot * CB : (slot + 1) * CB]


def responsibilities(rows, pos, weights, held):
    count = rows.shape[0] // RB
    feature_count = rows.shape[1]
    arrays = len(weights)
    shards = sum(w.shape[0] for w in weights)
    vmem = pl.BlockSpec(memory_space=pltpu.VMEM)
    pairs = count * CANDS
    return pl.pallas_call(
        functools.partial(density_body, count, held, shards, arrays),
        in_specs=[pl.BlockSpec(memory_space=pltpu.SMEM), vmem]
        + [pl.BlockSpec(memory_space=pl.ANY)] * arrays,
        out_specs=[vmem, vmem],
        out_shape=[
            pltpu.VMEM((count, CANDS, CB, RB), jnp.bfloat16),
            pltpu.VMEM((count, RB), jnp.float32),
        ],
        scratch_shapes=[
            pltpu.VMEM((2, 2, CANDS * CB, feature_count), jnp.bfloat16),
            pltpu.VMEM((shards, META, feature_count), jnp.bfloat16),
            pltpu.SemaphoreType.DMA((2, CANDS)),
            pltpu.SemaphoreType.DMA((shards,)),
        ],
        compiler_params=pltpu.CompilerParams(vmem_limit_bytes=VMEM_LIMIT),
        cost_estimate=pl.CostEstimate(
            flops=pairs * 4 * CB * RB * feature_count,
            bytes_accessed=pairs * CB * feature_count * 4 + rows.size * 2,
            transcendentals=pairs * CB * RB,
        ),
        name="responsibilities",
    )(pos, in_vmem(rows), *weights)


def pair_lists(pos, runs, group_blocks):
    run_of = []
    for index, count in enumerate(runs):
        run_of += [index] * (count * CANDS)
    run_of = jnp.array(run_of, jnp.int32)
    key = pos.reshape(-1) * len(runs) + run_of
    number = jnp.arange(key.shape[0], dtype=jnp.int32)
    before = jnp.logical_or(
        key[None, :] < key[:, None],
        jnp.logical_and(key[None, :] == key[:, None], number[None, :] < number[:, None]),
    )
    rank = jnp.sum(before.astype(jnp.int32), axis=1)
    order = jnp.sum(jnp.where(rank[None, :] == number[:, None], number[None, :], 0), axis=1)
    bounds = jnp.arange(group_blocks * len(runs) + 1, dtype=jnp.int32)
    starts = jnp.sum((key[None, :] < bounds[:, None]).astype(jnp.int32), axis=1)
    return order, starts


def moment_body(shards, held, runs, order_ref, start_ref, *rest):
    parts, outs = len(runs), len(shards)
    row_refs, resp_refs = rest[:parts], rest[parts : 2 * parts]
    out_refs = rest[2 * parts : 2 * parts + outs]
    sums, weight_sum = rest[2 * parts + outs :]
    owned = held * CB
    meta = slice(2 * owned, 2 * owned + META)
    feature_count = row_refs[0].shape[1]
    ones = jnp.ones((META, RB), jnp.float32)

    def block_sums(pos):
        sums[...] = jnp.zeros_like(sums)
        weight_sum[...] = jnp.zeros_like(weight_sum)
        base = 0
        for run in range(parts):
            entry = pos * parts + run
            low, high = start_ref[entry], start_ref[entry + 1]

            @pl.loop(0, lax.div(high - low + 1, 2))
            def _(step, base=base, run=run, low=low, high=high):
                one = low + 2 * step
                two = jnp.minimum(one + 1, high - 1)
                valid = jnp.full((CB, RB), (one + 1 < high).astype(jnp.float32))
                pair_a, pair_b = order_ref[one] - base, order_ref[two] - base
                row_a, row_b = lax.div(pair_a, CANDS), lax.div(pair_b, CANDS)
                weight_a = resp_refs[run][row_a, lax.rem(pair_a, CANDS)]
                weight_b = resp_refs[run][row_b, lax.rem(pair_b, CANDS)]
                weight_b = weight_b * valid.astype(jnp.bfloat16)
                weight = jnp.concatenate([weight_a, weight_b], axis=1)
                x = jnp.concatenate(
                    [
                        row_refs[run][pl.ds(pl.multiple_of(row_a * RB, RB), RB), :],
                        row_refs[run][pl.ds(pl.multiple_of(row_b * RB, RB), RB), :],
                    ],
                    axis=0,
                )
                sums[...] += jnp.dot(
                    weight,
                    jnp.concatenate([x, x * x], axis=1),
                    preferred_element_type=jnp.float32,
                )
                weight_sum[...] += weight_a.astype(jnp.float32) + weight_b.astype(jnp.float32)

            base += runs[run] * CANDS

    for shard, out_ref in zip(shards, out_refs):
        out_ref[meta, :] = jnp.zeros((META, out_ref.shape[1]), jnp.bfloat16)

        @pl.loop(0, held)
        def _(block, shard=shard, out_ref=out_ref):
            block_sums(shard * held + block)
            start = pl.multiple_of(block * CB, CB)
            out_ref[pl.ds(start, CB), :] = sums[:, :feature_count].astype(jnp.bfloat16)
            out_ref[pl.ds(owned + start, CB), :] = sums[:, feature_count:].astype(jnp.bfloat16)
            counts = lax.dot_general(
                ones,
                weight_sum[...],
                NT,
                precision=lax.Precision.HIGHEST,
                preferred_element_type=jnp.float32,
            )
            out_ref[meta, pl.ds(start, CB)] = counts.astype(jnp.bfloat16)


def moments(rows, resp, order, starts, held, shards):
    runs = tuple(r.shape[0] // RB for r in rows)
    feature_count = rows[0].shape[1]
    smem = pl.BlockSpec(memory_space=pltpu.SMEM)
    vmem = pl.BlockSpec(memory_space=pltpu.VMEM)
    pairs = sum(runs) * held * len(shards) // 8
    out_shape = pltpu.VMEM((2 * held * CB + META, feature_count), jnp.bfloat16)
    return pl.pallas_call(
        functools.partial(moment_body, tuple(shards), held, runs),
        in_specs=[smem, smem] + [vmem] * (2 * len(runs)),
        out_specs=[vmem] * len(shards),
        out_shape=[out_shape] * len(shards),
        scratch_shapes=[
            pltpu.VMEM((CB, 2 * feature_count), jnp.float32),
            pltpu.VMEM((CB, RB), jnp.float32),
        ],
        compiler_params=pltpu.CompilerParams(vmem_limit_bytes=VMEM_LIMIT),
        cost_estimate=pl.CostEstimate(
            flops=pairs * 4 * CB * RB * feature_count,
            bytes_accessed=pairs * RB * (feature_count + CB) * 2,
            transcendentals=0,
        ),
        name="moments",
    )(order, starts, *[in_vmem(r) for r in rows], *[in_vmem(r) for r in resp])


CHUNK = 80


def each_chunk(rows, step):
    whole = rows // CHUNK

    @pl.loop(0, whole)
    def _(i):
        step(pl.ds(pl.multiple_of(i * CHUNK, 16), CHUNK))

    if rows % CHUNK:
        step(slice(whole * CHUNK, rows))


def add_body(*refs):
    def step(here):
        terms = [ref[here, :].astype(jnp.float32) for ref in refs[:-1]]
        refs[-1][here, :] = functools.reduce(jnp.add, terms).astype(jnp.bfloat16)

    each_chunk(refs[-1].shape[0], step)


def join_body(*refs):
    start = 0
    for ref in refs[:-1]:
        refs[-1][start : start + ref.shape[0], :] = ref[...]
        start += ref.shape[0]


def small_step(body, shape, dtype, name, *operands):
    vmem = pl.BlockSpec(memory_space=pltpu.VMEM)
    return pl.pallas_call(
        body,
        in_specs=[vmem] * len(operands),
        out_specs=vmem,
        out_shape=pltpu.VMEM(shape, dtype),
        compiler_params=pltpu.CompilerParams(vmem_limit_bytes=VMEM_LIMIT),
        cost_estimate=pl.CostEstimate(
            flops=math.prod(shape), bytes_accessed=2 * math.prod(shape), transcendentals=0
        ),
        name=name,
    )(*[in_vmem(value) for value in operands])


def added(*terms):
    return small_step(add_body, terms[0].shape, jnp.bfloat16, "add_sums", *terms)


def joined(*norms):
    shape = (sum(n.shape[0] for n in norms), RB)
    return small_step(join_body, shape, jnp.float32, "join_norms", *norms)


def result_body(owned, end_ref, *refs):
    own_norm, end_norm, end_sum = refs[:3]
    terms, (count_ref, first_ref, second_ref, loglik_ref) = refs[3:-4], refs[-4:]
    is_end = end_ref[0] > 0
    block = pl.program_id(0)
    feature_count = first_ref.shape[1]

    def total(rows):
        inner = functools.reduce(jnp.add, [t[rows, :].astype(jnp.float32) for t in terms])
        return jnp.where(is_end, end_sum[rows, :].astype(jnp.float32), inner)

    start = pl.multiple_of(block * CB, CB)
    first_ref[...] = total(pl.ds(start, CB))
    second_ref[...] = total(pl.ds(owned + start, CB))
    count_ref[...] = total(slice(2 * owned, 2 * owned + META))[0:1, :owned]
    norm = jnp.where(is_end, end_norm[...], own_norm[...])
    loglik_ref[...] = norm * (1.0 / feature_count)


def results_of(is_end, own_norm, end_norm, end_sum, *terms):
    rows, feature_count = end_sum.shape
    owned = (rows - META) // 2
    vmem = pl.BlockSpec(memory_space=pltpu.VMEM)
    operands = (own_norm, end_norm, end_sum) + terms
    return pl.pallas_call(
        functools.partial(result_body, owned),
        grid=(owned // CB,),
        in_specs=[pl.BlockSpec(memory_space=pltpu.SMEM)] + [vmem] * len(operands),
        out_specs=[
            pl.BlockSpec((1, owned), lambda i: (0, 0)),
            pl.BlockSpec((CB, feature_count), lambda i: (i, 0)),
            pl.BlockSpec((CB, feature_count), lambda i: (i, 0)),
            pl.BlockSpec(own_norm.shape, lambda i: (0, 0)),
        ],
        out_shape=[
            jax.ShapeDtypeStruct((1, owned), jnp.float32),
            jax.ShapeDtypeStruct((owned, feature_count), jnp.float32),
            jax.ShapeDtypeStruct((owned, feature_count), jnp.float32),
            jax.ShapeDtypeStruct(own_norm.shape, jnp.float32),
        ],
        compiler_params=pltpu.CompilerParams(vmem_limit_bytes=VMEM_LIMIT),
        name="results",
    )(is_end.astype(jnp.int32).reshape(1), *[in_vmem(value) for value in operands])


def plain_plan(points, ids, parameters, held):
    weights = parameter_shard(*parameters, points, (0,))[0]
    dp_size = lax.axis_size("dp")
    all_weights = lax.all_gather(weights, "dp", axis=0, tiled=True)
    resp, norm = responsibilities(points, ids, [all_weights], held)
    order, starts = pair_lists(ids, (points.shape[0] // RB,), dp_size * held)
    sums = []
    for j in range(dp_size):
        sums += moments([points], [resp], order, starts, held, [j])
    total = lax.psum_scatter(jnp.concatenate(sums), "dp", scatter_dimension=0, tiled=True)
    total = total.astype(jnp.float32)
    owned = held * CB
    counts, first, second = total[2 * owned, :owned], total[:owned], total[owned : 2 * owned]
    return counts, first, second, norm.reshape(-1) / points.shape[1]


def line_pairs(links):
    return [(2 * a + c, 2 * b + c) for a, b in links for c in (0, 1)]


INWARD = line_pairs(((0, 1), (3, 2)))
OUTWARD = line_pairs(((1, 0), (2, 3)))
MIDDLE = line_pairs(((1, 2), (2, 1)))
CORES = [(2, 3), (3, 2), (4, 5), (5, 4)]


def move(value, pairs):
    return lax.ppermute(value, "dp", pairs)


def after(value, *others):
    return lax.optimization_barrier((value,) + others)[0]


def line_plan(points, ids, parameters, held):
    group_blocks = 8 * held
    index = lax.axis_index("dp")
    chip, core = index // 2, index % 2
    row_blocks = points.shape[0] // RB
    cuts = (0, row_blocks // 2, row_blocks - row_blocks // 8, row_blocks)
    weights, *pieces = parameter_shard(*parameters, points, [cut * RB for cut in cuts])

    outer = move(weights, INWARD)
    across = move(weights, MIDDLE)
    own_shared = move(weights, CORES)
    moved = [move(after(pieces[0], outer), INWARD)]
    far = move(outer, MIDDLE)
    outer_shared = move(outer, CORES)
    across_shared = move(across, CORES)
    moved.append(move(after(pieces[1], moved[0]), INWARD))
    moved.append(move(after(pieces[2], moved[0], far), INWARD))
    far_shared = move(far, CORES)
    shards = [weights, own_shared, outer, outer_shared, across, across_shared, far, far_shared]

    def place(nat):
        holder = nat // held
        z = jnp.where(chip < 2, holder // 2, 3 - holder // 2)
        z = jnp.where(z == 0, 1, jnp.where(z == 1, 0, z))
        other = (holder % 2 + core) % 2
        return (z * 2 + other) * held + nat % held

    end_pos = place(after(move(ids, INWARD), moved[0]))
    own_pos = place(ids)
    rows = [points] + moved
    runs = (row_blocks,) + tuple(b - a for a, b in zip(cuts[:-1], cuts[1:]))
    order, starts = pair_lists(jnp.concatenate([own_pos, end_pos]), runs, group_blocks)
    run_pos = [own_pos] + [end_pos[a:b] for a, b in zip(cuts[:-1], cuts[1:])]
    results = []
    for run_rows, pos in zip(rows, run_pos):
        if results:
            pos = after(pos, results[-1][1])
        results.append(responsibilities(run_rows, pos, shards, held))
    resp = [r[0] for r in results]

    def sums_of(position, *earlier):
        return moments(rows, resp, after(order, *earlier), starts, held, [position])[0]

    end_norm = move(joined(*[r[1] for r in results[1:]]), OUTWARD)
    far_other = sums_of(7)
    far_received = move(far_other, CORES)
    far_own = sums_of(6, far_other)
    far_part = added(far_own, far_received)
    far_sum = move(far_part, MIDDLE)
    across_other = sums_of(5, far_part, end_norm)
    across_received = move(across_other, CORES)
    across_own = sums_of(4, across_other)
    across_part = added(across_own, across_received)
    across_sum = move(across_part, MIDDLE)
    outer_other = sums_of(3, across_part)
    outer_received = move(outer_other, CORES)
    own_other = sums_of(1, outer_other)
    own_received = move(own_other, CORES)
    outer_own = sums_of(2, own_other)
    own_own = sums_of(0, outer_own)
    outer_sum = added(outer_own, outer_received, far_sum)
    end_sum = move(outer_sum, OUTWARD)
    is_end = jnp.logical_or(chip == 0, chip == 3)
    counts, first, second, loglik = results_of(
        is_end, results[0][1], end_norm, end_sum, own_own, own_received, across_sum
    )
    return counts.reshape(-1), first, second, loglik.reshape(-1)


def on_device(points, candidates, means, inv_var, log_weight):
    feature_count = points.shape[1]
    owner_count = lax.axis_size("comp")
    owned = means.shape[0]
    held = owned // CB
    ids = candidates // (owner_count * held) * held + candidates % held
    plan = line_plan if lax.axis_size("dp") == 8 else plain_plan
    return plan(points, ids, (means, inv_var, log_weight), held)


def solution(mesh):
    return jax.shard_map(
        on_device,
        mesh=mesh,
        in_specs=(
            P(("dp", "comp"), None),
            P(("dp", "comp"), None),
            P(("dp", "comp"), None),
            P(("dp", "comp"), None),
            P(("dp", "comp")),
        ),
        out_specs=(
            P(("dp", "comp")),
            P(("dp", "comp"), None),
            P(("dp", "comp"), None),
            P(("dp", "comp")),
        ),
        check_vma=False,
    )
```

time: 259 us -> 268 us (1.035)
  Pallas kernels: 68.8 us -> 105 us
  local copies, waits for them, and re-layouts: 39.5 us -> 14.3 us
  other arithmetic: 15.4 us -> 0.57 us
  waiting for transfers between devices: 91 us -> 99.9 us
  starting transfers between devices: 41.4 us -> 44.7 us
    pallas_call x5 -> x10, Pallas kernels: 31.1 us -> 59.7 us  [the longest x4 48 us: responsibilities(): pl.pallas_call(functools.partial(density_body, count, held, shards, array...]
    unnamed x60 -> x47, local copies, waits for them, and re-layouts: 32.1 us -> 11.5 us
    ppermute x19, waiting for transfers between devices: 91 us -> 99.9 us  [move(): return lax.ppermute(value, 'dp', pairs)]
    pallas_call x8, Pallas kernels: 37.7 us -> 45.1 us  [moments(): pl.pallas_call(functools.partial(moment_body, tuple(shards), held, runs),...]
    select_n x2 -> x0, other arithmetic: 5.22 us -> none  [total(): return jnp.where(is_end, end_sum[rows_of, columns].astype(jnp.float32), own)]
    convert_element_type x3 -> x0, other arithmetic: 3.92 us -> none  [the longest x1 1.83 us: line_plan(): outer_sum = (outer_part + far_sum.astype(jnp.float32)).astype(jnp.bfloat16)]
    ppermute x19, starting transfers between devices: 41.4 us -> 44.7 us  [move(): return lax.ppermute(value, 'dp', pairs)]
    slice x3 -> x0, local copies, waits for them, and re-layouts: 3.1 us -> none  [line_plan(): pieces = [points[a * RB:b * RB] for a, b in zip(cuts[:-1], cuts[1:])]]
  transfers between devices with their start and end apart: 19 -> 19, of which waited for: 3 -> 4; matrix products, arithmetic and copies ran while one was open for 13% -> 1% of each run, Pallas kernels for 22% -> 31%
where the time goes in v3:
time: 268 us; the launch traced here: 265 us
  Pallas kernels  105 us (39%)
  waiting for transfers between devices  99.9 us (37%)
  starting transfers between devices  44.7 us (17%)
  local copies, waits for them, and re-layouts  14.3 us (5%)
    ppermute x19, waiting for transfers between devices, move(): return lax.ppermute(value, 'dp', pairs)  99.9 us
    pallas_call x4, Pallas kernels, responsibilities(): pl.pallas_call(functools.partial(density_body, count, held, shards, array...  48 us
    pallas_call x8, Pallas kernels, moments(): pl.pallas_call(functools.partial(moment_body, tuple(shards), held, runs),...  45.1 us
    ppermute x19, starting transfers between devices, move(): return lax.ppermute(value, 'dp', pairs)  44.7 us
    unnamed x47, local copies, waits for them, and re-layouts  11.5 us
  transfers between devices with their start and end apart: 19, of which 4 were waited for; matrix products, arithmetic and copies ran while one was open for 1% of the time, Pallas kernels for 31%

profile of v3, /device:TPU:0, one launch (start us, length us, event | category | flops | bytes accessed | tf_op | source)
XLA Modules:
  0.0 265.4 jit_solution(6095238405819104528)
XLA Ops:
  1.3 1.9 copy-done
  5.5 3.1 %parameter_shard.1 = (bf16[1,2,528,768]{3,2,1,0:T(8,128)(2,1)}, bf16[1024,768]{1,0:T(8,128)(2,1)}, bf16[768,768]{1,0:T(8,128)(2,1)S(1)}, bf16[256,768]{1,0:T(8,128)(2,1)S(1)}) custom-call(bf16[512,768]{1,0:T(8,128)(2,1)S(1)} %copy-done.10, bf16[512,768]{1,0:T(8,128)(2,1)S(1)} %copy-done.11, bf16[1,512]{1,0:T(2,128)(2,1)S(1)} %reshape.30.log_ref, ...), custom_call_target="tpu_custom_call" | custom-call | flops 15728640 | bytes 3145728 | tf_op jit(solution)/shard_map/parameter_shard/pallas_call | solution.py:66
  10.3 6.1 %collective-permute-start.1 = (bf16[1,2,528,768]{3,2,1,0:T(8,128)(2,1)}, bf16[1,2,528,768]{3,2,1,0:T(8,128)(2,1)}, u32[]{:S(2)}, u32[]{:S(2)}) collective-permute-start(bf16[1,2,528,768]{3,2,1,0:T(8,128)(2,1)} %get-tuple-element.34.rest_0_), channel_id=1, source_target_pairs={{0,8},{4,12},{24,16},{28,20},{1,9},{5,13},{25,17},{29,21},{2,10},{... | collective-permute-start | bytes 4866056 | tf_op jit(solution)/shard_map/ppermute | solution.py:422
  16.5 1.9 collective-permute-start.3
  18.3 31.9 %collective-permute-done.1.rest_2_ = bf16[1,2,528,768]{3,2,1,0:T(8,128)(2,1)} collective-permute-done((bf16[1,2,528,768]{3,2,1,0:T(8,128)(2,1)}, bf16[1,2,528,768]{3,2,1,0:T(8,128)(2,1)}, u32[]{:S(2)}, u32[]{:S(2)}) %collective-permute-start.1) | collective-permute-done | bytes 1622048 | tf_op jit(solution)/shard_map/ppermute | solution.py:422
  50.3 1.9 collective-permute-start.5
  52.2 7.1 %collective-permute-start.8 = (bf16[1024,768]{1,0:T(8,128)(2,1)}, bf16[1024,768]{1,0:T(8,128)(2,1)}, u32[]{:S(2)}, u32[]{:S(2)}) collective-permute-start(bf16[1024,768]{1,0:T(8,128)(2,1)} %get-tuple-element.37), channel_id=1, source_target_pairs={{0,8},{4,12},{24,16},{28,20},{1,9},{5,13},{25,17},{29,21},{2,10},{... | collective-permute-start | bytes 4718600 | tf_op jit(solution)/shard_map/ppermute | solution.py:422
  59.3 1.8 collective-permute-start
  61.1 1.8 collective-permute-start.2
  62.9 1.9 collective-permute-start.4
  64.8 1.8 collective-permute-start.6
  66.8 24.2 %collective-permute-done.8.x_ref.rest_1_ = bf16[1024,768]{1,0:T(8,128)(2,1)} collective-permute-done((bf16[1024,768]{1,0:T(8,128)(2,1)}, bf16[1024,768]{1,0:T(8,128)(2,1)}, u32[]{:S(2)}, u32[]{:S(2)}) %collective-permute-start.8) | collective-permute-done | bytes 1572896 | tf_op jit(solution)/shard_map/ppermute | solution.py:422
  90.9 4.4 %collective-permute-start.7 = (s32[16,4]{1,0:T(8,128)S(1)}, s32[16,4]{1,0:T(8,128)S(1)}, u32[]{:S(2)}, u32[]{:S(2)}) collective-permute-start(s32[16,4]{1,0:T(8,128)S(1)} %get-tuple-element.65), channel_id=1, source_target_pairs={{0,8},{4,12},{24,16},{28,20},{1,9},{5,13},{25,17},{29,21},{2,10},{... | collective-permute-start | bytes 776 | tf_op jit(solution)/shard_map/ppermute | solution.py:422
  96.7 5.2 %collective-permute-start.9 = (bf16[768,768]{1,0:T(8,128)(2,1)}, bf16[768,768]{1,0:T(8,128)(2,1)}, u32[]{:S(2)}, u32[]{:S(2)}) collective-permute-start(bf16[768,768]{1,0:T(8,128)(2,1)} %copy-done.19), channel_id=1, source_target_pairs={{0,8},{4,12},{24,16},{28,20},{1,9},{5,13},{25,17},{29,21},{2,10},{... | collective-permute-start | bytes 3538952 | tf_op jit(solution)/shard_map/ppermute | solution.py:422
  105.8 19.5 %responsibilities.4 = (bf16[16,4,128,128]{3,2,1,0:T(8,128)(2,1)S(1)}, f32[16,128]{1,0:T(8,128)S(1)}) custom-call(s32[16,4]{1,0:T(8,128)S(1)} %get-tuple-element.64.pos_ref, bf16[2048,768]{1,0:T(8,128)(2,1)S(1)} %copy-done.1, bf16[1,2,528,768]{3,2,1,0:T(8,128)(2,1)} %get-tuple-element.34.rest_0_, bf16[1,2,528,768]{3,2,1,0:T(8,128)(2,1)} %collective-permute-done.rest_1_, ...), custom_call_target="tpu_custom_call" | custom-call | flops 3221225472 | bytes 28311552 | tf_op jit(solution)/shard_map/responsibilities/pallas_call | solution.py:164
  125.9 13.4 %responsibilities.5 = (bf16[8,4,128,128]{3,2,1,0:T(8,128)(2,1)S(1)}, f32[8,128]{1,0:T(8,128)S(1)}) custom-call(s32[8,4]{1,0:T(8,128)S(1)} %copy-done.13, bf16[1024,768]{1,0:T(8,128)(2,1)} %collective-permute-done.8.x_ref.rest_1_, bf16[1,2,528,768]{3,2,1,0:T(8,128)(2,1)} %get-tuple-element.34.rest_0_, bf16[1,2,528,768]{3,2,1,0:T(8,128)(2,1)} %collective-permute-done.rest_1_, ...), custom_call_target="tpu_custom_call" | custom-call | flops 1610612736 | bytes 14155776 | tf_op jit(solution)/shard_map/responsibilities/pallas_call | solution.py:164
  139.4 10.5 %responsibilities.6 = (bf16[6,4,128,128]{3,2,1,0:T(8,128)(2,1)S(1)}, f32[6,128]{1,0:T(8,128)S(1)}) custom-call(s32[6,4]{1,0:T(8,128)S(1)} %copy-done.12, bf16[768,768]{1,0:T(8,128)(2,1)} %collective-permute-done.9.x_ref.rest_2_, bf16[1,2,528,768]{3,2,1,0:T(8,128)(2,1)} %get-tuple-element.34.rest_0_, bf16[1,2,528,768]{3,2,1,0:T(8,128)(2,1)} %collective-permute-done.rest_1_, ...), custom_call_target="tpu_custom_call" | custom-call | flops 1207959552 | bytes 10616832 | tf_op jit(solution)/shard_map/responsibilities/pallas_call | solution.py:164
  149.9 4.6 %responsibilities.7 = (bf16[2,4,128,128]{3,2,1,0:T(8,128)(2,1)S(1)}, f32[2,128]{1,0:T(2,128)S(1)}) custom-call(s32[2,4]{1,0:T(2,128)S(1)} %copy-done.18, bf16[256,768]{1,0:T(8,128)(2,1)S(1)} %collective-permute-done.10.x_ref.rest_3_, bf16[1,2,528,768]{3,2,1,0:T(8,128)(2,1)} %get-tuple-element.34.rest_0_, ...), custom_call_target="tpu_custom_call" | custom-call | flops 402653184 | bytes 3538944 | tf_op jit(solution)/shard_map/responsibilities/pallas_call | solution.py:164
  154.6 5.0 %moments.8 = bf16[1040,768]{1,0:T(8,128)(2,1)S(1)} custom-call(s32[128]{0:T(128)S(1)} %select_reduce_fusion.order_ref, s32[129]{0:T(256)S(1)} %convert_reduce_fusion.start_ref, bf16[2048,768]{1,0:T(8,128)(2,1)S(1)} %copy-done.1, bf16[1024,768]{1,0:T(8,128)(2,1)} %collective-permute-done.8.x_ref.rest_1_, ...), custom_call_target="tpu_custom_call" | custom-call | flops 805306368 | bytes 3670016 | tf_op jit(solution)/shard_map/moments/pallas_call | solution.py:278
  161.7 3.8 %moments.9.refs_0_ = bf16[1040,768]{1,0:T(8,128)(2,1)S(1)} custom-call(s32[128]{0:T(128)S(1)} %select_reduce_fusion.order_ref, s32[129]{0:T(256)S(1)} %convert_reduce_fusion.start_ref, bf16[2048,768]{1,0:T(8,128)(2,1)S(1)} %copy-done.1, bf16[1024,768]{1,0:T(8,128)(2,1)} %collective-permute-done.8.x_ref.rest_1_, ...), custom_call_target="tpu_custom_call" | custom-call | flops 805306368 | bytes 3670016 | tf_op jit(solution)/shard_map/moments/pallas_call | solution.py:278
  166.0 4.4 %moments.10 = bf16[1040,768]{1,0:T(8,128)(2,1)S(1)} custom-call(s32[128]{0:T(128)S(1)} %select_reduce_fusion.order_ref, s32[129]{0:T(256)S(1)} %convert_reduce_fusion.start_ref, bf16[2048,768]{1,0:T(8,128)(2,1)S(1)} %copy-done.1, bf16[1024,768]{1,0:T(8,128)(2,1)} %collective-permute-done.8.x_ref.rest_1_, ...), custom_call_target="tpu_custom_call" | custom-call | flops 805306368 | bytes 3670016 | tf_op jit(solution)/shard_map/moments/pallas_call | solution.py:278
  172.1 4.1 %moments.11.refs_0_ = bf16[1040,768]{1,0:T(8,128)(2,1)S(1)} custom-call(s32[128]{0:T(128)S(1)} %select_reduce_fusion.order_ref, s32[129]{0:T(256)S(1)} %convert_reduce_fusion.start_ref, bf16[2048,768]{1,0:T(8,128)(2,1)S(1)} %copy-done.1, bf16[1024,768]{1,0:T(8,128)(2,1)} %collective-permute-done.8.x_ref.rest_1_, ...), custom_call_target="tpu_custom_call" | custom-call | flops 805306368 | bytes 3670016 | tf_op jit(solution)/shard_map/moments/pallas_call | solution.py:278
  176.2 1.7 add_sums.4
  177.9 4.7 %moments.12 = bf16[1040,768]{1,0:T(8,128)(2,1)S(1)} custom-call(s32[128]{0:T(128)S(1)} %select_reduce_fusion.order_ref, s32[129]{0:T(256)S(1)} %convert_reduce_fusion.start_ref, bf16[2048,768]{1,0:T(8,128)(2,1)S(1)} %copy-done.1, bf16[1024,768]{1,0:T(8,128)(2,1)} %collective-permute-done.8.x_ref.rest_1_, ...), custom_call_target="tpu_custom_call" | custom-call | flops 805306368 | bytes 3670016 | tf_op jit(solution)/shard_map/moments/pallas_call | solution.py:278
  183.4 5.0 %moments.13 = bf16[1040,768]{1,0:T(8,128)(2,1)} custom-call(s32[128]{0:T(128)S(1)} %select_reduce_fusion.order_ref, s32[129]{0:T(256)S(1)} %convert_reduce_fusion.start_ref, bf16[2048,768]{1,0:T(8,128)(2,1)S(1)} %copy-done.1, bf16[1024,768]{1,0:T(8,128)(2,1)} %collective-permute-done.8.x_ref.rest_1_, bf16[768,768]{1,0:T(8,128)(2,1)} %collective-permute-done.9.x_ref.rest_2_, ...), custom_call_target="tpu_custom_call" | custom-call | flops 805306368 | bytes 3670016 | tf_op jit(solution)/shard_map/moments/pallas_call | solution.py:278
  188.4 1.8 collective-permute-start.17
  190.2 1.8 collective-permute-start.18
  192.0 13.4 %moments.14.refs_0_ = bf16[1040,768]{1,0:T(8,128)(2,1)S(1)} custom-call(s32[128]{0:T(128)S(1)} %select_reduce_fusion.order_ref, s32[129]{0:T(256)S(1)} %convert_reduce_fusion.start_ref, bf16[2048,768]{1,0:T(8,128)(2,1)S(1)} %copy-done.1, bf16[1024,768]{1,0:T(8,128)(2,1)} %collective-permute-done.8.x_ref.rest_1_, ...), custom_call_target="tpu_custom_call" | custom-call | flops 805306368 | bytes 3670016 | tf_op jit(solution)/shard_map/moments/pallas_call | solution.py:278
  205.4 1.8 add_sums.5
  213.4 4.7 %moments.15.refs_3_ = bf16[1040,768]{1,0:T(8,128)(2,1)S(1)} custom-call(s32[128]{0:T(128)S(1)} %select_reduce_fusion.order_ref, s32[129]{0:T(256)S(1)} %convert_reduce_fusion.start_ref, bf16[2048,768]{1,0:T(8,128)(2,1)S(1)} %copy-done.1, bf16[1024,768]{1,0:T(8,128)(2,1)} %collective-permute-done.8.x_ref.rest_1_, ...), custom_call_target="tpu_custom_call" | custom-call | flops 805306368 | bytes 3670016 | tf_op jit(solution)/shard_map/moments/pallas_call | solution.py:278
  218.2 42.5 %collective-permute-done.16.refs_2_ = bf16[1040,768]{1,0:T(8,128)(2,1)} collective-permute-done((bf16[1040,768]{1,0:T(8,128)(2,1)}, bf16[1040,768]{1,0:T(8,128)(2,1)}, u32[]{:S(2)}, u32[]{:S(2)}) %collective-permute-start.16) | collective-permute-done | bytes 1597472 | tf_op jit(solution)/shard_map/ppermute | solution.py:422
  260.6 4.7 %results.1 = (f32[1,512]{1,0:T(1,128)}, f32[512,768]{1,0:T(8,128)}, f32[512,768]{1,0:T(8,128)}, f32[16,128]{1,0:T(8,128)}) custom-call(s32[1]{0:T(128)} %bitcast.end_ref, f32[16,128]{1,0:T(8,128)S(1)} %copy-done.15, f32[16,128]{1,0:T(8,128)S(1)} %copy-done.17, bf16[1040,768]{1,0:T(8,128)(2,1)} %collective-permute-done.16.refs_2_, ...), custom_call_target="tpu_custom_call" | custom-call | tf_op jit(solution)/shard_map/results/pallas_call | solution.py:374
  (85 shorter events, 21.9 us)
Async XLA Ops:
  5.5 61.2 %copy-start.21 = (s32[16,4]{0,1:T(4,128)S(1)}, s32[16,4]{0,1:T(4,128)}, u32[]{:S(2)}) copy-start(s32[16,4]{0,1:T(4,128)} %param.7) | copy-start | bytes 772
  5.5 98.3 %copy-start.22 = (s32[32,4]{0,1:T(4,128)S(1)}, s32[32,4]{0,1:T(4,128)}, u32[]{:S(2)}) copy-start(s32[32,4]{0,1:T(4,128)} %constant.132) | copy-start | bytes 1540
  5.5 100.3 %copy-start.1 = (bf16[2048,768]{1,0:T(8,128)(2,1)S(1)}, bf16[2048,768]{1,0:T(8,128)(2,1)}, u32[]{:S(2)}) copy-start(bf16[2048,768]{1,0:T(8,128)(2,1)} %rest_0_.15) | copy-start | bytes 9437188
  10.3 39.9 %collective-permute-start.1 = (bf16[1,2,528,768]{3,2,1,0:T(8,128)(2,1)}, bf16[1,2,528,768]{3,2,1,0:T(8,128)(2,1)}, u32[]{:S(2)}, u32[]{:S(2)}) collective-permute-start(bf16[1,2,528,768]{3,2,1,0:T(8,128)(2,1)} %get-tuple-element.34.rest_0_), channel_id=1, source_target_pairs={{0,8},{4,12},{24,16},{28,20},{1,9},{5,13},{25,17},{29,21},{2,10},{... | collective-permute-start | bytes 4866056 | tf_op jit(solution)/shard_map/ppermute | solution.py:422
  16.5 46.4 %collective-permute-start.3 = (bf16[1,2,528,768]{3,2,1,0:T(8,128)(2,1)}, bf16[1,2,528,768]{3,2,1,0:T(8,128)(2,1)}, u32[]{:S(2)}, u32[]{:S(2)}) collective-permute-start(bf16[1,2,528,768]{3,2,1,0:T(8,128)(2,1)} %get-tuple-element.34.rest_0_), channel_id=1, source_target_pairs={{8,16},{12,20},{16,8},{20,12},{9,17},{13,21},{17,9},{21,13},{10,18... | collective-permute-start | bytes 4866056 | tf_op jit(solution)/shard_map/ppermute | solution.py:422
  50.3 14.5 %collective-permute-start.5 = (bf16[1,2,528,768]{3,2,1,0:T(8,128)(2,1)}, bf16[1,2,528,768]{3,2,1,0:T(8,128)(2,1)}, u32[]{:S(2)}, u32[]{:S(2)}) collective-permute-start(bf16[1,2,528,768]{3,2,1,0:T(8,128)(2,1)} %collective-permute-done.1.rest_2_), channel_id=1, source_target_pairs={{8,16},{12,20},{16,8},{20,12},{9,17},{13,21},{17,9},{21,13},{10,18... | collective-permute-start | bytes 4866056 | tf_op jit(solution)/shard_map/ppermute | solution.py:422
  52.2 38.8 %collective-permute-start.8 = (bf16[1024,768]{1,0:T(8,128)(2,1)}, bf16[1024,768]{1,0:T(8,128)(2,1)}, u32[]{:S(2)}, u32[]{:S(2)}) collective-permute-start(bf16[1024,768]{1,0:T(8,128)(2,1)} %get-tuple-element.37), channel_id=1, source_target_pairs={{0,8},{4,12},{24,16},{28,20},{1,9},{5,13},{25,17},{29,21},{2,10},{... | collective-permute-start | bytes 4718600 | tf_op jit(solution)/shard_map/ppermute | solution.py:422
  59.3 45.2 %collective-permute-start = (bf16[1,2,528,768]{3,2,1,0:T(8,128)(2,1)}, bf16[1,2,528,768]{3,2,1,0:T(8,128)(2,1)}, u32[]{:S(2)}, u32[]{:S(2)}) collective-permute-start(bf16[1,2,528,768]{3,2,1,0:T(8,128)(2,1)} %get-tuple-element.34.rest_0_), channel_id=1, source_target_pairs={{8,12},{12,8},{16,20},{20,16},{9,13},{13,9},{17,21},{21,17},{10,14... | collective-permute-start | bytes 4866056 | tf_op jit(solution)/shard_map/ppermute | solution.py:422
  61.1 44.7 %collective-permute-start.2 = (bf16[1,2,528,768]{3,2,1,0:T(8,128)(2,1)}, bf16[1,2,528,768]{3,2,1,0:T(8,128)(2,1)}, u32[]{:S(2)}, u32[]{:S(2)}) collective-permute-start(bf16[1,2,528,768]{3,2,1,0:T(8,128)(2,1)} %collective-permute-done.1.rest_2_), channel_id=1, source_target_pairs={{8,12},{12,8},{16,20},{20,16},{9,13},{13,9},{17,21},{21,17},{10,14... | collective-permute-start | bytes 4866056 | tf_op jit(solution)/shard_map/ppermute | solution.py:422
  62.9 42.9 %collective-permute-start.4 = (bf16[1,2,528,768]{3,2,1,0:T(8,128)(2,1)}, bf16[1,2,528,768]{3,2,1,0:T(8,128)(2,1)}, u32[]{:S(2)}, u32[]{:S(2)}) collective-permute-start(bf16[1,2,528,768]{3,2,1,0:T(8,128)(2,1)} %collective-permute-done.3.rest_4_), channel_id=1, source_target_pairs={{8,12},{12,8},{16,20},{20,16},{9,13},{13,9},{17,21},{21,17},{10,14... | collective-permute-start | bytes 4866056 | tf_op jit(solution)/shard_map/ppermute | solution.py:422
  64.8 41.0 %collective-permute-start.6 = (bf16[1,2,528,768]{3,2,1,0:T(8,128)(2,1)}, bf16[1,2,528,768]{3,2,1,0:T(8,128)(2,1)}, u32[]{:S(2)}, u32[]{:S(2)}) collective-permute-start(bf16[1,2,528,768]{3,2,1,0:T(8,128)(2,1)} %collective-permute-done.5.rest_6_), channel_id=1, source_target_pairs={{8,12},{12,8},{16,20},{20,16},{9,13},{13,9},{17,21},{21,17},{10,14... | collective-permute-start | bytes 4866056 | tf_op jit(solution)/shard_map/ppermute | solution.py:422
  90.9 5.7 %collective-permute-start.7 = (s32[16,4]{1,0:T(8,128)S(1)}, s32[16,4]{1,0:T(8,128)S(1)}, u32[]{:S(2)}, u32[]{:S(2)}) collective-permute-start(s32[16,4]{1,0:T(8,128)S(1)} %get-tuple-element.65), channel_id=1, source_target_pairs={{0,8},{4,12},{24,16},{28,20},{1,9},{5,13},{25,17},{29,21},{2,10},{... | collective-permute-start | bytes 776 | tf_op jit(solution)/shard_map/ppermute | solution.py:422
  96.7 42.7 %collective-permute-start.9 = (bf16[768,768]{1,0:T(8,128)(2,1)}, bf16[768,768]{1,0:T(8,128)(2,1)}, u32[]{:S(2)}, u32[]{:S(2)}) collective-permute-start(bf16[768,768]{1,0:T(8,128)(2,1)} %copy-done.19), channel_id=1, source_target_pairs={{0,8},{4,12},{24,16},{28,20},{1,9},{5,13},{25,17},{29,21},{2,10},{... | collective-permute-start | bytes 3538952 | tf_op jit(solution)/shard_map/ppermute | solution.py:422
  104.4 21.5 %copy-start.13 = (s32[8,4]{1,0:T(8,128)S(1)}, s32[8,4]{1,0:T(8,128)}, u32[]{:S(2)}) copy-start(s32[8,4]{1,0:T(8,128)} %slice.12.pos_ref) | copy-start | bytes 388
  104.5 45.5 %collective-permute-start.10 = (bf16[256,768]{1,0:T(8,128)(2,1)}, bf16[256,768]{1,0:T(8,128)(2,1)S(1)}, u32[]{:S(2)}, u32[]{:S(2)}) collective-permute-start(bf16[256,768]{1,0:T(8,128)(2,1)} %copy-done.20), channel_id=1, source_target_pairs={{0,8},{4,12},{24,16},{28,20},{1,9},{5,13},{25,17},{29,21},{2,10},{... | collective-permute-start | bytes 1179656 | tf_op jit(solution)/shard_map/ppermute | solution.py:422
  125.9 66.1 %copy-start.2 = (bf16[16,4,128,128]{3,2,1,0:T(8,128)(2,1)}, bf16[16,4,128,128]{3,2,1,0:T(8,128)(2,1)S(1)}, u32[]{:S(2)}) copy-start(bf16[16,4,128,128]{3,2,1,0:T(8,128)(2,1)S(1)} %get-tuple-element.49.rest_4_) | copy-start | bytes 6291460
  125.9 13.5 %copy-start.12 = (s32[6,4]{1,0:T(8,128)S(1)}, s32[6,4]{1,0:T(8,128)}, u32[]{:S(2)}) copy-start(s32[6,4]{1,0:T(8,128)} %slice.13.pos_ref) | copy-start | bytes 292
  139.3 52.7 %copy-start.4 = (bf16[8,4,128,128]{3,2,1,0:T(8,128)(2,1)}, bf16[8,4,128,128]{3,2,1,0:T(8,128)(2,1)S(1)}, u32[]{:S(2)}) copy-start(bf16[8,4,128,128]{3,2,1,0:T(8,128)(2,1)S(1)} %get-tuple-element.50.rest_5_) | copy-start | bytes 3145732
  139.3 10.6 %copy-start.18 = (s32[2,4]{1,0:T(2,128)S(1)}, s32[2,4]{1,0:T(2,128)}, u32[]{:S(2)}) copy-start(s32[2,4]{1,0:T(2,128)} %slice.14.pos_ref) | copy-start | bytes 100
  149.9 42.1 %copy-start.6 = (bf16[6,4,128,128]{3,2,1,0:T(8,128)(2,1)}, bf16[6,4,128,128]{3,2,1,0:T(8,128)(2,1)S(1)}, u32[]{:S(2)}) copy-start(bf16[6,4,128,128]{3,2,1,0:T(8,128)(2,1)S(1)} %get-tuple-element.51.rest_6_) | copy-start | bytes 2359300
  154.6 37.5 %copy-start.8 = (bf16[2,4,128,128]{3,2,1,0:T(8,128)(2,1)}, bf16[2,4,128,128]{3,2,1,0:T(8,128)(2,1)S(1)}, u32[]{:S(2)}) copy-start(bf16[2,4,128,128]{3,2,1,0:T(8,128)(2,1)S(1)} %get-tuple-element.52.rest_7_) | copy-start | bytes 786436
  159.6 5.9 %collective-permute-start.12 = (bf16[1040,768]{1,0:T(8,128)(2,1)S(1)}, bf16[1040,768]{1,0:T(8,128)(2,1)S(1)}, u32[]{:S(2)}, u32[]{:S(2)}) collective-permute-start(bf16[1040,768]{1,0:T(8,128)(2,1)S(1)} %moments.8), channel_id=1, source_target_pairs={{8,12},{12,8},{16,20},{20,16},{9,13},{13,9},{17,21},{21,17},{10,14... | collective-permute-start | bytes 4792328 | tf_op jit(solution)/shard_map/ppermute | solution.py:422
  160.4 5.6 %collective-permute-start.11 = (f32[16,128]{1,0:T(8,128)S(1)}, f32[16,128]{1,0:T(8,128)S(1)}, u32[]{:S(2)}, u32[]{:S(2)}) collective-permute-start(f32[16,128]{1,0:T(8,128)S(1)} %join_norms.1), channel_id=1, source_target_pairs={{8,0},{12,4},{16,24},{20,28},{9,1},{13,5},{17,25},{21,29},{10,2},{... | collective-permute-start | bytes 24584 | tf_op jit(solution)/shard_map/ppermute | solution.py:422
  166.0 4.4 %copy-start.16 = (f32[16,128]{1,0:T(8,128)}, f32[16,128]{1,0:T(8,128)S(1)}, u32[]{:S(2)}) copy-start(f32[16,128]{1,0:T(8,128)S(1)} %collective-permute-done.11.refs_1_) | copy-start | bytes 24580
  170.4 5.8 %collective-permute-start.13 = (bf16[1040,768]{1,0:T(8,128)(2,1)S(1)}, bf16[1040,768]{1,0:T(8,128)(2,1)S(1)}, u32[]{:S(2)}, u32[]{:S(2)}) collective-permute-start(bf16[1040,768]{1,0:T(8,128)(2,1)S(1)} %moments.10), channel_id=1, source_target_pairs={{8,12},{12,8},{16,20},{20,16},{9,13},{13,9},{17,21},{21,17},{10,14... | collective-permute-start | bytes 4792328 | tf_op jit(solution)/shard_map/ppermute | solution.py:422
  171.2 34.3 %collective-permute-start.15 = (bf16[1040,768]{1,0:T(8,128)(2,1)S(1)}, bf16[1040,768]{1,0:T(8,128)(2,1)S(1)}, u32[]{:S(2)}, u32[]{:S(2)}) collective-permute-start(bf16[1040,768]{1,0:T(8,128)(2,1)S(1)} %add_sums.3), channel_id=1, source_target_pairs={{8,16},{12,20},{16,8},{20,12},{9,17},{13,21},{17,9},{21,13},{10,18... | collective-permute-start | bytes 4792328 | tf_op jit(solution)/shard_map/ppermute | solution.py:422
  182.6 22.8 %collective-permute-start.14 = (bf16[1040,768]{1,0:T(8,128)(2,1)S(1)}, bf16[1040,768]{1,0:T(8,128)(2,1)S(1)}, u32[]{:S(2)}, u32[]{:S(2)}) collective-permute-start(bf16[1040,768]{1,0:T(8,128)(2,1)S(1)} %moments.12), channel_id=1, source_target_pairs={{8,12},{12,8},{16,20},{20,16},{9,13},{13,9},{17,21},{21,17},{10,14... | collective-permute-start | bytes 4792328 | tf_op jit(solution)/shard_map/ppermute | solution.py:422
  188.4 29.8 %collective-permute-start.17 = (bf16[1040,768]{1,0:T(8,128)(2,1)}, bf16[1040,768]{1,0:T(8,128)(2,1)}, u32[]{:S(2)}, u32[]{:S(2)}) collective-permute-start(bf16[1040,768]{1,0:T(8,128)(2,1)} %moments.13), channel_id=1, source_target_pairs={{8,12},{12,8},{16,20},{20,16},{9,13},{13,9},{17,21},{21,17},{10,14... | collective-permute-start | bytes 4792328 | tf_op jit(solution)/shard_map/ppermute | solution.py:422
  190.2 28.0 %collective-permute-start.18 = (bf16[1040,768]{1,0:T(8,128)(2,1)}, bf16[1040,768]{1,0:T(8,128)(2,1)}, u32[]{:S(2)}, u32[]{:S(2)}) collective-permute-start(bf16[1040,768]{1,0:T(8,128)(2,1)} %add_sums.4), channel_id=1, source_target_pairs={{8,16},{12,20},{16,8},{20,12},{9,17},{13,21},{17,9},{21,13},{10,18... | collective-permute-start | bytes 4792328 | tf_op jit(solution)/shard_map/ppermute | solution.py:422
  207.2 53.4 %collective-permute-start.16 = (bf16[1040,768]{1,0:T(8,128)(2,1)}, bf16[1040,768]{1,0:T(8,128)(2,1)}, u32[]{:S(2)}, u32[]{:S(2)}) collective-permute-start(bf16[1040,768]{1,0:T(8,128)(2,1)} %add_sums.5), channel_id=1, source_target_pairs={{8,0},{12,4},{16,24},{20,28},{9,1},{13,5},{17,25},{21,29},{10,2},{... | collective-permute-start | bytes 4792328 | tf_op jit(solution)/shard_map/ppermute | solution.py:422
  213.4 47.2 %copy-start.15 = (f32[16,128]{1,0:T(8,128)S(1)}, f32[16,128]{1,0:T(8,128)}, u32[]{:S(2)}) copy-start(f32[16,128]{1,0:T(8,128)} %copy-done.14) | copy-start | bytes 24580
  213.4 47.2 %copy-start.17 = (f32[16,128]{1,0:T(8,128)S(1)}, f32[16,128]{1,0:T(8,128)}, u32[]{:S(2)}) copy-start(f32[16,128]{1,0:T(8,128)} %copy-done.16) | copy-start | bytes 24580
  (10 other events, 11.4 us)

commit v4 on v3

--- a/solution.py
+++ b/solution.py
@@ -21,8 +21,18 @@
     return pltpu.with_memory_space_constraint(value, pltpu.VMEM)
 
 
-def shard_body(cuts, means_ref, inv_ref, log_ref, points_ref, out_ref, *rest):
-    piece_refs, sems = rest[:-1], rest[-1]
+def in_hbm(value):
+    return pltpu.with_memory_space_constraint(value, pltpu.HBM)
+
+
+def shard_body(cuts, means_hbm, inv_hbm, log_ref, points_ref, out_ref, *rest):
+    piece_refs, (means_ref, inv_ref, own_sems, sems) = rest[:-4], rest[-4:]
+    own_copies = [
+        pltpu.make_async_copy(means_hbm, means_ref, own_sems.at[0]),
+        pltpu.make_async_copy(inv_hbm, inv_ref, own_sems.at[1]),
+    ]
+    for copy in own_copies:
+        copy.start()
     copies = [
         pltpu.make_async_copy(points_ref.at[pl.ds(cuts[j], piece.shape[0])], piece, sems.at[j])
         for j, piece in enumerate(piece_refs)
@@ -32,6 +42,8 @@
     owned, feature_count = means_ref.shape
     ones = jnp.ones((META, feature_count), jnp.float32)
     row = lax.broadcasted_iota(jnp.int32, (META, CB), 0)
+    for copy in own_copies:
+        copy.wait()
     for half in range(2):
         out_ref[0, half, owned:, :] = jnp.zeros((META, feature_count), jnp.bfloat16)
     for block in range(owned // CB):
@@ -61,15 +73,20 @@
 def parameter_shard(means, inv_var, log_weight, points, cuts):
     owned, feature_count = means.shape
     vmem = pl.BlockSpec(memory_space=pltpu.VMEM)
-    anywhere = pl.BlockSpec(memory_space=pl.ANY)
+    hbm = pl.BlockSpec(memory_space=pltpu.HBM)
     lengths = [b - a for a, b in zip(cuts[:-1], cuts[1:])]
     return pl.pallas_call(
         functools.partial(shard_body, cuts),
-        in_specs=[vmem, vmem, vmem, anywhere],
-        out_specs=[vmem] + [anywhere] * len(lengths),
+        in_specs=[hbm, hbm, vmem, hbm],
+        out_specs=[vmem] + [hbm] * len(lengths),
         out_shape=[pltpu.VMEM((1, 2, owned + META, feature_count), jnp.bfloat16)]
-        + [jax.ShapeDtypeStruct((length, feature_count), points.dtype) for length in lengths],
-        scratch_shapes=[pltpu.SemaphoreType.DMA((max(len(lengths), 1),))],
+        + [pltpu.HBM((length, feature_count), points.dtype) for length in lengths],
+        scratch_shapes=[
+            pltpu.VMEM((owned, feature_count), means.dtype),
+            pltpu.VMEM((owned, feature_count), inv_var.dtype),
+            pltpu.SemaphoreType.DMA((2,)),
+            pltpu.SemaphoreType.DMA((max(len(lengths), 1),)),
+        ],
         compiler_params=pltpu.CompilerParams(vmem_limit_bytes=VMEM_LIMIT),
         cost_estimate=pl.CostEstimate(
             flops=owned * feature_count * 40,
@@ -77,104 +94,59 @@
             transcendentals=owned * feature_count,
         ),
         name="parameter_shard",
-    )(in_vmem(means), in_vmem(inv_var), log_weight.reshape(1, owned), points)
-
-
-def density_body(count, held, shards, arrays, pos_ref, x_ref, *rest):
-    weight_refs = rest[:arrays]
-    resp_ref, norm_ref, chosen, metas, sems, meta_sems = rest[arrays:]
+    )(in_hbm(means), in_hbm(inv_var), log_weight.reshape(1, owned), in_hbm(points))
+
+
+def density_body(first, count, held, pos_ref, x_ref, weight_ref, resp_ref, norm_ref):
     owned = held * CB
-    per_array = shards // arrays
     row_index = lax.broadcasted_iota(jnp.int32, (META, RB), 0)
     pieces = jnp.where(row_index < 3, 1.0, 0.0).astype(jnp.bfloat16)
 
-    def block_copy(array, entry, start, half, slot):
-        return pltpu.make_async_copy(
-            weight_refs[array].at[entry, :, pl.ds(start, CB), :],
-            chosen.at[half, :, pl.ds(slot * CB, CB), :],
-            sems.at[half, slot],
-        )
-
-    def fetch(i, half):
-        for slot in range(CANDS):
-            pos = pos_ref[i, slot]
-            shard = lax.div(pos, held)
-            start = pl.multiple_of(lax.rem(pos, held) * CB, CB)
-            if arrays == 1:
-                block_copy(0, shard, start, half, slot).start()
-            for array in range(arrays if arrays > 1 else 0):
-
-                @pl.when(shard == array)
-                def _(array=array, start=start, slot=slot):
-                    block_copy(array, 0, start, half, slot).start()
-
-    fetch(0, 0)
-    meta_copies = [
-        pltpu.make_async_copy(
-            weight_refs[shard // per_array].at[shard % per_array, 0, pl.ds(owned, META), :],
-            metas.at[shard],
-            meta_sems.at[shard],
-        )
-        for shard in range(shards)
-    ]
-    for copy in meta_copies:
-        copy.start()
-    for copy in meta_copies:
-        copy.wait()
-
     @pl.loop(0, count)
     def _(i):
-        half = lax.rem(i, 2)
-
-        @pl.when(i + 1 < count)
-        def _():
-            fetch(i + 1, 1 - half)
-
         x = x_ref[pl.ds(pl.multiple_of(i * RB, RB), RB), :]
-        constants = []
+        half = x * x * -0.5
+        densities = []
         for slot in range(CANDS):
-            pos = pos_ref[i, slot]
-            start = pl.multiple_of(lax.rem(pos, held) * CB, CB)
-            constants.append(metas[lax.div(pos, held), :, pl.ds(start, CB)])
-        densities = lax.dot_general(
-            jnp.concatenate(constants, axis=1), pieces, TN, preferred_element_type=jnp.float32
+            pos = pos_ref[(first + i) * CANDS + slot]
+            shard, start = lax.div(pos, held), lax.rem(pos, held) * CB
+            here = pl.ds(pl.multiple_of(start, CB), CB)
+            linear = lax.dot_general(
+                weight_ref[shard, 0, here, :], x, NT, preferred_element_type=jnp.float32
+            )
+            quadratic = lax.dot_general(
+                weight_ref[shard, 1, here, :], half, NT, preferred_element_type=jnp.float32
+            )
+            constant = lax.dot_general(
+                weight_ref[shard, 0, owned:, here],
+                pieces,
+                TN,
+                preferred_element_type=jnp.float32,
+            )
+            densities.append(linear + quadratic + constant)
+        peak = functools.reduce(
+            jnp.maximum, [jnp.max(d, axis=0, keepdims=True) for d in densities]
         )
+        terms = [jnp.exp(d - peak) for d in densities]
+        total = functools.reduce(jnp.add, [jnp.sum(t, axis=0, keepdims=True) for t in terms])
+        norm_ref[pl.ds(i, 1), :] = peak + jnp.log(total)
+        inverse_total = 1.0 / total
         for slot in range(CANDS):
-            block_copy(0, 0, 0, half, slot).wait()
-        densities += lax.dot_general(chosen[half, 0], x, NT, preferred_element_type=jnp.float32)
-        densities += lax.dot_general(
-            chosen[half, 1], x * x * -0.5, NT, preferred_element_type=jnp.float32
-        )
-        peak = jnp.max(densities, axis=0, keepdims=True)
-        terms = jnp.exp(densities - peak)
-        total = jnp.sum(terms, axis=0, keepdims=True)
-        norm_ref[pl.ds(i, 1), :] = peak + jnp.log(total)
-        resp = (terms * (1.0 / total)).astype(jnp.bfloat16)
-        for slot in range(CANDS):
-            resp_ref[i, slot] = resp[slot * CB : (slot + 1) * CB]
-
-
-def responsibilities(rows, pos, weights, held):
+            resp_ref[i, slot] = (terms[slot] * inverse_total).astype(jnp.bfloat16)
+
+
+def responsibilities(rows, pos, first, weights, held):
     count = rows.shape[0] // RB
     feature_count = rows.shape[1]
-    arrays = len(weights)
-    shards = sum(w.shape[0] for w in weights)
     vmem = pl.BlockSpec(memory_space=pltpu.VMEM)
     pairs = count * CANDS
     return pl.pallas_call(
-        functools.partial(density_body, count, held, shards, arrays),
-        in_specs=[pl.BlockSpec(memory_space=pltpu.SMEM), vmem]
-        + [pl.BlockSpec(memory_space=pl.ANY)] * arrays,
+        functools.partial(density_body, first, count, held),
+        in_specs=[pl.BlockSpec(memory_space=pltpu.SMEM), vmem, vmem],
         out_specs=[vmem, vmem],
         out_shape=[
             pltpu.VMEM((count, CANDS, CB, RB), jnp.bfloat16),
             pltpu.VMEM((count, RB), jnp.float32),
-        ],
-        scratch_shapes=[
-            pltpu.VMEM((2, 2, CANDS * CB, feature_count), jnp.bfloat16),
-            pltpu.VMEM((shards, META, feature_count), jnp.bfloat16),
-            pltpu.SemaphoreType.DMA((2, CANDS)),
-            pltpu.SemaphoreType.DMA((shards,)),
         ],
         compiler_params=pltpu.CompilerParams(vmem_limit_bytes=VMEM_LIMIT),
         cost_estimate=pl.CostEstimate(
@@ -183,40 +155,80 @@
             transcendentals=pairs * CB * RB,
         ),
         name="responsibilities",
-    )(pos, in_vmem(rows), *weights)
-
-
-def pair_lists(pos, runs, group_blocks):
-    run_of = []
-    for index, count in enumerate(runs):
-        run_of += [index] * (count * CANDS)
-    run_of = jnp.array(run_of, jnp.int32)
-    key = pos.reshape(-1) * len(runs) + run_of
-    number = jnp.arange(key.shape[0], dtype=jnp.int32)
-    before = jnp.logical_or(
-        key[None, :] < key[:, None],
-        jnp.logical_and(key[None, :] == key[:, None], number[None, :] < number[:, None]),
-    )
-    rank = jnp.sum(before.astype(jnp.int32), axis=1)
-    order = jnp.sum(jnp.where(rank[None, :] == number[:, None], number[None, :], 0), axis=1)
-    bounds = jnp.arange(group_blocks * len(runs) + 1, dtype=jnp.int32)
-    starts = jnp.sum((key[None, :] < bounds[:, None]).astype(jnp.int32), axis=1)
-    return order, starts
+    )(pos, in_vmem(rows), in_vmem(weights))
+
+
+def list_body(runs, held, owners, place, known, *rest):
+    where = [ref[0] for ref in rest[:known]]
+    id_refs, (pos_ref, order_ref, start_ref, cursor) = rest[known:-4], rest[-4:]
+    bins = start_ref.shape[0]
+    number_of_runs = len(runs)
+    per_ref = sum(runs) // len(id_refs)
+    firsts = [sum(runs[:j]) for j in range(number_of_runs)]
+
+    def run_of(i):
+        return sum((i >= start).astype(jnp.int32) for start in firsts[1:]) if firsts[1:] else 0
+
+    @pl.loop(0, bins)
+    def _(j):
+        start_ref[j] = 0
+
+    for part, id_ref in enumerate(id_refs):
+
+        @pl.loop(0, per_ref)
+        def _(row, part=part, id_ref=id_ref):
+            i = part * per_ref + row
+            for slot in range(CANDS):
+                block = id_ref[slot, row]
+                holder = place(lax.div(block, owners * held), *where)
+                pos = holder * held + lax.rem(block, held)
+                pos_ref[i * CANDS + slot] = pos
+                key = pos * number_of_runs + run_of(i) + 1
+                start_ref[key] = start_ref[key] + 1
+
+    def prefix(j, total):
+        total = total + start_ref[j]
+        start_ref[j] = total
+        cursor[j] = total
+        return total
+
+    lax.fori_loop(0, bins, prefix, jnp.int32(0))
+
+    @pl.loop(0, sum(runs))
+    def _(i):
+        for slot in range(CANDS):
+            key = pos_ref[i * CANDS + slot] * number_of_runs + run_of(i)
+            order_ref[cursor[key]] = i * CANDS + slot
+            cursor[key] = cursor[key] + 1
+
+
+def pair_lists(candidates, runs, held, group_blocks, owners, place, where):
+    smem = pl.BlockSpec(memory_space=pltpu.SMEM)
+    pairs = sum(runs) * CANDS
+    bins = group_blocks * len(runs) + 1
+    return pl.pallas_call(
+        functools.partial(list_body, tuple(runs), held, owners, place, len(where)),
+        in_specs=[smem] * (len(where) + len(candidates)),
+        out_specs=[smem] * 3,
+        out_shape=[jax.ShapeDtypeStruct((n,), jnp.int32) for n in (pairs, pairs, bins)],
+        scratch_shapes=[pltpu.SMEM((bins,), jnp.int32)],
+        compiler_params=pltpu.CompilerParams(vmem_limit_bytes=VMEM_LIMIT),
+        name="pair_lists",
+    )(*where, *candidates)
 
 
 def moment_body(shards, held, runs, order_ref, start_ref, *rest):
     parts, outs = len(runs), len(shards)
     row_refs, resp_refs = rest[:parts], rest[parts : 2 * parts]
     out_refs = rest[2 * parts : 2 * parts + outs]
-    sums, weight_sum = rest[2 * parts + outs :]
+    sums, count_sum = rest[2 * parts + outs :]
     owned = held * CB
     meta = slice(2 * owned, 2 * owned + META)
-    feature_count = row_refs[0].shape[1]
-    ones = jnp.ones((META, RB), jnp.float32)
+    ones = jnp.ones((META, 2 * RB), jnp.bfloat16)
 
     def block_sums(pos):
         sums[...] = jnp.zeros_like(sums)
-        weight_sum[...] = jnp.zeros_like(weight_sum)
+        count_sum[...] = jnp.zeros_like(count_sum)
         base = 0
         for run in range(parts):
             entry = pos * parts + run
@@ -226,12 +238,12 @@
             def _(step, base=base, run=run, low=low, high=high):
                 one = low + 2 * step
                 two = jnp.minimum(one + 1, high - 1)
-                valid = jnp.full((CB, RB), (one + 1 < high).astype(jnp.float32))
+                valid = (one + 1 < high).astype(jnp.float32)
                 pair_a, pair_b = order_ref[one] - base, order_ref[two] - base
                 row_a, row_b = lax.div(pair_a, CANDS), lax.div(pair_b, CANDS)
                 weight_a = resp_refs[run][row_a, lax.rem(pair_a, CANDS)]
                 weight_b = resp_refs[run][row_b, lax.rem(pair_b, CANDS)]
-                weight_b = weight_b * valid.astype(jnp.bfloat16)
+                weight_b = (weight_b.astype(jnp.float32) * valid).astype(jnp.bfloat16)
                 weight = jnp.concatenate([weight_a, weight_b], axis=1)
                 x = jnp.concatenate(
                     [
@@ -240,12 +252,11 @@
                     ],
                     axis=0,
                 )
-                sums[...] += jnp.dot(
-                    weight,
-                    jnp.concatenate([x, x * x], axis=1),
-                    preferred_element_type=jnp.float32,
+                sums[0] += jnp.dot(weight, x, preferred_element_type=jnp.float32)
+                sums[1] += jnp.dot(weight, x * x, preferred_element_type=jnp.float32)
+                count_sum[...] += lax.dot_general(
+                    ones, weight, NT, preferred_element_type=jnp.float32
                 )
-                weight_sum[...] += weight_a.astype(jnp.float32) + weight_b.astype(jnp.float32)
 
             base += runs[run] * CANDS
 
@@ -256,16 +267,9 @@
         def _(block, shard=shard, out_ref=out_ref):
             block_sums(shard * held + block)
             start = pl.multiple_of(block * CB, CB)
-            out_ref[pl.ds(start, CB), :] = sums[:, :feature_count].astype(jnp.bfloat16)
-            out_ref[pl.ds(owned + start, CB), :] = sums[:, feature_count:].astype(jnp.bfloat16)
-            counts = lax.dot_general(
-                ones,
-                weight_sum[...],
-                NT,
-                precision=lax.Precision.HIGHEST,
-                preferred_element_type=jnp.float32,
-            )
-            out_ref[meta, pl.ds(start, CB)] = counts.astype(jnp.bfloat16)
+            out_ref[pl.ds(start, CB), :] = sums[0].astype(jnp.bfloat16)
+            out_ref[pl.ds(owned + start, CB), :] = sums[1].astype(jnp.bfloat16)
+            out_ref[meta, pl.ds(start, CB)] = count_sum[...].astype(jnp.bfloat16)
 
 
 def moments(rows, resp, order, starts, held, shards):
@@ -281,8 +285,8 @@
         out_specs=[vmem] * len(shards),
         out_shape=[out_shape] * len(shards),
         scratch_shapes=[
-            pltpu.VMEM((CB, 2 * feature_count), jnp.float32),
-            pltpu.VMEM((CB, RB), jnp.float32),
+            pltpu.VMEM((2, CB, feature_count), jnp.float32),
+            pltpu.VMEM((META, CB), jnp.float32),
         ],
         compiler_params=pltpu.CompilerParams(vmem_limit_bytes=VMEM_LIMIT),
         cost_estimate=pl.CostEstimate(
@@ -306,6 +310,34 @@
 
     if rows % CHUNK:
         step(slice(whole * CHUNK, rows))
+
+
+def copy_body(firsts, skip, *refs):
+    sources, target, sems = refs[skip:-2], refs[-2], refs[-1]
+    copies = [
+        pltpu.make_async_copy(source.at[0], target.at[index], sems.at[j])
+        for j, (index, source) in enumerate(zip(firsts, sources))
+    ]
+    for copy in copies:
+        copy.start()
+    for copy in copies:
+        copy.wait()
+
+
+def stacked(total, first, shards, *earlier):
+    vmem = pl.BlockSpec(memory_space=pltpu.VMEM)
+    anywhere = pl.BlockSpec(memory_space=pl.ANY)
+    places = range(first, first + len(shards))
+    return pl.pallas_call(
+        functools.partial(copy_body, places, len(earlier)),
+        in_specs=[vmem] * len(earlier) + [anywhere] * len(shards),
+        out_specs=vmem,
+        out_shape=pltpu.VMEM((total,) + shards[0].shape[1:], jnp.bfloat16),
+        scratch_shapes=[pltpu.SemaphoreType.DMA((len(shards),))],
+        input_output_aliases={0: 0} if earlier else {},
+        compiler_params=pltpu.CompilerParams(vmem_limit_bytes=VMEM_LIMIT),
+        name="stack_shards",
+    )(*[in_vmem(e) for e in earlier], *shards)
 
 
 def add_body(*refs):
@@ -392,12 +424,21 @@
     )(is_end.astype(jnp.int32).reshape(1), *[in_vmem(value) for value in operands])
 
 
-def plain_plan(points, ids, parameters, held):
+def plain_plan(points, candidates, parameters, held):
     weights = parameter_shard(*parameters, points, (0,))[0]
     dp_size = lax.axis_size("dp")
+    row_blocks = points.shape[0] // RB
+    pos, order, starts = pair_lists(
+        [candidates.T],
+        (row_blocks,),
+        held,
+        dp_size * held,
+        lax.axis_size("comp"),
+        lambda holder: holder,
+        [],
+    )
     all_weights = lax.all_gather(weights, "dp", axis=0, tiled=True)
-    resp, norm = responsibilities(points, ids, [all_weights], held)
-    order, starts = pair_lists(ids, (points.shape[0] // RB,), dp_size * held)
+    resp, norm = responsibilities(points, pos, 0, all_weights, held)
     sums = []
     for j in range(dp_size):
         sums += moments([points], [resp], order, starts, held, [j])
@@ -426,13 +467,24 @@
     return lax.optimization_barrier((value,) + others)[0]
 
 
-def line_plan(points, ids, parameters, held):
-    group_blocks = 8 * held
+def line_place(holder, chip, core):
+    z, other = lax.div(holder, 2), lax.rem(holder, 2)
+    z = jnp.where(chip < 2, z, 3 - z)
+    z = jnp.where(z == 0, 1, jnp.where(z == 1, 0, z))
+    return z * 2 + lax.rem(other + core, 2)
+
+
+def line_plan(points, candidates, parameters, held):
     index = lax.axis_index("dp")
     chip, core = index // 2, index % 2
+    where = [chip.reshape(1), core.reshape(1)]
     row_blocks = points.shape[0] // RB
     cuts = (0, row_blocks // 2, row_blocks - row_blocks // 8, row_blocks)
+    runs = (row_blocks,) + tuple(b - a for a, b in zip(cuts[:-1], cuts[1:]))
+    own_ids = candidates.T
+    end_ids = move(own_ids, INWARD)
     weights, *pieces = parameter_shard(*parameters, points, [cut * RB for cut in cuts])
+    weights, end_ids = lax.optimization_barrier((weights, end_ids))
 
     outer = move(weights, INWARD)
     across = move(weights, MIDDLE)
@@ -443,27 +495,20 @@
     across_shared = move(across, CORES)
     moved.append(move(after(pieces[1], moved[0]), INWARD))
     moved.append(move(after(pieces[2], moved[0], far), INWARD))
+    near = [weights, own_shared, outer, outer_shared, across, across_shared]
+    pos, order, starts = pair_lists(
+        [own_ids, end_ids], runs, held, 8 * held, lax.axis_size("comp"), line_place, where
+    )
+    near_weights = stacked(8, 0, [after(near[0], pos, order, starts)] + near[1:])
+    far, near_weights = lax.optimization_barrier((far, near_weights))
     far_shared = move(far, CORES)
-    shards = [weights, own_shared, outer, outer_shared, across, across_shared, far, far_shared]
-
-    def place(nat):
-        holder = nat // held
-        z = jnp.where(chip < 2, holder // 2, 3 - holder // 2)
-        z = jnp.where(z == 0, 1, jnp.where(z == 1, 0, z))
-        other = (holder % 2 + core) % 2
-        return (z * 2 + other) * held + nat % held
-
-    end_pos = place(after(move(ids, INWARD), moved[0]))
-    own_pos = place(ids)
+    all_weights = stacked(8, 6, [far, far_shared], near_weights)
     rows = [points] + moved
-    runs = (row_blocks,) + tuple(b - a for a, b in zip(cuts[:-1], cuts[1:]))
-    order, starts = pair_lists(jnp.concatenate([own_pos, end_pos]), runs, group_blocks)
-    run_pos = [own_pos] + [end_pos[a:b] for a, b in zip(cuts[:-1], cuts[1:])]
     results = []
-    for run_rows, pos in zip(rows, run_pos):
+    for j, run_rows in enumerate(rows):
         if results:
             pos = after(pos, results[-1][1])
-        results.append(responsibilities(run_rows, pos, shards, held))
+        results.append(responsibilities(run_rows, pos, sum(runs[:j]), all_weights, held))
     resp = [r[0] for r in results]
 
     def sums_of(position, *earlier):
@@ -496,13 +541,9 @@
 
 
 def on_device(points, candidates, means, inv_var, log_weight):
-    feature_count = points.shape[1]
-    owner_count = lax.axis_size("comp")
-    owned = means.shape[0]
-    held = owned // CB
-    ids = candidates // (owner_count * held) * held + candidates % held
+    held = means.shape[0] // CB
     plan = line_plan if lax.axis_size("dp") == 8 else plain_plan
-    return plan(points, ids, (means, inv_var, log_weight), held)
+    return plan(points, candidates, (means, inv_var, log_weight), held)
 
 
 def solution(mesh):

time: 268 us -> 335 us (1.25)
  Pallas kernels: 105 us -> 173 us
  waiting for transfers between devices: 99.9 us -> 108 us
  local copies, waits for them, and re-layouts: 14.3 us -> 10.2 us
  starting transfers between devices: 44.7 us -> 40.7 us
    pallas_call x5 -> x8, Pallas kernels: 51.1 us -> 134 us  [the longest x1 96.4 us: parameter_shard(): pl.pallas_call(functools.partial(shard_body, cuts), in_specs=[hbm, hbm, v...]
    pallas_call x8, Pallas kernels: 45.1 us -> 30.1 us  [moments(): pl.pallas_call(functools.partial(moment_body, tuple(shards), held, runs),...]
    ppermute x19, waiting for transfers between devices: 99.9 us -> 108 us  [move(): return lax.ppermute(value, 'dp', pairs)]
    ppermute x19, starting transfers between devices: 44.7 us -> 40.7 us  [move(): return lax.ppermute(value, 'dp', pairs)]
    unnamed x47 -> x38, local copies, waits for them, and re-layouts: 11.5 us -> 9.52 us
  transfers between devices with their start and end apart: 19 -> 19, of which waited for: 4 -> 6; matrix products, arithmetic and copies ran while one was open for 1% -> 0% of each run, Pallas kernels for 31% -> 48%
where the time goes in v4:
time: 335 us; the launch traced here: 333 us
  Pallas kernels  173 us (52%)
  waiting for transfers between devices  108 us (32%)
  starting transfers between devices  40.7 us (12%)
  local copies, waits for them, and re-layouts  10.2 us (3%)
    ppermute x19, waiting for transfers between devices, move(): return lax.ppermute(value, 'dp', pairs)  108 us
    pallas_call x1, Pallas kernels, parameter_shard(): pl.pallas_call(functools.partial(shard_body, cuts), in_specs=[hbm, hbm, v...  96.4 us
    ppermute x19, starting transfers between devices, move(): return lax.ppermute(value, 'dp', pairs)  40.7 us
    pallas_call x8, Pallas kernels, moments(): pl.pallas_call(functools.partial(moment_body, tuple(shards), held, runs),...  30.1 us
    pallas_call x4, Pallas kernels, responsibilities(): pl.pallas_call(functools.partial(density_body, first, count, held), in_sp...  26.6 us
    unnamed x38, local copies, waits for them, and re-layouts  9.52 us
  transfers between devices with their start and end apart: 19, of which 6 were waited for; matrix products, arithmetic and copies ran while one was open for 0% of the time, Pallas kernels for 48%

profile of v4, /device:TPU:0, one launch (start us, length us, event | category | flops | bytes accessed | tf_op | source)
XLA Modules:
  0.0 333.1 jit_solution(15546272473635806955)
XLA Ops:
  0.6 4.9 %collective-permute-start = (s32[4,16]{1,0:T(4,128)}, s32[4,16]{1,0:T(4,128)S(1)}, u32[]{:S(2)}, u32[]{:S(2)}) collective-permute-start(s32[4,16]{1,0:T(4,128)} %bitcast.6), channel_id=1, source_target_pairs={{0,8},{4,12},{24,16},{28,20},{1,9},{5,13},{25,17},{29,21},{2,10},{... | collective-permute-start | bytes 776 | tf_op jit(solution)/shard_map/ppermute | solution.py:463
  6.3 96.4 %parameter_shard.1 = (bf16[1,2,528,768]{3,2,1,0:T(8,128)(2,1)S(1)}, bf16[1024,768]{1,0:T(8,128)(2,1)}, bf16[768,768]{1,0:T(8,128)(2,1)}, bf16[256,768]{1,0:T(8,128)(2,1)}) custom-call(bf16[512,768]{1,0:T(8,128)(2,1)} %means_hbm.1, bf16[512,768]{1,0:T(8,128)(2,1)} %inv_hbm.1, bf16[1,512]{1,0:T(2,128)(2,1)S(1)} %reshape.32.log_ref, bf16[2048,768]{1,0:T(8,128)(2,1)} %rest_0_.15), custom_call_target="tpu_custom_call" | custom-call | flops 15728640 | bytes 3145728 | tf_op jit(solution)/shard_map/parameter_shard/pallas_call | solution.py:78
  102.7 1.8 collective-permute-start.5
  104.6 4.1 %collective-permute-start.1 = (bf16[1,2,528,768]{3,2,1,0:T(8,128)(2,1)S(1)}, bf16[1,2,528,768]{3,2,1,0:T(8,128)(2,1)}, u32[]{:S(2)}, u32[]{:S(2)}) collective-permute-start(bf16[1,2,528,768]{3,2,1,0:T(8,128)(2,1)S(1)} %get-tuple-element.47.refs_0_), channel_id=1, source_target_pairs={{0,8},{4,12},{24,16},{28,20},{1,9},{5,13},{25,17},{29,21},{2,10},{... | collective-permute-start | bytes 4866056 | tf_op jit(solution)/shard_map/ppermute | solution.py:463
  108.7 1.8 collective-permute-start.3
  110.5 1.9 collective-permute-start.6
  112.4 29.5 %collective-permute-done.1.refs_2_ = bf16[1,2,528,768]{3,2,1,0:T(8,128)(2,1)} collective-permute-done((bf16[1,2,528,768]{3,2,1,0:T(8,128)(2,1)S(1)}, bf16[1,2,528,768]{3,2,1,0:T(8,128)(2,1)}, u32[]{:S(2)}, u32[]{:S(2)}) %collective-permute-start.1) | collective-permute-done | bytes 1622048 | tf_op jit(solution)/shard_map/ppermute | solution.py:463
  141.9 1.9 collective-permute-start.4
  145.6 5.5 %collective-permute-start.8 = (bf16[1024,768]{1,0:T(8,128)(2,1)}, bf16[1024,768]{1,0:T(8,128)(2,1)S(1)}, u32[]{:S(2)}, u32[]{:S(2)}) collective-permute-start(bf16[1024,768]{1,0:T(8,128)(2,1)} %get-tuple-element.53), channel_id=1, source_target_pairs={{0,8},{4,12},{24,16},{28,20},{1,9},{5,13},{25,17},{29,21},{2,10},{... | collective-permute-start | bytes 4718600 | tf_op jit(solution)/shard_map/ppermute | solution.py:463
  151.2 5.5 %pair_lists.1 = (s32[128]{0:T(128)S(1)}, s32[128]{0:T(128)S(1)}, s32[129]{0:T(256)S(1)}) custom-call(s32[1]{0:T(128)} %bitcast.1.rest_0_, s32[1]{0:T(128)} %bitcast.2.rest_1_, s32[4,16]{1,0:T(4,128)S(1)} %bitcast.7, s32[4,16]{1,0:T(4,128)S(1)} %collective-permute-done.rest_3_), custom_call_target="tpu_custom_call" | custom-call | tf_op jit(solution)/shard_map/pair_lists/pallas_call | solution.py:209
  156.7 3.7 %stack_shards.2.refs_0_ = bf16[8,2,528,768]{3,2,1,0:T(8,128)(2,1)S(1)} custom-call(bf16[1,2,528,768]{3,2,1,0:T(8,128)(2,1)S(1)} %get-tuple-element.47.refs_0_, bf16[1,2,528,768]{3,2,1,0:T(8,128)(2,1)} %collective-permute-done.3.refs_1_, bf16[1,2,528,768]{3,2,1,0:T(8,128)(2,1)} %collective-permute-done.1.refs_2_, ...), custom_call_target="tpu_custom_call" | custom-call | tf_op jit(solution)/shard_map/stack_shards/pallas_call | solution.py:331
  161.2 23.8 %collective-permute-done.8.x_ref.rest_1_ = bf16[1024,768]{1,0:T(8,128)(2,1)S(1)} collective-permute-done((bf16[1024,768]{1,0:T(8,128)(2,1)}, bf16[1024,768]{1,0:T(8,128)(2,1)S(1)}, u32[]{:S(2)}, u32[]{:S(2)}) %collective-permute-start.8) | collective-permute-done | bytes 1572896 | tf_op jit(solution)/shard_map/ppermute | solution.py:463
  186.2 5.3 %collective-permute-start.9 = (bf16[768,768]{1,0:T(8,128)(2,1)S(1)}, bf16[768,768]{1,0:T(8,128)(2,1)S(1)}, u32[]{:S(2)}, u32[]{:S(2)}) collective-permute-start(bf16[768,768]{1,0:T(8,128)(2,1)S(1)} %copy-done.17), channel_id=1, source_target_pairs={{0,8},{4,12},{24,16},{28,20},{1,9},{5,13},{25,17},{29,21},{2,10},{... | collective-permute-start | bytes 3538952 | tf_op jit(solution)/shard_map/ppermute | solution.py:463
  195.3 12.8 %responsibilities.4 = (bf16[16,4,128,128]{3,2,1,0:T(8,128)(2,1)S(1)}, f32[16,128]{1,0:T(8,128)S(1)}) custom-call(s32[128]{0:T(128)S(1)} %get-tuple-element.59.pos_ref, bf16[2048,768]{1,0:T(8,128)(2,1)S(1)} %copy-done, bf16[8,2,528,768]{3,2,1,0:T(8,128)(2,1)S(1)} %stack_shards.3.weight_ref), custom_call_target="tpu_custom_call" | custom-call | flops 3221225472 | bytes 28311552 | tf_op jit(solution)/shard_map/responsibilities/pallas_call | solution.py:143
  208.1 6.6 %responsibilities.5 = (bf16[8,4,128,128]{3,2,1,0:T(8,128)(2,1)S(1)}, f32[8,128]{1,0:T(8,128)S(1)}) custom-call(s32[128]{0:T(128)S(1)} %get-tuple-element.59.pos_ref, bf16[1024,768]{1,0:T(8,128)(2,1)S(1)} %copy-done.4, bf16[8,2,528,768]{3,2,1,0:T(8,128)(2,1)S(1)} %stack_shards.3.weight_ref), custom_call_target="tpu_custom_call" | custom-call | flops 1610612736 | bytes 14155776 | tf_op jit(solution)/shard_map/responsibilities/pallas_call | solution.py:143
  214.8 2.9 collective-permute-done.9.x_ref.rest_2_
  217.7 5.1 %responsibilities.6 = (bf16[6,4,128,128]{3,2,1,0:T(8,128)(2,1)S(1)}, f32[6,128]{1,0:T(8,128)S(1)}) custom-call(s32[128]{0:T(128)S(1)} %get-tuple-element.59.pos_ref, bf16[768,768]{1,0:T(8,128)(2,1)S(1)} %collective-permute-done.9.x_ref.rest_2_, bf16[8,2,528,768]{3,2,1,0:T(8,128)(2,1)S(1)} %stack_shards.3.weight_ref), custom_call_target="tpu_custom_call" | custom-call | flops 1207959552 | bytes 10616832 | tf_op jit(solution)/shard_map/responsibilities/pallas_call | solution.py:143
  222.9 2.9 collective-permute-done.10.x_ref.rest_3_
  225.8 2.1 responsibilities.7
  227.8 2.2 moments.8
  232.2 2.8 moments.9.refs_0_
  235.4 4.2 %collective-permute-done.11.refs_1_ = f32[16,128]{1,0:T(8,128)S(1)} collective-permute-done((f32[16,128]{1,0:T(8,128)S(1)}, f32[16,128]{1,0:T(8,128)S(1)}, u32[]{:S(2)}, u32[]{:S(2)}) %collective-permute-start.11) | collective-permute-done | bytes 8224 | tf_op jit(solution)/shard_map/ppermute | solution.py:463
  239.7 2.5 moments.10
  243.9 2.5 moments.11.refs_0_
  248.1 2.5 moments.12
  251.4 3.7 %moments.13 = bf16[1040,768]{1,0:T(8,128)(2,1)} custom-call(s32[128]{0:T(128)S(1)} %get-tuple-element.73.order_ref, s32[129]{0:T(256)S(1)} %get-tuple-element.46.start_ref, bf16[2048,768]{1,0:T(8,128)(2,1)S(1)} %copy-done, bf16[1024,768]{1,0:T(8,128)(2,1)S(1)} %copy-done.4, bf16[768,768]{1,0:T(8,128)(2,1)S(1)} %collective-permute-done.9.x_ref.rest_2_, ...), custom_call_target="tpu_custom_call" | custom-call | flops 805306368 | bytes 3670016 | tf_op jit(solution)/shard_map/moments/pallas_call | solution.py:282
  255.0 1.8 collective-permute-start.17
  256.9 1.8 collective-permute-start.18
  258.7 12.0 %moments.14.refs_0_ = bf16[1040,768]{1,0:T(8,128)(2,1)S(1)} custom-call(s32[128]{0:T(128)S(1)} %get-tuple-element.73.order_ref, s32[129]{0:T(256)S(1)} %get-tuple-element.46.start_ref, bf16[2048,768]{1,0:T(8,128)(2,1)S(1)} %copy-done, bf16[1024,768]{1,0:T(8,128)(2,1)S(1)} %copy-done.4, bf16[768,768]{1,0:T(8,128)(2,1)S(1)} %collective-permute-done.9.x_ref.rest_2_, ...), custom_call_target="tpu_custom_call" | custom-call | flops 805306368 | bytes 3670016 | tf_op jit(solution)/shard_map/moments/pallas_call | solution.py:282
  281.4 1.9 moments.15.refs_3_
  283.4 45.0 %collective-permute-done.16.refs_2_ = bf16[1040,768]{1,0:T(8,128)(2,1)} collective-permute-done((bf16[1040,768]{1,0:T(8,128)(2,1)}, bf16[1040,768]{1,0:T(8,128)(2,1)}, u32[]{:S(2)}, u32[]{:S(2)}) %collective-permute-start.16) | collective-permute-done | bytes 1597472 | tf_op jit(solution)/shard_map/ppermute | solution.py:463
  328.4 4.6 %results.1 = (f32[1,512]{1,0:T(1,128)}, f32[512,768]{1,0:T(8,128)}, f32[512,768]{1,0:T(8,128)}, f32[16,128]{1,0:T(8,128)}) custom-call(s32[1]{0:T(128)} %bitcast.end_ref, f32[16,128]{1,0:T(8,128)S(1)} %get-tuple-element.50.refs_0_, f32[16,128]{1,0:T(8,128)S(1)} %copy-done.15, bf16[1040,768]{1,0:T(8,128)(2,1)} %collective-permute-done.16.refs_2_, ...), custom_call_target="tpu_custom_call" | custom-call | tf_op jit(solution)/shard_map/results/pallas_call | solution.py:406
  (66 shorter events, 25.4 us)
Async XLA Ops:
  0.6 102.1 %collective-permute-start = (s32[4,16]{1,0:T(4,128)}, s32[4,16]{1,0:T(4,128)S(1)}, u32[]{:S(2)}, u32[]{:S(2)}) collective-permute-start(s32[4,16]{1,0:T(4,128)} %bitcast.6), channel_id=1, source_target_pairs={{0,8},{4,12},{24,16},{28,20},{1,9},{5,13},{25,17},{29,21},{2,10},{... | collective-permute-start | bytes 776 | tf_op jit(solution)/shard_map/ppermute | solution.py:463
  6.3 144.9 %copy-start.16 = (s32[16,4]{0,1:T(4,128)S(1)}, s32[16,4]{0,1:T(4,128)}, u32[]{:S(2)}) copy-start(s32[16,4]{0,1:T(4,128)} %param.6) | copy-start | bytes 772
  102.7 7.8 %collective-permute-start.5 = (bf16[1,2,528,768]{3,2,1,0:T(8,128)(2,1)S(1)}, bf16[1,2,528,768]{3,2,1,0:T(8,128)(2,1)}, u32[]{:S(2)}, u32[]{:S(2)}) collective-permute-start(bf16[1,2,528,768]{3,2,1,0:T(8,128)(2,1)S(1)} %get-tuple-element.47.refs_0_), channel_id=1, source_target_pairs={{8,16},{12,20},{16,8},{20,12},{9,17},{13,21},{17,9},{21,13},{10,18... | collective-permute-start | bytes 4866056 | tf_op jit(solution)/shard_map/ppermute | solution.py:463
  104.6 37.4 %collective-permute-start.1 = (bf16[1,2,528,768]{3,2,1,0:T(8,128)(2,1)S(1)}, bf16[1,2,528,768]{3,2,1,0:T(8,128)(2,1)}, u32[]{:S(2)}, u32[]{:S(2)}) collective-permute-start(bf16[1,2,528,768]{3,2,1,0:T(8,128)(2,1)S(1)} %get-tuple-element.47.refs_0_), channel_id=1, source_target_pairs={{0,8},{4,12},{24,16},{28,20},{1,9},{5,13},{25,17},{29,21},{2,10},{... | collective-permute-start | bytes 4866056 | tf_op jit(solution)/shard_map/ppermute | solution.py:463
  108.7 48.0 %collective-permute-start.3 = (bf16[1,2,528,768]{3,2,1,0:T(8,128)(2,1)S(1)}, bf16[1,2,528,768]{3,2,1,0:T(8,128)(2,1)}, u32[]{:S(2)}, u32[]{:S(2)}) collective-permute-start(bf16[1,2,528,768]{3,2,1,0:T(8,128)(2,1)S(1)} %get-tuple-element.47.refs_0_), channel_id=1, source_target_pairs={{8,12},{12,8},{16,20},{20,16},{9,13},{13,9},{17,21},{21,17},{10,14... | collective-permute-start | bytes 4866056 | tf_op jit(solution)/shard_map/ppermute | solution.py:463
  110.5 46.2 %collective-permute-start.6 = (bf16[1,2,528,768]{3,2,1,0:T(8,128)(2,1)}, bf16[1,2,528,768]{3,2,1,0:T(8,128)(2,1)}, u32[]{:S(2)}, u32[]{:S(2)}) collective-permute-start(bf16[1,2,528,768]{3,2,1,0:T(8,128)(2,1)} %collective-permute-done.5.refs_4_), channel_id=1, source_target_pairs={{8,12},{12,8},{16,20},{20,16},{9,13},{13,9},{17,21},{21,17},{10,14... | collective-permute-start | bytes 4866056 | tf_op jit(solution)/shard_map/ppermute | solution.py:463
  141.9 14.8 %collective-permute-start.4 = (bf16[1,2,528,768]{3,2,1,0:T(8,128)(2,1)}, bf16[1,2,528,768]{3,2,1,0:T(8,128)(2,1)}, u32[]{:S(2)}, u32[]{:S(2)}) collective-permute-start(bf16[1,2,528,768]{3,2,1,0:T(8,128)(2,1)} %collective-permute-done.1.refs_2_), channel_id=1, source_target_pairs={{8,12},{12,8},{16,20},{20,16},{9,13},{13,9},{17,21},{21,17},{10,14... | collective-permute-start | bytes 4866056 | tf_op jit(solution)/shard_map/ppermute | solution.py:463
  143.8 16.6 %collective-permute-start.2 = (bf16[1,2,528,768]{3,2,1,0:T(8,128)(2,1)}, bf16[1,2,528,768]{3,2,1,0:T(8,128)(2,1)}, u32[]{:S(2)}, u32[]{:S(2)}) collective-permute-start(bf16[1,2,528,768]{3,2,1,0:T(8,128)(2,1)} %collective-permute-done.1.refs_2_), channel_id=1, source_target_pairs={{8,16},{12,20},{16,8},{20,12},{9,17},{13,21},{17,9},{21,13},{10,18... | collective-permute-start | bytes 4866056 | tf_op jit(solution)/shard_map/ppermute | solution.py:463
  145.6 39.4 %collective-permute-start.8 = (bf16[1024,768]{1,0:T(8,128)(2,1)}, bf16[1024,768]{1,0:T(8,128)(2,1)S(1)}, u32[]{:S(2)}, u32[]{:S(2)}) collective-permute-start(bf16[1024,768]{1,0:T(8,128)(2,1)} %get-tuple-element.53), channel_id=1, source_target_pairs={{0,8},{4,12},{24,16},{28,20},{1,9},{5,13},{25,17},{29,21},{2,10},{... | collective-permute-start | bytes 4718600 | tf_op jit(solution)/shard_map/ppermute | solution.py:463
  156.7 29.5 %copy-start.17 = (bf16[768,768]{1,0:T(8,128)(2,1)S(1)}, bf16[768,768]{1,0:T(8,128)(2,1)}, u32[]{:S(2)}) copy-start(bf16[768,768]{1,0:T(8,128)(2,1)} %get-tuple-element.57) | copy-start | bytes 3538948
  156.7 34.8 %copy-start.18 = (bf16[256,768]{1,0:T(8,128)(2,1)S(1)}, bf16[256,768]{1,0:T(8,128)(2,1)}, u32[]{:S(2)}) copy-start(bf16[256,768]{1,0:T(8,128)(2,1)} %get-tuple-element.61) | copy-start | bytes 1179652
  160.4 32.4 %collective-permute-start.7 = (bf16[1,2,528,768]{3,2,1,0:T(8,128)(2,1)}, bf16[1,2,528,768]{3,2,1,0:T(8,128)(2,1)S(1)}, u32[]{:S(2)}, u32[]{:S(2)}) collective-permute-start(bf16[1,2,528,768]{3,2,1,0:T(8,128)(2,1)} %collective-permute-done.2.refs_1_), channel_id=1, source_target_pairs={{8,12},{12,8},{16,20},{20,16},{9,13},{13,9},{17,21},{21,17},{10,14... | collective-permute-start | bytes 4866056 | tf_op jit(solution)/shard_map/ppermute | solution.py:463
  186.2 31.5 %collective-permute-start.9 = (bf16[768,768]{1,0:T(8,128)(2,1)S(1)}, bf16[768,768]{1,0:T(8,128)(2,1)S(1)}, u32[]{:S(2)}, u32[]{:S(2)}) collective-permute-start(bf16[768,768]{1,0:T(8,128)(2,1)S(1)} %copy-done.17), channel_id=1, source_target_pairs={{0,8},{4,12},{24,16},{28,20},{1,9},{5,13},{25,17},{29,21},{2,10},{... | collective-permute-start | bytes 3538952 | tf_op jit(solution)/shard_map/ppermute | solution.py:463
  191.5 34.2 %collective-permute-start.10 = (bf16[256,768]{1,0:T(8,128)(2,1)S(1)}, bf16[256,768]{1,0:T(8,128)(2,1)S(1)}, u32[]{:S(2)}, u32[]{:S(2)}) collective-permute-start(bf16[256,768]{1,0:T(8,128)(2,1)S(1)} %copy-done.18), channel_id=1, source_target_pairs={{0,8},{4,12},{24,16},{28,20},{1,9},{5,13},{25,17},{29,21},{2,10},{... | collective-permute-start | bytes 1179656 | tf_op jit(solution)/shard_map/ppermute | solution.py:463
  192.9 2.4 copy-start
  195.3 12.9 %copy-start.4 = (bf16[1024,768]{1,0:T(8,128)(2,1)S(1)}, bf16[1024,768]{1,0:T(8,128)(2,1)}, u32[]{:S(2)}) copy-start(bf16[1024,768]{1,0:T(8,128)(2,1)} %copy-done.3) | copy-start | bytes 4718596
  208.1 50.6 %copy-start.1 = (bf16[16,4,128,128]{3,2,1,0:T(8,128)(2,1)}, bf16[16,4,128,128]{3,2,1,0:T(8,128)(2,1)S(1)}, u32[]{:S(2)}) copy-start(bf16[16,4,128,128]{3,2,1,0:T(8,128)(2,1)S(1)} %get-tuple-element.63.rest_4_) | copy-start | bytes 6291460
  214.8 43.9 %copy-start.8 = (bf16[8,4,128,128]{3,2,1,0:T(8,128)(2,1)}, bf16[8,4,128,128]{3,2,1,0:T(8,128)(2,1)S(1)}, u32[]{:S(2)}) copy-start(bf16[8,4,128,128]{3,2,1,0:T(8,128)(2,1)S(1)} %get-tuple-element.64.rest_5_) | copy-start | bytes 3145732
  217.7 41.0 %copy-start.6 = (bf16[768,768]{1,0:T(8,128)(2,1)}, bf16[768,768]{1,0:T(8,128)(2,1)S(1)}, u32[]{:S(2)}) copy-start(bf16[768,768]{1,0:T(8,128)(2,1)S(1)} %collective-permute-done.9.x_ref.rest_2_) | copy-start | bytes 3538948
  222.8 35.9 %copy-start.10 = (bf16[6,4,128,128]{3,2,1,0:T(8,128)(2,1)}, bf16[6,4,128,128]{3,2,1,0:T(8,128)(2,1)S(1)}, u32[]{:S(2)}) copy-start(bf16[6,4,128,128]{3,2,1,0:T(8,128)(2,1)S(1)} %get-tuple-element.65.rest_6_) | copy-start | bytes 2359300
  227.8 30.9 %copy-start.12 = (bf16[2,4,128,128]{3,2,1,0:T(8,128)(2,1)}, bf16[2,4,128,128]{3,2,1,0:T(8,128)(2,1)S(1)}, u32[]{:S(2)}) copy-start(bf16[2,4,128,128]{3,2,1,0:T(8,128)(2,1)S(1)} %get-tuple-element.66.rest_7_) | copy-start | bytes 786436
  230.1 4.9 %collective-permute-start.12 = (bf16[1040,768]{1,0:T(8,128)(2,1)S(1)}, bf16[1040,768]{1,0:T(8,128)(2,1)S(1)}, u32[]{:S(2)}, u32[]{:S(2)}) collective-permute-start(bf16[1040,768]{1,0:T(8,128)(2,1)S(1)} %moments.8), channel_id=1, source_target_pairs={{8,12},{12,8},{16,20},{20,16},{9,13},{13,9},{17,21},{21,17},{10,14... | collective-permute-start | bytes 4792328 | tf_op jit(solution)/shard_map/ppermute | solution.py:463
  230.9 8.8 %collective-permute-start.11 = (f32[16,128]{1,0:T(8,128)S(1)}, f32[16,128]{1,0:T(8,128)S(1)}, u32[]{:S(2)}, u32[]{:S(2)}) collective-permute-start(f32[16,128]{1,0:T(8,128)S(1)} %join_norms.1), channel_id=1, source_target_pairs={{8,0},{12,4},{16,24},{20,28},{9,1},{13,5},{17,25},{21,29},{10,2},{... | collective-permute-start | bytes 24584 | tf_op jit(solution)/shard_map/ppermute | solution.py:463
  239.7 2.5 copy-start.14
  242.2 4.2 %collective-permute-start.13 = (bf16[1040,768]{1,0:T(8,128)(2,1)S(1)}, bf16[1040,768]{1,0:T(8,128)(2,1)S(1)}, u32[]{:S(2)}, u32[]{:S(2)}) collective-permute-start(bf16[1040,768]{1,0:T(8,128)(2,1)S(1)} %moments.10), channel_id=1, source_target_pairs={{8,12},{12,8},{16,20},{20,16},{9,13},{13,9},{17,21},{21,17},{10,14... | collective-permute-start | bytes 4792328 | tf_op jit(solution)/shard_map/ppermute | solution.py:463
  243.0 27.7 %collective-permute-start.15 = (bf16[1040,768]{1,0:T(8,128)(2,1)S(1)}, bf16[1040,768]{1,0:T(8,128)(2,1)S(1)}, u32[]{:S(2)}, u32[]{:S(2)}) collective-permute-start(bf16[1040,768]{1,0:T(8,128)(2,1)S(1)} %add_sums.3), channel_id=1, source_target_pairs={{8,16},{12,20},{16,8},{20,12},{9,17},{13,21},{17,9},{21,13},{10,18... | collective-permute-start | bytes 4792328 | tf_op jit(solution)/shard_map/ppermute | solution.py:463
  250.6 20.1 %collective-permute-start.14 = (bf16[1040,768]{1,0:T(8,128)(2,1)S(1)}, bf16[1040,768]{1,0:T(8,128)(2,1)S(1)}, u32[]{:S(2)}, u32[]{:S(2)}) collective-permute-start(bf16[1040,768]{1,0:T(8,128)(2,1)S(1)} %moments.12), channel_id=1, source_target_pairs={{8,12},{12,8},{16,20},{20,16},{9,13},{13,9},{17,21},{21,17},{10,14... | collective-permute-start | bytes 4792328 | tf_op jit(solution)/shard_map/ppermute | solution.py:463
  255.0 28.3 %collective-permute-start.17 = (bf16[1040,768]{1,0:T(8,128)(2,1)}, bf16[1040,768]{1,0:T(8,128)(2,1)}, u32[]{:S(2)}, u32[]{:S(2)}) collective-permute-start(bf16[1040,768]{1,0:T(8,128)(2,1)} %moments.13), channel_id=1, source_target_pairs={{8,12},{12,8},{16,20},{20,16},{9,13},{13,9},{17,21},{21,17},{10,14... | collective-permute-start | bytes 4792328 | tf_op jit(solution)/shard_map/ppermute | solution.py:463
  256.9 26.5 %collective-permute-start.18 = (bf16[1040,768]{1,0:T(8,128)(2,1)}, bf16[1040,768]{1,0:T(8,128)(2,1)}, u32[]{:S(2)}, u32[]{:S(2)}) collective-permute-start(bf16[1040,768]{1,0:T(8,128)(2,1)} %add_sums.4), channel_id=1, source_target_pairs={{8,16},{12,20},{16,8},{20,12},{9,17},{13,21},{17,9},{21,13},{10,18... | collective-permute-start | bytes 4792328 | tf_op jit(solution)/shard_map/ppermute | solution.py:463
  272.5 55.8 %collective-permute-start.16 = (bf16[1040,768]{1,0:T(8,128)(2,1)}, bf16[1040,768]{1,0:T(8,128)(2,1)}, u32[]{:S(2)}, u32[]{:S(2)}) collective-permute-start(bf16[1040,768]{1,0:T(8,128)(2,1)} %add_sums.5), channel_id=1, source_target_pairs={{8,0},{12,4},{16,24},{20,28},{9,1},{13,5},{17,25},{21,29},{10,2},{... | collective-permute-start | bytes 4792328 | tf_op jit(solution)/shard_map/ppermute | solution.py:463
  273.8 1.6 copy-start.2
  281.4 47.0 %copy-start.15 = (f32[16,128]{1,0:T(8,128)S(1)}, f32[16,128]{1,0:T(8,128)}, u32[]{:S(2)}) copy-start(f32[16,128]{1,0:T(8,128)} %copy-done.14) | copy-start | bytes 24580
  (6 other events, 7.1 us)

commit v5 on v3

v5 whole, which is shorter than its diff:
```python
import functools
import math

import jax
import jax.numpy as jnp
from jax import lax
from jax.experimental import pallas as pl
from jax.experimental.pallas import tpu as pltpu
from jax.sharding import PartitionSpec as P

CB = 128
RB = 128
CANDS = 4
META = 16
MIB = 1024 * 1024
NT = (((1,), (1,)), ((), ()))
TN = (((0,), (0,)), ((), ()))


def in_vmem(value):
    return pltpu.with_memory_space_constraint(value, pltpu.VMEM)


def in_hbm(value):
    return pltpu.with_memory_space_constraint(value, pltpu.HBM)


def shard_body(cuts, means_hbm, inv_hbm, log_ref, points_ref, out_ref, *rest):
    piece_refs, (means_ref, inv_ref, own_sems, sems) = rest[:-4], rest[-4:]
    own_copies = [
        pltpu.make_async_copy(means_hbm, means_ref, own_sems.at[0]),
        pltpu.make_async_copy(inv_hbm, inv_ref, own_sems.at[1]),
    ]
    for copy in own_copies:
        copy.start()
    copies = [
        pltpu.make_async_copy(points_ref.at[pl.ds(cuts[j], piece.shape[0])], piece, sems.at[j])
        for j, piece in enumerate(piece_refs)
    ]
    for copy in copies:
        copy.start()
    owned, feature_count = means_ref.shape
    ones = jnp.ones((META, feature_count), jnp.float32)
    row = lax.broadcasted_iota(jnp.int32, (META, CB), 0)
    for copy in own_copies:
        copy.wait()
    for half in range(2):
        out_ref[0, half, owned:, :] = jnp.zeros((META, feature_count), jnp.bfloat16)
    for block in range(owned // CB):
        here = slice(block * CB, (block + 1) * CB)
        inverse = inv_ref[here, :]
        mean_f = means_ref[here, :].astype(jnp.float32)
        inv_f = inverse.astype(jnp.float32)
        scaled = inv_f * mean_f
        out_ref[0, 0, here, :] = scaled.astype(jnp.bfloat16)
        out_ref[0, 1, here, :] = inverse
        terms = 0.5 * jnp.log(inv_f) - 0.5 * (scaled * mean_f)
        rest = lax.dot_general(
            ones, terms, NT, precision=lax.Precision.HIGHEST, preferred_element_type=jnp.float32
        )
        rest += log_ref[:, here].astype(jnp.float32)
        rest -= 0.5 * feature_count * math.log(2.0 * math.pi)
        high = rest.astype(jnp.bfloat16).astype(jnp.float32)
        rest -= high
        middle = rest.astype(jnp.bfloat16).astype(jnp.float32)
        low = rest - middle
        pieces = jnp.where(row == 0, high, jnp.where(row == 1, middle, low))
        out_ref[0, 0, owned:, here] = pieces.astype(jnp.bfloat16)
    for copy in copies:
        copy.wait()


def parameter_shard(means, inv_var, log_weight, points, cuts):
    owned, feature_count = means.shape
    vmem = pl.BlockSpec(memory_space=pltpu.VMEM)
    hbm = pl.BlockSpec(memory_space=pltpu.HBM)
    lengths = [b - a for a, b in zip(cuts[:-1], cuts[1:])]
    return pl.pallas_call(
        functools.partial(shard_body, cuts),
        in_specs=[hbm, hbm, vmem, hbm],
        out_specs=[vmem] + [vmem] * len(lengths),
        out_shape=[pltpu.VMEM((1, 2, owned + META, feature_count), jnp.bfloat16)]
        + [pltpu.VMEM((length, feature_count), points.dtype) for length in lengths],
        scratch_shapes=[
            pltpu.VMEM((owned, feature_count), means.dtype),
            pltpu.VMEM((owned, feature_count), inv_var.dtype),
            pltpu.SemaphoreType.DMA((2,)),
            pltpu.SemaphoreType.DMA((max(len(lengths), 1),)),
        ],
        compiler_params=pltpu.CompilerParams(vmem_limit_bytes=6 * MIB),
        cost_estimate=pl.CostEstimate(
            flops=owned * feature_count * 40,
            bytes_accessed=owned * feature_count * 8,
            transcendentals=owned * feature_count,
        ),
        name="parameter_shard",
    )(in_hbm(means), in_hbm(inv_var), log_weight.reshape(1, owned), in_hbm(points))


COLUMNS = 256


def group_of(blocks, feature_count):
    return [
        pltpu.VMEM((blocks, 2, CB, feature_count), jnp.float32),
        pltpu.VMEM((blocks, CB, RB), jnp.float32),
    ]


def run_body(first, count, held, owners, arrays, place, known, fresh, given, *refs):
    where = [ref[0] for ref in refs[:known]]
    id_ref, x_ref = refs[known : known + 2]
    weight_refs = refs[known + 2 : known + 2 + arrays]
    outs = refs[known + 2 + arrays + (0 if fresh else 2) : -7]
    sum_ref, weight_sum_ref, norm_ref = outs[:3]
    blocks, constants, rows, sems, row_sems, staging, out_sems = refs[-7:]
    owned = held * CB
    feature_count = x_ref.shape[1]
    row_index = lax.broadcasted_iota(jnp.int32, (META, RB), 0)
    pieces = jnp.where(row_index < 3, 1.0, 0.0).astype(jnp.bfloat16)

    def choice(i, slot):
        block = id_ref[slot, first + i]
        return place(lax.div(block, owners * held), *where), lax.rem(block, held)

    def copies(array, shard, block, half, slot):
        here = pl.ds(pl.multiple_of(block * CB, CB), CB)
        there = pl.ds(slot * CB, CB)
        source = weight_refs[array].at[shard]
        return (
            pltpu.make_async_copy(
                source.at[:, here, :], blocks.at[half, :, there, :], sems.at[half, slot, 0]
            ),
            pltpu.make_async_copy(
                source.at[0, pl.ds(owned, META), here],
                constants.at[half, :, there],
                sems.at[half, slot, 1],
            ),
        )

    def row_copy(i, half):
        here = pl.ds(pl.multiple_of(i * RB, RB), RB)
        return pltpu.make_async_copy(x_ref.at[here, :], rows.at[half], row_sems.at[half])

    def fetch(i, half):
        row_copy(i, half).start()
        for slot in range(CANDS):
            shard, block = choice(i, slot)
            if arrays == 1:
                for copy in copies(0, shard, block, half, slot):
                    copy.start()
            for array in range(arrays if arrays > 1 else 0):

                @pl.when(shard == array)
                def _(array=array, block=block, slot=slot):
                    for copy in copies(array, 0, block, half, slot):
                        copy.start()

    fetch(0, 0)
    if fresh:

        @pl.loop(0, sum_ref.shape[0])
        def _(i):
            sum_ref[i] = jnp.zeros(sum_ref.shape[1:], jnp.float32)
            weight_sum_ref[i] = jnp.zeros(weight_sum_ref.shape[1:], jnp.float32)

    @pl.loop(0, count)
    def _(i):
        half = lax.rem(i, 2)

        @pl.when(i + 1 < count)
        def _():
            fetch(i + 1, 1 - half)

        row_copy(0, half).wait()
        x = rows[half]
        squares = x * x
        for slot in range(CANDS):
            for copy in copies(0, 0, 0, half, slot):
                copy.wait()
        densities = lax.dot_general(blocks[half, 0], x, NT, preferred_element_type=jnp.float32)
        densities += lax.dot_general(
            blocks[half, 1], squares * -0.5, NT, preferred_element_type=jnp.float32
        )
        densities += lax.dot_general(
            constants[half], pieces, TN, preferred_element_type=jnp.float32
        )
        peak = jnp.max(densities, axis=0, keepdims=True)
        terms = jnp.exp(densities - peak)
        total = jnp.sum(terms, axis=0, keepdims=True)
        norm_ref[pl.ds(i, 1), :] = peak + jnp.log(total)
        resp = (terms * (1.0 / total)).astype(jnp.bfloat16)
        targets = []
        for slot in range(CANDS):
            shard, block = choice(i, slot)
            targets.append(shard * held + block)
        for moment, values in enumerate((x, squares)):
            for column in range(0, feature_count, COLUMNS):
                columns = slice(column, column + COLUMNS)
                part = jnp.dot(resp, values[:, columns], preferred_element_type=jnp.float32)
                for slot, target in enumerate(targets):
                    sum_ref[target, moment, :, columns] += part[slot * CB : (slot + 1) * CB]
        for slot, target in enumerate(targets):
            weight_sum_ref[target] += resp[slot * CB : (slot + 1) * CB].astype(jnp.float32)

    round_shards(given, held, sum_ref, weight_sum_ref, outs[3:], staging, out_sems)


def round_shards(given, held, sum_ref, weight_sum_ref, out_refs, staging, sems):
    owned = held * CB
    feature_count = staging.shape[2]
    ones = jnp.ones((META, RB), jnp.float32)
    copies = []
    for index, (shard, out_ref) in enumerate(zip(given, out_refs)):
        half = index % 2
        if index >= 2:
            copies[index - 2].wait()
        if feature_count > owned:
            zeros = jnp.zeros((META, feature_count - owned), jnp.bfloat16)
            staging[half, 2 * owned :, owned:] = zeros

        @pl.loop(0, held)
        def _(block, half=half, shard=shard):
            here = pl.ds(pl.multiple_of(block * CB, CB), CB)
            for moment in range(2):
                start = pl.multiple_of(moment * owned + block * CB, CB)
                staging[half, pl.ds(start, CB), :] = sum_ref[shard * held + block, moment].astype(
                    jnp.bfloat16
                )
            counts = lax.dot_general(
                ones,
                weight_sum_ref[shard * held + block],
                NT,
                precision=lax.Precision.HIGHEST,
                preferred_element_type=jnp.float32,
            )
            staging[half, 2 * owned :, here] = counts.astype(jnp.bfloat16)

        copies.append(pltpu.make_async_copy(staging.at[half], out_ref, sems.at[half]))
        copies[-1].start()
    for copy in copies[-2:]:
        copy.wait()


def part_shape(held, feature_count):
    return (2 * held * CB + META, feature_count)


def staging_of(held, feature_count):
    return [
        pltpu.VMEM((2,) + part_shape(held, feature_count), jnp.bfloat16),
        pltpu.SemaphoreType.DMA((2,)),
    ]


def rest_body(given, held, sum_ref, weight_sum_ref, *refs):
    round_shards(given, held, sum_ref, weight_sum_ref, refs[:-2], refs[-2], refs[-1])


def rounded(sums, held, given):
    feature_count = sums[0].shape[3]
    shape = part_shape(held, feature_count)
    return pl.pallas_call(
        functools.partial(rest_body, given, held),
        in_specs=[pl.BlockSpec(memory_space=pltpu.VMEM)] * 2,
        out_specs=[pl.BlockSpec(memory_space=pltpu.HBM)] * len(given),
        out_shape=[pltpu.HBM(shape, jnp.bfloat16)] * len(given),
        scratch_shapes=staging_of(held, feature_count),
        compiler_params=pltpu.CompilerParams(vmem_limit_bytes=5 * MIB),
        cost_estimate=pl.CostEstimate(
            flops=len(given) * math.prod(shape),
            bytes_accessed=len(given) * 2 * math.prod(shape),
            transcendentals=0,
        ),
        name="round_sums",
    )(*[in_vmem(value) for value in sums])


def add_run(sums, rows, ids, first, weights, held, owners, place, where, blocks, given):
    count = rows.shape[0] // RB
    feature_count = rows.shape[1]
    smem = pl.BlockSpec(memory_space=pltpu.SMEM)
    vmem = pl.BlockSpec(memory_space=pltpu.VMEM)
    pairs = count * CANDS
    known, arrays, fresh = len(where), len(weights), not sums
    part = pltpu.HBM(part_shape(held, feature_count), jnp.bfloat16)
    return pl.pallas_call(
        functools.partial(
            run_body, first, count, held, owners, arrays, place, known, fresh, given
        ),
        in_specs=[smem] * (known + 1)
        + [pl.BlockSpec(memory_space=pltpu.HBM)] * (1 + arrays)
        + [vmem] * len(sums),
        out_specs=[vmem] * 3 + [pl.BlockSpec(memory_space=pltpu.HBM)] * len(given),
        out_shape=group_of(blocks, feature_count)
        + [jax.ShapeDtypeStruct((count, RB), jnp.float32)]
        + [part] * len(given),
        scratch_shapes=[
            pltpu.VMEM((2, 2, CANDS * CB, feature_count), jnp.bfloat16),
            pltpu.VMEM((2, META, CANDS * CB), jnp.bfloat16),
            pltpu.VMEM((2, RB, feature_count), jnp.bfloat16),
            pltpu.SemaphoreType.DMA((2, CANDS, 2)),
            pltpu.SemaphoreType.DMA((2,)),
        ]
        + staging_of(held, feature_count),
        input_output_aliases={} if fresh else {known + 2 + arrays: 0, known + 3 + arrays: 1},
        compiler_params=pltpu.CompilerParams(vmem_limit_bytes=9 * MIB),
        cost_estimate=pl.CostEstimate(
            flops=pairs * 8 * CB * RB * feature_count,
            bytes_accessed=pairs * CB * feature_count * 4 + rows.size * 2,
            transcendentals=pairs * CB * RB,
        ),
        name="add_run",
    )(
        *where,
        ids,
        in_hbm(rows),
        *[in_hbm(w) for w in weights],
        *[in_vmem(value) for value in sums],
    )


CHUNK = 80


def add_body(*refs):
    rows = refs[-1].shape[0]

    def step(here):
        terms = [ref[here, :].astype(jnp.float32) for ref in refs[:-1]]
        refs[-1][here, :] = functools.reduce(jnp.add, terms).astype(jnp.bfloat16)

    @pl.loop(0, rows // CHUNK)
    def _(i):
        step(pl.ds(pl.multiple_of(i * CHUNK, 16), CHUNK))

    if rows % CHUNK:
        step(slice(rows // CHUNK * CHUNK, rows))


def added(*terms):
    vmem = pl.BlockSpec(memory_space=pltpu.VMEM)
    shape = terms[0].shape
    return pl.pallas_call(
        add_body,
        in_specs=[vmem] * len(terms),
        out_specs=vmem,
        out_shape=jax.ShapeDtypeStruct(shape, jnp.bfloat16),
        compiler_params=pltpu.CompilerParams(vmem_limit_bytes=8 * MIB),
        cost_estimate=pl.CostEstimate(
            flops=math.prod(shape), bytes_accessed=6 * math.prod(shape), transcendentals=0
        ),
        name="add_sums",
    )(*terms)


def join_body(*refs):
    start = 0
    for ref in refs[:-1]:
        refs[-1][start : start + ref.shape[0], :] = ref[...]
        start += ref.shape[0]


def joined(*norms):
    vmem = pl.BlockSpec(memory_space=pltpu.VMEM)
    return pl.pallas_call(
        join_body,
        in_specs=[vmem] * len(norms),
        out_specs=vmem,
        out_shape=pltpu.VMEM((sum(n.shape[0] for n in norms), RB), jnp.float32),
        compiler_params=pltpu.CompilerParams(vmem_limit_bytes=1 * MIB),
        name="join_norms",
    )(*norms)


def result_body(held, end_ref, own_norm, end_norm, end_sum, *refs):
    terms, (count_ref, first_ref, second_ref, loglik_ref) = refs[:-4], refs[-4:]
    is_end = end_ref[0] > 0
    owned = held * CB
    feature_count = first_ref.shape[1]
    start = pl.multiple_of(pl.program_id(0) * CB, CB)

    def total(rows):
        inner = functools.reduce(jnp.add, [t[rows, :].astype(jnp.float32) for t in terms])
        return jnp.where(is_end, end_sum[rows, :].astype(jnp.float32), inner)

    first_ref[...] = total(pl.ds(start, CB))
    second_ref[...] = total(pl.ds(owned + start, CB))
    count_ref[...] = total(slice(2 * owned, 2 * owned + META))[0:1, :owned]
    norm = jnp.where(is_end, end_norm[...], own_norm[...])
    loglik_ref[...] = norm * (1.0 / feature_count)


def results_of(held, is_end, own_norm, end_norm, end_sum, *terms):
    feature_count = end_sum.shape[1]
    owned = held * CB
    vmem = pl.BlockSpec(memory_space=pltpu.VMEM)
    operands = (own_norm, end_norm, end_sum) + terms
    return pl.pallas_call(
        functools.partial(result_body, held),
        grid=(held,),
        in_specs=[pl.BlockSpec(memory_space=pltpu.SMEM)] + [vmem] * len(operands),
        out_specs=[
            pl.BlockSpec((1, owned), lambda i: (0, 0)),
            pl.BlockSpec((CB, feature_count), lambda i: (i, 0)),
            pl.BlockSpec((CB, feature_count), lambda i: (i, 0)),
            pl.BlockSpec(own_norm.shape, lambda i: (0, 0)),
        ],
        out_shape=[
            jax.ShapeDtypeStruct((1, owned), jnp.float32),
            jax.ShapeDtypeStruct((owned, feature_count), jnp.float32),
            jax.ShapeDtypeStruct((owned, feature_count), jnp.float32),
            jax.ShapeDtypeStruct(own_norm.shape, jnp.float32),
        ],
        compiler_params=pltpu.CompilerParams(vmem_limit_bytes=10 * MIB),
        name="results",
    )(is_end.astype(jnp.int32).reshape(1), *[in_vmem(value) for value in operands])


def plain_plan(points, candidates, parameters, held):
    weights = parameter_shard(*parameters, points, (0,))[0]
    dp_size = lax.axis_size("dp")
    all_weights = lax.all_gather(weights, "dp", axis=0, tiled=True)
    outs = add_run(
        [],
        points,
        candidates.T,
        0,
        [all_weights],
        held,
        lax.axis_size("comp"),
        lambda holder: holder,
        [],
        dp_size * held,
        [],
    )
    norm, parts = outs[2], jnp.concatenate(rounded(outs[:2], held, list(range(dp_size))))
    total = lax.psum_scatter(parts, "dp", scatter_dimension=0, tiled=True)
    total = total.astype(jnp.float32)
    owned = held * CB
    counts, first, second = total[2 * owned, :owned], total[:owned], total[owned : 2 * owned]
    return counts, first, second, norm.reshape(-1) / points.shape[1]


def line_pairs(links):
    return [(2 * a + c, 2 * b + c) for a, b in links for c in (0, 1)]


INWARD = line_pairs(((0, 1), (3, 2)))
OUTWARD = line_pairs(((1, 0), (2, 3)))
MIDDLE = line_pairs(((1, 2), (2, 1)))
CORES = [(2, 3), (3, 2), (4, 5), (5, 4)]


def move(value, pairs):
    return lax.ppermute(value, "dp", pairs)


def after(value, *others):
    return lax.optimization_barrier((value,) + others)[0]


def line_place(holder, chip, core):
    z, other = lax.div(holder, 2), lax.rem(holder, 2)
    z = jnp.where(chip < 2, z, 3 - z)
    z = jnp.where(z == 0, 1, jnp.where(z == 1, 0, z))
    return z * 2 + lax.rem(other + core, 2)


def line_plan(points, candidates, parameters, held):
    index = lax.axis_index("dp")
    chip, core = index // 2, index % 2
    where = [chip.reshape(1), core.reshape(1)]
    owners = lax.axis_size("comp")
    row_blocks = points.shape[0] // RB
    cuts = (0, row_blocks // 2, row_blocks - row_blocks // 8, row_blocks)
    own_ids = candidates.T
    end_ids = move(own_ids, INWARD)
    weights, *pieces = parameter_shard(*parameters, points, [cut * RB for cut in cuts])
    weights, end_ids = lax.optimization_barrier((weights, end_ids))

    outer = move(weights, INWARD)
    across = move(weights, MIDDLE)
    own_shared = move(weights, CORES)
    far = move(outer, MIDDLE)
    moved = [move(pieces[0], INWARD)]
    moved.append(move(after(pieces[1], moved[0]), INWARD))
    moved.append(move(after(pieces[2], moved[0], far), INWARD))
    outer_shared = move(after(outer, moved[0]), CORES)
    across_shared = move(after(across, moved[0]), CORES)
    far_shared = move(far, CORES)
    shards = [weights, own_shared, outer, outer_shared, across, across_shared, far, far_shared]

    runs = [(points, own_ids, 0)]
    runs += [(piece, end_ids, cut) for piece, cut in zip(moved, cuts)]
    sums, norms = [], []
    for run_rows, ids, first in runs:
        outs = add_run(
            sums,
            run_rows,
            ids,
            first,
            shards,
            held,
            owners,
            line_place,
            where,
            8 * held,
            [7, 6] if len(norms) == len(runs) - 1 else [],
        )
        sums = outs[:2]
        norms.append(outs[2])
    far_other, far = outs[3:]
    far_received = move(far_other, CORES)
    across_other, across, outer_other, outer, own_other, own = rounded(
        [after(sums[0], far_other), sums[1]], held, [5, 4, 3, 2, 1, 0]
    )
    far_sum = move(added(after(far, own), far_received), MIDDLE)
    across_received = move(across_other, CORES)
    across_sum = move(added(across, across_received), MIDDLE)
    outer_received = move(outer_other, CORES)
    own_received = move(own_other, CORES)
    end_norm = move(joined(*norms[1:]), OUTWARD)
    end_sum = move(added(outer, outer_received, far_sum), OUTWARD)
    is_end = jnp.logical_or(chip == 0, chip == 3)
    counts, first, second, loglik = results_of(
        held, is_end, norms[0], end_norm, end_sum, own, own_received, across_sum
    )
    return counts.reshape(-1), first, second, loglik.reshape(-1)


def on_device(points, candidates, means, inv_var, log_weight):
    held = means.shape[0] // CB
    plan = line_plan if lax.axis_size("dp") == 8 else plain_plan
    return plan(points, candidates, (means, inv_var, log_weight), held)


def solution(mesh):
    return jax.shard_map(
        on_device,
        mesh=mesh,
        in_specs=(
            P(("dp", "comp"), None),
            P(("dp", "comp"), None),
            P(("dp", "comp"), None),
            P(("dp", "comp"), None),
            P(("dp", "comp")),
        ),
        out_specs=(
            P(("dp", "comp")),
            P(("dp", "comp"), None),
            P(("dp", "comp"), None),
            P(("dp", "comp")),
        ),
        check_vma=False,
    )
```

time: 268 us -> 280 us (1.045)
  waiting for transfers between devices: 99.9 us -> 133 us
  local copies, waits for them, and re-layouts: 14.3 us -> 1.45 us
  starting transfers between devices: 44.7 us -> 40.5 us
    ppermute x19, waiting for transfers between devices: 99.9 us -> 133 us  [move(): return lax.ppermute(value, 'dp', pairs)]
    unnamed x47 -> x16, local copies, waits for them, and re-layouts: 11.5 us -> 0.77 us
    ppermute x19, starting transfers between devices: 44.7 us -> 40.5 us  [move(): return lax.ppermute(value, 'dp', pairs)]
    pallas_call x18 -> x11, Pallas kernels: 105 us -> 103 us  [the longest x4 82.7 us: add_run(): pl.pallas_call(functools.partial(run_body, first, count, held, owners, ar...]
  transfers between devices with their start and end apart: 19 -> 19, of which waited for: 4 -> 3; matrix products, arithmetic and copies ran while one was open for 1% -> 0% of each run, Pallas kernels for 31% -> 32%
where the time goes in v5:
time: 280 us; the launch traced here: 279 us
  waiting for transfers between devices  133 us (48%)
  Pallas kernels  103 us (37%)
  starting transfers between devices  40.5 us (14%)
    ppermute x19, waiting for transfers between devices, move(): return lax.ppermute(value, 'dp', pairs)  133 us
    pallas_call x4, Pallas kernels, add_run(): pl.pallas_call(functools.partial(run_body, first, count, held, owners, ar...  82.7 us
    ppermute x19, starting transfers between devices, move(): return lax.ppermute(value, 'dp', pairs)  40.5 us
    pallas_call x1, Pallas kernels, rounded(): pl.pallas_call(functools.partial(rest_body, given, held), in_specs=[pl.Bl...  7.75 us
  transfers between devices with their start and end apart: 19, of which 3 were waited for; matrix products, arithmetic and copies ran while one was open for 0% of the time, Pallas kernels for 32%

profile of v5, /device:TPU:0, one launch (start us, length us, event | category | flops | bytes accessed | tf_op | source)
XLA Modules:
  0.0 279.1 jit_solution(18357781108449655993)
XLA Ops:
  0.6 4.9 %collective-permute-start = (s32[4,16]{1,0:T(4,128)}, s32[4,16]{1,0:T(4,128)S(1)}, u32[]{:S(2)}, u32[]{:S(2)}) collective-permute-start(s32[4,16]{1,0:T(4,128)} %bitcast.6), channel_id=1, source_target_pairs={{0,8},{4,12},{24,16},{28,20},{1,9},{5,13},{25,17},{29,21},{2,10},{... | collective-permute-start | bytes 776 | tf_op jit(solution)/shard_map/ppermute | solution.py:456
  6.3 4.4 %parameter_shard.1 = (bf16[1,2,528,768]{3,2,1,0:T(8,128)(2,1)S(1)}, bf16[1024,768]{1,0:T(8,128)(2,1)S(1)}, bf16[768,768]{1,0:T(8,128)(2,1)S(1)}, bf16[256,768]{1,0:T(8,128)(2,1)}) custom-call(bf16[512,768]{1,0:T(8,128)(2,1)} %means_hbm.1, bf16[512,768]{1,0:T(8,128)(2,1)} %inv_hbm.1, bf16[1,512]{1,0:T(2,128)(2,1)S(1)} %reshape.32.log_ref, ...), custom_call_target="tpu_custom_call" | custom-call | flops 15728640 | bytes 3145728 | tf_op jit(solution)/shard_map/parameter_shard/pallas_call | solution.py:78
  10.7 2.4 collective-permute-start.2
  13.2 1.9 collective-permute-start.5
  15.0 31.7 %collective-permute-done.2.refs_6_ = bf16[1,2,528,768]{3,2,1,0:T(8,128)(2,1)} collective-permute-done((bf16[1,2,528,768]{3,2,1,0:T(8,128)(2,1)S(1)}, bf16[1,2,528,768]{3,2,1,0:T(8,128)(2,1)}, u32[]{:S(2)}, u32[]{:S(2)}) %collective-permute-start.2) | collective-permute-done | bytes 1622048 | tf_op jit(solution)/shard_map/ppermute | solution.py:456
  46.7 1.8 collective-permute-start.7
  48.5 6.3 %collective-permute-start.3 = (bf16[1024,768]{1,0:T(8,128)(2,1)S(1)}, bf16[1024,768]{1,0:T(8,128)(2,1)S(1)}, u32[]{:S(2)}, u32[]{:S(2)}) collective-permute-start(bf16[1024,768]{1,0:T(8,128)(2,1)S(1)} %get-tuple-element.42), channel_id=1, source_target_pairs={{0,8},{4,12},{24,16},{28,20},{1,9},{5,13},{25,17},{29,21},{2,10},{... | collective-permute-start | bytes 4718600 | tf_op jit(solution)/shard_map/ppermute | solution.py:456
  54.8 1.8 collective-permute-start.1
  56.6 30.6 %collective-permute-done.3.refs_3_ = bf16[1024,768]{1,0:T(8,128)(2,1)S(1)} collective-permute-done((bf16[1024,768]{1,0:T(8,128)(2,1)S(1)}, bf16[1024,768]{1,0:T(8,128)(2,1)S(1)}, u32[]{:S(2)}, u32[]{:S(2)}) %collective-permute-start.3) | collective-permute-done | bytes 1572896 | tf_op jit(solution)/shard_map/ppermute | solution.py:456
  87.2 1.9 collective-permute-start.4
  89.0 1.9 collective-permute-start.6
  91.0 1.9 collective-permute-start.8
  92.9 6.0 %collective-permute-start.9 = (bf16[768,768]{1,0:T(8,128)(2,1)S(1)}, bf16[768,768]{1,0:T(8,128)(2,1)}, u32[]{:S(2)}, u32[]{:S(2)}) collective-permute-start(bf16[768,768]{1,0:T(8,128)(2,1)S(1)} %get-tuple-element.51), channel_id=1, source_target_pairs={{0,8},{4,12},{24,16},{28,20},{1,9},{5,13},{25,17},{29,21},{2,10},{... | collective-permute-start | bytes 3538952 | tf_op jit(solution)/shard_map/ppermute | solution.py:456
  98.9 1.3 collective-permute-start.10
  100.2 37.8 %add_run.4 = (f32[32,2,128,768]{3,2,1,0:T(8,128)S(1)}, f32[32,128,128]{2,1,0:T(8,128)S(1)}, f32[16,128]{1,0:T(8,128)S(1)}) custom-call(s32[1]{0:T(128)} %bitcast.1.refs_0_, s32[1]{0:T(128)} %bitcast.2.refs_1_, s32[4,16]{1,0:T(4,128)S(1)} %bitcast.7, bf16[2048,768]{1,0:T(8,128)(2,1)} %refs_3_.1, bf16[1,2,528,768]{3,2,1,0:T(8,128)(2,1)} %copy-done, ...), custom_call_target="tpu_custom_call" | custom-call | flops 6442450944 | bytes 28311552 | tf_op jit(solution)/shard_map/add_run/pallas_call | solution.py:287
  138.1 19.7 %add_run.5 = (f32[32,2,128,768]{3,2,1,0:T(8,128)S(1)}, f32[32,128,128]{2,1,0:T(8,128)S(1)}, f32[8,128]{1,0:T(8,128)S(1)}) custom-call(s32[1]{0:T(128)} %bitcast.1.refs_0_, s32[1]{0:T(128)} %bitcast.2.refs_1_, s32[4,16]{1,0:T(4,128)S(1)} %collective-permute-done.refs_2_, bf16[1024,768]{1,0:T(8,128)(2,1)} %copy-done.6, ...), custom_call_target="tpu_custom_call", output_to_operand_aliasing={{0}: (12, {}), {1}: (13, {})} | custom-call | flops 3221225472 | bytes 14155776 | tf_op jit(solution)/shard_map/add_run/pallas_call | solution.py:287
  157.8 15.3 %add_run.6 = (f32[32,2,128,768]{3,2,1,0:T(8,128)S(1)}, f32[32,128,128]{2,1,0:T(8,128)S(1)}, f32[6,128]{1,0:T(8,128)S(1)}) custom-call(s32[1]{0:T(128)} %bitcast.1.refs_0_, s32[1]{0:T(128)} %bitcast.2.refs_1_, s32[4,16]{1,0:T(4,128)S(1)} %collective-permute-done.refs_2_, ...), custom_call_target="tpu_custom_call", output_to_operand_aliasing={{0}: (12, {}), {1}: (13, {})} | custom-call | flops 2415919104 | bytes 10616832 | tf_op jit(solution)/shard_map/add_run/pallas_call | solution.py:287
  173.2 0.7 copy-done.7
  173.9 9.8 %add_run.7 = (f32[32,2,128,768]{3,2,1,0:T(8,128)S(1)}, f32[32,128,128]{2,1,0:T(8,128)S(1)}, f32[2,128]{1,0:T(2,128)S(1)}, bf16[1040,768]{1,0:T(8,128)(2,1)}, bf16[1040,768]{1,0:T(8,128)(2,1)}) custom-call(s32[1]{0:T(128)} %bitcast.1.refs_0_, s32[1]{0:T(128)} %bitcast.2.refs_1_, ...), custom_call_target="tpu_custom_call", output_to_operand_aliasing={{0}: (12, {}), {1}: (13, {})} | custom-call | flops 805306368 | bytes 3538944 | tf_op jit(solution)/shard_map/add_run/pallas_call | solution.py:287
  183.7 0.8 collective-permute-start.13
  184.5 7.7 %round_sums.1 = (bf16[1040,768]{1,0:T(8,128)(2,1)}, bf16[1040,768]{1,0:T(8,128)(2,1)}, bf16[1040,768]{1,0:T(8,128)(2,1)}, bf16[1040,768]{1,0:T(8,128)(2,1)}, bf1...) custom-call(f32[32,2,128,768]{3,2,1,0:T(8,128)S(1)} %get-tuple-element.62.sum_ref, ...), custom_call_target="tpu_custom_call" | custom-call | flops 4792320 | bytes 9584640 | tf_op jit(solution)/shard_map/round_sums/pallas_call | solution.py:263
  192.2 0.8 collective-permute-start.17
  193.0 0.9 collective-permute-start.12
  194.4 0.8 collective-permute-start.14
  195.2 0.8 collective-permute-start.16
  196.0 1.6 add_sums.5
  197.6 1.8 collective-permute-start.18
  199.5 1.9 add_sums.4
  201.3 1.3 collective-permute-start.15
  202.6 1.3 collective-permute-start.11
  204.0 71.0 %collective-permute-done.11.end_norm = f32[16,128]{1,0:T(8,128)S(1)} collective-permute-done((f32[16,128]{1,0:T(8,128)S(1)}, f32[16,128]{1,0:T(8,128)S(1)}, u32[]{:S(2)}, u32[]{:S(2)}) %collective-permute-start.11) | collective-permute-done | bytes 8224 | tf_op jit(solution)/shard_map/ppermute | solution.py:456
  275.0 4.2 %results.1 = (f32[1,512]{1,0:T(1,128)}, f32[512,768]{1,0:T(8,128)}, f32[512,768]{1,0:T(8,128)}, f32[16,128]{1,0:T(8,128)}) custom-call(s32[1]{0:T(128)} %bitcast.end_ref, f32[16,128]{1,0:T(8,128)S(1)} %get-tuple-element.45.own_norm, f32[16,128]{1,0:T(8,128)S(1)} %collective-permute-done.11.end_norm, bf16[1040,768]{1,0:T(8,128)(2,1)} %collective-permute-done.15.end_sum, ...), custom_call_target="tpu_custom_call" | custom-call | tf_op jit(solution)/shard_map/results/pallas_call | solution.py:399
  (34 shorter events, 1.2 us)
Async XLA Ops:
  0.6 10.1 %collective-permute-start = (s32[4,16]{1,0:T(4,128)}, s32[4,16]{1,0:T(4,128)S(1)}, u32[]{:S(2)}, u32[]{:S(2)}) collective-permute-start(s32[4,16]{1,0:T(4,128)} %bitcast.6), channel_id=1, source_target_pairs={{0,8},{4,12},{24,16},{28,20},{1,9},{5,13},{25,17},{29,21},{2,10},{... | collective-permute-start | bytes 776 | tf_op jit(solution)/shard_map/ppermute | solution.py:456
  6.3 94.0 %copy-start.5 = (s32[16,4]{0,1:T(4,128)S(1)}, s32[16,4]{0,1:T(4,128)}, u32[]{:S(2)}) copy-start(s32[16,4]{0,1:T(4,128)} %param.6) | copy-start | bytes 772
  10.7 89.5 %copy-start = (bf16[1,2,528,768]{3,2,1,0:T(8,128)(2,1)}, bf16[1,2,528,768]{3,2,1,0:T(8,128)(2,1)S(1)}, u32[]{:S(2)}) copy-start(bf16[1,2,528,768]{3,2,1,0:T(8,128)(2,1)S(1)} %get-tuple-element.41.refs_4_) | copy-start | bytes 4866052
  10.7 36.0 %collective-permute-start.2 = (bf16[1,2,528,768]{3,2,1,0:T(8,128)(2,1)S(1)}, bf16[1,2,528,768]{3,2,1,0:T(8,128)(2,1)}, u32[]{:S(2)}, u32[]{:S(2)}) collective-permute-start(bf16[1,2,528,768]{3,2,1,0:T(8,128)(2,1)S(1)} %get-tuple-element.41.refs_4_), channel_id=1, source_target_pairs={{0,8},{4,12},{24,16},{28,20},{1,9},{5,13},{25,17},{29,21},{2,10},{... | collective-permute-start | bytes 4866056 | tf_op jit(solution)/shard_map/ppermute | solution.py:456
  13.2 75.9 %collective-permute-start.5 = (bf16[1,2,528,768]{3,2,1,0:T(8,128)(2,1)S(1)}, bf16[1,2,528,768]{3,2,1,0:T(8,128)(2,1)}, u32[]{:S(2)}, u32[]{:S(2)}) collective-permute-start(bf16[1,2,528,768]{3,2,1,0:T(8,128)(2,1)S(1)} %get-tuple-element.41.refs_4_), channel_id=1, source_target_pairs={{8,16},{12,20},{16,8},{20,12},{9,17},{13,21},{17,9},{21,13},{10,18... | collective-permute-start | bytes 4866056 | tf_op jit(solution)/shard_map/ppermute | solution.py:456
  46.7 44.2 %collective-permute-start.7 = (bf16[1,2,528,768]{3,2,1,0:T(8,128)(2,1)}, bf16[1,2,528,768]{3,2,1,0:T(8,128)(2,1)}, u32[]{:S(2)}, u32[]{:S(2)}) collective-permute-start(bf16[1,2,528,768]{3,2,1,0:T(8,128)(2,1)} %collective-permute-done.2.refs_6_), channel_id=1, source_target_pairs={{8,16},{12,20},{16,8},{20,12},{9,17},{13,21},{17,9},{21,13},{10,18... | collective-permute-start | bytes 4866056 | tf_op jit(solution)/shard_map/ppermute | solution.py:456
  48.5 38.7 %collective-permute-start.3 = (bf16[1024,768]{1,0:T(8,128)(2,1)S(1)}, bf16[1024,768]{1,0:T(8,128)(2,1)S(1)}, u32[]{:S(2)}, u32[]{:S(2)}) collective-permute-start(bf16[1024,768]{1,0:T(8,128)(2,1)S(1)} %get-tuple-element.42), channel_id=1, source_target_pairs={{0,8},{4,12},{24,16},{28,20},{1,9},{5,13},{25,17},{29,21},{2,10},{... | collective-permute-start | bytes 4718600 | tf_op jit(solution)/shard_map/ppermute | solution.py:456
  54.8 44.1 %collective-permute-start.1 = (bf16[1,2,528,768]{3,2,1,0:T(8,128)(2,1)S(1)}, bf16[1,2,528,768]{3,2,1,0:T(8,128)(2,1)}, u32[]{:S(2)}, u32[]{:S(2)}) collective-permute-start(bf16[1,2,528,768]{3,2,1,0:T(8,128)(2,1)S(1)} %get-tuple-element.41.refs_4_), channel_id=1, source_target_pairs={{8,12},{12,8},{16,20},{20,16},{9,13},{13,9},{17,21},{21,17},{10,14... | collective-permute-start | bytes 4866056 | tf_op jit(solution)/shard_map/ppermute | solution.py:456
  87.2 11.7 %copy-start.6 = (bf16[1024,768]{1,0:T(8,128)(2,1)}, bf16[1024,768]{1,0:T(8,128)(2,1)S(1)}, u32[]{:S(2)}) copy-start(bf16[1024,768]{1,0:T(8,128)(2,1)S(1)} %collective-permute-done.3.refs_3_) | copy-start | bytes 4718596
  87.2 13.0 %collective-permute-start.4 = (bf16[1,2,528,768]{3,2,1,0:T(8,128)(2,1)}, bf16[1,2,528,768]{3,2,1,0:T(8,128)(2,1)}, u32[]{:S(2)}, u32[]{:S(2)}) collective-permute-start(bf16[1,2,528,768]{3,2,1,0:T(8,128)(2,1)} %collective-permute-done.2.refs_6_), channel_id=1, source_target_pairs={{8,12},{12,8},{16,20},{20,16},{9,13},{13,9},{17,21},{21,17},{10,14... | collective-permute-start | bytes 4866056 | tf_op jit(solution)/shard_map/ppermute | solution.py:456
  89.0 11.1 %collective-permute-start.6 = (bf16[1,2,528,768]{3,2,1,0:T(8,128)(2,1)}, bf16[1,2,528,768]{3,2,1,0:T(8,128)(2,1)}, u32[]{:S(2)}, u32[]{:S(2)}) collective-permute-start(bf16[1,2,528,768]{3,2,1,0:T(8,128)(2,1)} %collective-permute-done.5.refs_8_), channel_id=1, source_target_pairs={{8,12},{12,8},{16,20},{20,16},{9,13},{13,9},{17,21},{21,17},{10,14... | collective-permute-start | bytes 4866056 | tf_op jit(solution)/shard_map/ppermute | solution.py:456
  91.0 9.3 %collective-permute-start.8 = (bf16[1,2,528,768]{3,2,1,0:T(8,128)(2,1)}, bf16[1,2,528,768]{3,2,1,0:T(8,128)(2,1)}, u32[]{:S(2)}, u32[]{:S(2)}) collective-permute-start(bf16[1,2,528,768]{3,2,1,0:T(8,128)(2,1)} %collective-permute-done.7.refs_10_), channel_id=1, source_target_pairs={{8,12},{12,8},{16,20},{20,16},{9,13},{13,9},{17,21},{21,17},{10,14... | collective-permute-start | bytes 4866056 | tf_op jit(solution)/shard_map/ppermute | solution.py:456
  92.9 65.0 %collective-permute-start.9 = (bf16[768,768]{1,0:T(8,128)(2,1)S(1)}, bf16[768,768]{1,0:T(8,128)(2,1)}, u32[]{:S(2)}, u32[]{:S(2)}) collective-permute-start(bf16[768,768]{1,0:T(8,128)(2,1)S(1)} %get-tuple-element.51), channel_id=1, source_target_pairs={{0,8},{4,12},{24,16},{28,20},{1,9},{5,13},{25,17},{29,21},{2,10},{... | collective-permute-start | bytes 3538952 | tf_op jit(solution)/shard_map/ppermute | solution.py:456
  98.9 74.3 %collective-permute-start.10 = (bf16[256,768]{1,0:T(8,128)(2,1)}, bf16[256,768]{1,0:T(8,128)(2,1)S(1)}, u32[]{:S(2)}, u32[]{:S(2)}) collective-permute-start(bf16[256,768]{1,0:T(8,128)(2,1)} %get-tuple-element.56), channel_id=1, source_target_pairs={{0,8},{4,12},{24,16},{28,20},{1,9},{5,13},{25,17},{29,21},{2,10},{... | collective-permute-start | bytes 1179656 | tf_op jit(solution)/shard_map/ppermute | solution.py:456
  173.2 0.7 copy-start.7
  183.7 10.2 %collective-permute-start.13 = (bf16[1040,768]{1,0:T(8,128)(2,1)}, bf16[1040,768]{1,0:T(8,128)(2,1)S(1)}, u32[]{:S(2)}, u32[]{:S(2)}) collective-permute-start(bf16[1040,768]{1,0:T(8,128)(2,1)} %get-tuple-element.61), channel_id=1, source_target_pairs={{8,12},{12,8},{16,20},{20,16},{9,13},{13,9},{17,21},{21,17},{10,14... | collective-permute-start | bytes 4792328 | tf_op jit(solution)/shard_map/ppermute | solution.py:456
  184.5 9.5 %copy-start.3 = (bf16[1040,768]{1,0:T(8,128)(2,1)S(1)}, bf16[1040,768]{1,0:T(8,128)(2,1)}, u32[]{:S(2)}) copy-start(bf16[1040,768]{1,0:T(8,128)(2,1)} %get-tuple-element.68.refs_0_) | copy-start | bytes 4792324
  192.2 3.7 %collective-permute-start.17 = (bf16[1040,768]{1,0:T(8,128)(2,1)}, bf16[1040,768]{1,0:T(8,128)(2,1)S(1)}, u32[]{:S(2)}, u32[]{:S(2)}) collective-permute-start(bf16[1040,768]{1,0:T(8,128)(2,1)} %get-tuple-element.71), channel_id=1, source_target_pairs={{8,12},{12,8},{16,20},{20,16},{9,13},{13,9},{17,21},{21,17},{10,14... | collective-permute-start | bytes 4792328 | tf_op jit(solution)/shard_map/ppermute | solution.py:456
  193.0 2.9 %copy-start.4 = (bf16[1040,768]{1,0:T(8,128)(2,1)S(1)}, bf16[1040,768]{1,0:T(8,128)(2,1)}, u32[]{:S(2)}) copy-start(bf16[1040,768]{1,0:T(8,128)(2,1)} %get-tuple-element.70.refs_0_) | copy-start | bytes 4792324
  193.0 6.4 %collective-permute-start.12 = (bf16[1040,768]{1,0:T(8,128)(2,1)}, bf16[1040,768]{1,0:T(8,128)(2,1)S(1)}, u32[]{:S(2)}, u32[]{:S(2)}) collective-permute-start(bf16[1040,768]{1,0:T(8,128)(2,1)} %get-tuple-element.65), channel_id=1, source_target_pairs={{8,12},{12,8},{16,20},{20,16},{9,13},{13,9},{17,21},{21,17},{10,14... | collective-permute-start | bytes 4792328 | tf_op jit(solution)/shard_map/ppermute | solution.py:456
  194.4 5.1 %collective-permute-start.14 = (bf16[1040,768]{1,0:T(8,128)(2,1)S(1)}, bf16[1040,768]{1,0:T(8,128)(2,1)S(1)}, u32[]{:S(2)}, u32[]{:S(2)}) collective-permute-start(bf16[1040,768]{1,0:T(8,128)(2,1)S(1)} %add_sums.3), channel_id=1, source_target_pairs={{8,16},{12,20},{16,8},{20,12},{9,17},{13,21},{17,9},{21,13},{10,18... | collective-permute-start | bytes 4792328 | tf_op jit(solution)/shard_map/ppermute | solution.py:456
  195.2 79.8 %collective-permute-start.16 = (bf16[1040,768]{1,0:T(8,128)(2,1)}, bf16[1040,768]{1,0:T(8,128)(2,1)S(1)}, u32[]{:S(2)}, u32[]{:S(2)}) collective-permute-start(bf16[1040,768]{1,0:T(8,128)(2,1)} %get-tuple-element.69), channel_id=1, source_target_pairs={{8,12},{12,8},{16,20},{20,16},{9,13},{13,9},{17,21},{21,17},{10,14... | collective-permute-start | bytes 4792328 | tf_op jit(solution)/shard_map/ppermute | solution.py:456
  196.0 3.5 %copy-start.2 = (bf16[1040,768]{1,0:T(8,128)(2,1)S(1)}, bf16[1040,768]{1,0:T(8,128)(2,1)}, u32[]{:S(2)}) copy-start(bf16[1040,768]{1,0:T(8,128)(2,1)} %get-tuple-element.64.refs_0_) | copy-start | bytes 4792324
  197.6 77.3 %collective-permute-start.18 = (bf16[1040,768]{1,0:T(8,128)(2,1)}, bf16[1040,768]{1,0:T(8,128)(2,1)}, u32[]{:S(2)}, u32[]{:S(2)}) collective-permute-start(bf16[1040,768]{1,0:T(8,128)(2,1)} %add_sums.5), channel_id=1, source_target_pairs={{8,16},{12,20},{16,8},{20,12},{9,17},{13,21},{17,9},{21,13},{10,18... | collective-permute-start | bytes 4792328 | tf_op jit(solution)/shard_map/ppermute | solution.py:456
  199.5 75.5 %copy-start.1 = (bf16[1040,768]{1,0:T(8,128)(2,1)S(1)}, bf16[1040,768]{1,0:T(8,128)(2,1)}, u32[]{:S(2)}) copy-start(bf16[1040,768]{1,0:T(8,128)(2,1)} %get-tuple-element.67.refs_0_) | copy-start | bytes 4792324
  201.3 73.6 %collective-permute-start.15 = (bf16[1040,768]{1,0:T(8,128)(2,1)}, bf16[1040,768]{1,0:T(8,128)(2,1)}, u32[]{:S(2)}, u32[]{:S(2)}) collective-permute-start(bf16[1040,768]{1,0:T(8,128)(2,1)} %add_sums.4), channel_id=1, source_target_pairs={{8,0},{12,4},{16,24},{20,28},{9,1},{13,5},{17,25},{21,29},{10,2},{... | collective-permute-start | bytes 4792328 | tf_op jit(solution)/shard_map/ppermute | solution.py:456
  202.6 72.3 %collective-permute-start.11 = (f32[16,128]{1,0:T(8,128)S(1)}, f32[16,128]{1,0:T(8,128)S(1)}, u32[]{:S(2)}, u32[]{:S(2)}) collective-permute-start(f32[16,128]{1,0:T(8,128)S(1)} %join_norms.1), channel_id=1, source_target_pairs={{8,0},{12,4},{16,24},{20,28},{9,1},{13,5},{17,25},{21,29},{10,2},{... | collective-permute-start | bytes 24584 | tf_op jit(solution)/shard_map/ppermute | solution.py:456

commit v6 on v4

--- a/solution.py
+++ b/solution.py
@@ -78,9 +78,9 @@
     return pl.pallas_call(
         functools.partial(shard_body, cuts),
         in_specs=[hbm, hbm, vmem, hbm],
-        out_specs=[vmem] + [hbm] * len(lengths),
+        out_specs=[vmem] + [vmem] * len(lengths),
         out_shape=[pltpu.VMEM((1, 2, owned + META, feature_count), jnp.bfloat16)]
-        + [pltpu.HBM((length, feature_count), points.dtype) for length in lengths],
+        + [pltpu.VMEM((length, feature_count), points.dtype) for length in lengths],
         scratch_shapes=[
             pltpu.VMEM((owned, feature_count), means.dtype),
             pltpu.VMEM((owned, feature_count), inv_var.dtype),
@@ -514,13 +514,13 @@
     def sums_of(position, *earlier):
         return moments(rows, resp, after(order, *earlier), starts, held, [position])[0]
 
-    end_norm = move(joined(*[r[1] for r in results[1:]]), OUTWARD)
     far_other = sums_of(7)
     far_received = move(far_other, CORES)
     far_own = sums_of(6, far_other)
     far_part = added(far_own, far_received)
     far_sum = move(far_part, MIDDLE)
-    across_other = sums_of(5, far_part, end_norm)
+    across_other = sums_of(5, far_part)
+    end_norm = move(after(joined(*[r[1] for r in results[1:]]), across_other), OUTWARD)
     across_received = move(across_other, CORES)
     across_own = sums_of(4, across_other)
     across_part = added(across_own, across_received)
@@ -529,7 +529,7 @@
     outer_received = move(outer_other, CORES)
     own_other = sums_of(1, outer_other)
     own_received = move(own_other, CORES)
-    outer_own = sums_of(2, own_other)
+    outer_own = sums_of(2, own_other, end_norm)
     own_own = sums_of(0, outer_own)
     outer_sum = added(outer_own, outer_received, far_sum)
     end_sum = move(outer_sum, OUTWARD)

time: 335 us -> 242 us (0.72)
  Pallas kernels: 173 us -> 81.2 us
    pallas_call x1, Pallas kernels: 96.4 us -> 4.84 us  [parameter_shard(): pl.pallas_call(functools.partial(shard_body, cuts), in_specs=[hbm, hbm, v...]
    unnamed x38 -> x42, local copies, waits for them, and re-layouts: 9.52 us -> 11.3 us
  transfers between devices with their start and end apart: 19 -> 19, of which waited for: 6 -> 6; matrix products, arithmetic and copies ran while one was open for 0% -> 0% of each run, Pallas kernels for 48% -> 28%
where the time goes in v6:
time: 242 us; the launch traced here: 241 us
  waiting for transfers between devices  106 us (44%)
  Pallas kernels  81.2 us (34%)
  starting transfers between devices  40.8 us (17%)
  local copies, waits for them, and re-layouts  12 us (5%)
    ppermute x19, waiting for transfers between devices, move(): return lax.ppermute(value, 'dp', pairs)  106 us
    ppermute x19, starting transfers between devices, move(): return lax.ppermute(value, 'dp', pairs)  40.8 us
    pallas_call x8, Pallas kernels, moments(): pl.pallas_call(functools.partial(moment_body, tuple(shards), held, runs),...  30.3 us
    pallas_call x4, Pallas kernels, responsibilities(): pl.pallas_call(functools.partial(density_body, first, count, held), in_sp...  26.6 us
    unnamed x42, local copies, waits for them, and re-layouts  11.3 us
    pallas_call x1, Pallas kernels, pair_lists(): pl.pallas_call(functools.partial(list_body, tuple(runs), held, owners, pl...  5.52 us
    pallas_call x2, Pallas kernels, stacked(): pl.pallas_call(functools.partial(copy_body, places, len(earlier)), in_spe...  5.28 us
  transfers between devices with their start and end apart: 19, of which 6 were waited for; matrix products, arithmetic and copies ran while one was open for 0% of the time, Pallas kernels for 28%

profile of v6, /device:TPU:0, one launch (start us, length us, event | category | flops | bytes accessed | tf_op | source)
XLA Modules:
  0.0 240.8 jit_solution(17376878161033083965)
XLA Ops:
  0.6 4.9 %collective-permute-start = (s32[4,16]{1,0:T(4,128)}, s32[4,16]{1,0:T(4,128)S(1)}, u32[]{:S(2)}, u32[]{:S(2)}) collective-permute-start(s32[4,16]{1,0:T(4,128)} %bitcast.6), channel_id=1, source_target_pairs={{0,8},{4,12},{24,16},{28,20},{1,9},{5,13},{25,17},{29,21},{2,10},{... | collective-permute-start | bytes 776 | tf_op jit(solution)/shard_map/ppermute | solution.py:463
  6.3 4.8 %parameter_shard.1 = (bf16[1,2,528,768]{3,2,1,0:T(8,128)(2,1)S(1)}, bf16[1024,768]{1,0:T(8,128)(2,1)}, bf16[768,768]{1,0:T(8,128)(2,1)S(1)}, bf16[256,768]{1,0:T(8,128)(2,1)S(1)}) custom-call(bf16[512,768]{1,0:T(8,128)(2,1)} %means_hbm.1, bf16[512,768]{1,0:T(8,128)(2,1)} %inv_hbm.1, bf16[1,512]{1,0:T(2,128)(2,1)S(1)} %reshape.32.log_ref, ...), custom_call_target="tpu_custom_call" | custom-call | flops 15728640 | bytes 3145728 | tf_op jit(solution)/shard_map/parameter_shard/pallas_call | solution.py:78
  12.9 1.8 collective-permute-start.5
  14.7 4.1 %collective-permute-start.1 = (bf16[1,2,528,768]{3,2,1,0:T(8,128)(2,1)S(1)}, bf16[1,2,528,768]{3,2,1,0:T(8,128)(2,1)}, u32[]{:S(2)}, u32[]{:S(2)}) collective-permute-start(bf16[1,2,528,768]{3,2,1,0:T(8,128)(2,1)S(1)} %get-tuple-element.48.refs_0_), channel_id=1, source_target_pairs={{0,8},{4,12},{24,16},{28,20},{1,9},{5,13},{25,17},{29,21},{2,10},{... | collective-permute-start | bytes 4866056 | tf_op jit(solution)/shard_map/ppermute | solution.py:463
  18.9 1.8 collective-permute-start.3
  20.7 1.9 collective-permute-start.6
  22.6 29.5 %collective-permute-done.1.refs_2_ = bf16[1,2,528,768]{3,2,1,0:T(8,128)(2,1)} collective-permute-done((bf16[1,2,528,768]{3,2,1,0:T(8,128)(2,1)S(1)}, bf16[1,2,528,768]{3,2,1,0:T(8,128)(2,1)}, u32[]{:S(2)}, u32[]{:S(2)}) %collective-permute-start.1) | collective-permute-done | bytes 1622048 | tf_op jit(solution)/shard_map/ppermute | solution.py:463
  52.1 1.9 collective-permute-start.4
  55.8 5.5 %collective-permute-start.8 = (bf16[1024,768]{1,0:T(8,128)(2,1)}, bf16[1024,768]{1,0:T(8,128)(2,1)S(1)}, u32[]{:S(2)}, u32[]{:S(2)}) collective-permute-start(bf16[1024,768]{1,0:T(8,128)(2,1)} %get-tuple-element.54), channel_id=1, source_target_pairs={{0,8},{4,12},{24,16},{28,20},{1,9},{5,13},{25,17},{29,21},{2,10},{... | collective-permute-start | bytes 4718600 | tf_op jit(solution)/shard_map/ppermute | solution.py:463
  61.3 5.5 %pair_lists.1 = (s32[128]{0:T(128)S(1)}, s32[128]{0:T(128)S(1)}, s32[129]{0:T(256)S(1)}) custom-call(s32[1]{0:T(128)} %bitcast.1.rest_0_, s32[1]{0:T(128)} %bitcast.2.rest_1_, s32[4,16]{1,0:T(4,128)S(1)} %bitcast.7, s32[4,16]{1,0:T(4,128)S(1)} %collective-permute-done.rest_3_), custom_call_target="tpu_custom_call" | custom-call | tf_op jit(solution)/shard_map/pair_lists/pallas_call | solution.py:209
  66.9 3.7 %stack_shards.2.refs_0_ = bf16[8,2,528,768]{3,2,1,0:T(8,128)(2,1)S(1)} custom-call(bf16[1,2,528,768]{3,2,1,0:T(8,128)(2,1)S(1)} %get-tuple-element.48.refs_0_, bf16[1,2,528,768]{3,2,1,0:T(8,128)(2,1)} %collective-permute-done.3.refs_1_, bf16[1,2,528,768]{3,2,1,0:T(8,128)(2,1)} %collective-permute-done.1.refs_2_, ...), custom_call_target="tpu_custom_call" | custom-call | tf_op jit(solution)/shard_map/stack_shards/pallas_call | solution.py:331
  71.4 23.8 %collective-permute-done.8.x_ref.rest_1_ = bf16[1024,768]{1,0:T(8,128)(2,1)S(1)} collective-permute-done((bf16[1024,768]{1,0:T(8,128)(2,1)}, bf16[1024,768]{1,0:T(8,128)(2,1)S(1)}, u32[]{:S(2)}, u32[]{:S(2)}) %collective-permute-start.8) | collective-permute-done | bytes 1572896 | tf_op jit(solution)/shard_map/ppermute | solution.py:463
  96.3 5.3 %collective-permute-start.9 = (bf16[768,768]{1,0:T(8,128)(2,1)S(1)}, bf16[768,768]{1,0:T(8,128)(2,1)S(1)}, u32[]{:S(2)}, u32[]{:S(2)}) collective-permute-start(bf16[768,768]{1,0:T(8,128)(2,1)S(1)} %copy-done.18), channel_id=1, source_target_pairs={{0,8},{4,12},{24,16},{28,20},{1,9},{5,13},{25,17},{29,21},{2,10},{... | collective-permute-start | bytes 3538952 | tf_op jit(solution)/shard_map/ppermute | solution.py:463
  105.4 12.8 %responsibilities.4 = (bf16[16,4,128,128]{3,2,1,0:T(8,128)(2,1)S(1)}, f32[16,128]{1,0:T(8,128)S(1)}) custom-call(s32[128]{0:T(128)S(1)} %get-tuple-element.60.pos_ref, bf16[2048,768]{1,0:T(8,128)(2,1)S(1)} %copy-done, bf16[8,2,528,768]{3,2,1,0:T(8,128)(2,1)S(1)} %stack_shards.3.weight_ref), custom_call_target="tpu_custom_call" | custom-call | flops 3221225472 | bytes 28311552 | tf_op jit(solution)/shard_map/responsibilities/pallas_call | solution.py:143
  118.3 6.6 %responsibilities.5 = (bf16[8,4,128,128]{3,2,1,0:T(8,128)(2,1)S(1)}, f32[8,128]{1,0:T(8,128)S(1)}) custom-call(s32[128]{0:T(128)S(1)} %get-tuple-element.60.pos_ref, bf16[1024,768]{1,0:T(8,128)(2,1)S(1)} %copy-done.4, bf16[8,2,528,768]{3,2,1,0:T(8,128)(2,1)S(1)} %stack_shards.3.weight_ref), custom_call_target="tpu_custom_call" | custom-call | flops 1610612736 | bytes 14155776 | tf_op jit(solution)/shard_map/responsibilities/pallas_call | solution.py:143
  124.9 3.0 %collective-permute-done.9.x_ref.rest_2_ = bf16[768,768]{1,0:T(8,128)(2,1)S(1)} collective-permute-done((bf16[768,768]{1,0:T(8,128)(2,1)S(1)}, bf16[768,768]{1,0:T(8,128)(2,1)S(1)}, u32[]{:S(2)}, u32[]{:S(2)}) %collective-permute-start.9) | collective-permute-done | bytes 1179680 | tf_op jit(solution)/shard_map/ppermute | solution.py:463
  127.9 5.1 %responsibilities.6 = (bf16[6,4,128,128]{3,2,1,0:T(8,128)(2,1)S(1)}, f32[6,128]{1,0:T(8,128)S(1)}) custom-call(s32[128]{0:T(128)S(1)} %get-tuple-element.60.pos_ref, bf16[768,768]{1,0:T(8,128)(2,1)S(1)} %collective-permute-done.9.x_ref.rest_2_, bf16[8,2,528,768]{3,2,1,0:T(8,128)(2,1)S(1)} %stack_shards.3.weight_ref), custom_call_target="tpu_custom_call" | custom-call | flops 1207959552 | bytes 10616832 | tf_op jit(solution)/shard_map/responsibilities/pallas_call | solution.py:143
  133.0 2.9 %collective-permute-done.10.x_ref.rest_3_ = bf16[256,768]{1,0:T(8,128)(2,1)S(1)} collective-permute-done((bf16[256,768]{1,0:T(8,128)(2,1)S(1)}, bf16[256,768]{1,0:T(8,128)(2,1)S(1)}, u32[]{:S(2)}, u32[]{:S(2)}) %collective-permute-start.10) | collective-permute-done | bytes 393248 | tf_op jit(solution)/shard_map/ppermute | solution.py:463
  135.9 2.1 responsibilities.7
  138.0 3.1 %moments.8 = bf16[1040,768]{1,0:T(8,128)(2,1)S(1)} custom-call(s32[128]{0:T(128)S(1)} %get-tuple-element.75.order_ref, s32[129]{0:T(256)S(1)} %get-tuple-element.47.start_ref, bf16[2048,768]{1,0:T(8,128)(2,1)S(1)} %copy-done, bf16[1024,768]{1,0:T(8,128)(2,1)S(1)} %copy-done.4, bf16[768,768]{1,0:T(8,128)(2,1)S(1)} %collective-permute-done.9.x_ref.rest_2_, ...), custom_call_target="tpu_custom_call" | custom-call | flops 805306368 | bytes 3670016 | tf_op jit(solution)/shard_map/moments/pallas_call | solution.py:282
  141.9 1.9 moments.9.refs_0_
  144.3 2.5 %moments.10 = bf16[1040,768]{1,0:T(8,128)(2,1)S(1)} custom-call(s32[128]{0:T(128)S(1)} %get-tuple-element.75.order_ref, s32[129]{0:T(256)S(1)} %get-tuple-element.47.start_ref, bf16[2048,768]{1,0:T(8,128)(2,1)S(1)} %copy-done, bf16[1024,768]{1,0:T(8,128)(2,1)S(1)} %copy-done.4, bf16[768,768]{1,0:T(8,128)(2,1)S(1)} %collective-permute-done.9.x_ref.rest_2_, ...), custom_call_target="tpu_custom_call" | custom-call | flops 805306368 | bytes 3670016 | tf_op jit(solution)/shard_map/moments/pallas_call | solution.py:282
  148.5 2.5 %moments.11.refs_0_ = bf16[1040,768]{1,0:T(8,128)(2,1)S(1)} custom-call(s32[128]{0:T(128)S(1)} %get-tuple-element.75.order_ref, s32[129]{0:T(256)S(1)} %get-tuple-element.47.start_ref, bf16[2048,768]{1,0:T(8,128)(2,1)S(1)} %copy-done, bf16[1024,768]{1,0:T(8,128)(2,1)S(1)} %copy-done.4, bf16[768,768]{1,0:T(8,128)(2,1)S(1)} %collective-permute-done.9.x_ref.rest_2_, ...), custom_call_target="tpu_custom_call" | custom-call | flops 805306368 | bytes 3670016 | tf_op jit(solution)/shard_map/moments/pallas_call | solution.py:282
  156.4 1.9 collective-permute-start.18
  158.2 3.6 %moments.13 = bf16[1040,768]{1,0:T(8,128)(2,1)} custom-call(s32[128]{0:T(128)S(1)} %get-tuple-element.75.order_ref, s32[129]{0:T(256)S(1)} %get-tuple-element.47.start_ref, bf16[2048,768]{1,0:T(8,128)(2,1)S(1)} %copy-done, bf16[1024,768]{1,0:T(8,128)(2,1)S(1)} %copy-done.4, bf16[768,768]{1,0:T(8,128)(2,1)S(1)} %collective-permute-done.9.x_ref.rest_2_, ...), custom_call_target="tpu_custom_call" | custom-call | flops 805306368 | bytes 3670016 | tf_op jit(solution)/shard_map/moments/pallas_call | solution.py:282
  161.9 1.9 collective-permute-start.17
  163.7 14.7 %collective-permute-done.12.refs_1_ = f32[16,128]{1,0:T(8,128)S(1)} collective-permute-done((f32[16,128]{1,0:T(8,128)S(1)}, f32[16,128]{1,0:T(8,128)S(1)}, u32[]{:S(2)}, u32[]{:S(2)}) %collective-permute-start.12) | collective-permute-done | bytes 8224 | tf_op jit(solution)/shard_map/ppermute | solution.py:463
  178.5 12.5 %moments.14.refs_0_ = bf16[1040,768]{1,0:T(8,128)(2,1)S(1)} custom-call(s32[128]{0:T(128)S(1)} %get-tuple-element.75.order_ref, s32[129]{0:T(256)S(1)} %get-tuple-element.47.start_ref, bf16[2048,768]{1,0:T(8,128)(2,1)S(1)} %copy-done, bf16[1024,768]{1,0:T(8,128)(2,1)S(1)} %copy-done.4, bf16[768,768]{1,0:T(8,128)(2,1)S(1)} %collective-permute-done.9.x_ref.rest_2_, ...), custom_call_target="tpu_custom_call" | custom-call | flops 805306368 | bytes 3670016 | tf_op jit(solution)/shard_map/moments/pallas_call | solution.py:282
  191.0 1.8 add_sums.5
  201.7 2.5 %moments.15.refs_3_ = bf16[1040,768]{1,0:T(8,128)(2,1)S(1)} custom-call(s32[128]{0:T(128)S(1)} %get-tuple-element.75.order_ref, s32[129]{0:T(256)S(1)} %get-tuple-element.47.start_ref, bf16[2048,768]{1,0:T(8,128)(2,1)S(1)} %copy-done, bf16[1024,768]{1,0:T(8,128)(2,1)S(1)} %copy-done.5, bf16[768,768]{1,0:T(8,128)(2,1)S(1)} %copy-done.7, ...), custom_call_target="tpu_custom_call" | custom-call | flops 805306368 | bytes 3670016 | tf_op jit(solution)/shard_map/moments/pallas_call | solution.py:282
  204.3 31.8 %collective-permute-done.16.refs_2_ = bf16[1040,768]{1,0:T(8,128)(2,1)} collective-permute-done((bf16[1040,768]{1,0:T(8,128)(2,1)}, bf16[1040,768]{1,0:T(8,128)(2,1)}, u32[]{:S(2)}, u32[]{:S(2)}) %collective-permute-start.16) | collective-permute-done | bytes 1597472 | tf_op jit(solution)/shard_map/ppermute | solution.py:463
  236.1 4.6 %results.1 = (f32[1,512]{1,0:T(1,128)}, f32[512,768]{1,0:T(8,128)}, f32[512,768]{1,0:T(8,128)}, f32[16,128]{1,0:T(8,128)}) custom-call(s32[1]{0:T(128)} %bitcast.end_ref, f32[16,128]{1,0:T(8,128)S(1)} %get-tuple-element.51.refs_0_, f32[16,128]{1,0:T(8,128)S(1)} %copy-done.15, bf16[1040,768]{1,0:T(8,128)(2,1)} %collective-permute-done.16.refs_2_, ...), custom_call_target="tpu_custom_call" | custom-call | tf_op jit(solution)/shard_map/results/pallas_call | solution.py:406
  (70 shorter events, 27.0 us)
Async XLA Ops:
  0.6 12.3 %collective-permute-start = (s32[4,16]{1,0:T(4,128)}, s32[4,16]{1,0:T(4,128)S(1)}, u32[]{:S(2)}, u32[]{:S(2)}) collective-permute-start(s32[4,16]{1,0:T(4,128)} %bitcast.6), channel_id=1, source_target_pairs={{0,8},{4,12},{24,16},{28,20},{1,9},{5,13},{25,17},{29,21},{2,10},{... | collective-permute-start | bytes 776 | tf_op jit(solution)/shard_map/ppermute | solution.py:463
  6.3 55.1 %copy-start.16 = (s32[16,4]{0,1:T(4,128)S(1)}, s32[16,4]{0,1:T(4,128)}, u32[]{:S(2)}) copy-start(s32[16,4]{0,1:T(4,128)} %param.6) | copy-start | bytes 772
  12.9 7.8 %collective-permute-start.5 = (bf16[1,2,528,768]{3,2,1,0:T(8,128)(2,1)S(1)}, bf16[1,2,528,768]{3,2,1,0:T(8,128)(2,1)}, u32[]{:S(2)}, u32[]{:S(2)}) collective-permute-start(bf16[1,2,528,768]{3,2,1,0:T(8,128)(2,1)S(1)} %get-tuple-element.48.refs_0_), channel_id=1, source_target_pairs={{8,16},{12,20},{16,8},{20,12},{9,17},{13,21},{17,9},{21,13},{10,18... | collective-permute-start | bytes 4866056 | tf_op jit(solution)/shard_map/ppermute | solution.py:463
  14.7 37.4 %collective-permute-start.1 = (bf16[1,2,528,768]{3,2,1,0:T(8,128)(2,1)S(1)}, bf16[1,2,528,768]{3,2,1,0:T(8,128)(2,1)}, u32[]{:S(2)}, u32[]{:S(2)}) collective-permute-start(bf16[1,2,528,768]{3,2,1,0:T(8,128)(2,1)S(1)} %get-tuple-element.48.refs_0_), channel_id=1, source_target_pairs={{0,8},{4,12},{24,16},{28,20},{1,9},{5,13},{25,17},{29,21},{2,10},{... | collective-permute-start | bytes 4866056 | tf_op jit(solution)/shard_map/ppermute | solution.py:463
  18.9 48.0 %collective-permute-start.3 = (bf16[1,2,528,768]{3,2,1,0:T(8,128)(2,1)S(1)}, bf16[1,2,528,768]{3,2,1,0:T(8,128)(2,1)}, u32[]{:S(2)}, u32[]{:S(2)}) collective-permute-start(bf16[1,2,528,768]{3,2,1,0:T(8,128)(2,1)S(1)} %get-tuple-element.48.refs_0_), channel_id=1, source_target_pairs={{8,12},{12,8},{16,20},{20,16},{9,13},{13,9},{17,21},{21,17},{10,14... | collective-permute-start | bytes 4866056 | tf_op jit(solution)/shard_map/ppermute | solution.py:463
  20.7 46.2 %collective-permute-start.6 = (bf16[1,2,528,768]{3,2,1,0:T(8,128)(2,1)}, bf16[1,2,528,768]{3,2,1,0:T(8,128)(2,1)}, u32[]{:S(2)}, u32[]{:S(2)}) collective-permute-start(bf16[1,2,528,768]{3,2,1,0:T(8,128)(2,1)} %collective-permute-done.5.refs_4_), channel_id=1, source_target_pairs={{8,12},{12,8},{16,20},{20,16},{9,13},{13,9},{17,21},{21,17},{10,14... | collective-permute-start | bytes 4866056 | tf_op jit(solution)/shard_map/ppermute | solution.py:463
  52.1 14.8 %collective-permute-start.4 = (bf16[1,2,528,768]{3,2,1,0:T(8,128)(2,1)}, bf16[1,2,528,768]{3,2,1,0:T(8,128)(2,1)}, u32[]{:S(2)}, u32[]{:S(2)}) collective-permute-start(bf16[1,2,528,768]{3,2,1,0:T(8,128)(2,1)} %collective-permute-done.1.refs_2_), channel_id=1, source_target_pairs={{8,12},{12,8},{16,20},{20,16},{9,13},{13,9},{17,21},{21,17},{10,14... | collective-permute-start | bytes 4866056 | tf_op jit(solution)/shard_map/ppermute | solution.py:463
  54.0 16.6 %collective-permute-start.2 = (bf16[1,2,528,768]{3,2,1,0:T(8,128)(2,1)}, bf16[1,2,528,768]{3,2,1,0:T(8,128)(2,1)}, u32[]{:S(2)}, u32[]{:S(2)}) collective-permute-start(bf16[1,2,528,768]{3,2,1,0:T(8,128)(2,1)} %collective-permute-done.1.refs_2_), channel_id=1, source_target_pairs={{8,16},{12,20},{16,8},{20,12},{9,17},{13,21},{17,9},{21,13},{10,18... | collective-permute-start | bytes 4866056 | tf_op jit(solution)/shard_map/ppermute | solution.py:463
  55.8 39.4 %collective-permute-start.8 = (bf16[1024,768]{1,0:T(8,128)(2,1)}, bf16[1024,768]{1,0:T(8,128)(2,1)S(1)}, u32[]{:S(2)}, u32[]{:S(2)}) collective-permute-start(bf16[1024,768]{1,0:T(8,128)(2,1)} %get-tuple-element.54), channel_id=1, source_target_pairs={{0,8},{4,12},{24,16},{28,20},{1,9},{5,13},{25,17},{29,21},{2,10},{... | collective-permute-start | bytes 4718600 | tf_op jit(solution)/shard_map/ppermute | solution.py:463
  66.9 29.5 %copy-start.18 = (bf16[768,768]{1,0:T(8,128)(2,1)S(1)}, bf16[768,768]{1,0:T(8,128)(2,1)}, u32[]{:S(2)}) copy-start(bf16[768,768]{1,0:T(8,128)(2,1)} %copy-done.17) | copy-start | bytes 3538948
  66.9 34.8 %copy-start.20 = (bf16[256,768]{1,0:T(8,128)(2,1)S(1)}, bf16[256,768]{1,0:T(8,128)(2,1)}, u32[]{:S(2)}) copy-start(bf16[256,768]{1,0:T(8,128)(2,1)} %copy-done.19) | copy-start | bytes 1179652
  70.6 32.4 %collective-permute-start.7 = (bf16[1,2,528,768]{3,2,1,0:T(8,128)(2,1)}, bf16[1,2,528,768]{3,2,1,0:T(8,128)(2,1)S(1)}, u32[]{:S(2)}, u32[]{:S(2)}) collective-permute-start(bf16[1,2,528,768]{3,2,1,0:T(8,128)(2,1)} %collective-permute-done.2.refs_1_), channel_id=1, source_target_pairs={{8,12},{12,8},{16,20},{20,16},{9,13},{13,9},{17,21},{21,17},{10,14... | collective-permute-start | bytes 4866056 | tf_op jit(solution)/shard_map/ppermute | solution.py:463
  96.3 31.5 %collective-permute-start.9 = (bf16[768,768]{1,0:T(8,128)(2,1)S(1)}, bf16[768,768]{1,0:T(8,128)(2,1)S(1)}, u32[]{:S(2)}, u32[]{:S(2)}) collective-permute-start(bf16[768,768]{1,0:T(8,128)(2,1)S(1)} %copy-done.18), channel_id=1, source_target_pairs={{0,8},{4,12},{24,16},{28,20},{1,9},{5,13},{25,17},{29,21},{2,10},{... | collective-permute-start | bytes 3538952 | tf_op jit(solution)/shard_map/ppermute | solution.py:463
  101.7 34.2 %collective-permute-start.10 = (bf16[256,768]{1,0:T(8,128)(2,1)S(1)}, bf16[256,768]{1,0:T(8,128)(2,1)S(1)}, u32[]{:S(2)}, u32[]{:S(2)}) collective-permute-start(bf16[256,768]{1,0:T(8,128)(2,1)S(1)} %copy-done.20), channel_id=1, source_target_pairs={{0,8},{4,12},{24,16},{28,20},{1,9},{5,13},{25,17},{29,21},{2,10},{... | collective-permute-start | bytes 1179656 | tf_op jit(solution)/shard_map/ppermute | solution.py:463
  103.0 2.4 copy-start
  105.4 12.9 %copy-start.4 = (bf16[1024,768]{1,0:T(8,128)(2,1)S(1)}, bf16[1024,768]{1,0:T(8,128)(2,1)}, u32[]{:S(2)}) copy-start(bf16[1024,768]{1,0:T(8,128)(2,1)} %copy-done.3) | copy-start | bytes 4718596
  118.3 60.2 %copy-start.1 = (bf16[16,4,128,128]{3,2,1,0:T(8,128)(2,1)}, bf16[16,4,128,128]{3,2,1,0:T(8,128)(2,1)S(1)}, u32[]{:S(2)}) copy-start(bf16[16,4,128,128]{3,2,1,0:T(8,128)(2,1)S(1)} %get-tuple-element.64.rest_4_) | copy-start | bytes 6291460
  124.9 53.5 %copy-start.8 = (bf16[8,4,128,128]{3,2,1,0:T(8,128)(2,1)}, bf16[8,4,128,128]{3,2,1,0:T(8,128)(2,1)S(1)}, u32[]{:S(2)}) copy-start(bf16[8,4,128,128]{3,2,1,0:T(8,128)(2,1)S(1)} %get-tuple-element.65.rest_5_) | copy-start | bytes 3145732
  127.9 50.5 %copy-start.6 = (bf16[768,768]{1,0:T(8,128)(2,1)}, bf16[768,768]{1,0:T(8,128)(2,1)S(1)}, u32[]{:S(2)}) copy-start(bf16[768,768]{1,0:T(8,128)(2,1)S(1)} %collective-permute-done.9.x_ref.rest_2_) | copy-start | bytes 3538948
  133.0 45.4 %copy-start.10 = (bf16[6,4,128,128]{3,2,1,0:T(8,128)(2,1)}, bf16[6,4,128,128]{3,2,1,0:T(8,128)(2,1)S(1)}, u32[]{:S(2)}) copy-start(bf16[6,4,128,128]{3,2,1,0:T(8,128)(2,1)S(1)} %get-tuple-element.66.rest_6_) | copy-start | bytes 2359300
  138.0 40.5 %copy-start.12 = (bf16[2,4,128,128]{3,2,1,0:T(8,128)(2,1)}, bf16[2,4,128,128]{3,2,1,0:T(8,128)(2,1)S(1)}, u32[]{:S(2)}) copy-start(bf16[2,4,128,128]{3,2,1,0:T(8,128)(2,1)S(1)} %get-tuple-element.67.rest_7_) | copy-start | bytes 786436
  141.1 2.7 %collective-permute-start.11 = (bf16[1040,768]{1,0:T(8,128)(2,1)S(1)}, bf16[1040,768]{1,0:T(8,128)(2,1)S(1)}, u32[]{:S(2)}, u32[]{:S(2)}) collective-permute-start(bf16[1040,768]{1,0:T(8,128)(2,1)S(1)} %moments.8), channel_id=1, source_target_pairs={{8,12},{12,8},{16,20},{20,16},{9,13},{13,9},{17,21},{21,17},{10,14... | collective-permute-start | bytes 4792328 | tf_op jit(solution)/shard_map/ppermute | solution.py:463
  146.8 4.2 %collective-permute-start.13 = (bf16[1040,768]{1,0:T(8,128)(2,1)S(1)}, bf16[1040,768]{1,0:T(8,128)(2,1)S(1)}, u32[]{:S(2)}, u32[]{:S(2)}) collective-permute-start(bf16[1040,768]{1,0:T(8,128)(2,1)S(1)} %moments.10), channel_id=1, source_target_pairs={{8,12},{12,8},{16,20},{20,16},{9,13},{13,9},{17,21},{21,17},{10,14... | collective-permute-start | bytes 4792328 | tf_op jit(solution)/shard_map/ppermute | solution.py:463
  147.5 43.5 %collective-permute-start.15 = (bf16[1040,768]{1,0:T(8,128)(2,1)S(1)}, bf16[1040,768]{1,0:T(8,128)(2,1)S(1)}, u32[]{:S(2)}, u32[]{:S(2)}) collective-permute-start(bf16[1040,768]{1,0:T(8,128)(2,1)S(1)} %add_sums.3), channel_id=1, source_target_pairs={{8,16},{12,20},{16,8},{20,12},{9,17},{13,21},{17,9},{21,13},{10,18... | collective-permute-start | bytes 4792328 | tf_op jit(solution)/shard_map/ppermute | solution.py:463
  154.3 36.7 %collective-permute-start.14 = (bf16[1040,768]{1,0:T(8,128)(2,1)S(1)}, bf16[1040,768]{1,0:T(8,128)(2,1)S(1)}, u32[]{:S(2)}, u32[]{:S(2)}) collective-permute-start(bf16[1040,768]{1,0:T(8,128)(2,1)S(1)} %moments.12), channel_id=1, source_target_pairs={{8,12},{12,8},{16,20},{20,16},{9,13},{13,9},{17,21},{21,17},{10,14... | collective-permute-start | bytes 4792328 | tf_op jit(solution)/shard_map/ppermute | solution.py:463
  155.1 23.3 %collective-permute-start.12 = (f32[16,128]{1,0:T(8,128)S(1)}, f32[16,128]{1,0:T(8,128)S(1)}, u32[]{:S(2)}, u32[]{:S(2)}) collective-permute-start(f32[16,128]{1,0:T(8,128)S(1)} %join_norms.1), channel_id=1, source_target_pairs={{8,0},{12,4},{16,24},{20,28},{9,1},{13,5},{17,25},{21,29},{10,2},{... | collective-permute-start | bytes 24584 | tf_op jit(solution)/shard_map/ppermute | solution.py:463
  156.4 47.9 %collective-permute-start.18 = (bf16[1040,768]{1,0:T(8,128)(2,1)}, bf16[1040,768]{1,0:T(8,128)(2,1)}, u32[]{:S(2)}, u32[]{:S(2)}) collective-permute-start(bf16[1040,768]{1,0:T(8,128)(2,1)} %add_sums.4), channel_id=1, source_target_pairs={{8,16},{12,20},{16,8},{20,12},{9,17},{13,21},{17,9},{21,13},{10,18... | collective-permute-start | bytes 4792328 | tf_op jit(solution)/shard_map/ppermute | solution.py:463
  161.9 42.4 %collective-permute-start.17 = (bf16[1040,768]{1,0:T(8,128)(2,1)}, bf16[1040,768]{1,0:T(8,128)(2,1)}, u32[]{:S(2)}, u32[]{:S(2)}) collective-permute-start(bf16[1040,768]{1,0:T(8,128)(2,1)} %moments.13), channel_id=1, source_target_pairs={{8,12},{12,8},{16,20},{20,16},{9,13},{13,9},{17,21},{21,17},{10,14... | collective-permute-start | bytes 4792328 | tf_op jit(solution)/shard_map/ppermute | solution.py:463
  178.5 12.5 %copy-start.14 = (f32[16,128]{1,0:T(8,128)}, f32[16,128]{1,0:T(8,128)S(1)}, u32[]{:S(2)}) copy-start(f32[16,128]{1,0:T(8,128)S(1)} %collective-permute-done.12.refs_1_) | copy-start | bytes 24580
  192.9 43.2 %collective-permute-start.16 = (bf16[1040,768]{1,0:T(8,128)(2,1)}, bf16[1040,768]{1,0:T(8,128)(2,1)}, u32[]{:S(2)}, u32[]{:S(2)}) collective-permute-start(bf16[1040,768]{1,0:T(8,128)(2,1)} %add_sums.5), channel_id=1, source_target_pairs={{8,0},{12,4},{16,24},{20,28},{9,1},{13,5},{17,25},{21,29},{10,2},{... | collective-permute-start | bytes 4792328 | tf_op jit(solution)/shard_map/ppermute | solution.py:463
  194.2 1.6 copy-start.2
  201.7 34.3 %copy-start.15 = (f32[16,128]{1,0:T(8,128)S(1)}, f32[16,128]{1,0:T(8,128)}, u32[]{:S(2)}) copy-start(f32[16,128]{1,0:T(8,128)} %copy-done.14) | copy-start | bytes 24580
  (8 other events, 8.9 us)

commit v7 on v6

--- a/solution.py
+++ b/solution.py
@@ -312,11 +312,11 @@
         step(slice(whole * CHUNK, rows))
 
 
-def copy_body(firsts, skip, *refs):
+def copy_body(places, skip, *refs):
     sources, target, sems = refs[skip:-2], refs[-2], refs[-1]
     copies = [
         pltpu.make_async_copy(source.at[0], target.at[index], sems.at[j])
-        for j, (index, source) in enumerate(zip(firsts, sources))
+        for j, (index, source) in enumerate(zip(places, sources))
     ]
     for copy in copies:
         copy.start()
@@ -324,10 +324,9 @@
         copy.wait()
 
 
-def stacked(total, first, shards, *earlier):
+def stacked(total, places, shards, *earlier):
     vmem = pl.BlockSpec(memory_space=pltpu.VMEM)
     anywhere = pl.BlockSpec(memory_space=pl.ANY)
-    places = range(first, first + len(shards))
     return pl.pallas_call(
         functools.partial(copy_body, places, len(earlier)),
         in_specs=[vmem] * len(earlier) + [anywhere] * len(shards),
@@ -479,30 +478,33 @@
     chip, core = index // 2, index % 2
     where = [chip.reshape(1), core.reshape(1)]
     row_blocks = points.shape[0] // RB
-    cuts = (0, row_blocks // 2, row_blocks - row_blocks // 8, row_blocks)
+    small = row_blocks // 8
+    cuts = (0, small, 6 * small, row_blocks)
     runs = (row_blocks,) + tuple(b - a for a, b in zip(cuts[:-1], cuts[1:]))
     own_ids = candidates.T
     end_ids = move(own_ids, INWARD)
-    weights, *pieces = parameter_shard(*parameters, points, [cut * RB for cut in cuts])
-    weights, end_ids = lax.optimization_barrier((weights, end_ids))
-
-    outer = move(weights, INWARD)
+    before = move(points[: small * RB], INWARD)
+    weights, *pieces = parameter_shard(*parameters, points, [cut * RB for cut in cuts[1:]])
+    weights_then, end_ids, before = lax.optimization_barrier((weights, end_ids, before))
+
+    outer = move(weights_then, INWARD)
     across = move(weights, MIDDLE)
     own_shared = move(weights, CORES)
-    moved = [move(after(pieces[0], outer), INWARD)]
+    most = move(after(pieces[0], outer), INWARD)
     far = move(outer, MIDDLE)
-    outer_shared = move(outer, CORES)
-    across_shared = move(across, CORES)
-    moved.append(move(after(pieces[1], moved[0]), INWARD))
-    moved.append(move(after(pieces[2], moved[0], far), INWARD))
-    near = [weights, own_shared, outer, outer_shared, across, across_shared]
+    last = move(after(pieces[1], most), INWARD)
+    moved = [before, most, last]
     pos, order, starts = pair_lists(
         [own_ids, end_ids], runs, held, 8 * held, lax.axis_size("comp"), line_place, where
     )
-    near_weights = stacked(8, 0, [after(near[0], pos, order, starts)] + near[1:])
-    far, near_weights = lax.optimization_barrier((far, near_weights))
-    far_shared = move(far, CORES)
-    all_weights = stacked(8, 6, [far, far_shared], near_weights)
+    near = [after(weights, pos, order, starts), own_shared, outer, across]
+    near_weights = stacked(8, (0, 1, 2, 4), near)
+    far, outer, across, near_weights = lax.optimization_barrier(
+        (far, outer, across, near_weights)
+    )
+    shared = [move(w, CORES) for w in (outer, across, far)]
+    all_weights = stacked(8, (6, 3, 5, 7), [far] + shared, near_weights)
+
     rows = [points] + moved
     results = []
     for j, run_rows in enumerate(rows):

time: 242 us -> 238 us (0.983)
  waiting for transfers between devices: 106 us -> 103 us
    ppermute x19, waiting for transfers between devices: 106 us -> 103 us  [move(): return lax.ppermute(value, 'dp', pairs)]
    unnamed x42 -> x34, local copies, waits for them, and re-layouts: 11.3 us -> 9.86 us
  transfers between devices with their start and end apart: 19 -> 19, of which waited for: 6 -> 5; matrix products, arithmetic and copies ran while one was open for 0% -> 0% of each run, Pallas kernels for 28% -> 28%
where the time goes in v7:
time: 238 us; the launch traced here: 236 us
  waiting for transfers between devices  103 us (43%)
  Pallas kernels  81.3 us (34%)
  starting transfers between devices  39.5 us (17%)
  local copies, waits for them, and re-layouts  11.6 us (5%)
    ppermute x19, waiting for transfers between devices, move(): return lax.ppermute(value, 'dp', pairs)  103 us
    ppermute x19, starting transfers between devices, move(): return lax.ppermute(value, 'dp', pairs)  39.5 us
    pallas_call x8, Pallas kernels, moments(): pl.pallas_call(functools.partial(moment_body, tuple(shards), held, runs),...  30.6 us
    pallas_call x4, Pallas kernels, responsibilities(): pl.pallas_call(functools.partial(density_body, first, count, held), in_sp...  26.5 us
    unnamed x34, local copies, waits for them, and re-layouts  9.86 us
    pallas_call x1, Pallas kernels, pair_lists(): pl.pallas_call(functools.partial(list_body, tuple(runs), held, owners, pl...  5.52 us
    pallas_call x1, Pallas kernels, parameter_shard(): pl.pallas_call(functools.partial(shard_body, cuts), in_specs=[hbm, hbm, v...  5.49 us
  transfers between devices with their start and end apart: 19, of which 5 were waited for; matrix products, arithmetic and copies ran while one was open for 0% of the time, Pallas kernels for 28%

profile of v7, /device:TPU:0, one launch (start us, length us, event | category | flops | bytes accessed | tf_op | source)
XLA Modules:
  0.0 236.3 jit_solution(8050731682116776148)
XLA Ops:
  1.7 5.0 %collective-permute-start.1 = (bf16[256,768]{1,0:T(8,128)(2,1)S(1)}, bf16[256,768]{1,0:T(8,128)(2,1)S(1)}, u32[]{:S(2)}, u32[]{:S(2)}) collective-permute-start(bf16[256,768]{1,0:T(8,128)(2,1)S(1)} %slice.3), channel_id=1, source_target_pairs={{0,8},{4,12},{24,16},{28,20},{1,9},{5,13},{25,17},{29,21},{2,10},{... | collective-permute-start | bytes 1179656 | tf_op jit(solution)/shard_map/ppermute | solution.py:462
  8.6 5.5 %parameter_shard.1 = (bf16[1,2,528,768]{3,2,1,0:T(8,128)(2,1)}, bf16[1280,768]{1,0:T(8,128)(2,1)}, bf16[512,768]{1,0:T(8,128)(2,1)}) custom-call(bf16[512,768]{1,0:T(8,128)(2,1)} %means_hbm.1, bf16[512,768]{1,0:T(8,128)(2,1)} %inv_hbm.1, bf16[1,512]{1,0:T(2,128)(2,1)S(1)} %reshape.32.log_ref, bf16[2048,768]{1,0:T(8,128)(2,1)} %rest_0_.15), custom_call_target="tpu_custom_call" | custom-call | flops 15728640 | bytes 3145728 | tf_op jit(solution)/shard_map/parameter_shard/pallas_call | solution.py:78
  15.0 5.6 %collective-permute-start.2 = (bf16[1,2,528,768]{3,2,1,0:T(8,128)(2,1)}, bf16[1,2,528,768]{3,2,1,0:T(8,128)(2,1)}, u32[]{:S(2)}, u32[]{:S(2)}) collective-permute-start(bf16[1,2,528,768]{3,2,1,0:T(8,128)(2,1)} %get-tuple-element.49.refs_0_), channel_id=1, source_target_pairs={{0,8},{4,12},{24,16},{28,20},{1,9},{5,13},{25,17},{29,21},{2,10},{... | collective-permute-start | bytes 4866056 | tf_op jit(solution)/shard_map/ppermute | solution.py:462
  20.6 1.8 collective-permute-start.5
  22.4 1.8 collective-permute-start.4
  24.2 29.3 %collective-permute-done.2.refs_2_ = bf16[1,2,528,768]{3,2,1,0:T(8,128)(2,1)} collective-permute-done((bf16[1,2,528,768]{3,2,1,0:T(8,128)(2,1)}, bf16[1,2,528,768]{3,2,1,0:T(8,128)(2,1)}, u32[]{:S(2)}, u32[]{:S(2)}) %collective-permute-start.2) | collective-permute-done | bytes 1622048 | tf_op jit(solution)/shard_map/ppermute | solution.py:462
  53.5 1.9 collective-permute-start.3
  55.4 6.1 %collective-permute-start.9 = (bf16[1280,768]{1,0:T(8,128)(2,1)}, bf16[1280,768]{1,0:T(8,128)(2,1)S(1)}, u32[]{:S(2)}, u32[]{:S(2)}) collective-permute-start(bf16[1280,768]{1,0:T(8,128)(2,1)} %get-tuple-element.60), channel_id=1, source_target_pairs={{0,8},{4,12},{24,16},{28,20},{1,9},{5,13},{25,17},{29,21},{2,10},{... | collective-permute-start | bytes 5898248 | tf_op jit(solution)/shard_map/ppermute | solution.py:462
  61.5 5.5 %pair_lists.1 = (s32[128]{0:T(128)S(1)}, s32[128]{0:T(128)S(1)}, s32[129]{0:T(256)S(1)}) custom-call(s32[1]{0:T(128)} %bitcast.1.rest_0_, s32[1]{0:T(128)} %bitcast.2.rest_1_, s32[4,16]{1,0:T(4,128)S(1)} %bitcast.7, s32[4,16]{1,0:T(4,128)S(1)} %collective-permute-done.rest_3_), custom_call_target="tpu_custom_call" | custom-call | tf_op jit(solution)/shard_map/pair_lists/pallas_call | solution.py:209
  67.1 2.9 %stack_shards.2.refs_0_ = bf16[8,2,528,768]{3,2,1,0:T(8,128)(2,1)S(1)} custom-call(bf16[1,2,528,768]{3,2,1,0:T(8,128)(2,1)} %get-tuple-element.49.refs_0_, bf16[1,2,528,768]{3,2,1,0:T(8,128)(2,1)} %collective-permute-done.5.refs_1_, bf16[1,2,528,768]{3,2,1,0:T(8,128)(2,1)} %collective-permute-done.2.refs_2_, ...), custom_call_target="tpu_custom_call" | custom-call | tf_op jit(solution)/shard_map/stack_shards/pallas_call | solution.py:330
  72.4 29.3 %collective-permute-done.9.x_ref.rest_2_ = bf16[1280,768]{1,0:T(8,128)(2,1)S(1)} collective-permute-done((bf16[1280,768]{1,0:T(8,128)(2,1)}, bf16[1280,768]{1,0:T(8,128)(2,1)S(1)}, u32[]{:S(2)}, u32[]{:S(2)}) %collective-permute-start.9) | collective-permute-done | bytes 1966112 | tf_op jit(solution)/shard_map/ppermute | solution.py:462
  103.0 4.3 %collective-permute-start.10 = (bf16[512,768]{1,0:T(8,128)(2,1)}, bf16[512,768]{1,0:T(8,128)(2,1)S(1)}, u32[]{:S(2)}, u32[]{:S(2)}) collective-permute-start(bf16[512,768]{1,0:T(8,128)(2,1)} %get-tuple-element.64), channel_id=1, source_target_pairs={{0,8},{4,12},{24,16},{28,20},{1,9},{5,13},{25,17},{29,21},{2,10},{... | collective-permute-start | bytes 2359304 | tf_op jit(solution)/shard_map/ppermute | solution.py:462
  107.4 1.6 stack_shards.3.weight_ref
  109.7 12.8 %responsibilities.4 = (bf16[16,4,128,128]{3,2,1,0:T(8,128)(2,1)S(1)}, f32[16,128]{1,0:T(8,128)S(1)}) custom-call(s32[128]{0:T(128)S(1)} %get-tuple-element.62.pos_ref, bf16[2048,768]{1,0:T(8,128)(2,1)S(1)} %copy-done, bf16[8,2,528,768]{3,2,1,0:T(8,128)(2,1)S(1)} %stack_shards.3.weight_ref), custom_call_target="tpu_custom_call" | custom-call | flops 3221225472 | bytes 28311552 | tf_op jit(solution)/shard_map/responsibilities/pallas_call | solution.py:143
  122.5 2.1 responsibilities.5
  124.8 8.1 %responsibilities.6 = (bf16[10,4,128,128]{3,2,1,0:T(8,128)(2,1)S(1)}, f32[10,128]{1,0:T(8,128)S(1)}) custom-call(s32[128]{0:T(128)S(1)} %get-tuple-element.62.pos_ref, bf16[1280,768]{1,0:T(8,128)(2,1)S(1)} %copy-done.2, bf16[8,2,528,768]{3,2,1,0:T(8,128)(2,1)S(1)} %stack_shards.3.weight_ref), custom_call_target="tpu_custom_call" | custom-call | flops 2013265920 | bytes 17694720 | tf_op jit(solution)/shard_map/responsibilities/pallas_call | solution.py:143
  133.0 3.6 %responsibilities.7 = (bf16[4,4,128,128]{3,2,1,0:T(8,128)(2,1)S(1)}, f32[4,128]{1,0:T(4,128)S(1)}) custom-call(s32[128]{0:T(128)S(1)} %get-tuple-element.62.pos_ref, bf16[512,768]{1,0:T(8,128)(2,1)S(1)} %collective-permute-done.10.x_ref.rest_3_, bf16[8,2,528,768]{3,2,1,0:T(8,128)(2,1)S(1)} %stack_shards.3.weight_ref), custom_call_target="tpu_custom_call" | custom-call | flops 805306368 | bytes 7077888 | tf_op jit(solution)/shard_map/responsibilities/pallas_call | solution.py:143
  136.6 2.8 %moments.8 = bf16[1040,768]{1,0:T(8,128)(2,1)S(1)} custom-call(s32[128]{0:T(128)S(1)} %get-tuple-element.77.order_ref, s32[129]{0:T(256)S(1)} %get-tuple-element.48.start_ref, bf16[2048,768]{1,0:T(8,128)(2,1)S(1)} %copy-done, bf16[256,768]{1,0:T(8,128)(2,1)S(1)} %collective-permute-done.1.x_ref.rest_1_, bf16[1280,768]{1,0:T(8,128)(2,1)S(1)} %copy-done.2, ...), custom_call_target="tpu_custom_call" | custom-call | flops 805306368 | bytes 3670016 | tf_op jit(solution)/shard_map/moments/pallas_call | solution.py:282
  140.1 2.2 moments.9.refs_0_
  142.8 3.1 %moments.10 = bf16[1040,768]{1,0:T(8,128)(2,1)S(1)} custom-call(s32[128]{0:T(128)S(1)} %get-tuple-element.77.order_ref, s32[129]{0:T(256)S(1)} %get-tuple-element.48.start_ref, bf16[2048,768]{1,0:T(8,128)(2,1)S(1)} %copy-done, bf16[256,768]{1,0:T(8,128)(2,1)S(1)} %collective-permute-done.1.x_ref.rest_1_, bf16[1280,768]{1,0:T(8,128)(2,1)S(1)} %copy-done.2, ...), custom_call_target="tpu_custom_call" | custom-call | flops 805306368 | bytes 3670016 | tf_op jit(solution)/shard_map/moments/pallas_call | solution.py:282
  147.6 2.5 %moments.11.refs_0_ = bf16[1040,768]{1,0:T(8,128)(2,1)S(1)} custom-call(s32[128]{0:T(128)S(1)} %get-tuple-element.77.order_ref, s32[129]{0:T(256)S(1)} %get-tuple-element.48.start_ref, bf16[2048,768]{1,0:T(8,128)(2,1)S(1)} %copy-done, bf16[256,768]{1,0:T(8,128)(2,1)S(1)} %collective-permute-done.1.x_ref.rest_1_, bf16[1280,768]{1,0:T(8,128)(2,1)S(1)} %copy-done.2, ...), custom_call_target="tpu_custom_call" | custom-call | flops 805306368 | bytes 3670016 | tf_op jit(solution)/shard_map/moments/pallas_call | solution.py:282
  150.1 1.7 add_sums.4
  151.8 2.2 moments.12
  156.1 1.8 collective-permute-start.18
  158.0 3.7 %moments.13 = bf16[1040,768]{1,0:T(8,128)(2,1)} custom-call(s32[128]{0:T(128)S(1)} %get-tuple-element.77.order_ref, s32[129]{0:T(256)S(1)} %get-tuple-element.48.start_ref, bf16[2048,768]{1,0:T(8,128)(2,1)S(1)} %copy-done, bf16[256,768]{1,0:T(8,128)(2,1)S(1)} %collective-permute-done.1.x_ref.rest_1_, bf16[1280,768]{1,0:T(8,128)(2,1)S(1)} %copy-done.2, ...), custom_call_target="tpu_custom_call" | custom-call | flops 805306368 | bytes 3670016 | tf_op jit(solution)/shard_map/moments/pallas_call | solution.py:282
  161.6 1.8 collective-permute-start.17
  163.5 9.4 %collective-permute-done.12.refs_1_ = f32[16,128]{1,0:T(8,128)S(1)} collective-permute-done((f32[16,128]{1,0:T(8,128)S(1)}, f32[16,128]{1,0:T(8,128)S(1)}, u32[]{:S(2)}, u32[]{:S(2)}) %collective-permute-start.12) | collective-permute-done | bytes 8224 | tf_op jit(solution)/shard_map/ppermute | solution.py:462
  172.9 11.7 %moments.14.refs_0_ = bf16[1040,768]{1,0:T(8,128)(2,1)S(1)} custom-call(s32[128]{0:T(128)S(1)} %get-tuple-element.77.order_ref, s32[129]{0:T(256)S(1)} %get-tuple-element.48.start_ref, bf16[2048,768]{1,0:T(8,128)(2,1)S(1)} %copy-done, bf16[256,768]{1,0:T(8,128)(2,1)S(1)} %collective-permute-done.1.x_ref.rest_1_, bf16[1280,768]{1,0:T(8,128)(2,1)S(1)} %copy-done.2, ...), custom_call_target="tpu_custom_call" | custom-call | flops 805306368 | bytes 3670016 | tf_op jit(solution)/shard_map/moments/pallas_call | solution.py:282
  184.6 1.8 add_sums.5
  195.4 2.5 %moments.15.refs_3_ = bf16[1040,768]{1,0:T(8,128)(2,1)S(1)} custom-call(s32[128]{0:T(128)S(1)} %get-tuple-element.77.order_ref, s32[129]{0:T(256)S(1)} %get-tuple-element.48.start_ref, bf16[2048,768]{1,0:T(8,128)(2,1)S(1)} %copy-done, bf16[256,768]{1,0:T(8,128)(2,1)S(1)} %collective-permute-done.1.x_ref.rest_1_, bf16[1280,768]{1,0:T(8,128)(2,1)S(1)} %copy-done.3, ...), custom_call_target="tpu_custom_call" | custom-call | flops 805306368 | bytes 3670016 | tf_op jit(solution)/shard_map/moments/pallas_call | solution.py:282
  197.9 33.6 %collective-permute-done.16.refs_2_ = bf16[1040,768]{1,0:T(8,128)(2,1)} collective-permute-done((bf16[1040,768]{1,0:T(8,128)(2,1)}, bf16[1040,768]{1,0:T(8,128)(2,1)}, u32[]{:S(2)}, u32[]{:S(2)}) %collective-permute-start.16) | collective-permute-done | bytes 1597472 | tf_op jit(solution)/shard_map/ppermute | solution.py:462
  231.5 4.6 %results.1 = (f32[1,512]{1,0:T(1,128)}, f32[512,768]{1,0:T(8,128)}, f32[512,768]{1,0:T(8,128)}, f32[16,128]{1,0:T(8,128)}) custom-call(s32[1]{0:T(128)} %bitcast.end_ref, f32[16,128]{1,0:T(8,128)S(1)} %get-tuple-element.54.refs_0_, f32[16,128]{1,0:T(8,128)S(1)} %copy-done.15, bf16[1040,768]{1,0:T(8,128)(2,1)} %collective-permute-done.16.refs_2_, ...), custom_call_target="tpu_custom_call" | custom-call | tf_op jit(solution)/shard_map/results/pallas_call | solution.py:405
  (63 shorter events, 22.3 us)
Async XLA Ops:
  1.7 13.3 %collective-permute-start.1 = (bf16[256,768]{1,0:T(8,128)(2,1)S(1)}, bf16[256,768]{1,0:T(8,128)(2,1)S(1)}, u32[]{:S(2)}, u32[]{:S(2)}) collective-permute-start(bf16[256,768]{1,0:T(8,128)(2,1)S(1)} %slice.3), channel_id=1, source_target_pairs={{0,8},{4,12},{24,16},{28,20},{1,9},{5,13},{25,17},{29,21},{2,10},{... | collective-permute-start | bytes 1179656 | tf_op jit(solution)/shard_map/ppermute | solution.py:462
  6.6 8.4 %collective-permute-start = (s32[4,16]{1,0:T(4,128)}, s32[4,16]{1,0:T(4,128)S(1)}, u32[]{:S(2)}, u32[]{:S(2)}) collective-permute-start(s32[4,16]{1,0:T(4,128)} %bitcast.6), channel_id=1, source_target_pairs={{0,8},{4,12},{24,16},{28,20},{1,9},{5,13},{25,17},{29,21},{2,10},{... | collective-permute-start | bytes 776 | tf_op jit(solution)/shard_map/ppermute | solution.py:462
  8.6 52.9 %copy-start.16 = (s32[16,4]{0,1:T(4,128)S(1)}, s32[16,4]{0,1:T(4,128)}, u32[]{:S(2)}) copy-start(s32[16,4]{0,1:T(4,128)} %param.6) | copy-start | bytes 772
  15.0 38.5 %collective-permute-start.2 = (bf16[1,2,528,768]{3,2,1,0:T(8,128)(2,1)}, bf16[1,2,528,768]{3,2,1,0:T(8,128)(2,1)}, u32[]{:S(2)}, u32[]{:S(2)}) collective-permute-start(bf16[1,2,528,768]{3,2,1,0:T(8,128)(2,1)} %get-tuple-element.49.refs_0_), channel_id=1, source_target_pairs={{0,8},{4,12},{24,16},{28,20},{1,9},{5,13},{25,17},{29,21},{2,10},{... | collective-permute-start | bytes 4866056 | tf_op jit(solution)/shard_map/ppermute | solution.py:462
  20.6 46.5 %collective-permute-start.5 = (bf16[1,2,528,768]{3,2,1,0:T(8,128)(2,1)}, bf16[1,2,528,768]{3,2,1,0:T(8,128)(2,1)}, u32[]{:S(2)}, u32[]{:S(2)}) collective-permute-start(bf16[1,2,528,768]{3,2,1,0:T(8,128)(2,1)} %get-tuple-element.49.refs_0_), channel_id=1, source_target_pairs={{8,12},{12,8},{16,20},{20,16},{9,13},{13,9},{17,21},{21,17},{10,14... | collective-permute-start | bytes 4866056 | tf_op jit(solution)/shard_map/ppermute | solution.py:462
  22.4 44.7 %collective-permute-start.4 = (bf16[1,2,528,768]{3,2,1,0:T(8,128)(2,1)}, bf16[1,2,528,768]{3,2,1,0:T(8,128)(2,1)}, u32[]{:S(2)}, u32[]{:S(2)}) collective-permute-start(bf16[1,2,528,768]{3,2,1,0:T(8,128)(2,1)} %get-tuple-element.49.refs_0_), channel_id=1, source_target_pairs={{8,16},{12,20},{16,8},{20,12},{9,17},{13,21},{17,9},{21,13},{10,18... | collective-permute-start | bytes 4866056 | tf_op jit(solution)/shard_map/ppermute | solution.py:462
  53.5 16.5 %collective-permute-start.3 = (bf16[1,2,528,768]{3,2,1,0:T(8,128)(2,1)}, bf16[1,2,528,768]{3,2,1,0:T(8,128)(2,1)}, u32[]{:S(2)}, u32[]{:S(2)}) collective-permute-start(bf16[1,2,528,768]{3,2,1,0:T(8,128)(2,1)} %collective-permute-done.2.refs_2_), channel_id=1, source_target_pairs={{8,16},{12,20},{16,8},{20,12},{9,17},{13,21},{17,9},{21,13},{10,18... | collective-permute-start | bytes 4866056 | tf_op jit(solution)/shard_map/ppermute | solution.py:462
  55.4 46.3 %collective-permute-start.9 = (bf16[1280,768]{1,0:T(8,128)(2,1)}, bf16[1280,768]{1,0:T(8,128)(2,1)S(1)}, u32[]{:S(2)}, u32[]{:S(2)}) collective-permute-start(bf16[1280,768]{1,0:T(8,128)(2,1)} %get-tuple-element.60), channel_id=1, source_target_pairs={{0,8},{4,12},{24,16},{28,20},{1,9},{5,13},{25,17},{29,21},{2,10},{... | collective-permute-start | bytes 5898248 | tf_op jit(solution)/shard_map/ppermute | solution.py:462
  70.0 37.3 %collective-permute-start.6 = (bf16[1,2,528,768]{3,2,1,0:T(8,128)(2,1)}, bf16[1,2,528,768]{3,2,1,0:T(8,128)(2,1)S(1)}, u32[]{:S(2)}, u32[]{:S(2)}) collective-permute-start(bf16[1,2,528,768]{3,2,1,0:T(8,128)(2,1)} %collective-permute-done.2.refs_2_), channel_id=1, source_target_pairs={{8,12},{12,8},{16,20},{20,16},{9,13},{13,9},{17,21},{21,17},{10,14... | collective-permute-start | bytes 4866056 | tf_op jit(solution)/shard_map/ppermute | solution.py:462
  70.8 36.5 %collective-permute-start.7 = (bf16[1,2,528,768]{3,2,1,0:T(8,128)(2,1)}, bf16[1,2,528,768]{3,2,1,0:T(8,128)(2,1)S(1)}, u32[]{:S(2)}, u32[]{:S(2)}) collective-permute-start(bf16[1,2,528,768]{3,2,1,0:T(8,128)(2,1)} %collective-permute-done.4.refs_3_), channel_id=1, source_target_pairs={{8,12},{12,8},{16,20},{20,16},{9,13},{13,9},{17,21},{21,17},{10,14... | collective-permute-start | bytes 4866056 | tf_op jit(solution)/shard_map/ppermute | solution.py:462
  71.6 35.8 %collective-permute-start.8 = (bf16[1,2,528,768]{3,2,1,0:T(8,128)(2,1)}, bf16[1,2,528,768]{3,2,1,0:T(8,128)(2,1)S(1)}, u32[]{:S(2)}, u32[]{:S(2)}) collective-permute-start(bf16[1,2,528,768]{3,2,1,0:T(8,128)(2,1)} %collective-permute-done.3.refs_1_), channel_id=1, source_target_pairs={{8,12},{12,8},{16,20},{20,16},{9,13},{13,9},{17,21},{21,17},{10,14... | collective-permute-start | bytes 4866056 | tf_op jit(solution)/shard_map/ppermute | solution.py:462
  103.0 30.0 %collective-permute-start.10 = (bf16[512,768]{1,0:T(8,128)(2,1)}, bf16[512,768]{1,0:T(8,128)(2,1)S(1)}, u32[]{:S(2)}, u32[]{:S(2)}) collective-permute-start(bf16[512,768]{1,0:T(8,128)(2,1)} %get-tuple-element.64), channel_id=1, source_target_pairs={{0,8},{4,12},{24,16},{28,20},{1,9},{5,13},{25,17},{29,21},{2,10},{... | collective-permute-start | bytes 2359304 | tf_op jit(solution)/shard_map/ppermute | solution.py:462
  107.3 2.4 %copy-start = (bf16[2048,768]{1,0:T(8,128)(2,1)S(1)}, bf16[2048,768]{1,0:T(8,128)(2,1)}, u32[]{:S(2)}) copy-start(bf16[2048,768]{1,0:T(8,128)(2,1)} %rest_0_.15) | copy-start | bytes 9437188
  122.5 50.4 %copy-start.4 = (bf16[16,4,128,128]{3,2,1,0:T(8,128)(2,1)}, bf16[16,4,128,128]{3,2,1,0:T(8,128)(2,1)S(1)}, u32[]{:S(2)}) copy-start(bf16[16,4,128,128]{3,2,1,0:T(8,128)(2,1)S(1)} %get-tuple-element.66.rest_4_) | copy-start | bytes 6291460
  122.5 2.3 copy-start.2
  124.6 48.3 %copy-start.12 = (bf16[2,4,128,128]{3,2,1,0:T(8,128)(2,1)}, bf16[2,4,128,128]{3,2,1,0:T(8,128)(2,1)S(1)}, u32[]{:S(2)}) copy-start(bf16[2,4,128,128]{3,2,1,0:T(8,128)(2,1)S(1)} %get-tuple-element.67.rest_5_) | copy-start | bytes 786436
  133.0 39.9 %copy-start.6 = (bf16[10,4,128,128]{3,2,1,0:T(8,128)(2,1)}, bf16[10,4,128,128]{3,2,1,0:T(8,128)(2,1)S(1)}, u32[]{:S(2)}) copy-start(bf16[10,4,128,128]{3,2,1,0:T(8,128)(2,1)S(1)} %get-tuple-element.68.rest_6_) | copy-start | bytes 3932164
  133.0 39.9 %copy-start.8 = (bf16[512,768]{1,0:T(8,128)(2,1)}, bf16[512,768]{1,0:T(8,128)(2,1)S(1)}, u32[]{:S(2)}) copy-start(bf16[512,768]{1,0:T(8,128)(2,1)S(1)} %collective-permute-done.10.x_ref.rest_3_) | copy-start | bytes 2359300
  136.6 36.4 %copy-start.10 = (bf16[4,4,128,128]{3,2,1,0:T(8,128)(2,1)}, bf16[4,4,128,128]{3,2,1,0:T(8,128)(2,1)S(1)}, u32[]{:S(2)}) copy-start(bf16[4,4,128,128]{3,2,1,0:T(8,128)(2,1)S(1)} %get-tuple-element.69.rest_7_) | copy-start | bytes 1572868
  139.4 3.0 %collective-permute-start.11 = (bf16[1040,768]{1,0:T(8,128)(2,1)S(1)}, bf16[1040,768]{1,0:T(8,128)(2,1)S(1)}, u32[]{:S(2)}, u32[]{:S(2)}) collective-permute-start(bf16[1040,768]{1,0:T(8,128)(2,1)S(1)} %moments.8), channel_id=1, source_target_pairs={{8,12},{12,8},{16,20},{20,16},{9,13},{13,9},{17,21},{21,17},{10,14... | collective-permute-start | bytes 4792328 | tf_op jit(solution)/shard_map/ppermute | solution.py:462
  145.9 4.2 %collective-permute-start.13 = (bf16[1040,768]{1,0:T(8,128)(2,1)S(1)}, bf16[1040,768]{1,0:T(8,128)(2,1)S(1)}, u32[]{:S(2)}, u32[]{:S(2)}) collective-permute-start(bf16[1040,768]{1,0:T(8,128)(2,1)S(1)} %moments.10), channel_id=1, source_target_pairs={{8,12},{12,8},{16,20},{20,16},{9,13},{13,9},{17,21},{21,17},{10,14... | collective-permute-start | bytes 4792328 | tf_op jit(solution)/shard_map/ppermute | solution.py:462
  146.7 38.0 %collective-permute-start.15 = (bf16[1040,768]{1,0:T(8,128)(2,1)S(1)}, bf16[1040,768]{1,0:T(8,128)(2,1)S(1)}, u32[]{:S(2)}, u32[]{:S(2)}) collective-permute-start(bf16[1040,768]{1,0:T(8,128)(2,1)S(1)} %add_sums.3), channel_id=1, source_target_pairs={{8,16},{12,20},{16,8},{20,12},{9,17},{13,21},{17,9},{21,13},{10,18... | collective-permute-start | bytes 4792328 | tf_op jit(solution)/shard_map/ppermute | solution.py:462
  154.0 30.6 %collective-permute-start.14 = (bf16[1040,768]{1,0:T(8,128)(2,1)S(1)}, bf16[1040,768]{1,0:T(8,128)(2,1)S(1)}, u32[]{:S(2)}, u32[]{:S(2)}) collective-permute-start(bf16[1040,768]{1,0:T(8,128)(2,1)S(1)} %moments.12), channel_id=1, source_target_pairs={{8,12},{12,8},{16,20},{20,16},{9,13},{13,9},{17,21},{21,17},{10,14... | collective-permute-start | bytes 4792328 | tf_op jit(solution)/shard_map/ppermute | solution.py:462
  154.8 18.1 %collective-permute-start.12 = (f32[16,128]{1,0:T(8,128)S(1)}, f32[16,128]{1,0:T(8,128)S(1)}, u32[]{:S(2)}, u32[]{:S(2)}) collective-permute-start(f32[16,128]{1,0:T(8,128)S(1)} %join_norms.1), channel_id=1, source_target_pairs={{8,0},{12,4},{16,24},{20,28},{9,1},{13,5},{17,25},{21,29},{10,2},{... | collective-permute-start | bytes 24584 | tf_op jit(solution)/shard_map/ppermute | solution.py:462
  156.1 41.8 %collective-permute-start.18 = (bf16[1040,768]{1,0:T(8,128)(2,1)}, bf16[1040,768]{1,0:T(8,128)(2,1)}, u32[]{:S(2)}, u32[]{:S(2)}) collective-permute-start(bf16[1040,768]{1,0:T(8,128)(2,1)} %add_sums.4), channel_id=1, source_target_pairs={{8,16},{12,20},{16,8},{20,12},{9,17},{13,21},{17,9},{21,13},{10,18... | collective-permute-start | bytes 4792328 | tf_op jit(solution)/shard_map/ppermute | solution.py:462
  161.6 36.2 %collective-permute-start.17 = (bf16[1040,768]{1,0:T(8,128)(2,1)}, bf16[1040,768]{1,0:T(8,128)(2,1)}, u32[]{:S(2)}, u32[]{:S(2)}) collective-permute-start(bf16[1040,768]{1,0:T(8,128)(2,1)} %moments.13), channel_id=1, source_target_pairs={{8,12},{12,8},{16,20},{20,16},{9,13},{13,9},{17,21},{21,17},{10,14... | collective-permute-start | bytes 4792328 | tf_op jit(solution)/shard_map/ppermute | solution.py:462
  172.9 11.7 %copy-start.14 = (f32[16,128]{1,0:T(8,128)}, f32[16,128]{1,0:T(8,128)S(1)}, u32[]{:S(2)}) copy-start(f32[16,128]{1,0:T(8,128)S(1)} %collective-permute-done.12.refs_1_) | copy-start | bytes 24580
  186.5 45.1 %collective-permute-start.16 = (bf16[1040,768]{1,0:T(8,128)(2,1)}, bf16[1040,768]{1,0:T(8,128)(2,1)}, u32[]{:S(2)}, u32[]{:S(2)}) collective-permute-start(bf16[1040,768]{1,0:T(8,128)(2,1)} %add_sums.5), channel_id=1, source_target_pairs={{8,0},{12,4},{16,24},{20,28},{9,1},{13,5},{17,25},{21,29},{10,2},{... | collective-permute-start | bytes 4792328 | tf_op jit(solution)/shard_map/ppermute | solution.py:462
  187.8 1.5 copy-start.3
  189.3 1.6 copy-start.5
  190.9 1.3 copy-start.7
  195.4 36.2 %copy-start.15 = (f32[16,128]{1,0:T(8,128)S(1)}, f32[16,128]{1,0:T(8,128)}, u32[]{:S(2)}) copy-start(f32[16,128]{1,0:T(8,128)} %copy-done.14) | copy-start | bytes 24580
  (4 other events, 4.4 us)

commit v8 on v7

--- a/solution.py
+++ b/solution.py
@@ -106,33 +106,26 @@
     def _(i):
         x = x_ref[pl.ds(pl.multiple_of(i * RB, RB), RB), :]
         half = x * x * -0.5
-        densities = []
+        chosen = []
         for slot in range(CANDS):
             pos = pos_ref[(first + i) * CANDS + slot]
-            shard, start = lax.div(pos, held), lax.rem(pos, held) * CB
-            here = pl.ds(pl.multiple_of(start, CB), CB)
-            linear = lax.dot_general(
-                weight_ref[shard, 0, here, :], x, NT, preferred_element_type=jnp.float32
-            )
-            quadratic = lax.dot_general(
-                weight_ref[shard, 1, here, :], half, NT, preferred_element_type=jnp.float32
-            )
-            constant = lax.dot_general(
-                weight_ref[shard, 0, owned:, here],
-                pieces,
-                TN,
-                preferred_element_type=jnp.float32,
-            )
-            densities.append(linear + quadratic + constant)
-        peak = functools.reduce(
-            jnp.maximum, [jnp.max(d, axis=0, keepdims=True) for d in densities]
+            start = pl.multiple_of(lax.rem(pos, held) * CB, CB)
+            chosen.append((lax.div(pos, held), pl.ds(start, CB)))
+        scaled = jnp.concatenate([weight_ref[shard, 0, here, :] for shard, here in chosen])
+        inverse = jnp.concatenate([weight_ref[shard, 1, here, :] for shard, here in chosen])
+        constants = jnp.concatenate(
+            [weight_ref[shard, 0, owned:, here] for shard, here in chosen], axis=1
         )
-        terms = [jnp.exp(d - peak) for d in densities]
-        total = functools.reduce(jnp.add, [jnp.sum(t, axis=0, keepdims=True) for t in terms])
+        densities = lax.dot_general(scaled, x, NT, preferred_element_type=jnp.float32)
+        densities += lax.dot_general(inverse, half, NT, preferred_element_type=jnp.float32)
+        densities += lax.dot_general(constants, pieces, TN, preferred_element_type=jnp.float32)
+        peak = jnp.max(densities, axis=0, keepdims=True)
+        terms = jnp.exp(densities - peak)
+        total = jnp.sum(terms, axis=0, keepdims=True)
         norm_ref[pl.ds(i, 1), :] = peak + jnp.log(total)
-        inverse_total = 1.0 / total
+        resp = (terms * (1.0 / total)).astype(jnp.bfloat16)
         for slot in range(CANDS):
-            resp_ref[i, slot] = (terms[slot] * inverse_total).astype(jnp.bfloat16)
+            resp_ref[i, slot] = resp[slot * CB : (slot + 1) * CB]
 
 
 def responsibilities(rows, pos, first, weights, held):
@@ -479,11 +472,11 @@
     where = [chip.reshape(1), core.reshape(1)]
     row_blocks = points.shape[0] // RB
     small = row_blocks // 8
-    cuts = (0, small, 6 * small, row_blocks)
+    cuts = (0, 1, 1 + 5 * small, row_blocks)
     runs = (row_blocks,) + tuple(b - a for a, b in zip(cuts[:-1], cuts[1:]))
     own_ids = candidates.T
     end_ids = move(own_ids, INWARD)
-    before = move(points[: small * RB], INWARD)
+    before = move(points[: cuts[1] * RB], INWARD)
     weights, *pieces = parameter_shard(*parameters, points, [cut * RB for cut in cuts[1:]])
     weights_then, end_ids, before = lax.optimization_barrier((weights, end_ids, before))
 

time: 238 us -> 234 us (0.983)
  starting transfers between devices: 39.5 us -> 36.4 us
    ppermute x19, starting transfers between devices: 39.5 us -> 36.4 us  [move(): return lax.ppermute(value, 'dp', pairs)]
    unnamed x34 -> x26, local copies, waits for them, and re-layouts: 9.86 us -> 9.79 us
  transfers between devices with their start and end apart: 19 -> 19, of which waited for: 5 -> 4; matrix products, arithmetic and copies ran while one was open for 0% -> 0% of each run, Pallas kernels for 28% -> 29%
where the time goes in v8:
time: 234 us; the launch traced here: 231 us
  waiting for transfers between devices  102 us (44%)
  Pallas kernels  80 us (34%)
  starting transfers between devices  36.4 us (16%)
  local copies, waits for them, and re-layouts  11.4 us (5%)
    ppermute x19, waiting for transfers between devices, move(): return lax.ppermute(value, 'dp', pairs)  102 us
    ppermute x19, starting transfers between devices, move(): return lax.ppermute(value, 'dp', pairs)  36.4 us
    pallas_call x8, Pallas kernels, moments(): pl.pallas_call(functools.partial(moment_body, tuple(shards), held, runs),...  30.3 us
    pallas_call x4, Pallas kernels, responsibilities(): pl.pallas_call(functools.partial(density_body, first, count, held), in_sp...  25.5 us
    unnamed x26, local copies, waits for them, and re-layouts  9.79 us
    pallas_call x1, Pallas kernels, parameter_shard(): pl.pallas_call(functools.partial(shard_body, cuts), in_specs=[hbm, hbm, v...  5.56 us
    pallas_call x1, Pallas kernels, pair_lists(): pl.pallas_call(functools.partial(list_body, tuple(runs), held, owners, pl...  5.52 us
  transfers between devices with their start and end apart: 19, of which 4 were waited for; matrix products, arithmetic and copies ran while one was open for 0% of the time, Pallas kernels for 29%

profile of v8, /device:TPU:0, one launch (start us, length us, event | category | flops | bytes accessed | tf_op | source)
XLA Modules:
  0.0 231.4 jit_solution(3925057861202775085)
XLA Ops:
  1.6 4.9 %collective-permute-start.1 = (bf16[128,768]{1,0:T(8,128)(2,1)S(1)}, bf16[128,768]{1,0:T(8,128)(2,1)S(1)}, u32[]{:S(2)}, u32[]{:S(2)}) collective-permute-start(bf16[128,768]{1,0:T(8,128)(2,1)S(1)} %slice.3), channel_id=1, source_target_pairs={{0,8},{4,12},{24,16},{28,20},{1,9},{5,13},{25,17},{29,21},{2,10},{... | collective-permute-start | bytes 589832 | tf_op jit(solution)/shard_map/ppermute | solution.py:455
  8.5 5.6 %parameter_shard.1 = (bf16[1,2,528,768]{3,2,1,0:T(8,128)(2,1)}, bf16[1280,768]{1,0:T(8,128)(2,1)}, bf16[640,768]{1,0:T(8,128)(2,1)}) custom-call(bf16[512,768]{1,0:T(8,128)(2,1)} %means_hbm.1, bf16[512,768]{1,0:T(8,128)(2,1)} %inv_hbm.1, bf16[1,512]{1,0:T(2,128)(2,1)S(1)} %reshape.32.log_ref, bf16[2048,768]{1,0:T(8,128)(2,1)} %rest_0_.15), custom_call_target="tpu_custom_call" | custom-call | flops 15728640 | bytes 3145728 | tf_op jit(solution)/shard_map/parameter_shard/pallas_call | solution.py:78
  14.1 2.5 %collective-permute-start.2 = (bf16[1,2,528,768]{3,2,1,0:T(8,128)(2,1)}, bf16[1,2,528,768]{3,2,1,0:T(8,128)(2,1)}, u32[]{:S(2)}, u32[]{:S(2)}) collective-permute-start(bf16[1,2,528,768]{3,2,1,0:T(8,128)(2,1)} %get-tuple-element.49.refs_0_), channel_id=1, source_target_pairs={{0,8},{4,12},{24,16},{28,20},{1,9},{5,13},{25,17},{29,21},{2,10},{... | collective-permute-start | bytes 4866056 | tf_op jit(solution)/shard_map/ppermute | solution.py:455
  16.6 1.8 collective-permute-start.5
  18.4 1.8 collective-permute-start.4
  20.2 30.2 %collective-permute-done.2.refs_2_ = bf16[1,2,528,768]{3,2,1,0:T(8,128)(2,1)} collective-permute-done((bf16[1,2,528,768]{3,2,1,0:T(8,128)(2,1)}, bf16[1,2,528,768]{3,2,1,0:T(8,128)(2,1)}, u32[]{:S(2)}, u32[]{:S(2)}) %collective-permute-start.2) | collective-permute-done | bytes 1622048 | tf_op jit(solution)/shard_map/ppermute | solution.py:455
  50.4 1.9 collective-permute-start.3
  52.3 6.1 %collective-permute-start.9 = (bf16[1280,768]{1,0:T(8,128)(2,1)}, bf16[1280,768]{1,0:T(8,128)(2,1)S(1)}, u32[]{:S(2)}, u32[]{:S(2)}) collective-permute-start(bf16[1280,768]{1,0:T(8,128)(2,1)} %get-tuple-element.60), channel_id=1, source_target_pairs={{0,8},{4,12},{24,16},{28,20},{1,9},{5,13},{25,17},{29,21},{2,10},{... | collective-permute-start | bytes 5898248 | tf_op jit(solution)/shard_map/ppermute | solution.py:455
  58.4 5.5 %pair_lists.1 = (s32[128]{0:T(128)S(1)}, s32[128]{0:T(128)S(1)}, s32[129]{0:T(256)S(1)}) custom-call(s32[1]{0:T(128)} %bitcast.1.rest_0_, s32[1]{0:T(128)} %bitcast.2.rest_1_, s32[4,16]{1,0:T(4,128)S(1)} %bitcast.7, s32[4,16]{1,0:T(4,128)S(1)} %collective-permute-done.rest_3_), custom_call_target="tpu_custom_call" | custom-call | tf_op jit(solution)/shard_map/pair_lists/pallas_call | solution.py:202
  64.0 2.9 %stack_shards.2.refs_0_ = bf16[8,2,528,768]{3,2,1,0:T(8,128)(2,1)S(1)} custom-call(bf16[1,2,528,768]{3,2,1,0:T(8,128)(2,1)} %get-tuple-element.49.refs_0_, bf16[1,2,528,768]{3,2,1,0:T(8,128)(2,1)} %collective-permute-done.5.refs_1_, bf16[1,2,528,768]{3,2,1,0:T(8,128)(2,1)} %collective-permute-done.2.refs_2_, ...), custom_call_target="tpu_custom_call" | custom-call | tf_op jit(solution)/shard_map/stack_shards/pallas_call | solution.py:323
  69.2 30.3 %collective-permute-done.9.x_ref.rest_2_ = bf16[1280,768]{1,0:T(8,128)(2,1)S(1)} collective-permute-done((bf16[1280,768]{1,0:T(8,128)(2,1)}, bf16[1280,768]{1,0:T(8,128)(2,1)S(1)}, u32[]{:S(2)}, u32[]{:S(2)}) %collective-permute-start.9) | collective-permute-done | bytes 1966112 | tf_op jit(solution)/shard_map/ppermute | solution.py:455
  100.8 4.3 %collective-permute-start.10 = (bf16[640,768]{1,0:T(8,128)(2,1)}, bf16[640,768]{1,0:T(8,128)(2,1)S(1)}, u32[]{:S(2)}, u32[]{:S(2)}) collective-permute-start(bf16[640,768]{1,0:T(8,128)(2,1)} %get-tuple-element.64), channel_id=1, source_target_pairs={{0,8},{4,12},{24,16},{28,20},{1,9},{5,13},{25,17},{29,21},{2,10},{... | collective-permute-start | bytes 2949128 | tf_op jit(solution)/shard_map/ppermute | solution.py:455
  105.1 1.6 stack_shards.3.weight_ref
  107.5 12.2 %responsibilities.4 = (bf16[16,4,128,128]{3,2,1,0:T(8,128)(2,1)S(1)}, f32[16,128]{1,0:T(8,128)S(1)}) custom-call(s32[128]{0:T(128)S(1)} %get-tuple-element.62.pos_ref, bf16[2048,768]{1,0:T(8,128)(2,1)S(1)} %copy-done, bf16[8,2,528,768]{3,2,1,0:T(8,128)(2,1)S(1)} %stack_shards.3.weight_ref), custom_call_target="tpu_custom_call" | custom-call | flops 3221225472 | bytes 28311552 | tf_op jit(solution)/shard_map/responsibilities/pallas_call | solution.py:136
  122.0 7.8 %responsibilities.6 = (bf16[10,4,128,128]{3,2,1,0:T(8,128)(2,1)S(1)}, f32[10,128]{1,0:T(8,128)S(1)}) custom-call(s32[128]{0:T(128)S(1)} %get-tuple-element.62.pos_ref, bf16[1280,768]{1,0:T(8,128)(2,1)S(1)} %copy-done.2, bf16[8,2,528,768]{3,2,1,0:T(8,128)(2,1)S(1)} %stack_shards.3.weight_ref), custom_call_target="tpu_custom_call" | custom-call | flops 2013265920 | bytes 17694720 | tf_op jit(solution)/shard_map/responsibilities/pallas_call | solution.py:136
  129.9 4.2 %responsibilities.7 = (bf16[5,4,128,128]{3,2,1,0:T(8,128)(2,1)S(1)}, f32[5,128]{1,0:T(8,128)S(1)}) custom-call(s32[128]{0:T(128)S(1)} %get-tuple-element.62.pos_ref, bf16[640,768]{1,0:T(8,128)(2,1)S(1)} %collective-permute-done.10.x_ref.rest_3_, bf16[8,2,528,768]{3,2,1,0:T(8,128)(2,1)S(1)} %stack_shards.3.weight_ref), custom_call_target="tpu_custom_call" | custom-call | flops 1006632960 | bytes 8847360 | tf_op jit(solution)/shard_map/responsibilities/pallas_call | solution.py:136
  134.1 2.2 moments.8
  137.1 2.8 %moments.9.refs_0_ = bf16[1040,768]{1,0:T(8,128)(2,1)S(1)} custom-call(s32[128]{0:T(128)S(1)} %get-tuple-element.77.order_ref, s32[129]{0:T(256)S(1)} %get-tuple-element.48.start_ref, bf16[2048,768]{1,0:T(8,128)(2,1)S(1)} %copy-done, bf16[128,768]{1,0:T(8,128)(2,1)S(1)} %collective-permute-done.1.x_ref.rest_1_, bf16[1280,768]{1,0:T(8,128)(2,1)S(1)} %copy-done.2, ...), custom_call_target="tpu_custom_call" | custom-call | flops 805306368 | bytes 3670016 | tf_op jit(solution)/shard_map/moments/pallas_call | solution.py:275
  140.3 2.5 %moments.10 = bf16[1040,768]{1,0:T(8,128)(2,1)S(1)} custom-call(s32[128]{0:T(128)S(1)} %get-tuple-element.77.order_ref, s32[129]{0:T(256)S(1)} %get-tuple-element.48.start_ref, bf16[2048,768]{1,0:T(8,128)(2,1)S(1)} %copy-done, bf16[128,768]{1,0:T(8,128)(2,1)S(1)} %collective-permute-done.1.x_ref.rest_1_, bf16[1280,768]{1,0:T(8,128)(2,1)S(1)} %copy-done.2, ...), custom_call_target="tpu_custom_call" | custom-call | flops 805306368 | bytes 3670016 | tf_op jit(solution)/shard_map/moments/pallas_call | solution.py:275
  144.4 2.8 %moments.11.refs_0_ = bf16[1040,768]{1,0:T(8,128)(2,1)S(1)} custom-call(s32[128]{0:T(128)S(1)} %get-tuple-element.77.order_ref, s32[129]{0:T(256)S(1)} %get-tuple-element.48.start_ref, bf16[2048,768]{1,0:T(8,128)(2,1)S(1)} %copy-done, bf16[128,768]{1,0:T(8,128)(2,1)S(1)} %collective-permute-done.1.x_ref.rest_1_, bf16[1280,768]{1,0:T(8,128)(2,1)S(1)} %copy-done.2, ...), custom_call_target="tpu_custom_call" | custom-call | flops 805306368 | bytes 3670016 | tf_op jit(solution)/shard_map/moments/pallas_call | solution.py:275
  147.2 1.7 add_sums.4
  148.8 2.5 %moments.12 = bf16[1040,768]{1,0:T(8,128)(2,1)S(1)} custom-call(s32[128]{0:T(128)S(1)} %get-tuple-element.77.order_ref, s32[129]{0:T(256)S(1)} %get-tuple-element.48.start_ref, bf16[2048,768]{1,0:T(8,128)(2,1)S(1)} %copy-done, bf16[128,768]{1,0:T(8,128)(2,1)S(1)} %collective-permute-done.1.x_ref.rest_1_, bf16[1280,768]{1,0:T(8,128)(2,1)S(1)} %copy-done.2, ...), custom_call_target="tpu_custom_call" | custom-call | flops 805306368 | bytes 3670016 | tf_op jit(solution)/shard_map/moments/pallas_call | solution.py:275
  153.6 1.8 collective-permute-start.18
  155.4 3.7 %moments.13 = bf16[1040,768]{1,0:T(8,128)(2,1)} custom-call(s32[128]{0:T(128)S(1)} %get-tuple-element.77.order_ref, s32[129]{0:T(256)S(1)} %get-tuple-element.48.start_ref, bf16[2048,768]{1,0:T(8,128)(2,1)S(1)} %copy-done, bf16[128,768]{1,0:T(8,128)(2,1)S(1)} %collective-permute-done.1.x_ref.rest_1_, bf16[1280,768]{1,0:T(8,128)(2,1)S(1)} %copy-done.2, ...), custom_call_target="tpu_custom_call" | custom-call | flops 805306368 | bytes 3670016 | tf_op jit(solution)/shard_map/moments/pallas_call | solution.py:275
  159.1 1.8 collective-permute-start.17
  160.9 7.9 %collective-permute-done.12.refs_1_ = f32[16,128]{1,0:T(8,128)S(1)} collective-permute-done((f32[16,128]{1,0:T(8,128)S(1)}, f32[16,128]{1,0:T(8,128)S(1)}, u32[]{:S(2)}, u32[]{:S(2)}) %collective-permute-start.12) | collective-permute-done | bytes 8224 | tf_op jit(solution)/shard_map/ppermute | solution.py:455
  168.8 12.2 %moments.14.refs_0_ = bf16[1040,768]{1,0:T(8,128)(2,1)S(1)} custom-call(s32[128]{0:T(128)S(1)} %get-tuple-element.77.order_ref, s32[129]{0:T(256)S(1)} %get-tuple-element.48.start_ref, bf16[2048,768]{1,0:T(8,128)(2,1)S(1)} %copy-done, bf16[128,768]{1,0:T(8,128)(2,1)S(1)} %collective-permute-done.1.x_ref.rest_1_, bf16[1280,768]{1,0:T(8,128)(2,1)S(1)} %copy-done.2, ...), custom_call_target="tpu_custom_call" | custom-call | flops 805306368 | bytes 3670016 | tf_op jit(solution)/shard_map/moments/pallas_call | solution.py:275
  181.1 1.8 add_sums.5
  185.7 1.6 copy-done.5
  190.9 1.7 moments.15.refs_3_
  192.6 34.1 %collective-permute-done.16.refs_2_ = bf16[1040,768]{1,0:T(8,128)(2,1)} collective-permute-done((bf16[1040,768]{1,0:T(8,128)(2,1)}, bf16[1040,768]{1,0:T(8,128)(2,1)}, u32[]{:S(2)}, u32[]{:S(2)}) %collective-permute-start.16) | collective-permute-done | bytes 1597472 | tf_op jit(solution)/shard_map/ppermute | solution.py:455
  226.7 4.6 %results.1 = (f32[1,512]{1,0:T(1,128)}, f32[512,768]{1,0:T(8,128)}, f32[512,768]{1,0:T(8,128)}, f32[16,128]{1,0:T(8,128)}) custom-call(s32[1]{0:T(128)} %bitcast.end_ref, f32[16,128]{1,0:T(8,128)S(1)} %get-tuple-element.54.refs_0_, f32[16,128]{1,0:T(8,128)S(1)} %collective-permute-done.12.refs_1_, bf16[1040,768]{1,0:T(8,128)(2,1)} %collective-permute-done.16.refs_2_, ...), custom_call_target="tpu_custom_call" | custom-call | tf_op jit(solution)/shard_map/results/pallas_call | solution.py:398
  (55 shorter events, 21.0 us)
Async XLA Ops:
  1.6 12.5 %collective-permute-start.1 = (bf16[128,768]{1,0:T(8,128)(2,1)S(1)}, bf16[128,768]{1,0:T(8,128)(2,1)S(1)}, u32[]{:S(2)}, u32[]{:S(2)}) collective-permute-start(bf16[128,768]{1,0:T(8,128)(2,1)S(1)} %slice.3), channel_id=1, source_target_pairs={{0,8},{4,12},{24,16},{28,20},{1,9},{5,13},{25,17},{29,21},{2,10},{... | collective-permute-start | bytes 589832 | tf_op jit(solution)/shard_map/ppermute | solution.py:455
  6.5 7.6 %collective-permute-start = (s32[4,16]{1,0:T(4,128)}, s32[4,16]{1,0:T(4,128)S(1)}, u32[]{:S(2)}, u32[]{:S(2)}) collective-permute-start(s32[4,16]{1,0:T(4,128)} %bitcast.6), channel_id=1, source_target_pairs={{0,8},{4,12},{24,16},{28,20},{1,9},{5,13},{25,17},{29,21},{2,10},{... | collective-permute-start | bytes 776 | tf_op jit(solution)/shard_map/ppermute | solution.py:455
  8.5 49.9 %copy-start.12 = (s32[16,4]{0,1:T(4,128)S(1)}, s32[16,4]{0,1:T(4,128)}, u32[]{:S(2)}) copy-start(s32[16,4]{0,1:T(4,128)} %param.6) | copy-start | bytes 772
  14.1 36.3 %collective-permute-start.2 = (bf16[1,2,528,768]{3,2,1,0:T(8,128)(2,1)}, bf16[1,2,528,768]{3,2,1,0:T(8,128)(2,1)}, u32[]{:S(2)}, u32[]{:S(2)}) collective-permute-start(bf16[1,2,528,768]{3,2,1,0:T(8,128)(2,1)} %get-tuple-element.49.refs_0_), channel_id=1, source_target_pairs={{0,8},{4,12},{24,16},{28,20},{1,9},{5,13},{25,17},{29,21},{2,10},{... | collective-permute-start | bytes 4866056 | tf_op jit(solution)/shard_map/ppermute | solution.py:455
  16.6 47.4 %collective-permute-start.5 = (bf16[1,2,528,768]{3,2,1,0:T(8,128)(2,1)}, bf16[1,2,528,768]{3,2,1,0:T(8,128)(2,1)}, u32[]{:S(2)}, u32[]{:S(2)}) collective-permute-start(bf16[1,2,528,768]{3,2,1,0:T(8,128)(2,1)} %get-tuple-element.49.refs_0_), channel_id=1, source_target_pairs={{8,12},{12,8},{16,20},{20,16},{9,13},{13,9},{17,21},{21,17},{10,14... | collective-permute-start | bytes 4866056 | tf_op jit(solution)/shard_map/ppermute | solution.py:455
  18.4 45.6 %collective-permute-start.4 = (bf16[1,2,528,768]{3,2,1,0:T(8,128)(2,1)}, bf16[1,2,528,768]{3,2,1,0:T(8,128)(2,1)}, u32[]{:S(2)}, u32[]{:S(2)}) collective-permute-start(bf16[1,2,528,768]{3,2,1,0:T(8,128)(2,1)} %get-tuple-element.49.refs_0_), channel_id=1, source_target_pairs={{8,16},{12,20},{16,8},{20,12},{9,17},{13,21},{17,9},{21,13},{10,18... | collective-permute-start | bytes 4866056 | tf_op jit(solution)/shard_map/ppermute | solution.py:455
  50.4 16.5 %collective-permute-start.3 = (bf16[1,2,528,768]{3,2,1,0:T(8,128)(2,1)}, bf16[1,2,528,768]{3,2,1,0:T(8,128)(2,1)}, u32[]{:S(2)}, u32[]{:S(2)}) collective-permute-start(bf16[1,2,528,768]{3,2,1,0:T(8,128)(2,1)} %collective-permute-done.2.refs_2_), channel_id=1, source_target_pairs={{8,16},{12,20},{16,8},{20,12},{9,17},{13,21},{17,9},{21,13},{10,18... | collective-permute-start | bytes 4866056 | tf_op jit(solution)/shard_map/ppermute | solution.py:455
  52.3 47.2 %collective-permute-start.9 = (bf16[1280,768]{1,0:T(8,128)(2,1)}, bf16[1280,768]{1,0:T(8,128)(2,1)S(1)}, u32[]{:S(2)}, u32[]{:S(2)}) collective-permute-start(bf16[1280,768]{1,0:T(8,128)(2,1)} %get-tuple-element.60), channel_id=1, source_target_pairs={{0,8},{4,12},{24,16},{28,20},{1,9},{5,13},{25,17},{29,21},{2,10},{... | collective-permute-start | bytes 5898248 | tf_op jit(solution)/shard_map/ppermute | solution.py:455
  66.9 38.2 %collective-permute-start.6 = (bf16[1,2,528,768]{3,2,1,0:T(8,128)(2,1)}, bf16[1,2,528,768]{3,2,1,0:T(8,128)(2,1)S(1)}, u32[]{:S(2)}, u32[]{:S(2)}) collective-permute-start(bf16[1,2,528,768]{3,2,1,0:T(8,128)(2,1)} %collective-permute-done.2.refs_2_), channel_id=1, source_target_pairs={{8,12},{12,8},{16,20},{20,16},{9,13},{13,9},{17,21},{21,17},{10,14... | collective-permute-start | bytes 4866056 | tf_op jit(solution)/shard_map/ppermute | solution.py:455
  67.7 37.4 %collective-permute-start.7 = (bf16[1,2,528,768]{3,2,1,0:T(8,128)(2,1)}, bf16[1,2,528,768]{3,2,1,0:T(8,128)(2,1)S(1)}, u32[]{:S(2)}, u32[]{:S(2)}) collective-permute-start(bf16[1,2,528,768]{3,2,1,0:T(8,128)(2,1)} %collective-permute-done.4.refs_3_), channel_id=1, source_target_pairs={{8,12},{12,8},{16,20},{20,16},{9,13},{13,9},{17,21},{21,17},{10,14... | collective-permute-start | bytes 4866056 | tf_op jit(solution)/shard_map/ppermute | solution.py:455
  68.5 36.7 %collective-permute-start.8 = (bf16[1,2,528,768]{3,2,1,0:T(8,128)(2,1)}, bf16[1,2,528,768]{3,2,1,0:T(8,128)(2,1)S(1)}, u32[]{:S(2)}, u32[]{:S(2)}) collective-permute-start(bf16[1,2,528,768]{3,2,1,0:T(8,128)(2,1)} %collective-permute-done.3.refs_1_), channel_id=1, source_target_pairs={{8,12},{12,8},{16,20},{20,16},{9,13},{13,9},{17,21},{21,17},{10,14... | collective-permute-start | bytes 4866056 | tf_op jit(solution)/shard_map/ppermute | solution.py:455
  99.5 1.3 copy-start.1
  100.8 29.1 %collective-permute-start.10 = (bf16[640,768]{1,0:T(8,128)(2,1)}, bf16[640,768]{1,0:T(8,128)(2,1)S(1)}, u32[]{:S(2)}, u32[]{:S(2)}) collective-permute-start(bf16[640,768]{1,0:T(8,128)(2,1)} %get-tuple-element.64), channel_id=1, source_target_pairs={{0,8},{4,12},{24,16},{28,20},{1,9},{5,13},{25,17},{29,21},{2,10},{... | collective-permute-start | bytes 2949128 | tf_op jit(solution)/shard_map/ppermute | solution.py:455
  105.1 2.4 %copy-start = (bf16[2048,768]{1,0:T(8,128)(2,1)S(1)}, bf16[2048,768]{1,0:T(8,128)(2,1)}, u32[]{:S(2)}) copy-start(bf16[2048,768]{1,0:T(8,128)(2,1)} %rest_0_.15) | copy-start | bytes 9437188
  119.7 49.1 %copy-start.4 = (bf16[16,4,128,128]{3,2,1,0:T(8,128)(2,1)}, bf16[16,4,128,128]{3,2,1,0:T(8,128)(2,1)S(1)}, u32[]{:S(2)}) copy-start(bf16[16,4,128,128]{3,2,1,0:T(8,128)(2,1)S(1)} %get-tuple-element.66.rest_4_) | copy-start | bytes 6291460
  119.7 2.3 copy-start.2
  129.9 38.9 %copy-start.6 = (bf16[10,4,128,128]{3,2,1,0:T(8,128)(2,1)}, bf16[10,4,128,128]{3,2,1,0:T(8,128)(2,1)S(1)}, u32[]{:S(2)}) copy-start(bf16[10,4,128,128]{3,2,1,0:T(8,128)(2,1)S(1)} %get-tuple-element.68.rest_6_) | copy-start | bytes 3932164
  129.9 38.9 %copy-start.8 = (bf16[640,768]{1,0:T(8,128)(2,1)}, bf16[640,768]{1,0:T(8,128)(2,1)S(1)}, u32[]{:S(2)}) copy-start(bf16[640,768]{1,0:T(8,128)(2,1)S(1)} %collective-permute-done.10.x_ref.rest_3_) | copy-start | bytes 2949124
  134.1 34.7 %copy-start.10 = (bf16[5,4,128,128]{3,2,1,0:T(8,128)(2,1)}, bf16[5,4,128,128]{3,2,1,0:T(8,128)(2,1)S(1)}, u32[]{:S(2)}) copy-start(bf16[5,4,128,128]{3,2,1,0:T(8,128)(2,1)S(1)} %get-tuple-element.69.rest_7_) | copy-start | bytes 1966084
  136.3 3.6 %collective-permute-start.11 = (bf16[1040,768]{1,0:T(8,128)(2,1)S(1)}, bf16[1040,768]{1,0:T(8,128)(2,1)S(1)}, u32[]{:S(2)}, u32[]{:S(2)}) collective-permute-start(bf16[1040,768]{1,0:T(8,128)(2,1)S(1)} %moments.8), channel_id=1, source_target_pairs={{8,12},{12,8},{16,20},{20,16},{9,13},{13,9},{17,21},{21,17},{10,14... | collective-permute-start | bytes 4792328 | tf_op jit(solution)/shard_map/ppermute | solution.py:455
  142.8 4.3 %collective-permute-start.13 = (bf16[1040,768]{1,0:T(8,128)(2,1)S(1)}, bf16[1040,768]{1,0:T(8,128)(2,1)S(1)}, u32[]{:S(2)}, u32[]{:S(2)}) collective-permute-start(bf16[1040,768]{1,0:T(8,128)(2,1)S(1)} %moments.10), channel_id=1, source_target_pairs={{8,12},{12,8},{16,20},{20,16},{9,13},{13,9},{17,21},{21,17},{10,14... | collective-permute-start | bytes 4792328 | tf_op jit(solution)/shard_map/ppermute | solution.py:455
  143.6 37.5 %collective-permute-start.15 = (bf16[1040,768]{1,0:T(8,128)(2,1)S(1)}, bf16[1040,768]{1,0:T(8,128)(2,1)S(1)}, u32[]{:S(2)}, u32[]{:S(2)}) collective-permute-start(bf16[1040,768]{1,0:T(8,128)(2,1)S(1)} %add_sums.3), channel_id=1, source_target_pairs={{8,16},{12,20},{16,8},{20,12},{9,17},{13,21},{17,9},{21,13},{10,18... | collective-permute-start | bytes 4792328 | tf_op jit(solution)/shard_map/ppermute | solution.py:455
  151.3 29.7 %collective-permute-start.14 = (bf16[1040,768]{1,0:T(8,128)(2,1)S(1)}, bf16[1040,768]{1,0:T(8,128)(2,1)S(1)}, u32[]{:S(2)}, u32[]{:S(2)}) collective-permute-start(bf16[1040,768]{1,0:T(8,128)(2,1)S(1)} %moments.12), channel_id=1, source_target_pairs={{8,12},{12,8},{16,20},{20,16},{9,13},{13,9},{17,21},{21,17},{10,14... | collective-permute-start | bytes 4792328 | tf_op jit(solution)/shard_map/ppermute | solution.py:455
  152.3 16.5 %collective-permute-start.12 = (f32[16,128]{1,0:T(8,128)S(1)}, f32[16,128]{1,0:T(8,128)S(1)}, u32[]{:S(2)}, u32[]{:S(2)}) collective-permute-start(f32[16,128]{1,0:T(8,128)S(1)} %join_norms.1), channel_id=1, source_target_pairs={{8,0},{12,4},{16,24},{20,28},{9,1},{13,5},{17,25},{21,29},{10,2},{... | collective-permute-start | bytes 24584 | tf_op jit(solution)/shard_map/ppermute | solution.py:455
  153.6 39.0 %collective-permute-start.18 = (bf16[1040,768]{1,0:T(8,128)(2,1)}, bf16[1040,768]{1,0:T(8,128)(2,1)}, u32[]{:S(2)}, u32[]{:S(2)}) collective-permute-start(bf16[1040,768]{1,0:T(8,128)(2,1)} %add_sums.4), channel_id=1, source_target_pairs={{8,16},{12,20},{16,8},{20,12},{9,17},{13,21},{17,9},{21,13},{10,18... | collective-permute-start | bytes 4792328 | tf_op jit(solution)/shard_map/ppermute | solution.py:455
  159.1 33.5 %collective-permute-start.17 = (bf16[1040,768]{1,0:T(8,128)(2,1)}, bf16[1040,768]{1,0:T(8,128)(2,1)}, u32[]{:S(2)}, u32[]{:S(2)}) collective-permute-start(bf16[1040,768]{1,0:T(8,128)(2,1)} %moments.13), channel_id=1, source_target_pairs={{8,12},{12,8},{16,20},{20,16},{9,13},{13,9},{17,21},{21,17},{10,14... | collective-permute-start | bytes 4792328 | tf_op jit(solution)/shard_map/ppermute | solution.py:455
  182.9 43.8 %collective-permute-start.16 = (bf16[1040,768]{1,0:T(8,128)(2,1)}, bf16[1040,768]{1,0:T(8,128)(2,1)}, u32[]{:S(2)}, u32[]{:S(2)}) collective-permute-start(bf16[1040,768]{1,0:T(8,128)(2,1)} %add_sums.5), channel_id=1, source_target_pairs={{8,0},{12,4},{16,24},{20,28},{9,1},{13,5},{17,25},{21,29},{10,2},{... | collective-permute-start | bytes 4792328 | tf_op jit(solution)/shard_map/ppermute | solution.py:455
  184.2 1.5 copy-start.3
  185.7 1.6 copy-start.5
  187.3 1.3 copy-start.7
  188.7 1.2 copy-start.9
  189.9 1.1 copy-start.11

commit v9 on v8

--- a/solution.py
+++ b/solution.py
@@ -25,24 +25,17 @@
     return pltpu.with_memory_space_constraint(value, pltpu.HBM)
 
 
-def shard_body(cuts, means_hbm, inv_hbm, log_ref, points_ref, out_ref, *rest):
-    piece_refs, (means_ref, inv_ref, own_sems, sems) = rest[:-4], rest[-4:]
-    own_copies = [
-        pltpu.make_async_copy(means_hbm, means_ref, own_sems.at[0]),
-        pltpu.make_async_copy(inv_hbm, inv_ref, own_sems.at[1]),
-    ]
-    for copy in own_copies:
-        copy.start()
+def shard_body(means_hbm, inv_hbm, log_ref, out_ref, means_ref, inv_ref, sems):
     copies = [
-        pltpu.make_async_copy(points_ref.at[pl.ds(cuts[j], piece.shape[0])], piece, sems.at[j])
-        for j, piece in enumerate(piece_refs)
+        pltpu.make_async_copy(means_hbm, means_ref, sems.at[0]),
+        pltpu.make_async_copy(inv_hbm, inv_ref, sems.at[1]),
     ]
     for copy in copies:
         copy.start()
     owned, feature_count = means_ref.shape
     ones = jnp.ones((META, feature_count), jnp.float32)
     row = lax.broadcasted_iota(jnp.int32, (META, CB), 0)
-    for copy in own_copies:
+    for copy in copies:
         copy.wait()
     for half in range(2):
         out_ref[0, half, owned:, :] = jnp.zeros((META, feature_count), jnp.bfloat16)
@@ -66,26 +59,21 @@
         low = rest - middle
         pieces = jnp.where(row == 0, high, jnp.where(row == 1, middle, low))
         out_ref[0, 0, owned:, here] = pieces.astype(jnp.bfloat16)
-    for copy in copies:
-        copy.wait()
-
-
-def parameter_shard(means, inv_var, log_weight, points, cuts):
+
+
+def parameter_shard(means, inv_var, log_weight):
     owned, feature_count = means.shape
     vmem = pl.BlockSpec(memory_space=pltpu.VMEM)
     hbm = pl.BlockSpec(memory_space=pltpu.HBM)
-    lengths = [b - a for a, b in zip(cuts[:-1], cuts[1:])]
-    return pl.pallas_call(
-        functools.partial(shard_body, cuts),
-        in_specs=[hbm, hbm, vmem, hbm],
-        out_specs=[vmem] + [vmem] * len(lengths),
-        out_shape=[pltpu.VMEM((1, 2, owned + META, feature_count), jnp.bfloat16)]
-        + [pltpu.VMEM((length, feature_count), points.dtype) for length in lengths],
+    return pl.pallas_call(
+        shard_body,
+        in_specs=[hbm, hbm, vmem],
+        out_specs=vmem,
+        out_shape=pltpu.VMEM((1, 2, owned + META, feature_count), jnp.bfloat16),
         scratch_shapes=[
             pltpu.VMEM((owned, feature_count), means.dtype),
             pltpu.VMEM((owned, feature_count), inv_var.dtype),
             pltpu.SemaphoreType.DMA((2,)),
-            pltpu.SemaphoreType.DMA((max(len(lengths), 1),)),
         ],
         compiler_params=pltpu.CompilerParams(vmem_limit_bytes=VMEM_LIMIT),
         cost_estimate=pl.CostEstimate(
@@ -94,7 +82,46 @@
             transcendentals=owned * feature_count,
         ),
         name="parameter_shard",
-    )(in_hbm(means), in_hbm(inv_var), log_weight.reshape(1, owned), in_hbm(points))
+    )(in_hbm(means), in_hbm(inv_var), log_weight.reshape(1, owned))
+
+
+def cut_body(cuts, points_ref, *refs):
+    piece_refs, (staging, sems) = refs[:-2], refs[-2:]
+    ways = []
+    for j, piece in enumerate(piece_refs):
+        here = pl.ds(cuts[j], piece.shape[0])
+        there = pl.ds(cuts[j] - cuts[0], piece.shape[0])
+        ways.append(
+            (
+                pltpu.make_async_copy(points_ref.at[here, :], staging.at[there, :], sems.at[0, j]),
+                pltpu.make_async_copy(staging.at[there, :], piece, sems.at[1, j]),
+            )
+        )
+    for inward, _ in ways:
+        inward.start()
+    for inward, outward in ways:
+        inward.wait()
+        outward.start()
+    for _, outward in ways:
+        outward.wait()
+
+
+def cut_rows(points, cuts):
+    feature_count = points.shape[1]
+    hbm = pl.BlockSpec(memory_space=pltpu.HBM)
+    lengths = [b - a for a, b in zip(cuts[:-1], cuts[1:])]
+    return pl.pallas_call(
+        functools.partial(cut_body, cuts),
+        in_specs=[hbm],
+        out_specs=[hbm] * len(lengths),
+        out_shape=[pltpu.HBM((length, feature_count), points.dtype) for length in lengths],
+        scratch_shapes=[
+            pltpu.VMEM((sum(lengths), feature_count), points.dtype),
+            pltpu.SemaphoreType.DMA((2, len(lengths))),
+        ],
+        compiler_params=pltpu.CompilerParams(vmem_limit_bytes=VMEM_LIMIT),
+        name="cut_rows",
+    )(in_hbm(points))
 
 
 def density_body(first, count, held, pos_ref, x_ref, weight_ref, resp_ref, norm_ref):
@@ -417,7 +444,7 @@
 
 
 def plain_plan(points, candidates, parameters, held):
-    weights = parameter_shard(*parameters, points, (0,))[0]
+    weights = parameter_shard(*parameters)
     dp_size = lax.axis_size("dp")
     row_blocks = points.shape[0] // RB
     pos, order, starts = pair_lists(
@@ -472,31 +499,29 @@
     where = [chip.reshape(1), core.reshape(1)]
     row_blocks = points.shape[0] // RB
     small = row_blocks // 8
-    cuts = (0, 1, 1 + 5 * small, row_blocks)
+    cuts = (0, 1, 2 + 4 * small, row_blocks - small, row_blocks)
     runs = (row_blocks,) + tuple(b - a for a, b in zip(cuts[:-1], cuts[1:]))
     own_ids = candidates.T
     end_ids = move(own_ids, INWARD)
     before = move(points[: cuts[1] * RB], INWARD)
-    weights, *pieces = parameter_shard(*parameters, points, [cut * RB for cut in cuts[1:]])
+    weights = parameter_shard(*parameters)
     weights_then, end_ids, before = lax.optimization_barrier((weights, end_ids, before))
 
     outer = move(weights_then, INWARD)
     across = move(weights, MIDDLE)
-    own_shared = move(weights, CORES)
+    pieces = cut_rows(after(points, weights_then), [cut * RB for cut in cuts[1:]])
+    own_shared = move(after(weights, *pieces), CORES)
     most = move(after(pieces[0], outer), INWARD)
     far = move(outer, MIDDLE)
-    last = move(after(pieces[1], most), INWARD)
-    moved = [before, most, last]
+    moved = [before, most] + [move(after(piece, far), INWARD) for piece in pieces[1:]]
     pos, order, starts = pair_lists(
         [own_ids, end_ids], runs, held, 8 * held, lax.axis_size("comp"), line_place, where
     )
     near = [after(weights, pos, order, starts), own_shared, outer, across]
     near_weights = stacked(8, (0, 1, 2, 4), near)
-    far, outer, across, near_weights = lax.optimization_barrier(
-        (far, outer, across, near_weights)
-    )
+    far, near_weights = lax.optimization_barrier((far, near_weights))
     shared = [move(w, CORES) for w in (outer, across, far)]
-    all_weights = stacked(8, (6, 3, 5, 7), [far] + shared, near_weights)
+    all_weights = stacked(8, (6, 3, 5, 7), [after(far, most)] + shared, near_weights)
 
     rows = [points] + moved
     results = []

time: 234 us -> 228 us (0.974); the launches traced: 231 us -> 228 us
  waiting for transfers between devices: 102 us -> 67.2 us
  starting transfers between devices: 36.4 us -> 63.8 us
  local copies, waits for them, and re-layouts: 11.4 us -> 13.9 us
    ppermute x19 -> x20, waiting for transfers between devices: 102 us -> 67.2 us  [move(): return lax.ppermute(value, 'dp', pairs)]
    ppermute x19 -> x20, starting transfers between devices: 36.4 us -> 63.8 us  [move(): return lax.ppermute(value, 'dp', pairs)]
    unnamed x26 -> x48, local copies, waits for them, and re-layouts: 9.79 us -> 12.2 us
    pallas_call x4 -> x5, Pallas kernels: 25.5 us -> 26 us  [responsibilities(): pl.pallas_call(functools.partial(density_body, first, count, held), in_sp...]
    pallas_call x1 -> x2, Pallas kernels: 5.56 us -> 5.93 us  [the longest x1 3.11 us: cut_rows(): pl.pallas_call(functools.partial(cut_body, cuts), in_specs=[hbm], out_spe...]
  transfers between devices with their start and end apart: 19 -> 20, of which waited for: 4 -> 3; matrix products, arithmetic and copies ran while one was open for 0% -> 0% of each run, Pallas kernels for 29% -> 30%
where the time goes in v9:
time: 228 us
  Pallas kernels  81.6 us (36%)
  waiting for transfers between devices  67.2 us (29%)
  starting transfers between devices  63.8 us (28%)
  local copies, waits for them, and re-layouts  13.9 us (6%)
    ppermute x20, waiting for transfers between devices, move(): return lax.ppermute(value, 'dp', pairs)  67.2 us
    ppermute x20, starting transfers between devices, move(): return lax.ppermute(value, 'dp', pairs)  63.8 us
    pallas_call x8, Pallas kernels, moments(): pl.pallas_call(functools.partial(moment_body, tuple(shards), held, runs),...  30.9 us
    pallas_call x5, Pallas kernels, responsibilities(): pl.pallas_call(functools.partial(density_body, first, count, held), in_sp...  26 us
    unnamed x48, local copies, waits for them, and re-layouts  12.2 us
    pallas_call x1, Pallas kernels, pair_lists(): pl.pallas_call(functools.partial(list_body, tuple(runs), held, owners, pl...  6.02 us
    pallas_call x1, Pallas kernels, results_of(): pl.pallas_call(functools.partial(result_body, owned), grid=(owned // CB,)...  4.63 us
  transfers between devices with their start and end apart: 20, of which 3 were waited for; matrix products, arithmetic and copies ran while one was open for 0% of the time, Pallas kernels for 30%

profile of v9, /device:TPU:0, one launch (start us, length us, event | category | flops | bytes accessed | tf_op | source)
XLA Modules:
  0.0 227.9 jit_solution(266262993901933366)
XLA Ops:
  1.6 4.9 %collective-permute-start.1 = (bf16[128,768]{1,0:T(8,128)(2,1)S(1)}, bf16[128,768]{1,0:T(8,128)(2,1)S(1)}, u32[]{:S(2)}, u32[]{:S(2)}) collective-permute-start(bf16[128,768]{1,0:T(8,128)(2,1)S(1)} %slice.3), channel_id=1, source_target_pairs={{0,8},{4,12},{24,16},{28,20},{1,9},{5,13},{25,17},{29,21},{2,10},{... | collective-permute-start | bytes 589832 | tf_op jit(solution)/shard_map/ppermute | solution.py:482
  8.5 2.8 %parameter_shard.1.refs_0_ = bf16[1,2,528,768]{3,2,1,0:T(8,128)(2,1)S(1)} custom-call(bf16[512,768]{1,0:T(8,128)(2,1)} %means_hbm.1, bf16[512,768]{1,0:T(8,128)(2,1)} %inv_hbm.1, bf16[1,512]{1,0:T(2,128)(2,1)S(1)} %reshape.32.log_ref), custom_call_target="tpu_custom_call" | custom-call | flops 15728640 | bytes 3145728 | tf_op jit(solution)/shard_map/parameter_shard/pallas_call | solution.py:68
  11.4 4.9 %collective-permute-start.2 = (bf16[1,2,528,768]{3,2,1,0:T(8,128)(2,1)S(1)}, bf16[1,2,528,768]{3,2,1,0:T(8,128)(2,1)}, u32[]{:S(2)}, u32[]{:S(2)}) collective-permute-start(bf16[1,2,528,768]{3,2,1,0:T(8,128)(2,1)S(1)} %parameter_shard.1.refs_0_), channel_id=1, source_target_pairs={{0,8},{4,12},{24,16},{28,20},{1,9},{5,13},{25,17},{29,21},{2,10},{... | collective-permute-start | bytes 4866056 | tf_op jit(solution)/shard_map/ppermute | solution.py:482
  16.3 1.8 collective-permute-start.5
  18.1 3.1 %cut_rows.1 = (bf16[1152,768]{1,0:T(8,128)(2,1)}, bf16[512,768]{1,0:T(8,128)(2,1)}, bf16[256,768]{1,0:T(8,128)(2,1)}) custom-call(bf16[2048,768]{1,0:T(8,128)(2,1)} %rest_0_.15), custom_call_target="tpu_custom_call" | custom-call | tf_op jit(solution)/shard_map/cut_rows/pallas_call | solution.py:113
  21.2 1.8 collective-permute-start.4
  23.0 25.9 %collective-permute-done.2.refs_2_ = bf16[1,2,528,768]{3,2,1,0:T(8,128)(2,1)} collective-permute-done((bf16[1,2,528,768]{3,2,1,0:T(8,128)(2,1)S(1)}, bf16[1,2,528,768]{3,2,1,0:T(8,128)(2,1)}, u32[]{:S(2)}, u32[]{:S(2)}) %collective-permute-start.2) | collective-permute-done | bytes 1622048 | tf_op jit(solution)/shard_map/ppermute | solution.py:482
  48.9 1.9 collective-permute-start.3
  50.8 6.2 %collective-permute-start.6 = (bf16[1152,768]{1,0:T(8,128)(2,1)}, bf16[1152,768]{1,0:T(8,128)(2,1)S(1)}, u32[]{:S(2)}, u32[]{:S(2)}) collective-permute-start(bf16[1152,768]{1,0:T(8,128)(2,1)} %get-tuple-element.61), channel_id=1, source_target_pairs={{0,8},{4,12},{24,16},{28,20},{1,9},{5,13},{25,17},{29,21},{2,10},{... | collective-permute-start | bytes 5308424 | tf_op jit(solution)/shard_map/ppermute | solution.py:482
  57.0 6.0 %pair_lists.1 = (s32[128]{0:T(128)S(1)}, s32[128]{0:T(128)S(1)}, s32[161]{0:T(256)S(1)}) custom-call(s32[1]{0:T(128)} %bitcast.1.rest_0_, s32[1]{0:T(128)} %bitcast.2.rest_1_, s32[4,16]{1,0:T(4,128)S(1)} %bitcast.7, s32[4,16]{1,0:T(4,128)S(1)} %collective-permute-done.rest_3_), custom_call_target="tpu_custom_call" | custom-call | tf_op jit(solution)/shard_map/pair_lists/pallas_call | solution.py:229
  64.8 2.6 %stack_shards.2.refs_0_ = bf16[8,2,528,768]{3,2,1,0:T(8,128)(2,1)S(1)} custom-call(bf16[1,2,528,768]{3,2,1,0:T(8,128)(2,1)S(1)} %parameter_shard.1.refs_0_, bf16[1,2,528,768]{3,2,1,0:T(8,128)(2,1)} %collective-permute-done.4.refs_1_, bf16[1,2,528,768]{3,2,1,0:T(8,128)(2,1)} %collective-permute-done.2.refs_2_, ...), custom_call_target="tpu_custom_call" | custom-call | tf_op jit(solution)/shard_map/stack_shards/pallas_call | solution.py:350
  68.2 24.8 %collective-permute-start.10 = (bf16[512,768]{1,0:T(8,128)(2,1)S(1)}, bf16[512,768]{1,0:T(8,128)(2,1)S(1)}, u32[]{:S(2)}, u32[]{:S(2)}) collective-permute-start(bf16[512,768]{1,0:T(8,128)(2,1)S(1)} %copy-done.22), channel_id=1, source_target_pairs={{0,8},{4,12},{24,16},{28,20},{1,9},{5,13},{25,17},{29,21},{2,10},{... | collective-permute-start | bytes 2359304 | tf_op jit(solution)/shard_map/ppermute | solution.py:482
  94.2 4.3 %collective-permute-start.11 = (bf16[256,768]{1,0:T(8,128)(2,1)S(1)}, bf16[256,768]{1,0:T(8,128)(2,1)S(1)}, u32[]{:S(2)}, u32[]{:S(2)}) collective-permute-start(bf16[256,768]{1,0:T(8,128)(2,1)S(1)} %copy-done.23), channel_id=1, source_target_pairs={{0,8},{4,12},{24,16},{28,20},{1,9},{5,13},{25,17},{29,21},{2,10},{... | collective-permute-start | bytes 1179656 | tf_op jit(solution)/shard_map/ppermute | solution.py:482
  100.9 12.2 %responsibilities.5 = (bf16[16,4,128,128]{3,2,1,0:T(8,128)(2,1)S(1)}, f32[16,128]{1,0:T(8,128)S(1)}) custom-call(s32[128]{0:T(128)S(1)} %get-tuple-element.72.pos_ref, bf16[2048,768]{1,0:T(8,128)(2,1)S(1)} %copy-done, bf16[8,2,528,768]{3,2,1,0:T(8,128)(2,1)S(1)} %stack_shards.3.weight_ref), custom_call_target="tpu_custom_call" | custom-call | flops 3221225472 | bytes 28311552 | tf_op jit(solution)/shard_map/responsibilities/pallas_call | solution.py:163
  115.4 7.1 %responsibilities.7 = (bf16[9,4,128,128]{3,2,1,0:T(8,128)(2,1)S(1)}, f32[9,128]{1,0:T(8,128)S(1)}) custom-call(s32[128]{0:T(128)S(1)} %get-tuple-element.72.pos_ref, bf16[1152,768]{1,0:T(8,128)(2,1)S(1)} %copy-done.2, bf16[8,2,528,768]{3,2,1,0:T(8,128)(2,1)S(1)} %stack_shards.3.weight_ref), custom_call_target="tpu_custom_call" | custom-call | flops 1811939328 | bytes 15925248 | tf_op jit(solution)/shard_map/responsibilities/pallas_call | solution.py:163
  122.5 3.5 %responsibilities.8 = (bf16[4,4,128,128]{3,2,1,0:T(8,128)(2,1)S(1)}, f32[4,128]{1,0:T(4,128)S(1)}) custom-call(s32[128]{0:T(128)S(1)} %get-tuple-element.72.pos_ref, bf16[512,768]{1,0:T(8,128)(2,1)S(1)} %collective-permute-done.10.x_ref.rest_3_, bf16[8,2,528,768]{3,2,1,0:T(8,128)(2,1)S(1)} %stack_shards.3.weight_ref), custom_call_target="tpu_custom_call" | custom-call | flops 805306368 | bytes 7077888 | tf_op jit(solution)/shard_map/responsibilities/pallas_call | solution.py:163
  126.0 2.0 responsibilities.9
  128.0 2.6 %moments.8 = bf16[1040,768]{1,0:T(8,128)(2,1)S(1)} custom-call(s32[128]{0:T(128)S(1)} %get-tuple-element.87.order_ref, s32[161]{0:T(256)S(1)} %get-tuple-element.52.start_ref, bf16[2048,768]{1,0:T(8,128)(2,1)S(1)} %copy-done, bf16[128,768]{1,0:T(8,128)(2,1)S(1)} %copy-done.15, bf16[1152,768]{1,0:T(8,128)(2,1)S(1)} %copy-done.2, ...), custom_call_target="tpu_custom_call" | custom-call | flops 805306368 | bytes 3670016 | tf_op jit(solution)/shard_map/moments/pallas_call | solution.py:302
  131.3 2.6 %moments.9.refs_0_ = bf16[1040,768]{1,0:T(8,128)(2,1)S(1)} custom-call(s32[128]{0:T(128)S(1)} %get-tuple-element.87.order_ref, s32[161]{0:T(256)S(1)} %get-tuple-element.52.start_ref, bf16[2048,768]{1,0:T(8,128)(2,1)S(1)} %copy-done, bf16[128,768]{1,0:T(8,128)(2,1)S(1)} %copy-done.15, bf16[1152,768]{1,0:T(8,128)(2,1)S(1)} %copy-done.2, ...), custom_call_target="tpu_custom_call" | custom-call | flops 805306368 | bytes 3670016 | tf_op jit(solution)/shard_map/moments/pallas_call | solution.py:302
  134.4 2.6 %moments.10 = bf16[1040,768]{1,0:T(8,128)(2,1)S(1)} custom-call(s32[128]{0:T(128)S(1)} %get-tuple-element.87.order_ref, s32[161]{0:T(256)S(1)} %get-tuple-element.52.start_ref, bf16[2048,768]{1,0:T(8,128)(2,1)S(1)} %copy-done, bf16[128,768]{1,0:T(8,128)(2,1)S(1)} %copy-done.15, bf16[1152,768]{1,0:T(8,128)(2,1)S(1)} %copy-done.2, ...), custom_call_target="tpu_custom_call" | custom-call | flops 805306368 | bytes 3670016 | tf_op jit(solution)/shard_map/moments/pallas_call | solution.py:302
  138.7 2.3 %moments.11.refs_0_ = bf16[1040,768]{1,0:T(8,128)(2,1)S(1)} custom-call(s32[128]{0:T(128)S(1)} %get-tuple-element.87.order_ref, s32[161]{0:T(256)S(1)} %get-tuple-element.52.start_ref, bf16[2048,768]{1,0:T(8,128)(2,1)S(1)} %copy-done, bf16[128,768]{1,0:T(8,128)(2,1)S(1)} %copy-done.15, bf16[1152,768]{1,0:T(8,128)(2,1)S(1)} %copy-done.2, ...), custom_call_target="tpu_custom_call" | custom-call | flops 805306368 | bytes 3670016 | tf_op jit(solution)/shard_map/moments/pallas_call | solution.py:302
  141.0 1.7 add_sums.4
  142.7 2.3 moments.12
  147.0 1.8 collective-permute-start.19
  148.9 3.4 %moments.13 = bf16[1040,768]{1,0:T(8,128)(2,1)} custom-call(s32[128]{0:T(128)S(1)} %get-tuple-element.87.order_ref, s32[161]{0:T(256)S(1)} %get-tuple-element.52.start_ref, bf16[2048,768]{1,0:T(8,128)(2,1)S(1)} %copy-done, bf16[128,768]{1,0:T(8,128)(2,1)S(1)} %copy-done.15, bf16[1152,768]{1,0:T(8,128)(2,1)S(1)} %copy-done.2, ...), custom_call_target="tpu_custom_call" | custom-call | flops 805306368 | bytes 3670016 | tf_op jit(solution)/shard_map/moments/pallas_call | solution.py:302
  152.3 1.8 collective-permute-start.18
  154.1 10.8 %collective-permute-done.13.refs_1_ = f32[16,128]{1,0:T(8,128)S(1)} collective-permute-done((f32[16,128]{1,0:T(8,128)S(1)}, f32[16,128]{1,0:T(8,128)S(1)}, u32[]{:S(2)}, u32[]{:S(2)}) %collective-permute-start.13) | collective-permute-done | bytes 8224 | tf_op jit(solution)/shard_map/ppermute | solution.py:482
  165.0 12.6 %moments.14.refs_0_ = bf16[1040,768]{1,0:T(8,128)(2,1)S(1)} custom-call(s32[128]{0:T(128)S(1)} %get-tuple-element.87.order_ref, s32[161]{0:T(256)S(1)} %get-tuple-element.52.start_ref, bf16[2048,768]{1,0:T(8,128)(2,1)S(1)} %copy-done, bf16[128,768]{1,0:T(8,128)(2,1)S(1)} %copy-done.15, bf16[1152,768]{1,0:T(8,128)(2,1)S(1)} %copy-done.2, ...), custom_call_target="tpu_custom_call" | custom-call | flops 805306368 | bytes 3670016 | tf_op jit(solution)/shard_map/moments/pallas_call | solution.py:302
  177.6 1.8 add_sums.5
  190.0 2.6 %moments.15.refs_3_ = bf16[1040,768]{1,0:T(8,128)(2,1)S(1)} custom-call(s32[128]{0:T(128)S(1)} %get-tuple-element.87.order_ref, s32[161]{0:T(256)S(1)} %get-tuple-element.52.start_ref, bf16[2048,768]{1,0:T(8,128)(2,1)S(1)} %copy-done, bf16[128,768]{1,0:T(8,128)(2,1)S(1)} %copy-done.16, bf16[1152,768]{1,0:T(8,128)(2,1)S(1)} %copy-done.3, ...), custom_call_target="tpu_custom_call" | custom-call | flops 805306368 | bytes 3670016 | tf_op jit(solution)/shard_map/moments/pallas_call | solution.py:302
  192.6 30.5 %collective-permute-done.17.refs_2_ = bf16[1040,768]{1,0:T(8,128)(2,1)} collective-permute-done((bf16[1040,768]{1,0:T(8,128)(2,1)}, bf16[1040,768]{1,0:T(8,128)(2,1)}, u32[]{:S(2)}, u32[]{:S(2)}) %collective-permute-start.17) | collective-permute-done | bytes 1597472 | tf_op jit(solution)/shard_map/ppermute | solution.py:482
  223.1 4.6 %results.1 = (f32[1,512]{1,0:T(1,128)}, f32[512,768]{1,0:T(8,128)}, f32[512,768]{1,0:T(8,128)}, f32[16,128]{1,0:T(8,128)}) custom-call(s32[1]{0:T(128)} %bitcast.end_ref, f32[16,128]{1,0:T(8,128)S(1)} %get-tuple-element.63.refs_0_, f32[16,128]{1,0:T(8,128)S(1)} %copy-done.20, bf16[1040,768]{1,0:T(8,128)(2,1)} %collective-permute-done.17.refs_2_, ...), custom_call_target="tpu_custom_call" | custom-call | tf_op jit(solution)/shard_map/results/pallas_call | solution.py:425
  (81 shorter events, 26.8 us)
Async XLA Ops:
  1.6 9.8 %collective-permute-start.1 = (bf16[128,768]{1,0:T(8,128)(2,1)S(1)}, bf16[128,768]{1,0:T(8,128)(2,1)S(1)}, u32[]{:S(2)}, u32[]{:S(2)}) collective-permute-start(bf16[128,768]{1,0:T(8,128)(2,1)S(1)} %slice.3), channel_id=1, source_target_pairs={{0,8},{4,12},{24,16},{28,20},{1,9},{5,13},{25,17},{29,21},{2,10},{... | collective-permute-start | bytes 589832 | tf_op jit(solution)/shard_map/ppermute | solution.py:482
  6.5 4.8 %collective-permute-start = (s32[4,16]{1,0:T(4,128)}, s32[4,16]{1,0:T(4,128)S(1)}, u32[]{:S(2)}, u32[]{:S(2)}) collective-permute-start(s32[4,16]{1,0:T(4,128)} %bitcast.6), channel_id=1, source_target_pairs={{0,8},{4,12},{24,16},{28,20},{1,9},{5,13},{25,17},{29,21},{2,10},{... | collective-permute-start | bytes 776 | tf_op jit(solution)/shard_map/ppermute | solution.py:482
  11.3 45.7 %copy-start.21 = (s32[16,4]{0,1:T(4,128)S(1)}, s32[16,4]{0,1:T(4,128)}, u32[]{:S(2)}) copy-start(s32[16,4]{0,1:T(4,128)} %param.6) | copy-start | bytes 772
  11.4 37.5 %copy-start.14 = (bf16[128,768]{1,0:T(8,128)(2,1)}, bf16[128,768]{1,0:T(8,128)(2,1)S(1)}, u32[]{:S(2)}) copy-start(bf16[128,768]{1,0:T(8,128)(2,1)S(1)} %collective-permute-done.1.x_ref.rest_1_) | copy-start | bytes 589828
  11.4 37.5 %collective-permute-start.2 = (bf16[1,2,528,768]{3,2,1,0:T(8,128)(2,1)S(1)}, bf16[1,2,528,768]{3,2,1,0:T(8,128)(2,1)}, u32[]{:S(2)}, u32[]{:S(2)}) collective-permute-start(bf16[1,2,528,768]{3,2,1,0:T(8,128)(2,1)S(1)} %parameter_shard.1.refs_0_), channel_id=1, source_target_pairs={{0,8},{4,12},{24,16},{28,20},{1,9},{5,13},{25,17},{29,21},{2,10},{... | collective-permute-start | bytes 4866056 | tf_op jit(solution)/shard_map/ppermute | solution.py:482
  16.3 46.8 %collective-permute-start.5 = (bf16[1,2,528,768]{3,2,1,0:T(8,128)(2,1)S(1)}, bf16[1,2,528,768]{3,2,1,0:T(8,128)(2,1)}, u32[]{:S(2)}, u32[]{:S(2)}) collective-permute-start(bf16[1,2,528,768]{3,2,1,0:T(8,128)(2,1)S(1)} %parameter_shard.1.refs_0_), channel_id=1, source_target_pairs={{8,16},{12,20},{16,8},{20,12},{9,17},{13,21},{17,9},{21,13},{10,18... | collective-permute-start | bytes 4866056 | tf_op jit(solution)/shard_map/ppermute | solution.py:482
  21.2 43.6 %collective-permute-start.4 = (bf16[1,2,528,768]{3,2,1,0:T(8,128)(2,1)S(1)}, bf16[1,2,528,768]{3,2,1,0:T(8,128)(2,1)}, u32[]{:S(2)}, u32[]{:S(2)}) collective-permute-start(bf16[1,2,528,768]{3,2,1,0:T(8,128)(2,1)S(1)} %parameter_shard.1.refs_0_), channel_id=1, source_target_pairs={{8,12},{12,8},{16,20},{20,16},{9,13},{13,9},{17,21},{21,17},{10,14... | collective-permute-start | bytes 4866056 | tf_op jit(solution)/shard_map/ppermute | solution.py:482
  48.9 18.5 %collective-permute-start.3 = (bf16[1,2,528,768]{3,2,1,0:T(8,128)(2,1)}, bf16[1,2,528,768]{3,2,1,0:T(8,128)(2,1)}, u32[]{:S(2)}, u32[]{:S(2)}) collective-permute-start(bf16[1,2,528,768]{3,2,1,0:T(8,128)(2,1)} %collective-permute-done.2.refs_2_), channel_id=1, source_target_pairs={{8,16},{12,20},{16,8},{20,12},{9,17},{13,21},{17,9},{21,13},{10,18... | collective-permute-start | bytes 4866056 | tf_op jit(solution)/shard_map/ppermute | solution.py:482
  50.8 42.2 %collective-permute-start.6 = (bf16[1152,768]{1,0:T(8,128)(2,1)}, bf16[1152,768]{1,0:T(8,128)(2,1)S(1)}, u32[]{:S(2)}, u32[]{:S(2)}) collective-permute-start(bf16[1152,768]{1,0:T(8,128)(2,1)} %get-tuple-element.61), channel_id=1, source_target_pairs={{0,8},{4,12},{24,16},{28,20},{1,9},{5,13},{25,17},{29,21},{2,10},{... | collective-permute-start | bytes 5308424 | tf_op jit(solution)/shard_map/ppermute | solution.py:482
  63.1 31.1 %copy-start.23 = (bf16[256,768]{1,0:T(8,128)(2,1)S(1)}, bf16[256,768]{1,0:T(8,128)(2,1)}, u32[]{:S(2)}) copy-start(bf16[256,768]{1,0:T(8,128)(2,1)} %get-tuple-element.73) | copy-start | bytes 1179652
  63.1 35.4 %collective-permute-start.8 = (bf16[1,2,528,768]{3,2,1,0:T(8,128)(2,1)}, bf16[1,2,528,768]{3,2,1,0:T(8,128)(2,1)S(1)}, u32[]{:S(2)}, u32[]{:S(2)}) collective-permute-start(bf16[1,2,528,768]{3,2,1,0:T(8,128)(2,1)} %collective-permute-done.5.refs_3_), channel_id=1, source_target_pairs={{8,12},{12,8},{16,20},{20,16},{9,13},{13,9},{17,21},{21,17},{10,14... | collective-permute-start | bytes 4866056 | tf_op jit(solution)/shard_map/ppermute | solution.py:482
  64.0 34.5 %collective-permute-start.7 = (bf16[1,2,528,768]{3,2,1,0:T(8,128)(2,1)}, bf16[1,2,528,768]{3,2,1,0:T(8,128)(2,1)S(1)}, u32[]{:S(2)}, u32[]{:S(2)}) collective-permute-start(bf16[1,2,528,768]{3,2,1,0:T(8,128)(2,1)} %collective-permute-done.2.refs_2_), channel_id=1, source_target_pairs={{8,12},{12,8},{16,20},{20,16},{9,13},{13,9},{17,21},{21,17},{10,14... | collective-permute-start | bytes 4866056 | tf_op jit(solution)/shard_map/ppermute | solution.py:482
  67.4 31.1 %collective-permute-start.9 = (bf16[1,2,528,768]{3,2,1,0:T(8,128)(2,1)}, bf16[1,2,528,768]{3,2,1,0:T(8,128)(2,1)S(1)}, u32[]{:S(2)}, u32[]{:S(2)}) collective-permute-start(bf16[1,2,528,768]{3,2,1,0:T(8,128)(2,1)} %collective-permute-done.3.refs_1_), channel_id=1, source_target_pairs={{8,12},{12,8},{16,20},{20,16},{9,13},{13,9},{17,21},{21,17},{10,14... | collective-permute-start | bytes 4866056 | tf_op jit(solution)/shard_map/ppermute | solution.py:482
  68.2 54.3 %collective-permute-start.10 = (bf16[512,768]{1,0:T(8,128)(2,1)S(1)}, bf16[512,768]{1,0:T(8,128)(2,1)S(1)}, u32[]{:S(2)}, u32[]{:S(2)}) collective-permute-start(bf16[512,768]{1,0:T(8,128)(2,1)S(1)} %copy-done.22), channel_id=1, source_target_pairs={{0,8},{4,12},{24,16},{28,20},{1,9},{5,13},{25,17},{29,21},{2,10},{... | collective-permute-start | bytes 2359304 | tf_op jit(solution)/shard_map/ppermute | solution.py:482
  94.2 31.8 %collective-permute-start.11 = (bf16[256,768]{1,0:T(8,128)(2,1)S(1)}, bf16[256,768]{1,0:T(8,128)(2,1)S(1)}, u32[]{:S(2)}, u32[]{:S(2)}) collective-permute-start(bf16[256,768]{1,0:T(8,128)(2,1)S(1)} %copy-done.23), channel_id=1, source_target_pairs={{0,8},{4,12},{24,16},{28,20},{1,9},{5,13},{25,17},{29,21},{2,10},{... | collective-permute-start | bytes 1179656 | tf_op jit(solution)/shard_map/ppermute | solution.py:482
  100.9 12.2 %copy-start.15 = (bf16[128,768]{1,0:T(8,128)(2,1)S(1)}, bf16[128,768]{1,0:T(8,128)(2,1)}, u32[]{:S(2)}) copy-start(bf16[128,768]{1,0:T(8,128)(2,1)} %copy-done.14) | copy-start | bytes 589828
  113.1 51.8 %copy-start.4 = (bf16[16,4,128,128]{3,2,1,0:T(8,128)(2,1)}, bf16[16,4,128,128]{3,2,1,0:T(8,128)(2,1)S(1)}, u32[]{:S(2)}) copy-start(bf16[16,4,128,128]{3,2,1,0:T(8,128)(2,1)S(1)} %get-tuple-element.75.rest_5_) | copy-start | bytes 6291460
  114.4 50.5 %copy-start.17 = (bf16[1,4,128,128]{3,2,1,0:T(8,128)(2,1)}, bf16[1,4,128,128]{3,2,1,0:T(8,128)(2,1)S(1)}, u32[]{:S(2)}) copy-start(bf16[1,4,128,128]{3,2,1,0:T(8,128)(2,1)S(1)} %get-tuple-element.76.rest_6_) | copy-start | bytes 393220
  122.5 42.5 %copy-start.6 = (bf16[9,4,128,128]{3,2,1,0:T(8,128)(2,1)}, bf16[9,4,128,128]{3,2,1,0:T(8,128)(2,1)S(1)}, u32[]{:S(2)}) copy-start(bf16[9,4,128,128]{3,2,1,0:T(8,128)(2,1)S(1)} %get-tuple-element.77.rest_7_) | copy-start | bytes 3538948
  122.5 42.4 %copy-start.8 = (bf16[512,768]{1,0:T(8,128)(2,1)}, bf16[512,768]{1,0:T(8,128)(2,1)S(1)}, u32[]{:S(2)}) copy-start(bf16[512,768]{1,0:T(8,128)(2,1)S(1)} %collective-permute-done.10.x_ref.rest_3_) | copy-start | bytes 2359300
  126.0 39.0 %copy-start.10 = (bf16[4,4,128,128]{3,2,1,0:T(8,128)(2,1)}, bf16[4,4,128,128]{3,2,1,0:T(8,128)(2,1)S(1)}, u32[]{:S(2)}) copy-start(bf16[4,4,128,128]{3,2,1,0:T(8,128)(2,1)S(1)} %get-tuple-element.78.rest_8_) | copy-start | bytes 1572868
  128.0 37.0 %copy-start.12 = (bf16[2,4,128,128]{3,2,1,0:T(8,128)(2,1)}, bf16[2,4,128,128]{3,2,1,0:T(8,128)(2,1)S(1)}, u32[]{:S(2)}) copy-start(bf16[2,4,128,128]{3,2,1,0:T(8,128)(2,1)S(1)} %get-tuple-element.79.rest_9_) | copy-start | bytes 786436
  130.6 3.4 %collective-permute-start.12 = (bf16[1040,768]{1,0:T(8,128)(2,1)S(1)}, bf16[1040,768]{1,0:T(8,128)(2,1)S(1)}, u32[]{:S(2)}, u32[]{:S(2)}) collective-permute-start(bf16[1040,768]{1,0:T(8,128)(2,1)S(1)} %moments.8), channel_id=1, source_target_pairs={{8,12},{12,8},{16,20},{20,16},{9,13},{13,9},{17,21},{21,17},{10,14... | collective-permute-start | bytes 4792328 | tf_op jit(solution)/shard_map/ppermute | solution.py:482
  137.0 4.0 %collective-permute-start.14 = (bf16[1040,768]{1,0:T(8,128)(2,1)S(1)}, bf16[1040,768]{1,0:T(8,128)(2,1)S(1)}, u32[]{:S(2)}, u32[]{:S(2)}) collective-permute-start(bf16[1040,768]{1,0:T(8,128)(2,1)S(1)} %moments.10), channel_id=1, source_target_pairs={{8,12},{12,8},{16,20},{20,16},{9,13},{13,9},{17,21},{21,17},{10,14... | collective-permute-start | bytes 4792328 | tf_op jit(solution)/shard_map/ppermute | solution.py:482
  137.7 39.8 %collective-permute-start.16 = (bf16[1040,768]{1,0:T(8,128)(2,1)S(1)}, bf16[1040,768]{1,0:T(8,128)(2,1)S(1)}, u32[]{:S(2)}, u32[]{:S(2)}) collective-permute-start(bf16[1040,768]{1,0:T(8,128)(2,1)S(1)} %add_sums.3), channel_id=1, source_target_pairs={{8,16},{12,20},{16,8},{20,12},{9,17},{13,21},{17,9},{21,13},{10,18... | collective-permute-start | bytes 4792328 | tf_op jit(solution)/shard_map/ppermute | solution.py:482
  144.9 32.6 %collective-permute-start.15 = (bf16[1040,768]{1,0:T(8,128)(2,1)S(1)}, bf16[1040,768]{1,0:T(8,128)(2,1)S(1)}, u32[]{:S(2)}, u32[]{:S(2)}) collective-permute-start(bf16[1040,768]{1,0:T(8,128)(2,1)S(1)} %moments.12), channel_id=1, source_target_pairs={{8,12},{12,8},{16,20},{20,16},{9,13},{13,9},{17,21},{21,17},{10,14... | collective-permute-start | bytes 4792328 | tf_op jit(solution)/shard_map/ppermute | solution.py:482
  145.7 19.2 %collective-permute-start.13 = (f32[16,128]{1,0:T(8,128)S(1)}, f32[16,128]{1,0:T(8,128)S(1)}, u32[]{:S(2)}, u32[]{:S(2)}) collective-permute-start(f32[16,128]{1,0:T(8,128)S(1)} %join_norms.1), channel_id=1, source_target_pairs={{8,0},{12,4},{16,24},{20,28},{9,1},{13,5},{17,25},{21,29},{10,2},{... | collective-permute-start | bytes 24584 | tf_op jit(solution)/shard_map/ppermute | solution.py:482
  147.0 45.6 %collective-permute-start.19 = (bf16[1040,768]{1,0:T(8,128)(2,1)}, bf16[1040,768]{1,0:T(8,128)(2,1)}, u32[]{:S(2)}, u32[]{:S(2)}) collective-permute-start(bf16[1040,768]{1,0:T(8,128)(2,1)} %add_sums.4), channel_id=1, source_target_pairs={{8,16},{12,20},{16,8},{20,12},{9,17},{13,21},{17,9},{21,13},{10,18... | collective-permute-start | bytes 4792328 | tf_op jit(solution)/shard_map/ppermute | solution.py:482
  152.3 40.3 %collective-permute-start.18 = (bf16[1040,768]{1,0:T(8,128)(2,1)}, bf16[1040,768]{1,0:T(8,128)(2,1)}, u32[]{:S(2)}, u32[]{:S(2)}) collective-permute-start(bf16[1040,768]{1,0:T(8,128)(2,1)} %moments.13), channel_id=1, source_target_pairs={{8,12},{12,8},{16,20},{20,16},{9,13},{13,9},{17,21},{21,17},{10,14... | collective-permute-start | bytes 4792328 | tf_op jit(solution)/shard_map/ppermute | solution.py:482
  165.0 12.6 %copy-start.19 = (f32[16,128]{1,0:T(8,128)}, f32[16,128]{1,0:T(8,128)S(1)}, u32[]{:S(2)}) copy-start(f32[16,128]{1,0:T(8,128)S(1)} %collective-permute-done.13.refs_1_) | copy-start | bytes 24580
  179.4 43.7 %collective-permute-start.17 = (bf16[1040,768]{1,0:T(8,128)(2,1)}, bf16[1040,768]{1,0:T(8,128)(2,1)}, u32[]{:S(2)}, u32[]{:S(2)}) collective-permute-start(bf16[1040,768]{1,0:T(8,128)(2,1)} %add_sums.5), channel_id=1, source_target_pairs={{8,0},{12,4},{16,24},{20,28},{9,1},{13,5},{17,25},{21,29},{10,2},{... | collective-permute-start | bytes 4792328 | tf_op jit(solution)/shard_map/ppermute | solution.py:482
  190.0 33.1 %copy-start.20 = (f32[16,128]{1,0:T(8,128)S(1)}, f32[16,128]{1,0:T(8,128)}, u32[]{:S(2)}) copy-start(f32[16,128]{1,0:T(8,128)} %copy-done.19) | copy-start | bytes 24580
  (12 other events, 20.2 us)

commit v10 on v9

--- a/solution.py
+++ b/solution.py
@@ -12,6 +12,7 @@
 RB = 128
 CANDS = 4
 META = 16
+COLUMNS = 256
 VMEM_LIMIT = 8 * 1024 * 1024
 NT = (((1,), (1,)), ((), ()))
 TN = (((0,), (0,)), ((), ()))
@@ -241,14 +242,15 @@
     parts, outs = len(runs), len(shards)
     row_refs, resp_refs = rest[:parts], rest[parts : 2 * parts]
     out_refs = rest[2 * parts : 2 * parts + outs]
-    sums, count_sum = rest[2 * parts + outs :]
+    sums, weight_sum = rest[2 * parts + outs :]
     owned = held * CB
     meta = slice(2 * owned, 2 * owned + META)
-    ones = jnp.ones((META, 2 * RB), jnp.bfloat16)
+    ones = jnp.ones((META, RB), jnp.float32)
+    feature_count = row_refs[0].shape[1]
 
     def block_sums(pos):
         sums[...] = jnp.zeros_like(sums)
-        count_sum[...] = jnp.zeros_like(count_sum)
+        weight_sum[...] = jnp.zeros_like(weight_sum)
         base = 0
         for run in range(parts):
             entry = pos * parts + run
@@ -272,11 +274,13 @@
                     ],
                     axis=0,
                 )
-                sums[0] += jnp.dot(weight, x, preferred_element_type=jnp.float32)
-                sums[1] += jnp.dot(weight, x * x, preferred_element_type=jnp.float32)
-                count_sum[...] += lax.dot_general(
-                    ones, weight, NT, preferred_element_type=jnp.float32
-                )
+                for moment, values in enumerate((x, x * x)):
+                    for column in range(0, feature_count, COLUMNS):
+                        columns = slice(column, column + COLUMNS)
+                        sums[moment, :, columns] += jnp.dot(
+                            weight, values[:, columns], preferred_element_type=jnp.float32
+                        )
+                weight_sum[...] += weight_a.astype(jnp.float32) + weight_b.astype(jnp.float32)
 
             base += runs[run] * CANDS
 
@@ -289,7 +293,14 @@
             start = pl.multiple_of(block * CB, CB)
             out_ref[pl.ds(start, CB), :] = sums[0].astype(jnp.bfloat16)
             out_ref[pl.ds(owned + start, CB), :] = sums[1].astype(jnp.bfloat16)
-            out_ref[meta, pl.ds(start, CB)] = count_sum[...].astype(jnp.bfloat16)
+            counts = lax.dot_general(
+                ones,
+                weight_sum[...],
+                NT,
+                precision=lax.Precision.HIGHEST,
+                preferred_element_type=jnp.float32,
+            )
+            out_ref[meta, pl.ds(start, CB)] = counts.astype(jnp.bfloat16)
 
 
 def moments(rows, resp, order, starts, held, shards):
@@ -306,7 +317,7 @@
         out_shape=[out_shape] * len(shards),
         scratch_shapes=[
             pltpu.VMEM((2, CB, feature_count), jnp.float32),
-            pltpu.VMEM((META, CB), jnp.float32),
+            pltpu.VMEM((CB, RB), jnp.float32),
         ],
         compiler_params=pltpu.CompilerParams(vmem_limit_bytes=VMEM_LIMIT),
         cost_estimate=pl.CostEstimate(
@@ -398,49 +409,102 @@
     return small_step(join_body, shape, jnp.float32, "join_norms", *norms)
 
 
-def result_body(owned, end_ref, *refs):
-    own_norm, end_norm, end_sum = refs[:3]
-    terms, (count_ref, first_ref, second_ref, loglik_ref) = refs[3:-4], refs[-4:]
+def result_body(
+    held,
+    end_ref,
+    own_norm,
+    end_norm,
+    end_sum,
+    own_sum,
+    moved_sum,
+    count_ref,
+    first_ref,
+    second_ref,
+    loglik_ref,
+    main,
+    more,
+    staging,
+    main_sems,
+    more_sems,
+    out_sems,
+):
     is_end = end_ref[0] > 0
-    block = pl.program_id(0)
-    feature_count = first_ref.shape[1]
-
-    def total(rows):
-        inner = functools.reduce(jnp.add, [t[rows, :].astype(jnp.float32) for t in terms])
-        return jnp.where(is_end, end_sum[rows, :].astype(jnp.float32), inner)
-
-    start = pl.multiple_of(block * CB, CB)
-    first_ref[...] = total(pl.ds(start, CB))
-    second_ref[...] = total(pl.ds(owned + start, CB))
-    count_ref[...] = total(slice(2 * owned, 2 * owned + META))[0:1, :owned]
+    owned = held * CB
+    feature_count = main.shape[1]
+    pieces = [(j * CB, CB) for j in range(2 * held)] + [(2 * owned, META)]
+
+    def copy_in(source, target, sems, j):
+        here = pl.ds(*pieces[j])
+        return pltpu.make_async_copy(source.at[here, :], target.at[here, :], sems.at[j])
+
+    @pl.when(is_end)
+    def _():
+        for j in range(len(pieces)):
+            copy_in(end_sum, main, main_sems, j).start()
+
+    @pl.when(jnp.logical_not(is_end))
+    def _():
+        for j in range(len(pieces)):
+            copy_in(moved_sum, main, main_sems, j).start()
+            copy_in(own_sum, more, more_sems, j).start()
+
     norm = jnp.where(is_end, end_norm[...], own_norm[...])
     loglik_ref[...] = norm * (1.0 / feature_count)
-
-
-def results_of(is_end, own_norm, end_norm, end_sum, *terms):
+    outward = []
+    for j, (start, length) in enumerate(pieces):
+        copy_in(end_sum, main, main_sems, j).wait()
+
+        @pl.when(jnp.logical_not(is_end))
+        def _(j=j):
+            copy_in(own_sum, more, more_sems, j).wait()
+
+        here = slice(start, start + length)
+        value = main[here, :].astype(jnp.float32)
+        value = jnp.where(is_end, value, value + more[here, :].astype(jnp.float32))
+        if start == 2 * owned:
+            count_ref[...] = value[0:1, :owned]
+            break
+        if j >= 2:
+            outward[j - 2].wait()
+        staging[j % 2] = value
+        target = first_ref if start < owned else second_ref
+        rows = pl.ds(start % owned, CB)
+        outward.append(
+            pltpu.make_async_copy(staging.at[j % 2], target.at[rows, :], out_sems.at[j % 2])
+        )
+        outward[-1].start()
+    for copy in outward[-2:]:
+        copy.wait()
+
+
+def results_of(held, is_end, own_norm, end_norm, end_sum, own_sum, moved_sum):
     rows, feature_count = end_sum.shape
-    owned = (rows - META) // 2
+    owned = held * CB
     vmem = pl.BlockSpec(memory_space=pltpu.VMEM)
-    operands = (own_norm, end_norm, end_sum) + terms
-    return pl.pallas_call(
-        functools.partial(result_body, owned),
-        grid=(owned // CB,),
-        in_specs=[pl.BlockSpec(memory_space=pltpu.SMEM)] + [vmem] * len(operands),
-        out_specs=[
-            pl.BlockSpec((1, owned), lambda i: (0, 0)),
-            pl.BlockSpec((CB, feature_count), lambda i: (i, 0)),
-            pl.BlockSpec((CB, feature_count), lambda i: (i, 0)),
-            pl.BlockSpec(own_norm.shape, lambda i: (0, 0)),
-        ],
+    anywhere = pl.BlockSpec(memory_space=pl.ANY)
+    pieces = 2 * held + 1
+    moments_shape = jax.ShapeDtypeStruct((owned, feature_count), jnp.float32)
+    return pl.pallas_call(
+        functools.partial(result_body, held),
+        in_specs=[pl.BlockSpec(memory_space=pltpu.SMEM), vmem, vmem] + [anywhere] * 3,
+        out_specs=[vmem, anywhere, anywhere, vmem],
         out_shape=[
             jax.ShapeDtypeStruct((1, owned), jnp.float32),
-            jax.ShapeDtypeStruct((owned, feature_count), jnp.float32),
-            jax.ShapeDtypeStruct((owned, feature_count), jnp.float32),
+            moments_shape,
+            moments_shape,
             jax.ShapeDtypeStruct(own_norm.shape, jnp.float32),
         ],
+        scratch_shapes=[
+            pltpu.VMEM((rows, feature_count), jnp.bfloat16),
+            pltpu.VMEM((rows, feature_count), jnp.bfloat16),
+            pltpu.VMEM((2, CB, feature_count), jnp.float32),
+            pltpu.SemaphoreType.DMA((pieces,)),
+            pltpu.SemaphoreType.DMA((pieces,)),
+            pltpu.SemaphoreType.DMA((2,)),
+        ],
         compiler_params=pltpu.CompilerParams(vmem_limit_bytes=VMEM_LIMIT),
         name="results",
-    )(is_end.astype(jnp.int32).reshape(1), *[in_vmem(value) for value in operands])
+    )(is_end.astype(jnp.int32).reshape(1), own_norm, end_norm, end_sum, own_sum, moved_sum)
 
 
 def plain_plan(points, candidates, parameters, held):
@@ -554,8 +618,9 @@
     outer_sum = added(outer_own, outer_received, far_sum)
     end_sum = move(outer_sum, OUTWARD)
     is_end = jnp.logical_or(chip == 0, chip == 3)
+    own_sum = added(own_own, own_received)
     counts, first, second, loglik = results_of(
-        is_end, results[0][1], end_norm, end_sum, own_own, own_received, across_sum
+        held, is_end, results[0][1], end_norm, end_sum, own_sum, across_sum
     )
     return counts.reshape(-1), first, second, loglik.reshape(-1)
 

time: 228 us -> 232 us (1.018)
  Pallas kernels: 81.6 us -> 89.8 us
  waiting for transfers between devices: 67.2 us -> 62.8 us
    pallas_call x8, Pallas kernels: 30.9 us -> 37 us  [moments(): pl.pallas_call(functools.partial(moment_body, tuple(shards), held, runs),...]
    ppermute x20, waiting for transfers between devices: 67.2 us -> 62.8 us  [move(): return lax.ppermute(value, 'dp', pairs)]
    pallas_call x4 -> x5, Pallas kernels: 3.97 us -> 5.73 us  [small_step(): pl.pallas_call(body, in_specs=[vmem] * len(operands), out_specs=vmem, out...]
  transfers between devices with their start and end apart: 20 -> 20, of which waited for: 3 -> 3; matrix products, arithmetic and copies ran while one was open for 0% -> 0% of each run, Pallas kernels for 30% -> 33%
where the time goes in v10:
time: 232 us
  Pallas kernels  89.8 us (39%)
  starting transfers between devices  63.8 us (28%)
  waiting for transfers between devices  62.8 us (27%)
  local copies, waits for them, and re-layouts  13.9 us (6%)
    ppermute x20, starting transfers between devices, move(): return lax.ppermute(value, 'dp', pairs)  63.8 us
    ppermute x20, waiting for transfers between devices, move(): return lax.ppermute(value, 'dp', pairs)  62.8 us
    pallas_call x8, Pallas kernels, moments(): pl.pallas_call(functools.partial(moment_body, tuple(shards), held, runs),...  37 us
    pallas_call x5, Pallas kernels, responsibilities(): pl.pallas_call(functools.partial(density_body, first, count, held), in_sp...  26 us
    unnamed x48, local copies, waits for them, and re-layouts  12.2 us
    pallas_call x1, Pallas kernels, pair_lists(): pl.pallas_call(functools.partial(list_body, tuple(runs), held, owners, pl...  6.02 us
    pallas_call x5, Pallas kernels, small_step(): pl.pallas_call(body, in_specs=[vmem] * len(operands), out_specs=vmem, out...  5.73 us
    pallas_call x1, Pallas kernels, results_of(): pl.pallas_call(functools.partial(result_body, held), in_specs=[pl.BlockSp...  4.96 us
  transfers between devices with their start and end apart: 20, of which 3 were waited for; matrix products, arithmetic and copies ran while one was open for 0% of the time, Pallas kernels for 33%

profile of v10, /device:TPU:0, one launch (start us, length us, event | category | flops | bytes accessed | tf_op | source)
XLA Modules:
  0.0 231.6 jit_solution(9576949507175819565)
XLA Ops:
  1.6 4.9 %collective-permute-start.1 = (bf16[128,768]{1,0:T(8,128)(2,1)S(1)}, bf16[128,768]{1,0:T(8,128)(2,1)S(1)}, u32[]{:S(2)}, u32[]{:S(2)}) collective-permute-start(bf16[128,768]{1,0:T(8,128)(2,1)S(1)} %slice.3), channel_id=1, source_target_pairs={{0,8},{4,12},{24,16},{28,20},{1,9},{5,13},{25,17},{29,21},{2,10},{... | collective-permute-start | bytes 589832 | tf_op jit(solution)/shard_map/ppermute | solution.py:546
  8.5 2.8 %parameter_shard.1.refs_0_ = bf16[1,2,528,768]{3,2,1,0:T(8,128)(2,1)S(1)} custom-call(bf16[512,768]{1,0:T(8,128)(2,1)} %means_hbm.1, bf16[512,768]{1,0:T(8,128)(2,1)} %inv_hbm.1, bf16[1,512]{1,0:T(2,128)(2,1)S(1)} %reshape.32.log_ref), custom_call_target="tpu_custom_call" | custom-call | flops 15728640 | bytes 3145728 | tf_op jit(solution)/shard_map/parameter_shard/pallas_call | solution.py:69
  11.4 4.9 %collective-permute-start.2 = (bf16[1,2,528,768]{3,2,1,0:T(8,128)(2,1)S(1)}, bf16[1,2,528,768]{3,2,1,0:T(8,128)(2,1)}, u32[]{:S(2)}, u32[]{:S(2)}) collective-permute-start(bf16[1,2,528,768]{3,2,1,0:T(8,128)(2,1)S(1)} %parameter_shard.1.refs_0_), channel_id=1, source_target_pairs={{0,8},{4,12},{24,16},{28,20},{1,9},{5,13},{25,17},{29,21},{2,10},{... | collective-permute-start | bytes 4866056 | tf_op jit(solution)/shard_map/ppermute | solution.py:546
  16.3 1.8 collective-permute-start.5
  18.1 3.1 %cut_rows.1 = (bf16[1152,768]{1,0:T(8,128)(2,1)}, bf16[512,768]{1,0:T(8,128)(2,1)}, bf16[256,768]{1,0:T(8,128)(2,1)}) custom-call(bf16[2048,768]{1,0:T(8,128)(2,1)} %rest_0_.15), custom_call_target="tpu_custom_call" | custom-call | tf_op jit(solution)/shard_map/cut_rows/pallas_call | solution.py:114
  21.2 1.8 collective-permute-start.4
  23.0 25.9 %collective-permute-done.2.refs_2_ = bf16[1,2,528,768]{3,2,1,0:T(8,128)(2,1)} collective-permute-done((bf16[1,2,528,768]{3,2,1,0:T(8,128)(2,1)S(1)}, bf16[1,2,528,768]{3,2,1,0:T(8,128)(2,1)}, u32[]{:S(2)}, u32[]{:S(2)}) %collective-permute-start.2) | collective-permute-done | bytes 1622048 | tf_op jit(solution)/shard_map/ppermute | solution.py:546
  48.9 1.9 collective-permute-start.3
  50.8 6.2 %collective-permute-start.6 = (bf16[1152,768]{1,0:T(8,128)(2,1)}, bf16[1152,768]{1,0:T(8,128)(2,1)S(1)}, u32[]{:S(2)}, u32[]{:S(2)}) collective-permute-start(bf16[1152,768]{1,0:T(8,128)(2,1)} %get-tuple-element.61), channel_id=1, source_target_pairs={{0,8},{4,12},{24,16},{28,20},{1,9},{5,13},{25,17},{29,21},{2,10},{... | collective-permute-start | bytes 5308424 | tf_op jit(solution)/shard_map/ppermute | solution.py:546
  57.0 6.0 %pair_lists.1 = (s32[128]{0:T(128)S(1)}, s32[128]{0:T(128)S(1)}, s32[161]{0:T(256)S(1)}) custom-call(s32[1]{0:T(128)} %bitcast.1.rest_0_, s32[1]{0:T(128)} %bitcast.2.rest_1_, s32[4,16]{1,0:T(4,128)S(1)} %bitcast.7, s32[4,16]{1,0:T(4,128)S(1)} %collective-permute-done.rest_3_), custom_call_target="tpu_custom_call" | custom-call | tf_op jit(solution)/shard_map/pair_lists/pallas_call | solution.py:230
  64.8 2.6 %stack_shards.2.refs_0_ = bf16[8,2,528,768]{3,2,1,0:T(8,128)(2,1)S(1)} custom-call(bf16[1,2,528,768]{3,2,1,0:T(8,128)(2,1)S(1)} %parameter_shard.1.refs_0_, bf16[1,2,528,768]{3,2,1,0:T(8,128)(2,1)} %collective-permute-done.4.refs_1_, bf16[1,2,528,768]{3,2,1,0:T(8,128)(2,1)} %collective-permute-done.2.refs_2_, ...), custom_call_target="tpu_custom_call" | custom-call | tf_op jit(solution)/shard_map/stack_shards/pallas_call | solution.py:361
  68.2 24.8 %collective-permute-start.10 = (bf16[512,768]{1,0:T(8,128)(2,1)S(1)}, bf16[512,768]{1,0:T(8,128)(2,1)S(1)}, u32[]{:S(2)}, u32[]{:S(2)}) collective-permute-start(bf16[512,768]{1,0:T(8,128)(2,1)S(1)} %copy-done.22), channel_id=1, source_target_pairs={{0,8},{4,12},{24,16},{28,20},{1,9},{5,13},{25,17},{29,21},{2,10},{... | collective-permute-start | bytes 2359304 | tf_op jit(solution)/shard_map/ppermute | solution.py:546
  94.2 4.3 %collective-permute-start.11 = (bf16[256,768]{1,0:T(8,128)(2,1)S(1)}, bf16[256,768]{1,0:T(8,128)(2,1)S(1)}, u32[]{:S(2)}, u32[]{:S(2)}) collective-permute-start(bf16[256,768]{1,0:T(8,128)(2,1)S(1)} %copy-done.23), channel_id=1, source_target_pairs={{0,8},{4,12},{24,16},{28,20},{1,9},{5,13},{25,17},{29,21},{2,10},{... | collective-permute-start | bytes 1179656 | tf_op jit(solution)/shard_map/ppermute | solution.py:546
  100.9 12.2 %responsibilities.5 = (bf16[16,4,128,128]{3,2,1,0:T(8,128)(2,1)S(1)}, f32[16,128]{1,0:T(8,128)S(1)}) custom-call(s32[128]{0:T(128)S(1)} %get-tuple-element.72.pos_ref, bf16[2048,768]{1,0:T(8,128)(2,1)S(1)} %copy-done, bf16[8,2,528,768]{3,2,1,0:T(8,128)(2,1)S(1)} %stack_shards.3.weight_ref), custom_call_target="tpu_custom_call" | custom-call | flops 3221225472 | bytes 28311552 | tf_op jit(solution)/shard_map/responsibilities/pallas_call | solution.py:164
  115.4 7.1 %responsibilities.7 = (bf16[9,4,128,128]{3,2,1,0:T(8,128)(2,1)S(1)}, f32[9,128]{1,0:T(8,128)S(1)}) custom-call(s32[128]{0:T(128)S(1)} %get-tuple-element.72.pos_ref, bf16[1152,768]{1,0:T(8,128)(2,1)S(1)} %copy-done.2, bf16[8,2,528,768]{3,2,1,0:T(8,128)(2,1)S(1)} %stack_shards.3.weight_ref), custom_call_target="tpu_custom_call" | custom-call | flops 1811939328 | bytes 15925248 | tf_op jit(solution)/shard_map/responsibilities/pallas_call | solution.py:164
  122.5 3.5 %responsibilities.8 = (bf16[4,4,128,128]{3,2,1,0:T(8,128)(2,1)S(1)}, f32[4,128]{1,0:T(4,128)S(1)}) custom-call(s32[128]{0:T(128)S(1)} %get-tuple-element.72.pos_ref, bf16[512,768]{1,0:T(8,128)(2,1)S(1)} %collective-permute-done.10.x_ref.rest_3_, bf16[8,2,528,768]{3,2,1,0:T(8,128)(2,1)S(1)} %stack_shards.3.weight_ref), custom_call_target="tpu_custom_call" | custom-call | flops 805306368 | bytes 7077888 | tf_op jit(solution)/shard_map/responsibilities/pallas_call | solution.py:164
  126.0 2.0 responsibilities.9
  128.0 3.0 %moments.8 = bf16[1040,768]{1,0:T(8,128)(2,1)S(1)} custom-call(s32[128]{0:T(128)S(1)} %get-tuple-element.87.order_ref, s32[161]{0:T(256)S(1)} %get-tuple-element.52.start_ref, bf16[2048,768]{1,0:T(8,128)(2,1)S(1)} %copy-done, bf16[128,768]{1,0:T(8,128)(2,1)S(1)} %copy-done.15, bf16[1152,768]{1,0:T(8,128)(2,1)S(1)} %copy-done.2, ...), custom_call_target="tpu_custom_call" | custom-call | flops 805306368 | bytes 3670016 | tf_op jit(solution)/shard_map/moments/pallas_call | solution.py:313
  131.7 3.5 %moments.9.refs_0_ = bf16[1040,768]{1,0:T(8,128)(2,1)S(1)} custom-call(s32[128]{0:T(128)S(1)} %get-tuple-element.87.order_ref, s32[161]{0:T(256)S(1)} %get-tuple-element.52.start_ref, bf16[2048,768]{1,0:T(8,128)(2,1)S(1)} %copy-done, bf16[128,768]{1,0:T(8,128)(2,1)S(1)} %copy-done.15, bf16[1152,768]{1,0:T(8,128)(2,1)S(1)} %copy-done.2, ...), custom_call_target="tpu_custom_call" | custom-call | flops 805306368 | bytes 3670016 | tf_op jit(solution)/shard_map/moments/pallas_call | solution.py:313
  135.7 3.3 %moments.10 = bf16[1040,768]{1,0:T(8,128)(2,1)S(1)} custom-call(s32[128]{0:T(128)S(1)} %get-tuple-element.87.order_ref, s32[161]{0:T(256)S(1)} %get-tuple-element.52.start_ref, bf16[2048,768]{1,0:T(8,128)(2,1)S(1)} %copy-done, bf16[128,768]{1,0:T(8,128)(2,1)S(1)} %copy-done.15, bf16[1152,768]{1,0:T(8,128)(2,1)S(1)} %copy-done.2, ...), custom_call_target="tpu_custom_call" | custom-call | flops 805306368 | bytes 3670016 | tf_op jit(solution)/shard_map/moments/pallas_call | solution.py:313
  140.7 3.5 %moments.11.refs_0_ = bf16[1040,768]{1,0:T(8,128)(2,1)S(1)} custom-call(s32[128]{0:T(128)S(1)} %get-tuple-element.87.order_ref, s32[161]{0:T(256)S(1)} %get-tuple-element.52.start_ref, bf16[2048,768]{1,0:T(8,128)(2,1)S(1)} %copy-done, bf16[128,768]{1,0:T(8,128)(2,1)S(1)} %copy-done.15, bf16[1152,768]{1,0:T(8,128)(2,1)S(1)} %copy-done.2, ...), custom_call_target="tpu_custom_call" | custom-call | flops 805306368 | bytes 3670016 | tf_op jit(solution)/shard_map/moments/pallas_call | solution.py:313
  145.9 3.3 %moments.12 = bf16[1040,768]{1,0:T(8,128)(2,1)S(1)} custom-call(s32[128]{0:T(128)S(1)} %get-tuple-element.87.order_ref, s32[161]{0:T(256)S(1)} %get-tuple-element.52.start_ref, bf16[2048,768]{1,0:T(8,128)(2,1)S(1)} %copy-done, bf16[128,768]{1,0:T(8,128)(2,1)S(1)} %copy-done.15, bf16[1152,768]{1,0:T(8,128)(2,1)S(1)} %copy-done.2, ...), custom_call_target="tpu_custom_call" | custom-call | flops 805306368 | bytes 3670016 | tf_op jit(solution)/shard_map/moments/pallas_call | solution.py:313
  151.2 1.8 collective-permute-start.19
  153.0 4.2 %moments.13 = bf16[1040,768]{1,0:T(8,128)(2,1)} custom-call(s32[128]{0:T(128)S(1)} %get-tuple-element.87.order_ref, s32[161]{0:T(256)S(1)} %get-tuple-element.52.start_ref, bf16[2048,768]{1,0:T(8,128)(2,1)S(1)} %copy-done, bf16[128,768]{1,0:T(8,128)(2,1)S(1)} %copy-done.15, bf16[1152,768]{1,0:T(8,128)(2,1)S(1)} %copy-done.2, ...), custom_call_target="tpu_custom_call" | custom-call | flops 805306368 | bytes 3670016 | tf_op jit(solution)/shard_map/moments/pallas_call | solution.py:313
  157.2 1.8 collective-permute-start.18
  159.0 10.8 %collective-permute-done.13.end_norm = f32[16,128]{1,0:T(8,128)S(1)} collective-permute-done((f32[16,128]{1,0:T(8,128)S(1)}, f32[16,128]{1,0:T(8,128)S(1)}, u32[]{:S(2)}, u32[]{:S(2)}) %collective-permute-start.13) | collective-permute-done | bytes 8224 | tf_op jit(solution)/shard_map/ppermute | solution.py:546
  169.9 13.2 %moments.14.refs_0_ = bf16[1040,768]{1,0:T(8,128)(2,1)S(1)} custom-call(s32[128]{0:T(128)S(1)} %get-tuple-element.87.order_ref, s32[161]{0:T(256)S(1)} %get-tuple-element.52.start_ref, bf16[2048,768]{1,0:T(8,128)(2,1)S(1)} %copy-done, bf16[128,768]{1,0:T(8,128)(2,1)S(1)} %copy-done.15, bf16[1152,768]{1,0:T(8,128)(2,1)S(1)} %copy-done.2, ...), custom_call_target="tpu_custom_call" | custom-call | flops 805306368 | bytes 3670016 | tf_op jit(solution)/shard_map/moments/pallas_call | solution.py:313
  183.1 1.8 add_sums.6
  195.6 3.0 %moments.15.refs_0_ = bf16[1040,768]{1,0:T(8,128)(2,1)S(1)} custom-call(s32[128]{0:T(128)S(1)} %get-tuple-element.87.order_ref, s32[161]{0:T(256)S(1)} %get-tuple-element.52.start_ref, bf16[2048,768]{1,0:T(8,128)(2,1)S(1)} %copy-done, bf16[128,768]{1,0:T(8,128)(2,1)S(1)} %copy-done.16, bf16[1152,768]{1,0:T(8,128)(2,1)S(1)} %copy-done.3, ...), custom_call_target="tpu_custom_call" | custom-call | flops 805306368 | bytes 3670016 | tf_op jit(solution)/shard_map/moments/pallas_call | solution.py:313
  198.6 1.9 add_sums.7.own_sum
  200.4 26.1 %collective-permute-done.17.end_sum = bf16[1040,768]{1,0:T(8,128)(2,1)} collective-permute-done((bf16[1040,768]{1,0:T(8,128)(2,1)}, bf16[1040,768]{1,0:T(8,128)(2,1)}, u32[]{:S(2)}, u32[]{:S(2)}) %collective-permute-start.17) | collective-permute-done | bytes 1597472 | tf_op jit(solution)/shard_map/ppermute | solution.py:546
  226.5 5.0 %results.1 = (f32[1,512]{1,0:T(1,128)}, f32[512,768]{1,0:T(8,128)}, f32[512,768]{1,0:T(8,128)}, f32[16,128]{1,0:T(8,128)}) custom-call(s32[1]{0:T(128)} %bitcast.end_ref, f32[16,128]{1,0:T(8,128)S(1)} %get-tuple-element.63.own_norm, f32[16,128]{1,0:T(8,128)S(1)} %copy-done.20, bf16[1040,768]{1,0:T(8,128)(2,1)} %collective-permute-done.17.end_sum, ...), custom_call_target="tpu_custom_call" | custom-call | tf_op jit(solution)/shard_map/results/pallas_call | solution.py:487
  (82 shorter events, 28.3 us)
Async XLA Ops:
  1.6 9.8 %collective-permute-start.1 = (bf16[128,768]{1,0:T(8,128)(2,1)S(1)}, bf16[128,768]{1,0:T(8,128)(2,1)S(1)}, u32[]{:S(2)}, u32[]{:S(2)}) collective-permute-start(bf16[128,768]{1,0:T(8,128)(2,1)S(1)} %slice.3), channel_id=1, source_target_pairs={{0,8},{4,12},{24,16},{28,20},{1,9},{5,13},{25,17},{29,21},{2,10},{... | collective-permute-start | bytes 589832 | tf_op jit(solution)/shard_map/ppermute | solution.py:546
  6.5 4.8 %collective-permute-start = (s32[4,16]{1,0:T(4,128)}, s32[4,16]{1,0:T(4,128)S(1)}, u32[]{:S(2)}, u32[]{:S(2)}) collective-permute-start(s32[4,16]{1,0:T(4,128)} %bitcast.6), channel_id=1, source_target_pairs={{0,8},{4,12},{24,16},{28,20},{1,9},{5,13},{25,17},{29,21},{2,10},{... | collective-permute-start | bytes 776 | tf_op jit(solution)/shard_map/ppermute | solution.py:546
  11.3 45.7 %copy-start.21 = (s32[16,4]{0,1:T(4,128)S(1)}, s32[16,4]{0,1:T(4,128)}, u32[]{:S(2)}) copy-start(s32[16,4]{0,1:T(4,128)} %param.6) | copy-start | bytes 772
  11.4 37.5 %copy-start.14 = (bf16[128,768]{1,0:T(8,128)(2,1)}, bf16[128,768]{1,0:T(8,128)(2,1)S(1)}, u32[]{:S(2)}) copy-start(bf16[128,768]{1,0:T(8,128)(2,1)S(1)} %collective-permute-done.1.x_ref.rest_1_) | copy-start | bytes 589828
  11.4 37.5 %collective-permute-start.2 = (bf16[1,2,528,768]{3,2,1,0:T(8,128)(2,1)S(1)}, bf16[1,2,528,768]{3,2,1,0:T(8,128)(2,1)}, u32[]{:S(2)}, u32[]{:S(2)}) collective-permute-start(bf16[1,2,528,768]{3,2,1,0:T(8,128)(2,1)S(1)} %parameter_shard.1.refs_0_), channel_id=1, source_target_pairs={{0,8},{4,12},{24,16},{28,20},{1,9},{5,13},{25,17},{29,21},{2,10},{... | collective-permute-start | bytes 4866056 | tf_op jit(solution)/shard_map/ppermute | solution.py:546
  16.3 46.8 %collective-permute-start.5 = (bf16[1,2,528,768]{3,2,1,0:T(8,128)(2,1)S(1)}, bf16[1,2,528,768]{3,2,1,0:T(8,128)(2,1)}, u32[]{:S(2)}, u32[]{:S(2)}) collective-permute-start(bf16[1,2,528,768]{3,2,1,0:T(8,128)(2,1)S(1)} %parameter_shard.1.refs_0_), channel_id=1, source_target_pairs={{8,16},{12,20},{16,8},{20,12},{9,17},{13,21},{17,9},{21,13},{10,18... | collective-permute-start | bytes 4866056 | tf_op jit(solution)/shard_map/ppermute | solution.py:546
  21.2 43.6 %collective-permute-start.4 = (bf16[1,2,528,768]{3,2,1,0:T(8,128)(2,1)S(1)}, bf16[1,2,528,768]{3,2,1,0:T(8,128)(2,1)}, u32[]{:S(2)}, u32[]{:S(2)}) collective-permute-start(bf16[1,2,528,768]{3,2,1,0:T(8,128)(2,1)S(1)} %parameter_shard.1.refs_0_), channel_id=1, source_target_pairs={{8,12},{12,8},{16,20},{20,16},{9,13},{13,9},{17,21},{21,17},{10,14... | collective-permute-start | bytes 4866056 | tf_op jit(solution)/shard_map/ppermute | solution.py:546
  48.9 18.5 %collective-permute-start.3 = (bf16[1,2,528,768]{3,2,1,0:T(8,128)(2,1)}, bf16[1,2,528,768]{3,2,1,0:T(8,128)(2,1)}, u32[]{:S(2)}, u32[]{:S(2)}) collective-permute-start(bf16[1,2,528,768]{3,2,1,0:T(8,128)(2,1)} %collective-permute-done.2.refs_2_), channel_id=1, source_target_pairs={{8,16},{12,20},{16,8},{20,12},{9,17},{13,21},{17,9},{21,13},{10,18... | collective-permute-start | bytes 4866056 | tf_op jit(solution)/shard_map/ppermute | solution.py:546
  50.8 42.2 %collective-permute-start.6 = (bf16[1152,768]{1,0:T(8,128)(2,1)}, bf16[1152,768]{1,0:T(8,128)(2,1)S(1)}, u32[]{:S(2)}, u32[]{:S(2)}) collective-permute-start(bf16[1152,768]{1,0:T(8,128)(2,1)} %get-tuple-element.61), channel_id=1, source_target_pairs={{0,8},{4,12},{24,16},{28,20},{1,9},{5,13},{25,17},{29,21},{2,10},{... | collective-permute-start | bytes 5308424 | tf_op jit(solution)/shard_map/ppermute | solution.py:546
  63.1 31.1 %copy-start.23 = (bf16[256,768]{1,0:T(8,128)(2,1)S(1)}, bf16[256,768]{1,0:T(8,128)(2,1)}, u32[]{:S(2)}) copy-start(bf16[256,768]{1,0:T(8,128)(2,1)} %get-tuple-element.73) | copy-start | bytes 1179652
  63.1 35.4 %collective-permute-start.8 = (bf16[1,2,528,768]{3,2,1,0:T(8,128)(2,1)}, bf16[1,2,528,768]{3,2,1,0:T(8,128)(2,1)S(1)}, u32[]{:S(2)}, u32[]{:S(2)}) collective-permute-start(bf16[1,2,528,768]{3,2,1,0:T(8,128)(2,1)} %collective-permute-done.5.refs_3_), channel_id=1, source_target_pairs={{8,12},{12,8},{16,20},{20,16},{9,13},{13,9},{17,21},{21,17},{10,14... | collective-permute-start | bytes 4866056 | tf_op jit(solution)/shard_map/ppermute | solution.py:546
  64.0 34.5 %collective-permute-start.7 = (bf16[1,2,528,768]{3,2,1,0:T(8,128)(2,1)}, bf16[1,2,528,768]{3,2,1,0:T(8,128)(2,1)S(1)}, u32[]{:S(2)}, u32[]{:S(2)}) collective-permute-start(bf16[1,2,528,768]{3,2,1,0:T(8,128)(2,1)} %collective-permute-done.2.refs_2_), channel_id=1, source_target_pairs={{8,12},{12,8},{16,20},{20,16},{9,13},{13,9},{17,21},{21,17},{10,14... | collective-permute-start | bytes 4866056 | tf_op jit(solution)/shard_map/ppermute | solution.py:546
  67.4 31.1 %collective-permute-start.9 = (bf16[1,2,528,768]{3,2,1,0:T(8,128)(2,1)}, bf16[1,2,528,768]{3,2,1,0:T(8,128)(2,1)S(1)}, u32[]{:S(2)}, u32[]{:S(2)}) collective-permute-start(bf16[1,2,528,768]{3,2,1,0:T(8,128)(2,1)} %collective-permute-done.3.refs_1_), channel_id=1, source_target_pairs={{8,12},{12,8},{16,20},{20,16},{9,13},{13,9},{17,21},{21,17},{10,14... | collective-permute-start | bytes 4866056 | tf_op jit(solution)/shard_map/ppermute | solution.py:546
  68.2 54.3 %collective-permute-start.10 = (bf16[512,768]{1,0:T(8,128)(2,1)S(1)}, bf16[512,768]{1,0:T(8,128)(2,1)S(1)}, u32[]{:S(2)}, u32[]{:S(2)}) collective-permute-start(bf16[512,768]{1,0:T(8,128)(2,1)S(1)} %copy-done.22), channel_id=1, source_target_pairs={{0,8},{4,12},{24,16},{28,20},{1,9},{5,13},{25,17},{29,21},{2,10},{... | collective-permute-start | bytes 2359304 | tf_op jit(solution)/shard_map/ppermute | solution.py:546
  94.2 31.8 %collective-permute-start.11 = (bf16[256,768]{1,0:T(8,128)(2,1)S(1)}, bf16[256,768]{1,0:T(8,128)(2,1)S(1)}, u32[]{:S(2)}, u32[]{:S(2)}) collective-permute-start(bf16[256,768]{1,0:T(8,128)(2,1)S(1)} %copy-done.23), channel_id=1, source_target_pairs={{0,8},{4,12},{24,16},{28,20},{1,9},{5,13},{25,17},{29,21},{2,10},{... | collective-permute-start | bytes 1179656 | tf_op jit(solution)/shard_map/ppermute | solution.py:546
  100.9 12.2 %copy-start.15 = (bf16[128,768]{1,0:T(8,128)(2,1)S(1)}, bf16[128,768]{1,0:T(8,128)(2,1)}, u32[]{:S(2)}) copy-start(bf16[128,768]{1,0:T(8,128)(2,1)} %copy-done.14) | copy-start | bytes 589828
  113.1 56.7 %copy-start.4 = (bf16[16,4,128,128]{3,2,1,0:T(8,128)(2,1)}, bf16[16,4,128,128]{3,2,1,0:T(8,128)(2,1)S(1)}, u32[]{:S(2)}) copy-start(bf16[16,4,128,128]{3,2,1,0:T(8,128)(2,1)S(1)} %get-tuple-element.75.rest_5_) | copy-start | bytes 6291460
  114.4 55.4 %copy-start.17 = (bf16[1,4,128,128]{3,2,1,0:T(8,128)(2,1)}, bf16[1,4,128,128]{3,2,1,0:T(8,128)(2,1)S(1)}, u32[]{:S(2)}) copy-start(bf16[1,4,128,128]{3,2,1,0:T(8,128)(2,1)S(1)} %get-tuple-element.76.rest_6_) | copy-start | bytes 393220
  122.5 47.4 %copy-start.6 = (bf16[9,4,128,128]{3,2,1,0:T(8,128)(2,1)}, bf16[9,4,128,128]{3,2,1,0:T(8,128)(2,1)S(1)}, u32[]{:S(2)}) copy-start(bf16[9,4,128,128]{3,2,1,0:T(8,128)(2,1)S(1)} %get-tuple-element.77.rest_7_) | copy-start | bytes 3538948
  122.5 47.4 %copy-start.8 = (bf16[512,768]{1,0:T(8,128)(2,1)}, bf16[512,768]{1,0:T(8,128)(2,1)S(1)}, u32[]{:S(2)}) copy-start(bf16[512,768]{1,0:T(8,128)(2,1)S(1)} %collective-permute-done.10.x_ref.rest_3_) | copy-start | bytes 2359300
  126.0 43.9 %copy-start.10 = (bf16[4,4,128,128]{3,2,1,0:T(8,128)(2,1)}, bf16[4,4,128,128]{3,2,1,0:T(8,128)(2,1)S(1)}, u32[]{:S(2)}) copy-start(bf16[4,4,128,128]{3,2,1,0:T(8,128)(2,1)S(1)} %get-tuple-element.78.rest_8_) | copy-start | bytes 1572868
  128.0 41.9 %copy-start.12 = (bf16[2,4,128,128]{3,2,1,0:T(8,128)(2,1)}, bf16[2,4,128,128]{3,2,1,0:T(8,128)(2,1)S(1)}, u32[]{:S(2)}) copy-start(bf16[2,4,128,128]{3,2,1,0:T(8,128)(2,1)S(1)} %get-tuple-element.79.rest_9_) | copy-start | bytes 786436
  131.0 4.3 %collective-permute-start.12 = (bf16[1040,768]{1,0:T(8,128)(2,1)S(1)}, bf16[1040,768]{1,0:T(8,128)(2,1)S(1)}, u32[]{:S(2)}, u32[]{:S(2)}) collective-permute-start(bf16[1040,768]{1,0:T(8,128)(2,1)S(1)} %moments.8), channel_id=1, source_target_pairs={{8,12},{12,8},{16,20},{20,16},{9,13},{13,9},{17,21},{21,17},{10,14... | collective-permute-start | bytes 4792328 | tf_op jit(solution)/shard_map/ppermute | solution.py:546
  139.0 5.3 %collective-permute-start.14 = (bf16[1040,768]{1,0:T(8,128)(2,1)S(1)}, bf16[1040,768]{1,0:T(8,128)(2,1)S(1)}, u32[]{:S(2)}, u32[]{:S(2)}) collective-permute-start(bf16[1040,768]{1,0:T(8,128)(2,1)S(1)} %moments.10), channel_id=1, source_target_pairs={{8,12},{12,8},{16,20},{20,16},{9,13},{13,9},{17,21},{21,17},{10,14... | collective-permute-start | bytes 4792328 | tf_op jit(solution)/shard_map/ppermute | solution.py:546
  139.8 43.3 %collective-permute-start.16 = (bf16[1040,768]{1,0:T(8,128)(2,1)S(1)}, bf16[1040,768]{1,0:T(8,128)(2,1)S(1)}, u32[]{:S(2)}, u32[]{:S(2)}) collective-permute-start(bf16[1040,768]{1,0:T(8,128)(2,1)S(1)} %add_sums.4), channel_id=1, source_target_pairs={{8,16},{12,20},{16,8},{20,12},{9,17},{13,21},{17,9},{21,13},{10,18... | collective-permute-start | bytes 4792328 | tf_op jit(solution)/shard_map/ppermute | solution.py:546
  149.1 34.0 %collective-permute-start.15 = (bf16[1040,768]{1,0:T(8,128)(2,1)S(1)}, bf16[1040,768]{1,0:T(8,128)(2,1)S(1)}, u32[]{:S(2)}, u32[]{:S(2)}) collective-permute-start(bf16[1040,768]{1,0:T(8,128)(2,1)S(1)} %moments.12), channel_id=1, source_target_pairs={{8,12},{12,8},{16,20},{20,16},{9,13},{13,9},{17,21},{21,17},{10,14... | collective-permute-start | bytes 4792328 | tf_op jit(solution)/shard_map/ppermute | solution.py:546
  149.9 19.9 %collective-permute-start.13 = (f32[16,128]{1,0:T(8,128)S(1)}, f32[16,128]{1,0:T(8,128)S(1)}, u32[]{:S(2)}, u32[]{:S(2)}) collective-permute-start(f32[16,128]{1,0:T(8,128)S(1)} %join_norms.1), channel_id=1, source_target_pairs={{8,0},{12,4},{16,24},{20,28},{9,1},{13,5},{17,25},{21,29},{10,2},{... | collective-permute-start | bytes 24584 | tf_op jit(solution)/shard_map/ppermute | solution.py:546
  151.2 49.2 %collective-permute-start.19 = (bf16[1040,768]{1,0:T(8,128)(2,1)}, bf16[1040,768]{1,0:T(8,128)(2,1)}, u32[]{:S(2)}, u32[]{:S(2)}) collective-permute-start(bf16[1040,768]{1,0:T(8,128)(2,1)} %add_sums.5), channel_id=1, source_target_pairs={{8,16},{12,20},{16,8},{20,12},{9,17},{13,21},{17,9},{21,13},{10,18... | collective-permute-start | bytes 4792328 | tf_op jit(solution)/shard_map/ppermute | solution.py:546
  157.2 41.3 %collective-permute-start.18 = (bf16[1040,768]{1,0:T(8,128)(2,1)}, bf16[1040,768]{1,0:T(8,128)(2,1)}, u32[]{:S(2)}, u32[]{:S(2)}) collective-permute-start(bf16[1040,768]{1,0:T(8,128)(2,1)} %moments.13), channel_id=1, source_target_pairs={{8,12},{12,8},{16,20},{20,16},{9,13},{13,9},{17,21},{21,17},{10,14... | collective-permute-start | bytes 4792328 | tf_op jit(solution)/shard_map/ppermute | solution.py:546
  169.9 13.2 %copy-start.19 = (f32[16,128]{1,0:T(8,128)}, f32[16,128]{1,0:T(8,128)S(1)}, u32[]{:S(2)}) copy-start(f32[16,128]{1,0:T(8,128)S(1)} %collective-permute-done.13.end_norm) | copy-start | bytes 24580
  185.0 41.6 %collective-permute-start.17 = (bf16[1040,768]{1,0:T(8,128)(2,1)}, bf16[1040,768]{1,0:T(8,128)(2,1)}, u32[]{:S(2)}, u32[]{:S(2)}) collective-permute-start(bf16[1040,768]{1,0:T(8,128)(2,1)} %add_sums.6), channel_id=1, source_target_pairs={{8,0},{12,4},{16,24},{20,28},{9,1},{13,5},{17,25},{21,29},{10,2},{... | collective-permute-start | bytes 4792328 | tf_op jit(solution)/shard_map/ppermute | solution.py:546
  198.5 28.0 %copy-start.20 = (f32[16,128]{1,0:T(8,128)S(1)}, f32[16,128]{1,0:T(8,128)}, u32[]{:S(2)}) copy-start(f32[16,128]{1,0:T(8,128)} %copy-done.19) | copy-start | bytes 24580
  (12 other events, 20.2 us)

commit v11 on v9

--- a/solution.py
+++ b/solution.py
@@ -155,6 +155,104 @@
             resp_ref[i, slot] = resp[slot * CB : (slot + 1) * CB]
 
 
+def is_one_of(shard, shards):
+    return functools.reduce(jnp.logical_or, [shard == j for j in shards])
+
+
+def slot_density(weight_ref, pos, held, x, half, pieces):
+    owned = held * CB
+    shard = lax.div(pos, held)
+    here = pl.ds(pl.multiple_of(lax.rem(pos, held) * CB, CB), CB)
+    linear = lax.dot_general(
+        weight_ref[shard, 0, here, :], x, NT, preferred_element_type=jnp.float32
+    )
+    quadratic = lax.dot_general(
+        weight_ref[shard, 1, here, :], half, NT, preferred_element_type=jnp.float32
+    )
+    constant = lax.dot_general(
+        weight_ref[shard, 0, owned:, here], pieces, TN, preferred_element_type=jnp.float32
+    )
+    return linear + quadratic + constant
+
+
+def piece_mask():
+    row_index = lax.broadcasted_iota(jnp.int32, (META, RB), 0)
+    return jnp.where(row_index < 3, 1.0, 0.0).astype(jnp.bfloat16)
+
+
+def early_body(count, held, near, pos_ref, x_ref, weight_ref, density_ref):
+    pieces = piece_mask()
+
+    @pl.loop(0, count)
+    def _(i):
+        x = x_ref[pl.ds(pl.multiple_of(i * RB, RB), RB), :]
+        half = x * x * -0.5
+        for slot in range(CANDS):
+            pos = pos_ref[i * CANDS + slot]
+
+            @pl.when(is_one_of(lax.div(pos, held), near))
+            def _(pos=pos, slot=slot):
+                density_ref[i, slot] = slot_density(weight_ref, pos, held, x, half, pieces)
+
+
+def late_body(count, held, near, pos_ref, x_ref, weight_ref, _, density_ref, resp_ref, norm_ref):
+    pieces = piece_mask()
+
+    @pl.loop(0, count)
+    def _(i):
+        x = x_ref[pl.ds(pl.multiple_of(i * RB, RB), RB), :]
+        half = x * x * -0.5
+        for slot in range(CANDS):
+            pos = pos_ref[i * CANDS + slot]
+
+            @pl.when(jnp.logical_not(is_one_of(lax.div(pos, held), near)))
+            def _(pos=pos, slot=slot):
+                density_ref[i, slot] = slot_density(weight_ref, pos, held, x, half, pieces)
+
+        densities = [density_ref[i, slot] for slot in range(CANDS)]
+        peak = functools.reduce(
+            jnp.maximum, [jnp.max(d, axis=0, keepdims=True) for d in densities]
+        )
+        terms = [jnp.exp(d - peak) for d in densities]
+        total = functools.reduce(jnp.add, [jnp.sum(t, axis=0, keepdims=True) for t in terms])
+        norm_ref[pl.ds(i, 1), :] = peak + jnp.log(total)
+        inverse_total = 1.0 / total
+        for slot in range(CANDS):
+            resp_ref[i, slot] = (terms[slot] * inverse_total).astype(jnp.bfloat16)
+
+
+def early_densities(rows, pos, weights, held, near):
+    count = rows.shape[0] // RB
+    vmem = pl.BlockSpec(memory_space=pltpu.VMEM)
+    return pl.pallas_call(
+        functools.partial(early_body, count, held, near),
+        in_specs=[pl.BlockSpec(memory_space=pltpu.SMEM), vmem, vmem],
+        out_specs=vmem,
+        out_shape=pltpu.VMEM((count, CANDS, CB, RB), jnp.float32),
+        compiler_params=pltpu.CompilerParams(vmem_limit_bytes=VMEM_LIMIT),
+        name="early_densities",
+    )(pos, in_vmem(rows), in_vmem(weights))
+
+
+def late_responsibilities(rows, pos, weights, held, near, densities):
+    count = rows.shape[0] // RB
+    vmem = pl.BlockSpec(memory_space=pltpu.VMEM)
+    outs = pl.pallas_call(
+        functools.partial(late_body, count, held, near),
+        in_specs=[pl.BlockSpec(memory_space=pltpu.SMEM), vmem, vmem, vmem],
+        out_specs=[vmem] * 3,
+        out_shape=[
+            pltpu.VMEM(densities.shape, jnp.float32),
+            pltpu.VMEM((count, CANDS, CB, RB), jnp.bfloat16),
+            pltpu.VMEM((count, RB), jnp.float32),
+        ],
+        input_output_aliases={3: 0},
+        compiler_params=pltpu.CompilerParams(vmem_limit_bytes=VMEM_LIMIT),
+        name="late_responsibilities",
+    )(pos, in_vmem(rows), in_vmem(weights), in_vmem(densities))
+    return outs[1:]
+
+
 def responsibilities(rows, pos, first, weights, held):
     count = rows.shape[0] // RB
     feature_count = rows.shape[1]
@@ -519,15 +617,16 @@
     )
     near = [after(weights, pos, order, starts), own_shared, outer, across]
     near_weights = stacked(8, (0, 1, 2, 4), near)
-    far, near_weights = lax.optimization_barrier((far, near_weights))
+    near_places = (0, 1, 2, 4)
+    densities = early_densities(points, pos, near_weights, held, near_places)
+    far, near_weights, densities = lax.optimization_barrier((far, near_weights, densities))
     shared = [move(w, CORES) for w in (outer, across, far)]
     all_weights = stacked(8, (6, 3, 5, 7), [after(far, most)] + shared, near_weights)
 
     rows = [points] + moved
-    results = []
-    for j, run_rows in enumerate(rows):
-        if results:
-            pos = after(pos, results[-1][1])
+    results = [late_responsibilities(points, pos, all_weights, held, near_places, densities)]
+    for j, run_rows in enumerate(rows[1:], 1):
+        pos = after(pos, results[-1][1])
         results.append(responsibilities(run_rows, pos, sum(runs[:j]), all_weights, held))
     resp = [r[0] for r in results]
 
@@ -551,11 +650,11 @@
     own_received = move(own_other, CORES)
     outer_own = sums_of(2, own_other, end_norm)
     own_own = sums_of(0, outer_own)
-    outer_sum = added(outer_own, outer_received, far_sum)
+    outer_sum = added(added(outer_own, outer_received), far_sum)
     end_sum = move(outer_sum, OUTWARD)
     is_end = jnp.logical_or(chip == 0, chip == 3)
     counts, first, second, loglik = results_of(
-        is_end, results[0][1], end_norm, end_sum, own_own, own_received, across_sum
+        is_end, results[0][1], end_norm, end_sum, added(own_own, own_received), across_sum
     )
     return counts.reshape(-1), first, second, loglik.reshape(-1)
 

time: 228 us -> 246 us (1.079)
  Pallas kernels: 81.6 us -> 103 us
  starting transfers between devices: 63.8 us -> 45.8 us
  waiting for transfers between devices: 67.2 us -> 79 us
    pallas_call x0 -> x2, Pallas kernels: none -> 24.8 us  [the longest x1 12.9 us: early_densities(): pl.pallas_call(functools.partial(early_body, count, held, near), in_specs...]
    ppermute x20, starting transfers between devices: 63.8 us -> 45.8 us  [move(): return lax.ppermute(value, 'dp', pairs)]
    ppermute x20, waiting for transfers between devices: 67.2 us -> 79 us  [move(): return lax.ppermute(value, 'dp', pairs)]
    pallas_call x5 -> x4, Pallas kernels: 26 us -> 14.8 us  [responsibilities(): pl.pallas_call(functools.partial(density_body, first, count, held), in_sp...]
    pallas_call x8, Pallas kernels: 30.9 us -> 37.9 us  [moments(): pl.pallas_call(functools.partial(moment_body, tuple(shards), held, runs),...]
    pallas_call x4 -> x6, Pallas kernels: 3.97 us -> 5.94 us  [small_step(): pl.pallas_call(body, in_specs=[vmem] * len(operands), out_specs=vmem, out...]
    unnamed x48 -> x50, local copies, waits for them, and re-layouts: 12.2 us -> 14.1 us
  transfers between devices with their start and end apart: 20 -> 20, of which waited for: 3 -> 3; matrix products, arithmetic and copies ran while one was open for 0% -> 0% of each run, Pallas kernels for 30% -> 35%
where the time goes in v11:
time: 246 us; the launch traced here: 245 us
  Pallas kernels  103 us (42%)
  waiting for transfers between devices  79 us (32%)
  starting transfers between devices  45.8 us (19%)
  local copies, waits for them, and re-layouts  15.8 us (6%)
    ppermute x20, waiting for transfers between devices, move(): return lax.ppermute(value, 'dp', pairs)  79 us
    ppermute x20, starting transfers between devices, move(): return lax.ppermute(value, 'dp', pairs)  45.8 us
    pallas_call x8, Pallas kernels, moments(): pl.pallas_call(functools.partial(moment_body, tuple(shards), held, runs),...  37.9 us
    pallas_call x4, Pallas kernels, responsibilities(): pl.pallas_call(functools.partial(density_body, first, count, held), in_sp...  14.8 us
    unnamed x50, local copies, waits for them, and re-layouts  14.1 us
    pallas_call x1, Pallas kernels, early_densities(): pl.pallas_call(functools.partial(early_body, count, held, near), in_specs...  12.9 us
    pallas_call x1, Pallas kernels, late_responsibilities(): pl.pallas_call(functools.partial(late_body, count, held, near), in_specs=...  12 us
    pallas_call x1, Pallas kernels, pair_lists(): pl.pallas_call(functools.partial(list_body, tuple(runs), held, owners, pl...  6.01 us
  transfers between devices with their start and end apart: 20, of which 3 were waited for; matrix products, arithmetic and copies ran while one was open for 0% of the time, Pallas kernels for 35%

profile of v11, /device:TPU:0, one launch (start us, length us, event | category | flops | bytes accessed | tf_op | source)
XLA Modules:
  0.0 245.2 jit_solution(2174854533985167480)
XLA Ops:
  1.6 4.9 %collective-permute-start.1 = (bf16[128,768]{1,0:T(8,128)(2,1)S(1)}, bf16[128,768]{1,0:T(8,128)(2,1)S(1)}, u32[]{:S(2)}, u32[]{:S(2)}) collective-permute-start(bf16[128,768]{1,0:T(8,128)(2,1)S(1)} %slice.3), channel_id=1, source_target_pairs={{0,8},{4,12},{24,16},{28,20},{1,9},{5,13},{25,17},{29,21},{2,10},{... | collective-permute-start | bytes 589832 | tf_op jit(solution)/shard_map/ppermute | solution.py:580
  8.5 2.8 %parameter_shard.1.refs_0_ = bf16[1,2,528,768]{3,2,1,0:T(8,128)(2,1)S(1)} custom-call(bf16[512,768]{1,0:T(8,128)(2,1)} %means_hbm.1, bf16[512,768]{1,0:T(8,128)(2,1)} %inv_hbm.1, bf16[1,512]{1,0:T(2,128)(2,1)S(1)} %reshape.32.log_ref), custom_call_target="tpu_custom_call" | custom-call | flops 15728640 | bytes 3145728 | tf_op jit(solution)/shard_map/parameter_shard/pallas_call | solution.py:68
  12.1 4.9 %collective-permute-start.2 = (bf16[1,2,528,768]{3,2,1,0:T(8,128)(2,1)S(1)}, bf16[1,2,528,768]{3,2,1,0:T(8,128)(2,1)}, u32[]{:S(2)}, u32[]{:S(2)}) collective-permute-start(bf16[1,2,528,768]{3,2,1,0:T(8,128)(2,1)S(1)} %parameter_shard.1.refs_0_), channel_id=1, source_target_pairs={{0,8},{4,12},{24,16},{28,20},{1,9},{5,13},{25,17},{29,21},{2,10},{... | collective-permute-start | bytes 4866056 | tf_op jit(solution)/shard_map/ppermute | solution.py:580
  16.9 1.8 collective-permute-start.5
  18.8 3.1 %cut_rows.1 = (bf16[1152,768]{1,0:T(8,128)(2,1)}, bf16[512,768]{1,0:T(8,128)(2,1)}, bf16[256,768]{1,0:T(8,128)(2,1)}) custom-call(bf16[2048,768]{1,0:T(8,128)(2,1)} %rest_0_.15), custom_call_target="tpu_custom_call" | custom-call | tf_op jit(solution)/shard_map/cut_rows/pallas_call | solution.py:113
  23.8 25.8 %collective-permute-done.2.refs_2_ = bf16[1,2,528,768]{3,2,1,0:T(8,128)(2,1)} collective-permute-done((bf16[1,2,528,768]{3,2,1,0:T(8,128)(2,1)S(1)}, bf16[1,2,528,768]{3,2,1,0:T(8,128)(2,1)}, u32[]{:S(2)}, u32[]{:S(2)}) %collective-permute-start.2) | collective-permute-done | bytes 1622048 | tf_op jit(solution)/shard_map/ppermute | solution.py:580
  49.6 1.9 collective-permute-start.3
  51.5 7.3 %collective-permute-start.6 = (bf16[1152,768]{1,0:T(8,128)(2,1)}, bf16[1152,768]{1,0:T(8,128)(2,1)}, u32[]{:S(2)}, u32[]{:S(2)}) collective-permute-start(bf16[1152,768]{1,0:T(8,128)(2,1)} %get-tuple-element.62), channel_id=1, source_target_pairs={{0,8},{4,12},{24,16},{28,20},{1,9},{5,13},{25,17},{29,21},{2,10},{... | collective-permute-start | bytes 5308424 | tf_op jit(solution)/shard_map/ppermute | solution.py:580
  58.8 6.0 %pair_lists.1 = (s32[128]{0:T(128)S(1)}, s32[128]{0:T(128)S(1)}, s32[161]{0:T(256)S(1)}) custom-call(s32[1]{0:T(128)} %bitcast.1.rest_0_, s32[1]{0:T(128)} %bitcast.2.rest_1_, s32[4,16]{1,0:T(4,128)S(1)} %bitcast.7, s32[4,16]{1,0:T(4,128)S(1)} %collective-permute-done.rest_3_), custom_call_target="tpu_custom_call" | custom-call | tf_op jit(solution)/shard_map/pair_lists/pallas_call | solution.py:327
  69.6 2.4 stack_shards.2.weight_ref.refs_0_
  72.5 12.9 %early_densities.1._ = f32[16,4,128,128]{3,2,1,0:T(8,128)S(1)} custom-call(s32[128]{0:T(128)S(1)} %get-tuple-element.74.pos_ref, bf16[2048,768]{1,0:T(8,128)(2,1)S(1)} %copy-done, bf16[8,2,528,768]{3,2,1,0:T(8,128)(2,1)S(1)} %stack_shards.2.weight_ref.refs_0_), custom_call_target="tpu_custom_call" | custom-call | tf_op jit(solution)/shard_map/early_densities/pallas_call | solution.py:227
  86.9 6.7 %collective-permute-start.10 = (bf16[512,768]{1,0:T(8,128)(2,1)S(1)}, bf16[512,768]{1,0:T(8,128)(2,1)S(1)}, u32[]{:S(2)}, u32[]{:S(2)}) collective-permute-start(bf16[512,768]{1,0:T(8,128)(2,1)S(1)} %copy-done.23), channel_id=1, source_target_pairs={{0,8},{4,12},{24,16},{28,20},{1,9},{5,13},{25,17},{29,21},{2,10},{... | collective-permute-start | bytes 2359304 | tf_op jit(solution)/shard_map/ppermute | solution.py:580
  93.7 4.4 %collective-permute-start.11 = (bf16[256,768]{1,0:T(8,128)(2,1)S(1)}, bf16[256,768]{1,0:T(8,128)(2,1)S(1)}, u32[]{:S(2)}, u32[]{:S(2)}) collective-permute-start(bf16[256,768]{1,0:T(8,128)(2,1)S(1)} %copy-done.24), channel_id=1, source_target_pairs={{0,8},{4,12},{24,16},{28,20},{1,9},{5,13},{25,17},{29,21},{2,10},{... | collective-permute-start | bytes 1179656 | tf_op jit(solution)/shard_map/ppermute | solution.py:580
  99.6 12.0 %late_responsibilities.1 = (f32[16,4,128,128]{3,2,1,0:T(8,128)S(1)}, bf16[16,4,128,128]{3,2,1,0:T(8,128)(2,1)S(1)}, f32[16,128]{1,0:T(8,128)S(1)}) custom-call(s32[128]{0:T(128)S(1)} %get-tuple-element.74.pos_ref, bf16[2048,768]{1,0:T(8,128)(2,1)S(1)} %copy-done, ...), custom_call_target="tpu_custom_call", output_to_operand_aliasing={{0}: (3, {})} | custom-call | tf_op jit(solution)/shard_map/late_responsibilities/pallas_call | solution.py:240
  112.9 8.1 %responsibilities.5 = (bf16[9,4,128,128]{3,2,1,0:T(8,128)(2,1)S(1)}, f32[9,128]{1,0:T(8,128)S(1)}) custom-call(s32[128]{0:T(128)S(1)} %get-tuple-element.74.pos_ref, bf16[1152,768]{1,0:T(8,128)(2,1)} %collective-permute-done.6.x_ref.rest_2_, bf16[8,2,528,768]{3,2,1,0:T(8,128)(2,1)S(1)} %stack_shards.3.weight_ref), custom_call_target="tpu_custom_call" | custom-call | flops 1811939328 | bytes 15925248 | tf_op jit(solution)/shard_map/responsibilities/pallas_call | solution.py:261
  121.0 3.5 %responsibilities.6 = (bf16[4,4,128,128]{3,2,1,0:T(8,128)(2,1)S(1)}, f32[4,128]{1,0:T(4,128)S(1)}) custom-call(s32[128]{0:T(128)S(1)} %get-tuple-element.74.pos_ref, bf16[512,768]{1,0:T(8,128)(2,1)S(1)} %collective-permute-done.10.x_ref.rest_3_, bf16[8,2,528,768]{3,2,1,0:T(8,128)(2,1)S(1)} %stack_shards.3.weight_ref), custom_call_target="tpu_custom_call" | custom-call | flops 805306368 | bytes 7077888 | tf_op jit(solution)/shard_map/responsibilities/pallas_call | solution.py:261
  124.5 2.0 responsibilities.7
  126.5 3.3 %moments.8 = bf16[1040,768]{1,0:T(8,128)(2,1)S(1)} custom-call(s32[128]{0:T(128)S(1)} %get-tuple-element.89.order_ref, s32[161]{0:T(256)S(1)} %get-tuple-element.53.start_ref, bf16[2048,768]{1,0:T(8,128)(2,1)S(1)} %copy-done, bf16[128,768]{1,0:T(8,128)(2,1)S(1)} %copy-done.12, bf16[1152,768]{1,0:T(8,128)(2,1)} %collective-permute-done.6.x_ref.rest_2_, ...), custom_call_target="tpu_custom_call" | custom-call | flops 805306368 | bytes 3670016 | tf_op jit(solution)/shard_map/moments/pallas_call | solution.py:400
  130.6 3.5 %moments.9.refs_0_ = bf16[1040,768]{1,0:T(8,128)(2,1)S(1)} custom-call(s32[128]{0:T(128)S(1)} %get-tuple-element.89.order_ref, s32[161]{0:T(256)S(1)} %get-tuple-element.53.start_ref, bf16[2048,768]{1,0:T(8,128)(2,1)S(1)} %copy-done, bf16[128,768]{1,0:T(8,128)(2,1)S(1)} %copy-done.12, bf16[1152,768]{1,0:T(8,128)(2,1)} %collective-permute-done.6.x_ref.rest_2_, ...), custom_call_target="tpu_custom_call" | custom-call | flops 805306368 | bytes 3670016 | tf_op jit(solution)/shard_map/moments/pallas_call | solution.py:400
  134.5 2.9 %moments.10 = bf16[1040,768]{1,0:T(8,128)(2,1)S(1)} custom-call(s32[128]{0:T(128)S(1)} %get-tuple-element.89.order_ref, s32[161]{0:T(256)S(1)} %get-tuple-element.53.start_ref, bf16[2048,768]{1,0:T(8,128)(2,1)S(1)} %copy-done, bf16[128,768]{1,0:T(8,128)(2,1)S(1)} %copy-done.12, bf16[1152,768]{1,0:T(8,128)(2,1)} %collective-permute-done.6.x_ref.rest_2_, ...), custom_call_target="tpu_custom_call" | custom-call | flops 805306368 | bytes 3670016 | tf_op jit(solution)/shard_map/moments/pallas_call | solution.py:400
  138.4 3.8 %moments.11.refs_0_ = bf16[1040,768]{1,0:T(8,128)(2,1)S(1)} custom-call(s32[128]{0:T(128)S(1)} %get-tuple-element.89.order_ref, s32[161]{0:T(256)S(1)} %get-tuple-element.53.start_ref, bf16[2048,768]{1,0:T(8,128)(2,1)S(1)} %copy-done, bf16[128,768]{1,0:T(8,128)(2,1)S(1)} %copy-done.12, bf16[1152,768]{1,0:T(8,128)(2,1)} %collective-permute-done.6.x_ref.rest_2_, ...), custom_call_target="tpu_custom_call" | custom-call | flops 805306368 | bytes 3670016 | tf_op jit(solution)/shard_map/moments/pallas_call | solution.py:400
  143.8 3.5 %moments.12 = bf16[1040,768]{1,0:T(8,128)(2,1)S(1)} custom-call(s32[128]{0:T(128)S(1)} %get-tuple-element.89.order_ref, s32[161]{0:T(256)S(1)} %get-tuple-element.53.start_ref, bf16[2048,768]{1,0:T(8,128)(2,1)S(1)} %copy-done, bf16[128,768]{1,0:T(8,128)(2,1)S(1)} %copy-done.12, bf16[1152,768]{1,0:T(8,128)(2,1)} %collective-permute-done.6.x_ref.rest_2_, ...), custom_call_target="tpu_custom_call" | custom-call | flops 805306368 | bytes 3670016 | tf_op jit(solution)/shard_map/moments/pallas_call | solution.py:400
  150.2 1.8 collective-permute-start.19
  152.0 4.7 %moments.13 = bf16[1040,768]{1,0:T(8,128)(2,1)} custom-call(s32[128]{0:T(128)S(1)} %get-tuple-element.89.order_ref, s32[161]{0:T(256)S(1)} %get-tuple-element.53.start_ref, bf16[2048,768]{1,0:T(8,128)(2,1)S(1)} %copy-done, bf16[128,768]{1,0:T(8,128)(2,1)S(1)} %copy-done.12, bf16[1152,768]{1,0:T(8,128)(2,1)} %collective-permute-done.6.x_ref.rest_2_, ...), custom_call_target="tpu_custom_call" | custom-call | flops 805306368 | bytes 3670016 | tf_op jit(solution)/shard_map/moments/pallas_call | solution.py:400
  156.7 1.8 collective-permute-start.18
  158.5 11.7 %collective-permute-done.13.refs_1_ = f32[16,128]{1,0:T(8,128)S(1)} collective-permute-done((f32[16,128]{1,0:T(8,128)S(1)}, f32[16,128]{1,0:T(8,128)S(1)}, u32[]{:S(2)}, u32[]{:S(2)}) %collective-permute-start.13) | collective-permute-done | bytes 8224 | tf_op jit(solution)/shard_map/ppermute | solution.py:580
  170.3 13.3 %moments.14.refs_0_ = bf16[1040,768]{1,0:T(8,128)(2,1)S(1)} custom-call(s32[128]{0:T(128)S(1)} %get-tuple-element.89.order_ref, s32[161]{0:T(256)S(1)} %get-tuple-element.53.start_ref, bf16[2048,768]{1,0:T(8,128)(2,1)S(1)} %copy-done, bf16[128,768]{1,0:T(8,128)(2,1)S(1)} %copy-done.12, bf16[1152,768]{1,0:T(8,128)(2,1)} %collective-permute-done.6.x_ref.rest_2_, ...), custom_call_target="tpu_custom_call" | custom-call | flops 805306368 | bytes 3670016 | tf_op jit(solution)/shard_map/moments/pallas_call | solution.py:400
  184.0 1.6 add_sums.8
  194.8 2.9 %moments.15.refs_0_ = bf16[1040,768]{1,0:T(8,128)(2,1)S(1)} custom-call(s32[128]{0:T(128)S(1)} %get-tuple-element.89.order_ref, s32[161]{0:T(256)S(1)} %get-tuple-element.53.start_ref, bf16[2048,768]{1,0:T(8,128)(2,1)S(1)} %copy-done, bf16[128,768]{1,0:T(8,128)(2,1)S(1)} %copy-done.13, bf16[1152,768]{1,0:T(8,128)(2,1)} %collective-permute-done.6.x_ref.rest_2_, ...), custom_call_target="tpu_custom_call" | custom-call | flops 805306368 | bytes 3670016 | tf_op jit(solution)/shard_map/moments/pallas_call | solution.py:400
  197.7 1.8 add_sums.9.refs_3_
  199.6 41.5 %collective-permute-done.17.refs_2_ = bf16[1040,768]{1,0:T(8,128)(2,1)} collective-permute-done((bf16[1040,768]{1,0:T(8,128)(2,1)}, bf16[1040,768]{1,0:T(8,128)(2,1)}, u32[]{:S(2)}, u32[]{:S(2)}) %collective-permute-start.17) | collective-permute-done | bytes 1597472 | tf_op jit(solution)/shard_map/ppermute | solution.py:580
  241.0 4.0 %results.1 = (f32[1,512]{1,0:T(1,128)}, f32[512,768]{1,0:T(8,128)}, f32[512,768]{1,0:T(8,128)}, f32[16,128]{1,0:T(8,128)}) custom-call(s32[1]{0:T(128)} %bitcast.end_ref, f32[16,128]{1,0:T(8,128)S(1)} %get-tuple-element.65.refs_0_, f32[16,128]{1,0:T(8,128)S(1)} %copy-done.21, bf16[1040,768]{1,0:T(8,128)(2,1)} %collective-permute-done.17.refs_2_, ...), custom_call_target="tpu_custom_call" | custom-call | tf_op jit(solution)/shard_map/results/pallas_call | solution.py:523
  (86 shorter events, 31.2 us)
Async XLA Ops:
  1.6 9.8 %collective-permute-start.1 = (bf16[128,768]{1,0:T(8,128)(2,1)S(1)}, bf16[128,768]{1,0:T(8,128)(2,1)S(1)}, u32[]{:S(2)}, u32[]{:S(2)}) collective-permute-start(bf16[128,768]{1,0:T(8,128)(2,1)S(1)} %slice.3), channel_id=1, source_target_pairs={{0,8},{4,12},{24,16},{28,20},{1,9},{5,13},{25,17},{29,21},{2,10},{... | collective-permute-start | bytes 589832 | tf_op jit(solution)/shard_map/ppermute | solution.py:580
  6.5 4.8 %collective-permute-start = (s32[4,16]{1,0:T(4,128)}, s32[4,16]{1,0:T(4,128)S(1)}, u32[]{:S(2)}, u32[]{:S(2)}) collective-permute-start(s32[4,16]{1,0:T(4,128)} %bitcast.6), channel_id=1, source_target_pairs={{0,8},{4,12},{24,16},{28,20},{1,9},{5,13},{25,17},{29,21},{2,10},{... | collective-permute-start | bytes 776 | tf_op jit(solution)/shard_map/ppermute | solution.py:580
  11.3 47.5 %copy-start.22 = (s32[16,4]{0,1:T(4,128)S(1)}, s32[16,4]{0,1:T(4,128)}, u32[]{:S(2)}) copy-start(s32[16,4]{0,1:T(4,128)} %param.6) | copy-start | bytes 772
  12.1 37.5 %collective-permute-start.2 = (bf16[1,2,528,768]{3,2,1,0:T(8,128)(2,1)S(1)}, bf16[1,2,528,768]{3,2,1,0:T(8,128)(2,1)}, u32[]{:S(2)}, u32[]{:S(2)}) collective-permute-start(bf16[1,2,528,768]{3,2,1,0:T(8,128)(2,1)S(1)} %parameter_shard.1.refs_0_), channel_id=1, source_target_pairs={{0,8},{4,12},{24,16},{28,20},{1,9},{5,13},{25,17},{29,21},{2,10},{... | collective-permute-start | bytes 4866056 | tf_op jit(solution)/shard_map/ppermute | solution.py:580
  16.9 47.9 %collective-permute-start.5 = (bf16[1,2,528,768]{3,2,1,0:T(8,128)(2,1)S(1)}, bf16[1,2,528,768]{3,2,1,0:T(8,128)(2,1)}, u32[]{:S(2)}, u32[]{:S(2)}) collective-permute-start(bf16[1,2,528,768]{3,2,1,0:T(8,128)(2,1)S(1)} %parameter_shard.1.refs_0_), channel_id=1, source_target_pairs={{8,16},{12,20},{16,8},{20,12},{9,17},{13,21},{17,9},{21,13},{10,18... | collective-permute-start | bytes 4866056 | tf_op jit(solution)/shard_map/ppermute | solution.py:580
  21.9 43.7 %collective-permute-start.4 = (bf16[1,2,528,768]{3,2,1,0:T(8,128)(2,1)S(1)}, bf16[1,2,528,768]{3,2,1,0:T(8,128)(2,1)S(1)}, u32[]{:S(2)}, u32[]{:S(2)}) collective-permute-start(bf16[1,2,528,768]{3,2,1,0:T(8,128)(2,1)S(1)} %parameter_shard.1.refs_0_), channel_id=1, source_target_pairs={{8,12},{12,8},{16,20},{20,16},{9,13},{13,9},{17,21},{21,17},{10,14... | collective-permute-start | bytes 4866056 | tf_op jit(solution)/shard_map/ppermute | solution.py:580
  49.6 36.6 %collective-permute-start.3 = (bf16[1,2,528,768]{3,2,1,0:T(8,128)(2,1)}, bf16[1,2,528,768]{3,2,1,0:T(8,128)(2,1)}, u32[]{:S(2)}, u32[]{:S(2)}) collective-permute-start(bf16[1,2,528,768]{3,2,1,0:T(8,128)(2,1)} %collective-permute-done.2.refs_2_), channel_id=1, source_target_pairs={{8,16},{12,20},{16,8},{20,12},{9,17},{13,21},{17,9},{21,13},{10,18... | collective-permute-start | bytes 4866056 | tf_op jit(solution)/shard_map/ppermute | solution.py:580
  51.5 42.2 %collective-permute-start.6 = (bf16[1152,768]{1,0:T(8,128)(2,1)}, bf16[1152,768]{1,0:T(8,128)(2,1)}, u32[]{:S(2)}, u32[]{:S(2)}) collective-permute-start(bf16[1152,768]{1,0:T(8,128)(2,1)} %get-tuple-element.62), channel_id=1, source_target_pairs={{0,8},{4,12},{24,16},{28,20},{1,9},{5,13},{25,17},{29,21},{2,10},{... | collective-permute-start | bytes 5308424 | tf_op jit(solution)/shard_map/ppermute | solution.py:580
  64.8 33.2 %collective-permute-start.8 = (bf16[1,2,528,768]{3,2,1,0:T(8,128)(2,1)}, bf16[1,2,528,768]{3,2,1,0:T(8,128)(2,1)S(1)}, u32[]{:S(2)}, u32[]{:S(2)}) collective-permute-start(bf16[1,2,528,768]{3,2,1,0:T(8,128)(2,1)} %collective-permute-done.5.refs_3_), channel_id=1, source_target_pairs={{8,12},{12,8},{16,20},{20,16},{9,13},{13,9},{17,21},{21,17},{10,14... | collective-permute-start | bytes 4866056 | tf_op jit(solution)/shard_map/ppermute | solution.py:580
  72.5 14.4 %copy-start.23 = (bf16[512,768]{1,0:T(8,128)(2,1)S(1)}, bf16[512,768]{1,0:T(8,128)(2,1)}, u32[]{:S(2)}) copy-start(bf16[512,768]{1,0:T(8,128)(2,1)} %get-tuple-element.72) | copy-start | bytes 2359300
  72.5 21.2 %copy-start.24 = (bf16[256,768]{1,0:T(8,128)(2,1)S(1)}, bf16[256,768]{1,0:T(8,128)(2,1)}, u32[]{:S(2)}) copy-start(bf16[256,768]{1,0:T(8,128)(2,1)} %get-tuple-element.75) | copy-start | bytes 1179652
  85.4 12.7 %collective-permute-start.7 = (bf16[1,2,528,768]{3,2,1,0:T(8,128)(2,1)}, bf16[1,2,528,768]{3,2,1,0:T(8,128)(2,1)S(1)}, u32[]{:S(2)}, u32[]{:S(2)}) collective-permute-start(bf16[1,2,528,768]{3,2,1,0:T(8,128)(2,1)} %collective-permute-done.2.refs_2_), channel_id=1, source_target_pairs={{8,12},{12,8},{16,20},{20,16},{9,13},{13,9},{17,21},{21,17},{10,14... | collective-permute-start | bytes 4866056 | tf_op jit(solution)/shard_map/ppermute | solution.py:580
  86.2 11.9 %collective-permute-start.9 = (bf16[1,2,528,768]{3,2,1,0:T(8,128)(2,1)}, bf16[1,2,528,768]{3,2,1,0:T(8,128)(2,1)S(1)}, u32[]{:S(2)}, u32[]{:S(2)}) collective-permute-start(bf16[1,2,528,768]{3,2,1,0:T(8,128)(2,1)} %collective-permute-done.3.refs_1_), channel_id=1, source_target_pairs={{8,12},{12,8},{16,20},{20,16},{9,13},{13,9},{17,21},{21,17},{10,14... | collective-permute-start | bytes 4866056 | tf_op jit(solution)/shard_map/ppermute | solution.py:580
  86.9 34.0 %collective-permute-start.10 = (bf16[512,768]{1,0:T(8,128)(2,1)S(1)}, bf16[512,768]{1,0:T(8,128)(2,1)S(1)}, u32[]{:S(2)}, u32[]{:S(2)}) collective-permute-start(bf16[512,768]{1,0:T(8,128)(2,1)S(1)} %copy-done.23), channel_id=1, source_target_pairs={{0,8},{4,12},{24,16},{28,20},{1,9},{5,13},{25,17},{29,21},{2,10},{... | collective-permute-start | bytes 2359304 | tf_op jit(solution)/shard_map/ppermute | solution.py:580
  93.7 30.8 %collective-permute-start.11 = (bf16[256,768]{1,0:T(8,128)(2,1)S(1)}, bf16[256,768]{1,0:T(8,128)(2,1)S(1)}, u32[]{:S(2)}, u32[]{:S(2)}) collective-permute-start(bf16[256,768]{1,0:T(8,128)(2,1)S(1)} %copy-done.24), channel_id=1, source_target_pairs={{0,8},{4,12},{24,16},{28,20},{1,9},{5,13},{25,17},{29,21},{2,10},{... | collective-permute-start | bytes 1179656 | tf_op jit(solution)/shard_map/ppermute | solution.py:580
  99.6 12.0 %copy-start.12 = (bf16[128,768]{1,0:T(8,128)(2,1)S(1)}, bf16[128,768]{1,0:T(8,128)(2,1)}, u32[]{:S(2)}) copy-start(bf16[128,768]{1,0:T(8,128)(2,1)} %copy-done.11) | copy-start | bytes 589828
  111.6 58.6 %copy-start.1 = (bf16[16,4,128,128]{3,2,1,0:T(8,128)(2,1)}, bf16[16,4,128,128]{3,2,1,0:T(8,128)(2,1)S(1)}, u32[]{:S(2)}) copy-start(bf16[16,4,128,128]{3,2,1,0:T(8,128)(2,1)S(1)} %get-tuple-element.77.rest_5_) | copy-start | bytes 6291460
  112.9 57.3 %copy-start.14 = (bf16[1,4,128,128]{3,2,1,0:T(8,128)(2,1)}, bf16[1,4,128,128]{3,2,1,0:T(8,128)(2,1)S(1)}, u32[]{:S(2)}) copy-start(bf16[1,4,128,128]{3,2,1,0:T(8,128)(2,1)S(1)} %get-tuple-element.78.rest_6_) | copy-start | bytes 393220
  121.0 49.3 %copy-start.3 = (bf16[9,4,128,128]{3,2,1,0:T(8,128)(2,1)}, bf16[9,4,128,128]{3,2,1,0:T(8,128)(2,1)S(1)}, u32[]{:S(2)}) copy-start(bf16[9,4,128,128]{3,2,1,0:T(8,128)(2,1)S(1)} %get-tuple-element.79.rest_7_) | copy-start | bytes 3538948
  121.0 49.2 %copy-start.5 = (bf16[512,768]{1,0:T(8,128)(2,1)}, bf16[512,768]{1,0:T(8,128)(2,1)S(1)}, u32[]{:S(2)}) copy-start(bf16[512,768]{1,0:T(8,128)(2,1)S(1)} %collective-permute-done.10.x_ref.rest_3_) | copy-start | bytes 2359300
  124.4 45.8 %copy-start.7 = (bf16[4,4,128,128]{3,2,1,0:T(8,128)(2,1)}, bf16[4,4,128,128]{3,2,1,0:T(8,128)(2,1)S(1)}, u32[]{:S(2)}) copy-start(bf16[4,4,128,128]{3,2,1,0:T(8,128)(2,1)S(1)} %get-tuple-element.80.rest_8_) | copy-start | bytes 1572868
  126.5 43.8 %copy-start.9 = (bf16[2,4,128,128]{3,2,1,0:T(8,128)(2,1)}, bf16[2,4,128,128]{3,2,1,0:T(8,128)(2,1)S(1)}, u32[]{:S(2)}) copy-start(bf16[2,4,128,128]{3,2,1,0:T(8,128)(2,1)S(1)} %get-tuple-element.81.rest_9_) | copy-start | bytes 786436
  129.8 4.3 %collective-permute-start.12 = (bf16[1040,768]{1,0:T(8,128)(2,1)S(1)}, bf16[1040,768]{1,0:T(8,128)(2,1)S(1)}, u32[]{:S(2)}, u32[]{:S(2)}) collective-permute-start(bf16[1040,768]{1,0:T(8,128)(2,1)S(1)} %moments.8), channel_id=1, source_target_pairs={{8,12},{12,8},{16,20},{20,16},{9,13},{13,9},{17,21},{21,17},{10,14... | collective-permute-start | bytes 4792328 | tf_op jit(solution)/shard_map/ppermute | solution.py:580
  137.5 4.7 %collective-permute-start.14 = (bf16[1040,768]{1,0:T(8,128)(2,1)S(1)}, bf16[1040,768]{1,0:T(8,128)(2,1)S(1)}, u32[]{:S(2)}, u32[]{:S(2)}) collective-permute-start(bf16[1040,768]{1,0:T(8,128)(2,1)S(1)} %moments.10), channel_id=1, source_target_pairs={{8,12},{12,8},{16,20},{20,16},{9,13},{13,9},{17,21},{21,17},{10,14... | collective-permute-start | bytes 4792328 | tf_op jit(solution)/shard_map/ppermute | solution.py:580
  147.3 36.3 %collective-permute-start.15 = (bf16[1040,768]{1,0:T(8,128)(2,1)S(1)}, bf16[1040,768]{1,0:T(8,128)(2,1)S(1)}, u32[]{:S(2)}, u32[]{:S(2)}) collective-permute-start(bf16[1040,768]{1,0:T(8,128)(2,1)S(1)} %moments.12), channel_id=1, source_target_pairs={{8,12},{12,8},{16,20},{20,16},{9,13},{13,9},{17,21},{21,17},{10,14... | collective-permute-start | bytes 4792328 | tf_op jit(solution)/shard_map/ppermute | solution.py:580
  148.1 35.9 %collective-permute-start.16 = (bf16[1040,768]{1,0:T(8,128)(2,1)S(1)}, bf16[1040,768]{1,0:T(8,128)(2,1)S(1)}, u32[]{:S(2)}, u32[]{:S(2)}) collective-permute-start(bf16[1040,768]{1,0:T(8,128)(2,1)S(1)} %add_sums.5), channel_id=1, source_target_pairs={{8,16},{12,20},{16,8},{20,12},{9,17},{13,21},{17,9},{21,13},{10,18... | collective-permute-start | bytes 4792328 | tf_op jit(solution)/shard_map/ppermute | solution.py:580
  148.9 21.3 %collective-permute-start.13 = (f32[16,128]{1,0:T(8,128)S(1)}, f32[16,128]{1,0:T(8,128)S(1)}, u32[]{:S(2)}, u32[]{:S(2)}) collective-permute-start(f32[16,128]{1,0:T(8,128)S(1)} %join_norms.1), channel_id=1, source_target_pairs={{8,0},{12,4},{16,24},{20,28},{9,1},{13,5},{17,25},{21,29},{10,2},{... | collective-permute-start | bytes 24584 | tf_op jit(solution)/shard_map/ppermute | solution.py:580
  150.2 49.4 %collective-permute-start.19 = (bf16[1040,768]{1,0:T(8,128)(2,1)}, bf16[1040,768]{1,0:T(8,128)(2,1)}, u32[]{:S(2)}, u32[]{:S(2)}) collective-permute-start(bf16[1040,768]{1,0:T(8,128)(2,1)} %add_sums.6), channel_id=1, source_target_pairs={{8,16},{12,20},{16,8},{20,12},{9,17},{13,21},{17,9},{21,13},{10,18... | collective-permute-start | bytes 4792328 | tf_op jit(solution)/shard_map/ppermute | solution.py:580
  156.7 41.0 %collective-permute-start.18 = (bf16[1040,768]{1,0:T(8,128)(2,1)}, bf16[1040,768]{1,0:T(8,128)(2,1)}, u32[]{:S(2)}, u32[]{:S(2)}) collective-permute-start(bf16[1040,768]{1,0:T(8,128)(2,1)} %moments.13), channel_id=1, source_target_pairs={{8,12},{12,8},{16,20},{20,16},{9,13},{13,9},{17,21},{21,17},{10,14... | collective-permute-start | bytes 4792328 | tf_op jit(solution)/shard_map/ppermute | solution.py:580
  170.2 13.3 %copy-start.20 = (f32[16,128]{1,0:T(8,128)}, f32[16,128]{1,0:T(8,128)S(1)}, u32[]{:S(2)}) copy-start(f32[16,128]{1,0:T(8,128)S(1)} %collective-permute-done.13.refs_1_) | copy-start | bytes 24580
  185.6 55.4 %collective-permute-start.17 = (bf16[1040,768]{1,0:T(8,128)(2,1)}, bf16[1040,768]{1,0:T(8,128)(2,1)}, u32[]{:S(2)}, u32[]{:S(2)}) collective-permute-start(bf16[1040,768]{1,0:T(8,128)(2,1)} %add_sums.8), channel_id=1, source_target_pairs={{8,0},{12,4},{16,24},{20,28},{9,1},{13,5},{17,25},{21,29},{10,2},{... | collective-permute-start | bytes 4792328 | tf_op jit(solution)/shard_map/ppermute | solution.py:580
  197.7 43.4 %copy-start.21 = (f32[16,128]{1,0:T(8,128)S(1)}, f32[16,128]{1,0:T(8,128)}, u32[]{:S(2)}) copy-start(f32[16,128]{1,0:T(8,128)} %copy-done.20) | copy-start | bytes 24580
  (13 other events, 16.6 us)

commit v12 on v9

--- a/solution.py
+++ b/solution.py
@@ -367,6 +367,29 @@
     each_chunk(refs[-1].shape[0], step)
 
 
+def add_two_body(a_ref, b_ref, c_ref, d_ref, e_ref, first_ref, second_ref):
+    def step(here):
+        first = a_ref[here, :].astype(jnp.float32) + b_ref[here, :].astype(jnp.float32)
+        first_ref[here, :] = first.astype(jnp.bfloat16)
+        second = c_ref[here, :].astype(jnp.float32) + d_ref[here, :].astype(jnp.float32)
+        second_ref[here, :] = (second + e_ref[here, :].astype(jnp.float32)).astype(jnp.bfloat16)
+
+    each_chunk(first_ref.shape[0], step)
+
+
+def added_two(*terms):
+    vmem = pl.BlockSpec(memory_space=pltpu.VMEM)
+    shape = terms[0].shape
+    return pl.pallas_call(
+        add_two_body,
+        in_specs=[vmem] * 5,
+        out_specs=[vmem] * 2,
+        out_shape=[pltpu.VMEM(shape, jnp.bfloat16)] * 2,
+        compiler_params=pltpu.CompilerParams(vmem_limit_bytes=12 * 1024 * 1024),
+        name="add_both_sums",
+    )(*[in_vmem(value) for value in terms])
+
+
 def join_body(*refs):
     start = 0
     for ref in refs[:-1]:
@@ -540,22 +563,24 @@
     far_part = added(far_own, far_received)
     far_sum = move(far_part, MIDDLE)
     across_other = sums_of(5, far_part)
-    end_norm = move(after(joined(*[r[1] for r in results[1:]]), across_other), OUTWARD)
     across_received = move(across_other, CORES)
-    across_own = sums_of(4, across_other)
-    across_part = added(across_own, across_received)
-    across_sum = move(across_part, MIDDLE)
-    outer_other = sums_of(3, across_part)
+    outer_other = sums_of(3, across_other)
     outer_received = move(outer_other, CORES)
     own_other = sums_of(1, outer_other)
     own_received = move(own_other, CORES)
-    outer_own = sums_of(2, own_other, end_norm)
-    own_own = sums_of(0, outer_own)
-    outer_sum = added(outer_own, outer_received, far_sum)
+    end_norm = move(after(joined(*[r[1] for r in results[1:]]), across_other), OUTWARD)
+    across_own = sums_of(4, own_other)
+    outer_own = sums_of(2, across_own, end_norm)
+    far_sum, outer_own, across_own = lax.optimization_barrier((far_sum, outer_own, across_own))
+    across_part, outer_sum = added_two(
+        across_own, across_received, outer_own, outer_received, far_sum
+    )
+    across_sum = move(across_part, MIDDLE)
     end_sum = move(outer_sum, OUTWARD)
+    own_own = sums_of(0, across_part, outer_sum)
     is_end = jnp.logical_or(chip == 0, chip == 3)
     counts, first, second, loglik = results_of(
-        is_end, results[0][1], end_norm, end_sum, own_own, own_received, across_sum
+        is_end, results[0][1], end_norm, end_sum, added(own_own, own_received), across_sum
     )
     return counts.reshape(-1), first, second, loglik.reshape(-1)
 

time: 228 us -> 225 us (0.987); the launches traced: 228 us -> 222 us
  waiting for transfers between devices: 67.2 us -> 61.1 us
    ppermute x20, waiting for transfers between devices: 67.2 us -> 61.1 us  [move(): return lax.ppermute(value, 'dp', pairs)]
    pallas_call x0 -> x1, Pallas kernels: none -> 2.69 us  [added_two(): pl.pallas_call(add_two_body, in_specs=[vmem] * 5, out_specs=[vmem] * 2, o...]
  transfers between devices with their start and end apart: 20 -> 20, of which waited for: 3 -> 3; matrix products, arithmetic and copies ran while one was open for 0% -> 0% of each run, Pallas kernels for 30% -> 33%
where the time goes in v12:
time: 225 us; the launch traced here: 222 us
  Pallas kernels  81.5 us (36%)
  starting transfers between devices  63.8 us (28%)
  waiting for transfers between devices  61.1 us (27%)
  local copies, waits for them, and re-layouts  13.9 us (6%)
    ppermute x20, starting transfers between devices, move(): return lax.ppermute(value, 'dp', pairs)  63.8 us
    ppermute x20, waiting for transfers between devices, move(): return lax.ppermute(value, 'dp', pairs)  61.1 us
    pallas_call x8, Pallas kernels, moments(): pl.pallas_call(functools.partial(moment_body, tuple(shards), held, runs),...  30.3 us
    pallas_call x5, Pallas kernels, responsibilities(): pl.pallas_call(functools.partial(density_body, first, count, held), in_sp...  26 us
    unnamed x48, local copies, waits for them, and re-layouts  12.3 us
    pallas_call x1, Pallas kernels, pair_lists(): pl.pallas_call(functools.partial(list_body, tuple(runs), held, owners, pl...  6.02 us
  transfers between devices with their start and end apart: 20, of which 3 were waited for; matrix products, arithmetic and copies ran while one was open for 0% of the time, Pallas kernels for 33%

profile of v12, /device:TPU:0, one launch (start us, length us, event | category | flops | bytes accessed | tf_op | source)
XLA Modules:
  0.0 221.7 jit_solution(1831234424550398691)
XLA Ops:
  1.6 4.9 %collective-permute-start.1 = (bf16[128,768]{1,0:T(8,128)(2,1)S(1)}, bf16[128,768]{1,0:T(8,128)(2,1)S(1)}, u32[]{:S(2)}, u32[]{:S(2)}) collective-permute-start(bf16[128,768]{1,0:T(8,128)(2,1)S(1)} %slice.3), channel_id=1, source_target_pairs={{0,8},{4,12},{24,16},{28,20},{1,9},{5,13},{25,17},{29,21},{2,10},{... | collective-permute-start | bytes 589832 | tf_op jit(solution)/shard_map/ppermute | solution.py:505
  8.5 2.8 %parameter_shard.1.refs_0_ = bf16[1,2,528,768]{3,2,1,0:T(8,128)(2,1)S(1)} custom-call(bf16[512,768]{1,0:T(8,128)(2,1)} %means_hbm.1, bf16[512,768]{1,0:T(8,128)(2,1)} %inv_hbm.1, bf16[1,512]{1,0:T(2,128)(2,1)S(1)} %reshape.32.log_ref), custom_call_target="tpu_custom_call" | custom-call | flops 15728640 | bytes 3145728 | tf_op jit(solution)/shard_map/parameter_shard/pallas_call | solution.py:68
  11.4 4.9 %collective-permute-start.2 = (bf16[1,2,528,768]{3,2,1,0:T(8,128)(2,1)S(1)}, bf16[1,2,528,768]{3,2,1,0:T(8,128)(2,1)}, u32[]{:S(2)}, u32[]{:S(2)}) collective-permute-start(bf16[1,2,528,768]{3,2,1,0:T(8,128)(2,1)S(1)} %parameter_shard.1.refs_0_), channel_id=1, source_target_pairs={{0,8},{4,12},{24,16},{28,20},{1,9},{5,13},{25,17},{29,21},{2,10},{... | collective-permute-start | bytes 4866056 | tf_op jit(solution)/shard_map/ppermute | solution.py:505
  16.3 1.8 collective-permute-start.5
  18.1 3.1 %cut_rows.1 = (bf16[1152,768]{1,0:T(8,128)(2,1)}, bf16[512,768]{1,0:T(8,128)(2,1)}, bf16[256,768]{1,0:T(8,128)(2,1)}) custom-call(bf16[2048,768]{1,0:T(8,128)(2,1)} %rest_0_.15), custom_call_target="tpu_custom_call" | custom-call | tf_op jit(solution)/shard_map/cut_rows/pallas_call | solution.py:113
  21.2 1.8 collective-permute-start.4
  23.0 25.9 %collective-permute-done.2.refs_2_ = bf16[1,2,528,768]{3,2,1,0:T(8,128)(2,1)} collective-permute-done((bf16[1,2,528,768]{3,2,1,0:T(8,128)(2,1)S(1)}, bf16[1,2,528,768]{3,2,1,0:T(8,128)(2,1)}, u32[]{:S(2)}, u32[]{:S(2)}) %collective-permute-start.2) | collective-permute-done | bytes 1622048 | tf_op jit(solution)/shard_map/ppermute | solution.py:505
  48.9 1.9 collective-permute-start.3
  50.8 6.2 %collective-permute-start.6 = (bf16[1152,768]{1,0:T(8,128)(2,1)}, bf16[1152,768]{1,0:T(8,128)(2,1)S(1)}, u32[]{:S(2)}, u32[]{:S(2)}) collective-permute-start(bf16[1152,768]{1,0:T(8,128)(2,1)} %get-tuple-element.66), channel_id=1, source_target_pairs={{0,8},{4,12},{24,16},{28,20},{1,9},{5,13},{25,17},{29,21},{2,10},{... | collective-permute-start | bytes 5308424 | tf_op jit(solution)/shard_map/ppermute | solution.py:505
  57.0 6.0 %pair_lists.1 = (s32[128]{0:T(128)S(1)}, s32[128]{0:T(128)S(1)}, s32[161]{0:T(256)S(1)}) custom-call(s32[1]{0:T(128)} %bitcast.1.rest_0_, s32[1]{0:T(128)} %bitcast.2.rest_1_, s32[4,16]{1,0:T(4,128)S(1)} %bitcast.7, s32[4,16]{1,0:T(4,128)S(1)} %collective-permute-done.rest_3_), custom_call_target="tpu_custom_call" | custom-call | tf_op jit(solution)/shard_map/pair_lists/pallas_call | solution.py:229
  64.8 2.6 %stack_shards.2.refs_0_ = bf16[8,2,528,768]{3,2,1,0:T(8,128)(2,1)S(1)} custom-call(bf16[1,2,528,768]{3,2,1,0:T(8,128)(2,1)S(1)} %parameter_shard.1.refs_0_, bf16[1,2,528,768]{3,2,1,0:T(8,128)(2,1)} %collective-permute-done.4.refs_1_, bf16[1,2,528,768]{3,2,1,0:T(8,128)(2,1)} %collective-permute-done.2.refs_2_, ...), custom_call_target="tpu_custom_call" | custom-call | tf_op jit(solution)/shard_map/stack_shards/pallas_call | solution.py:350
  68.2 24.8 %collective-permute-start.10 = (bf16[512,768]{1,0:T(8,128)(2,1)S(1)}, bf16[512,768]{1,0:T(8,128)(2,1)S(1)}, u32[]{:S(2)}, u32[]{:S(2)}) collective-permute-start(bf16[512,768]{1,0:T(8,128)(2,1)S(1)} %copy-done.22), channel_id=1, source_target_pairs={{0,8},{4,12},{24,16},{28,20},{1,9},{5,13},{25,17},{29,21},{2,10},{... | collective-permute-start | bytes 2359304 | tf_op jit(solution)/shard_map/ppermute | solution.py:505
  94.2 4.3 %collective-permute-start.11 = (bf16[256,768]{1,0:T(8,128)(2,1)S(1)}, bf16[256,768]{1,0:T(8,128)(2,1)S(1)}, u32[]{:S(2)}, u32[]{:S(2)}) collective-permute-start(bf16[256,768]{1,0:T(8,128)(2,1)S(1)} %copy-done.23), channel_id=1, source_target_pairs={{0,8},{4,12},{24,16},{28,20},{1,9},{5,13},{25,17},{29,21},{2,10},{... | collective-permute-start | bytes 1179656 | tf_op jit(solution)/shard_map/ppermute | solution.py:505
  100.9 12.2 %responsibilities.5 = (bf16[16,4,128,128]{3,2,1,0:T(8,128)(2,1)S(1)}, f32[16,128]{1,0:T(8,128)S(1)}) custom-call(s32[128]{0:T(128)S(1)} %get-tuple-element.77.pos_ref, bf16[2048,768]{1,0:T(8,128)(2,1)S(1)} %copy-done, bf16[8,2,528,768]{3,2,1,0:T(8,128)(2,1)S(1)} %stack_shards.3.weight_ref), custom_call_target="tpu_custom_call" | custom-call | flops 3221225472 | bytes 28311552 | tf_op jit(solution)/shard_map/responsibilities/pallas_call | solution.py:163
  115.4 7.1 %responsibilities.7 = (bf16[9,4,128,128]{3,2,1,0:T(8,128)(2,1)S(1)}, f32[9,128]{1,0:T(8,128)S(1)}) custom-call(s32[128]{0:T(128)S(1)} %get-tuple-element.77.pos_ref, bf16[1152,768]{1,0:T(8,128)(2,1)S(1)} %copy-done.2, bf16[8,2,528,768]{3,2,1,0:T(8,128)(2,1)S(1)} %stack_shards.3.weight_ref), custom_call_target="tpu_custom_call" | custom-call | flops 1811939328 | bytes 15925248 | tf_op jit(solution)/shard_map/responsibilities/pallas_call | solution.py:163
  122.5 3.5 %responsibilities.8 = (bf16[4,4,128,128]{3,2,1,0:T(8,128)(2,1)S(1)}, f32[4,128]{1,0:T(4,128)S(1)}) custom-call(s32[128]{0:T(128)S(1)} %get-tuple-element.77.pos_ref, bf16[512,768]{1,0:T(8,128)(2,1)S(1)} %collective-permute-done.10.x_ref.rest_3_, bf16[8,2,528,768]{3,2,1,0:T(8,128)(2,1)S(1)} %stack_shards.3.weight_ref), custom_call_target="tpu_custom_call" | custom-call | flops 805306368 | bytes 7077888 | tf_op jit(solution)/shard_map/responsibilities/pallas_call | solution.py:163
  126.0 2.0 responsibilities.9
  128.0 2.6 %moments.8 = bf16[1040,768]{1,0:T(8,128)(2,1)S(1)} custom-call(s32[128]{0:T(128)S(1)} %get-tuple-element.97.order_ref, s32[161]{0:T(256)S(1)} %get-tuple-element.57.start_ref, bf16[2048,768]{1,0:T(8,128)(2,1)S(1)} %copy-done, bf16[128,768]{1,0:T(8,128)(2,1)S(1)} %copy-done.15, bf16[1152,768]{1,0:T(8,128)(2,1)S(1)} %copy-done.2, ...), custom_call_target="tpu_custom_call" | custom-call | flops 805306368 | bytes 3670016 | tf_op jit(solution)/shard_map/moments/pallas_call | solution.py:302
  131.3 2.0 moments.9.refs_0_
  134.8 2.9 %moments.10 = bf16[1040,768]{1,0:T(8,128)(2,1)S(1)} custom-call(s32[128]{0:T(128)S(1)} %get-tuple-element.97.order_ref, s32[161]{0:T(256)S(1)} %get-tuple-element.57.start_ref, bf16[2048,768]{1,0:T(8,128)(2,1)S(1)} %copy-done, bf16[128,768]{1,0:T(8,128)(2,1)S(1)} %copy-done.15, bf16[1152,768]{1,0:T(8,128)(2,1)S(1)} %copy-done.2, ...), custom_call_target="tpu_custom_call" | custom-call | flops 805306368 | bytes 3670016 | tf_op jit(solution)/shard_map/moments/pallas_call | solution.py:302
  137.6 2.3 %moments.11 = bf16[1040,768]{1,0:T(8,128)(2,1)S(1)} custom-call(s32[128]{0:T(128)S(1)} %get-tuple-element.97.order_ref, s32[161]{0:T(256)S(1)} %get-tuple-element.57.start_ref, bf16[2048,768]{1,0:T(8,128)(2,1)S(1)} %copy-done, bf16[128,768]{1,0:T(8,128)(2,1)S(1)} %copy-done.15, bf16[1152,768]{1,0:T(8,128)(2,1)S(1)} %copy-done.2, ...), custom_call_target="tpu_custom_call" | custom-call | flops 805306368 | bytes 3670016 | tf_op jit(solution)/shard_map/moments/pallas_call | solution.py:302
  141.5 3.7 %moments.12 = bf16[1040,768]{1,0:T(8,128)(2,1)} custom-call(s32[128]{0:T(128)S(1)} %get-tuple-element.97.order_ref, s32[161]{0:T(256)S(1)} %get-tuple-element.57.start_ref, bf16[2048,768]{1,0:T(8,128)(2,1)S(1)} %copy-done, bf16[128,768]{1,0:T(8,128)(2,1)S(1)} %copy-done.15, bf16[1152,768]{1,0:T(8,128)(2,1)S(1)} %copy-done.2, ...), custom_call_target="tpu_custom_call" | custom-call | flops 805306368 | bytes 3670016 | tf_op jit(solution)/shard_map/moments/pallas_call | solution.py:302
  145.2 1.8 collective-permute-start.18
  148.3 2.3 %moments.13.a_ref = bf16[1040,768]{1,0:T(8,128)(2,1)S(1)} custom-call(s32[128]{0:T(128)S(1)} %get-tuple-element.97.order_ref, s32[161]{0:T(256)S(1)} %get-tuple-element.57.start_ref, bf16[2048,768]{1,0:T(8,128)(2,1)S(1)} %copy-done, bf16[128,768]{1,0:T(8,128)(2,1)S(1)} %copy-done.15, bf16[1152,768]{1,0:T(8,128)(2,1)S(1)} %copy-done.2, ...), custom_call_target="tpu_custom_call" | custom-call | flops 805306368 | bytes 3670016 | tf_op jit(solution)/shard_map/moments/pallas_call | solution.py:302
  150.6 16.4 %collective-permute-done.13.refs_1_ = f32[16,128]{1,0:T(8,128)S(1)} collective-permute-done((f32[16,128]{1,0:T(8,128)S(1)}, f32[16,128]{1,0:T(8,128)S(1)}, u32[]{:S(2)}, u32[]{:S(2)}) %collective-permute-start.13) | collective-permute-done | bytes 8224 | tf_op jit(solution)/shard_map/ppermute | solution.py:505
  167.0 12.0 %moments.14.c_ref = bf16[1040,768]{1,0:T(8,128)(2,1)S(1)} custom-call(s32[128]{0:T(128)S(1)} %get-tuple-element.97.order_ref, s32[161]{0:T(256)S(1)} %get-tuple-element.57.start_ref, bf16[2048,768]{1,0:T(8,128)(2,1)S(1)} %copy-done, bf16[128,768]{1,0:T(8,128)(2,1)S(1)} %copy-done.15, bf16[1152,768]{1,0:T(8,128)(2,1)S(1)} %copy-done.2, ...), custom_call_target="tpu_custom_call" | custom-call | flops 805306368 | bytes 3670016 | tf_op jit(solution)/shard_map/moments/pallas_call | solution.py:302
  179.1 2.7 %add_both_sums.1 = (bf16[1040,768]{1,0:T(8,128)(2,1)}, bf16[1040,768]{1,0:T(8,128)(2,1)}) custom-call(bf16[1040,768]{1,0:T(8,128)(2,1)S(1)} %moments.13.a_ref, bf16[1040,768]{1,0:T(8,128)(2,1)S(1)} %collective-permute-done.15.b_ref, bf16[1040,768]{1,0:T(8,128)(2,1)S(1)} %moments.14.c_ref, bf16[1040,768]{1,0:T(8,128)(2,1)S(1)} %collective-permute-done.16.d_ref, ...), custom_call_target="tpu_custom_call" | custom-call | tf_op jit(solution)/shard_map/add_both_sums/pallas_call | solution.py:383
  183.1 1.8 collective-permute-start.19
  194.2 2.6 %moments.15.refs_0_ = bf16[1040,768]{1,0:T(8,128)(2,1)S(1)} custom-call(s32[128]{0:T(128)S(1)} %get-tuple-element.97.order_ref, s32[161]{0:T(256)S(1)} %get-tuple-element.57.start_ref, bf16[2048,768]{1,0:T(8,128)(2,1)S(1)} %copy-done, bf16[128,768]{1,0:T(8,128)(2,1)S(1)} %copy-done.16, bf16[1152,768]{1,0:T(8,128)(2,1)S(1)} %copy-done.3, ...), custom_call_target="tpu_custom_call" | custom-call | flops 805306368 | bytes 3670016 | tf_op jit(solution)/shard_map/moments/pallas_call | solution.py:302
  196.8 1.8 add_sums.3.refs_3_
  198.7 18.8 %collective-permute-done.17.refs_2_ = bf16[1040,768]{1,0:T(8,128)(2,1)} collective-permute-done((bf16[1040,768]{1,0:T(8,128)(2,1)}, bf16[1040,768]{1,0:T(8,128)(2,1)}, u32[]{:S(2)}, u32[]{:S(2)}) %collective-permute-start.17) | collective-permute-done | bytes 1597472 | tf_op jit(solution)/shard_map/ppermute | solution.py:505
  217.5 4.1 %results.1 = (f32[1,512]{1,0:T(1,128)}, f32[512,768]{1,0:T(8,128)}, f32[512,768]{1,0:T(8,128)}, f32[16,128]{1,0:T(8,128)}) custom-call(s32[1]{0:T(128)} %bitcast.end_ref, f32[16,128]{1,0:T(8,128)S(1)} %get-tuple-element.68.refs_0_, f32[16,128]{1,0:T(8,128)S(1)} %copy-done.20, bf16[1040,768]{1,0:T(8,128)(2,1)} %collective-permute-done.17.refs_2_, ...), custom_call_target="tpu_custom_call" | custom-call | tf_op jit(solution)/shard_map/results/pallas_call | solution.py:448
  (81 shorter events, 26.8 us)
Async XLA Ops:
  1.6 9.8 %collective-permute-start.1 = (bf16[128,768]{1,0:T(8,128)(2,1)S(1)}, bf16[128,768]{1,0:T(8,128)(2,1)S(1)}, u32[]{:S(2)}, u32[]{:S(2)}) collective-permute-start(bf16[128,768]{1,0:T(8,128)(2,1)S(1)} %slice.3), channel_id=1, source_target_pairs={{0,8},{4,12},{24,16},{28,20},{1,9},{5,13},{25,17},{29,21},{2,10},{... | collective-permute-start | bytes 589832 | tf_op jit(solution)/shard_map/ppermute | solution.py:505
  6.5 4.8 %collective-permute-start = (s32[4,16]{1,0:T(4,128)}, s32[4,16]{1,0:T(4,128)S(1)}, u32[]{:S(2)}, u32[]{:S(2)}) collective-permute-start(s32[4,16]{1,0:T(4,128)} %bitcast.6), channel_id=1, source_target_pairs={{0,8},{4,12},{24,16},{28,20},{1,9},{5,13},{25,17},{29,21},{2,10},{... | collective-permute-start | bytes 776 | tf_op jit(solution)/shard_map/ppermute | solution.py:505
  11.3 45.7 %copy-start.21 = (s32[16,4]{0,1:T(4,128)S(1)}, s32[16,4]{0,1:T(4,128)}, u32[]{:S(2)}) copy-start(s32[16,4]{0,1:T(4,128)} %param.6) | copy-start | bytes 772
  11.4 37.5 %copy-start.14 = (bf16[128,768]{1,0:T(8,128)(2,1)}, bf16[128,768]{1,0:T(8,128)(2,1)S(1)}, u32[]{:S(2)}) copy-start(bf16[128,768]{1,0:T(8,128)(2,1)S(1)} %collective-permute-done.1.x_ref.rest_1_) | copy-start | bytes 589828
  11.4 37.5 %collective-permute-start.2 = (bf16[1,2,528,768]{3,2,1,0:T(8,128)(2,1)S(1)}, bf16[1,2,528,768]{3,2,1,0:T(8,128)(2,1)}, u32[]{:S(2)}, u32[]{:S(2)}) collective-permute-start(bf16[1,2,528,768]{3,2,1,0:T(8,128)(2,1)S(1)} %parameter_shard.1.refs_0_), channel_id=1, source_target_pairs={{0,8},{4,12},{24,16},{28,20},{1,9},{5,13},{25,17},{29,21},{2,10},{... | collective-permute-start | bytes 4866056 | tf_op jit(solution)/shard_map/ppermute | solution.py:505
  16.3 46.8 %collective-permute-start.5 = (bf16[1,2,528,768]{3,2,1,0:T(8,128)(2,1)S(1)}, bf16[1,2,528,768]{3,2,1,0:T(8,128)(2,1)}, u32[]{:S(2)}, u32[]{:S(2)}) collective-permute-start(bf16[1,2,528,768]{3,2,1,0:T(8,128)(2,1)S(1)} %parameter_shard.1.refs_0_), channel_id=1, source_target_pairs={{8,16},{12,20},{16,8},{20,12},{9,17},{13,21},{17,9},{21,13},{10,18... | collective-permute-start | bytes 4866056 | tf_op jit(solution)/shard_map/ppermute | solution.py:505
  21.2 43.6 %collective-permute-start.4 = (bf16[1,2,528,768]{3,2,1,0:T(8,128)(2,1)S(1)}, bf16[1,2,528,768]{3,2,1,0:T(8,128)(2,1)}, u32[]{:S(2)}, u32[]{:S(2)}) collective-permute-start(bf16[1,2,528,768]{3,2,1,0:T(8,128)(2,1)S(1)} %parameter_shard.1.refs_0_), channel_id=1, source_target_pairs={{8,12},{12,8},{16,20},{20,16},{9,13},{13,9},{17,21},{21,17},{10,14... | collective-permute-start | bytes 4866056 | tf_op jit(solution)/shard_map/ppermute | solution.py:505
  48.9 18.5 %collective-permute-start.3 = (bf16[1,2,528,768]{3,2,1,0:T(8,128)(2,1)}, bf16[1,2,528,768]{3,2,1,0:T(8,128)(2,1)}, u32[]{:S(2)}, u32[]{:S(2)}) collective-permute-start(bf16[1,2,528,768]{3,2,1,0:T(8,128)(2,1)} %collective-permute-done.2.refs_2_), channel_id=1, source_target_pairs={{8,16},{12,20},{16,8},{20,12},{9,17},{13,21},{17,9},{21,13},{10,18... | collective-permute-start | bytes 4866056 | tf_op jit(solution)/shard_map/ppermute | solution.py:505
  50.8 42.2 %collective-permute-start.6 = (bf16[1152,768]{1,0:T(8,128)(2,1)}, bf16[1152,768]{1,0:T(8,128)(2,1)S(1)}, u32[]{:S(2)}, u32[]{:S(2)}) collective-permute-start(bf16[1152,768]{1,0:T(8,128)(2,1)} %get-tuple-element.66), channel_id=1, source_target_pairs={{0,8},{4,12},{24,16},{28,20},{1,9},{5,13},{25,17},{29,21},{2,10},{... | collective-permute-start | bytes 5308424 | tf_op jit(solution)/shard_map/ppermute | solution.py:505
  63.1 31.2 %copy-start.23 = (bf16[256,768]{1,0:T(8,128)(2,1)S(1)}, bf16[256,768]{1,0:T(8,128)(2,1)}, u32[]{:S(2)}) copy-start(bf16[256,768]{1,0:T(8,128)(2,1)} %get-tuple-element.78) | copy-start | bytes 1179652
  63.1 35.4 %collective-permute-start.8 = (bf16[1,2,528,768]{3,2,1,0:T(8,128)(2,1)}, bf16[1,2,528,768]{3,2,1,0:T(8,128)(2,1)S(1)}, u32[]{:S(2)}, u32[]{:S(2)}) collective-permute-start(bf16[1,2,528,768]{3,2,1,0:T(8,128)(2,1)} %collective-permute-done.5.refs_3_), channel_id=1, source_target_pairs={{8,12},{12,8},{16,20},{20,16},{9,13},{13,9},{17,21},{21,17},{10,14... | collective-permute-start | bytes 4866056 | tf_op jit(solution)/shard_map/ppermute | solution.py:505
  64.0 34.5 %collective-permute-start.7 = (bf16[1,2,528,768]{3,2,1,0:T(8,128)(2,1)}, bf16[1,2,528,768]{3,2,1,0:T(8,128)(2,1)S(1)}, u32[]{:S(2)}, u32[]{:S(2)}) collective-permute-start(bf16[1,2,528,768]{3,2,1,0:T(8,128)(2,1)} %collective-permute-done.2.refs_2_), channel_id=1, source_target_pairs={{8,12},{12,8},{16,20},{20,16},{9,13},{13,9},{17,21},{21,17},{10,14... | collective-permute-start | bytes 4866056 | tf_op jit(solution)/shard_map/ppermute | solution.py:505
  67.4 31.1 %collective-permute-start.9 = (bf16[1,2,528,768]{3,2,1,0:T(8,128)(2,1)}, bf16[1,2,528,768]{3,2,1,0:T(8,128)(2,1)S(1)}, u32[]{:S(2)}, u32[]{:S(2)}) collective-permute-start(bf16[1,2,528,768]{3,2,1,0:T(8,128)(2,1)} %collective-permute-done.3.refs_1_), channel_id=1, source_target_pairs={{8,12},{12,8},{16,20},{20,16},{9,13},{13,9},{17,21},{21,17},{10,14... | collective-permute-start | bytes 4866056 | tf_op jit(solution)/shard_map/ppermute | solution.py:505
  68.2 54.3 %collective-permute-start.10 = (bf16[512,768]{1,0:T(8,128)(2,1)S(1)}, bf16[512,768]{1,0:T(8,128)(2,1)S(1)}, u32[]{:S(2)}, u32[]{:S(2)}) collective-permute-start(bf16[512,768]{1,0:T(8,128)(2,1)S(1)} %copy-done.22), channel_id=1, source_target_pairs={{0,8},{4,12},{24,16},{28,20},{1,9},{5,13},{25,17},{29,21},{2,10},{... | collective-permute-start | bytes 2359304 | tf_op jit(solution)/shard_map/ppermute | solution.py:505
  94.2 31.8 %collective-permute-start.11 = (bf16[256,768]{1,0:T(8,128)(2,1)S(1)}, bf16[256,768]{1,0:T(8,128)(2,1)S(1)}, u32[]{:S(2)}, u32[]{:S(2)}) collective-permute-start(bf16[256,768]{1,0:T(8,128)(2,1)S(1)} %copy-done.23), channel_id=1, source_target_pairs={{0,8},{4,12},{24,16},{28,20},{1,9},{5,13},{25,17},{29,21},{2,10},{... | collective-permute-start | bytes 1179656 | tf_op jit(solution)/shard_map/ppermute | solution.py:505
  100.9 12.2 %copy-start.15 = (bf16[128,768]{1,0:T(8,128)(2,1)S(1)}, bf16[128,768]{1,0:T(8,128)(2,1)}, u32[]{:S(2)}) copy-start(bf16[128,768]{1,0:T(8,128)(2,1)} %copy-done.14) | copy-start | bytes 589828
  113.1 53.9 %copy-start.4 = (bf16[16,4,128,128]{3,2,1,0:T(8,128)(2,1)}, bf16[16,4,128,128]{3,2,1,0:T(8,128)(2,1)S(1)}, u32[]{:S(2)}) copy-start(bf16[16,4,128,128]{3,2,1,0:T(8,128)(2,1)S(1)} %get-tuple-element.80.rest_5_) | copy-start | bytes 6291460
  114.4 52.6 %copy-start.17 = (bf16[1,4,128,128]{3,2,1,0:T(8,128)(2,1)}, bf16[1,4,128,128]{3,2,1,0:T(8,128)(2,1)S(1)}, u32[]{:S(2)}) copy-start(bf16[1,4,128,128]{3,2,1,0:T(8,128)(2,1)S(1)} %get-tuple-element.81.rest_6_) | copy-start | bytes 393220
  122.5 44.5 %copy-start.6 = (bf16[9,4,128,128]{3,2,1,0:T(8,128)(2,1)}, bf16[9,4,128,128]{3,2,1,0:T(8,128)(2,1)S(1)}, u32[]{:S(2)}) copy-start(bf16[9,4,128,128]{3,2,1,0:T(8,128)(2,1)S(1)} %get-tuple-element.82.rest_7_) | copy-start | bytes 3538948
  122.5 44.5 %copy-start.8 = (bf16[512,768]{1,0:T(8,128)(2,1)}, bf16[512,768]{1,0:T(8,128)(2,1)S(1)}, u32[]{:S(2)}) copy-start(bf16[512,768]{1,0:T(8,128)(2,1)S(1)} %collective-permute-done.10.x_ref.rest_3_) | copy-start | bytes 2359300
  126.0 41.0 %copy-start.10 = (bf16[4,4,128,128]{3,2,1,0:T(8,128)(2,1)}, bf16[4,4,128,128]{3,2,1,0:T(8,128)(2,1)S(1)}, u32[]{:S(2)}) copy-start(bf16[4,4,128,128]{3,2,1,0:T(8,128)(2,1)S(1)} %get-tuple-element.83.rest_8_) | copy-start | bytes 1572868
  128.0 39.0 %copy-start.12 = (bf16[2,4,128,128]{3,2,1,0:T(8,128)(2,1)}, bf16[2,4,128,128]{3,2,1,0:T(8,128)(2,1)S(1)}, u32[]{:S(2)}) copy-start(bf16[2,4,128,128]{3,2,1,0:T(8,128)(2,1)S(1)} %get-tuple-element.84.rest_9_) | copy-start | bytes 786436
  130.6 2.8 %collective-permute-start.12 = (bf16[1040,768]{1,0:T(8,128)(2,1)S(1)}, bf16[1040,768]{1,0:T(8,128)(2,1)S(1)}, u32[]{:S(2)}, u32[]{:S(2)}) collective-permute-start(bf16[1040,768]{1,0:T(8,128)(2,1)S(1)} %moments.8), channel_id=1, source_target_pairs={{8,12},{12,8},{16,20},{20,16},{9,13},{13,9},{17,21},{21,17},{10,14... | collective-permute-start | bytes 4792328 | tf_op jit(solution)/shard_map/ppermute | solution.py:505
  133.8 45.3 %collective-permute-start.14 = (bf16[1040,768]{1,0:T(8,128)(2,1)S(1)}, bf16[1040,768]{1,0:T(8,128)(2,1)S(1)}, u32[]{:S(2)}, u32[]{:S(2)}) collective-permute-start(bf16[1040,768]{1,0:T(8,128)(2,1)S(1)} %add_sums.2), channel_id=1, source_target_pairs={{8,16},{12,20},{16,8},{20,12},{9,17},{13,21},{17,9},{21,13},{10,18... | collective-permute-start | bytes 4792328 | tf_op jit(solution)/shard_map/ppermute | solution.py:505
  139.9 39.2 %collective-permute-start.16 = (bf16[1040,768]{1,0:T(8,128)(2,1)S(1)}, bf16[1040,768]{1,0:T(8,128)(2,1)S(1)}, u32[]{:S(2)}, u32[]{:S(2)}) collective-permute-start(bf16[1040,768]{1,0:T(8,128)(2,1)S(1)} %moments.11), channel_id=1, source_target_pairs={{8,12},{12,8},{16,20},{20,16},{9,13},{13,9},{17,21},{21,17},{10,14... | collective-permute-start | bytes 4792328 | tf_op jit(solution)/shard_map/ppermute | solution.py:505
  140.7 38.4 %collective-permute-start.15 = (bf16[1040,768]{1,0:T(8,128)(2,1)S(1)}, bf16[1040,768]{1,0:T(8,128)(2,1)S(1)}, u32[]{:S(2)}, u32[]{:S(2)}) collective-permute-start(bf16[1040,768]{1,0:T(8,128)(2,1)S(1)} %moments.10), channel_id=1, source_target_pairs={{8,12},{12,8},{16,20},{20,16},{9,13},{13,9},{17,21},{21,17},{10,14... | collective-permute-start | bytes 4792328 | tf_op jit(solution)/shard_map/ppermute | solution.py:505
  145.2 51.6 %collective-permute-start.18 = (bf16[1040,768]{1,0:T(8,128)(2,1)}, bf16[1040,768]{1,0:T(8,128)(2,1)}, u32[]{:S(2)}, u32[]{:S(2)}) collective-permute-start(bf16[1040,768]{1,0:T(8,128)(2,1)} %moments.12), channel_id=1, source_target_pairs={{8,12},{12,8},{16,20},{20,16},{9,13},{13,9},{17,21},{21,17},{10,14... | collective-permute-start | bytes 4792328 | tf_op jit(solution)/shard_map/ppermute | solution.py:505
  147.0 20.0 %collective-permute-start.13 = (f32[16,128]{1,0:T(8,128)S(1)}, f32[16,128]{1,0:T(8,128)S(1)}, u32[]{:S(2)}, u32[]{:S(2)}) collective-permute-start(f32[16,128]{1,0:T(8,128)S(1)} %join_norms.1), channel_id=1, source_target_pairs={{8,0},{12,4},{16,24},{20,28},{9,1},{13,5},{17,25},{21,29},{10,2},{... | collective-permute-start | bytes 24584 | tf_op jit(solution)/shard_map/ppermute | solution.py:505
  167.0 12.0 %copy-start.19 = (f32[16,128]{1,0:T(8,128)}, f32[16,128]{1,0:T(8,128)S(1)}, u32[]{:S(2)}) copy-start(f32[16,128]{1,0:T(8,128)S(1)} %collective-permute-done.13.refs_1_) | copy-start | bytes 24580
  181.8 35.7 %collective-permute-start.17 = (bf16[1040,768]{1,0:T(8,128)(2,1)}, bf16[1040,768]{1,0:T(8,128)(2,1)}, u32[]{:S(2)}, u32[]{:S(2)}) collective-permute-start(bf16[1040,768]{1,0:T(8,128)(2,1)} %get-tuple-element.95), channel_id=1, source_target_pairs={{8,0},{12,4},{16,24},{20,28},{9,1},{13,5},{17,25},{21,29},{10,2},{... | collective-permute-start | bytes 4792328 | tf_op jit(solution)/shard_map/ppermute | solution.py:505
  183.1 34.4 %collective-permute-start.19 = (bf16[1040,768]{1,0:T(8,128)(2,1)}, bf16[1040,768]{1,0:T(8,128)(2,1)}, u32[]{:S(2)}, u32[]{:S(2)}) collective-permute-start(bf16[1040,768]{1,0:T(8,128)(2,1)} %get-tuple-element.96), channel_id=1, source_target_pairs={{8,16},{12,20},{16,8},{20,12},{9,17},{13,21},{17,9},{21,13},{10,18... | collective-permute-start | bytes 4792328 | tf_op jit(solution)/shard_map/ppermute | solution.py:505
  196.8 20.7 %copy-start.20 = (f32[16,128]{1,0:T(8,128)S(1)}, f32[16,128]{1,0:T(8,128)}, u32[]{:S(2)}) copy-start(f32[16,128]{1,0:T(8,128)} %copy-done.19) | copy-start | bytes 24580
  (12 other events, 20.3 us)

commit v13 on v12

--- a/solution.py
+++ b/solution.py
@@ -566,10 +566,8 @@
     across_received = move(across_other, CORES)
     outer_other = sums_of(3, across_other)
     outer_received = move(outer_other, CORES)
-    own_other = sums_of(1, outer_other)
-    own_received = move(own_other, CORES)
     end_norm = move(after(joined(*[r[1] for r in results[1:]]), across_other), OUTWARD)
-    across_own = sums_of(4, own_other)
+    across_own = sums_of(4, outer_other)
     outer_own = sums_of(2, across_own, end_norm)
     far_sum, outer_own, across_own = lax.optimization_barrier((far_sum, outer_own, across_own))
     across_part, outer_sum = added_two(
@@ -577,10 +575,13 @@
     )
     across_sum = move(across_part, MIDDLE)
     end_sum = move(outer_sum, OUTWARD)
-    own_own = sums_of(0, across_part, outer_sum)
+    own_other = sums_of(1, across_part, outer_sum)
+    own_received = move(own_other, CORES)
+    own_own = sums_of(0, own_other)
+    across_sum, end_sum, own_own = lax.optimization_barrier((across_sum, end_sum, own_own))
     is_end = jnp.logical_or(chip == 0, chip == 3)
     counts, first, second, loglik = results_of(
-        is_end, results[0][1], end_norm, end_sum, added(own_own, own_received), across_sum
+        is_end, results[0][1], end_norm, end_sum, own_own, own_received, across_sum
     )
     return counts.reshape(-1), first, second, loglik.reshape(-1)
 

time: 225 us -> 225 us (level)
  transfers between devices with their start and end apart: 20 -> 20, of which waited for: 3 -> 3; matrix products, arithmetic and copies ran while one was open for 0% -> 0% of each run, Pallas kernels for 33% -> 31%
where the time goes in v13:
time: 225 us; the launch traced here: 222 us
  Pallas kernels  80.4 us (36%)
  starting transfers between devices  63.8 us (28%)
  waiting for transfers between devices  62.6 us (28%)
  local copies, waits for them, and re-layouts  13.9 us (6%)
    ppermute x20, starting transfers between devices, move(): return lax.ppermute(value, 'dp', pairs)  63.8 us
    ppermute x20, waiting for transfers between devices, move(): return lax.ppermute(value, 'dp', pairs)  62.6 us
    pallas_call x8, Pallas kernels, moments(): pl.pallas_call(functools.partial(moment_body, tuple(shards), held, runs),...  30.3 us
    pallas_call x5, Pallas kernels, responsibilities(): pl.pallas_call(functools.partial(density_body, first, count, held), in_sp...  26 us
    unnamed x48, local copies, waits for them, and re-layouts  12.3 us
    pallas_call x1, Pallas kernels, pair_lists(): pl.pallas_call(functools.partial(list_body, tuple(runs), held, owners, pl...  6.02 us
    pallas_call x1, Pallas kernels, results_of(): pl.pallas_call(functools.partial(result_body, owned), grid=(owned // CB,)...  4.65 us
  transfers between devices with their start and end apart: 20, of which 3 were waited for; matrix products, arithmetic and copies ran while one was open for 0% of the time, Pallas kernels for 31%

profile of v13, /device:TPU:0, one launch (start us, length us, event | category | flops | bytes accessed | tf_op | source)
XLA Modules:
  0.0 222.0 jit_solution(9245875055668232343)
XLA Ops:
  1.6 4.9 %collective-permute-start.1 = (bf16[128,768]{1,0:T(8,128)(2,1)S(1)}, bf16[128,768]{1,0:T(8,128)(2,1)S(1)}, u32[]{:S(2)}, u32[]{:S(2)}) collective-permute-start(bf16[128,768]{1,0:T(8,128)(2,1)S(1)} %slice.3), channel_id=1, source_target_pairs={{0,8},{4,12},{24,16},{28,20},{1,9},{5,13},{25,17},{29,21},{2,10},{... | collective-permute-start | bytes 589832 | tf_op jit(solution)/shard_map/ppermute | solution.py:505
  8.5 2.8 %parameter_shard.1.refs_0_ = bf16[1,2,528,768]{3,2,1,0:T(8,128)(2,1)S(1)} custom-call(bf16[512,768]{1,0:T(8,128)(2,1)} %means_hbm.1, bf16[512,768]{1,0:T(8,128)(2,1)} %inv_hbm.1, bf16[1,512]{1,0:T(2,128)(2,1)S(1)} %reshape.32.log_ref), custom_call_target="tpu_custom_call" | custom-call | flops 15728640 | bytes 3145728 | tf_op jit(solution)/shard_map/parameter_shard/pallas_call | solution.py:68
  11.4 4.9 %collective-permute-start.2 = (bf16[1,2,528,768]{3,2,1,0:T(8,128)(2,1)S(1)}, bf16[1,2,528,768]{3,2,1,0:T(8,128)(2,1)}, u32[]{:S(2)}, u32[]{:S(2)}) collective-permute-start(bf16[1,2,528,768]{3,2,1,0:T(8,128)(2,1)S(1)} %parameter_shard.1.refs_0_), channel_id=1, source_target_pairs={{0,8},{4,12},{24,16},{28,20},{1,9},{5,13},{25,17},{29,21},{2,10},{... | collective-permute-start | bytes 4866056 | tf_op jit(solution)/shard_map/ppermute | solution.py:505
  16.3 1.8 collective-permute-start.5
  18.1 3.1 %cut_rows.1 = (bf16[1152,768]{1,0:T(8,128)(2,1)}, bf16[512,768]{1,0:T(8,128)(2,1)}, bf16[256,768]{1,0:T(8,128)(2,1)}) custom-call(bf16[2048,768]{1,0:T(8,128)(2,1)} %rest_0_.15), custom_call_target="tpu_custom_call" | custom-call | tf_op jit(solution)/shard_map/cut_rows/pallas_call | solution.py:113
  21.2 1.8 collective-permute-start.4
  23.0 25.9 %collective-permute-done.2.refs_2_ = bf16[1,2,528,768]{3,2,1,0:T(8,128)(2,1)} collective-permute-done((bf16[1,2,528,768]{3,2,1,0:T(8,128)(2,1)S(1)}, bf16[1,2,528,768]{3,2,1,0:T(8,128)(2,1)}, u32[]{:S(2)}, u32[]{:S(2)}) %collective-permute-start.2) | collective-permute-done | bytes 1622048 | tf_op jit(solution)/shard_map/ppermute | solution.py:505
  48.9 1.9 collective-permute-start.3
  50.8 6.2 %collective-permute-start.6 = (bf16[1152,768]{1,0:T(8,128)(2,1)}, bf16[1152,768]{1,0:T(8,128)(2,1)S(1)}, u32[]{:S(2)}, u32[]{:S(2)}) collective-permute-start(bf16[1152,768]{1,0:T(8,128)(2,1)} %get-tuple-element.69), channel_id=1, source_target_pairs={{0,8},{4,12},{24,16},{28,20},{1,9},{5,13},{25,17},{29,21},{2,10},{... | collective-permute-start | bytes 5308424 | tf_op jit(solution)/shard_map/ppermute | solution.py:505
  57.0 6.0 %pair_lists.1 = (s32[128]{0:T(128)S(1)}, s32[128]{0:T(128)S(1)}, s32[161]{0:T(256)S(1)}) custom-call(s32[1]{0:T(128)} %bitcast.1.rest_0_, s32[1]{0:T(128)} %bitcast.2.rest_1_, s32[4,16]{1,0:T(4,128)S(1)} %bitcast.7, s32[4,16]{1,0:T(4,128)S(1)} %collective-permute-done.rest_3_), custom_call_target="tpu_custom_call" | custom-call | tf_op jit(solution)/shard_map/pair_lists/pallas_call | solution.py:229
  64.8 2.6 %stack_shards.2.refs_0_ = bf16[8,2,528,768]{3,2,1,0:T(8,128)(2,1)S(1)} custom-call(bf16[1,2,528,768]{3,2,1,0:T(8,128)(2,1)S(1)} %parameter_shard.1.refs_0_, bf16[1,2,528,768]{3,2,1,0:T(8,128)(2,1)} %collective-permute-done.4.refs_1_, bf16[1,2,528,768]{3,2,1,0:T(8,128)(2,1)} %collective-permute-done.2.refs_2_, ...), custom_call_target="tpu_custom_call" | custom-call | tf_op jit(solution)/shard_map/stack_shards/pallas_call | solution.py:350
  68.2 24.8 %collective-permute-start.10 = (bf16[512,768]{1,0:T(8,128)(2,1)S(1)}, bf16[512,768]{1,0:T(8,128)(2,1)S(1)}, u32[]{:S(2)}, u32[]{:S(2)}) collective-permute-start(bf16[512,768]{1,0:T(8,128)(2,1)S(1)} %copy-done.22), channel_id=1, source_target_pairs={{0,8},{4,12},{24,16},{28,20},{1,9},{5,13},{25,17},{29,21},{2,10},{... | collective-permute-start | bytes 2359304 | tf_op jit(solution)/shard_map/ppermute | solution.py:505
  94.2 4.3 %collective-permute-start.11 = (bf16[256,768]{1,0:T(8,128)(2,1)S(1)}, bf16[256,768]{1,0:T(8,128)(2,1)S(1)}, u32[]{:S(2)}, u32[]{:S(2)}) collective-permute-start(bf16[256,768]{1,0:T(8,128)(2,1)S(1)} %copy-done.23), channel_id=1, source_target_pairs={{0,8},{4,12},{24,16},{28,20},{1,9},{5,13},{25,17},{29,21},{2,10},{... | collective-permute-start | bytes 1179656 | tf_op jit(solution)/shard_map/ppermute | solution.py:505
  98.6 1.6 stack_shards.3.weight_ref
  100.9 12.2 %responsibilities.5 = (bf16[16,4,128,128]{3,2,1,0:T(8,128)(2,1)S(1)}, f32[16,128]{1,0:T(8,128)S(1)}) custom-call(s32[128]{0:T(128)S(1)} %get-tuple-element.80.pos_ref, bf16[2048,768]{1,0:T(8,128)(2,1)S(1)} %copy-done, bf16[8,2,528,768]{3,2,1,0:T(8,128)(2,1)S(1)} %stack_shards.3.weight_ref), custom_call_target="tpu_custom_call" | custom-call | flops 3221225472 | bytes 28311552 | tf_op jit(solution)/shard_map/responsibilities/pallas_call | solution.py:163
  115.4 7.1 %responsibilities.7 = (bf16[9,4,128,128]{3,2,1,0:T(8,128)(2,1)S(1)}, f32[9,128]{1,0:T(8,128)S(1)}) custom-call(s32[128]{0:T(128)S(1)} %get-tuple-element.80.pos_ref, bf16[1152,768]{1,0:T(8,128)(2,1)S(1)} %copy-done.2, bf16[8,2,528,768]{3,2,1,0:T(8,128)(2,1)S(1)} %stack_shards.3.weight_ref), custom_call_target="tpu_custom_call" | custom-call | flops 1811939328 | bytes 15925248 | tf_op jit(solution)/shard_map/responsibilities/pallas_call | solution.py:163
  122.5 3.5 %responsibilities.8 = (bf16[4,4,128,128]{3,2,1,0:T(8,128)(2,1)S(1)}, f32[4,128]{1,0:T(4,128)S(1)}) custom-call(s32[128]{0:T(128)S(1)} %get-tuple-element.80.pos_ref, bf16[512,768]{1,0:T(8,128)(2,1)S(1)} %collective-permute-done.10.x_ref.rest_3_, bf16[8,2,528,768]{3,2,1,0:T(8,128)(2,1)S(1)} %stack_shards.3.weight_ref), custom_call_target="tpu_custom_call" | custom-call | flops 805306368 | bytes 7077888 | tf_op jit(solution)/shard_map/responsibilities/pallas_call | solution.py:163
  126.0 2.0 responsibilities.9
  128.0 2.0 moments.8
  130.8 3.1 %moments.9.refs_0_ = bf16[1040,768]{1,0:T(8,128)(2,1)S(1)} custom-call(s32[128]{0:T(128)S(1)} %get-tuple-element.100.order_ref, s32[161]{0:T(256)S(1)} %get-tuple-element.60.start_ref, bf16[2048,768]{1,0:T(8,128)(2,1)S(1)} %copy-done, bf16[128,768]{1,0:T(8,128)(2,1)S(1)} %copy-done.15, bf16[1152,768]{1,0:T(8,128)(2,1)S(1)} %copy-done.2, ...), custom_call_target="tpu_custom_call" | custom-call | flops 805306368 | bytes 3670016 | tf_op jit(solution)/shard_map/moments/pallas_call | solution.py:302
  135.3 2.3 %moments.10 = bf16[1040,768]{1,0:T(8,128)(2,1)S(1)} custom-call(s32[128]{0:T(128)S(1)} %get-tuple-element.100.order_ref, s32[161]{0:T(256)S(1)} %get-tuple-element.60.start_ref, bf16[2048,768]{1,0:T(8,128)(2,1)S(1)} %copy-done, bf16[128,768]{1,0:T(8,128)(2,1)S(1)} %copy-done.15, bf16[1152,768]{1,0:T(8,128)(2,1)S(1)} %copy-done.2, ...), custom_call_target="tpu_custom_call" | custom-call | flops 805306368 | bytes 3670016 | tf_op jit(solution)/shard_map/moments/pallas_call | solution.py:302
  137.6 2.6 %moments.11 = bf16[1040,768]{1,0:T(8,128)(2,1)S(1)} custom-call(s32[128]{0:T(128)S(1)} %get-tuple-element.100.order_ref, s32[161]{0:T(256)S(1)} %get-tuple-element.60.start_ref, bf16[2048,768]{1,0:T(8,128)(2,1)S(1)} %copy-done, bf16[128,768]{1,0:T(8,128)(2,1)S(1)} %copy-done.15, bf16[1152,768]{1,0:T(8,128)(2,1)S(1)} %copy-done.2, ...), custom_call_target="tpu_custom_call" | custom-call | flops 805306368 | bytes 3670016 | tf_op jit(solution)/shard_map/moments/pallas_call | solution.py:302
  143.0 2.0 moments.12.a_ref
  145.0 12.6 %collective-permute-done.13.refs_1_ = f32[16,128]{1,0:T(8,128)S(1)} collective-permute-done((f32[16,128]{1,0:T(8,128)S(1)}, f32[16,128]{1,0:T(8,128)S(1)}, u32[]{:S(2)}, u32[]{:S(2)}) %collective-permute-start.13) | collective-permute-done | bytes 8224 | tf_op jit(solution)/shard_map/ppermute | solution.py:505
  157.6 12.6 %moments.13.c_ref = bf16[1040,768]{1,0:T(8,128)(2,1)S(1)} custom-call(s32[128]{0:T(128)S(1)} %get-tuple-element.100.order_ref, s32[161]{0:T(256)S(1)} %get-tuple-element.60.start_ref, bf16[2048,768]{1,0:T(8,128)(2,1)S(1)} %copy-done, bf16[128,768]{1,0:T(8,128)(2,1)S(1)} %copy-done.15, bf16[1152,768]{1,0:T(8,128)(2,1)S(1)} %copy-done.2, ...), custom_call_target="tpu_custom_call" | custom-call | flops 805306368 | bytes 3670016 | tf_op jit(solution)/shard_map/moments/pallas_call | solution.py:302
  170.2 2.8 %add_both_sums.1 = (bf16[1040,768]{1,0:T(8,128)(2,1)}, bf16[1040,768]{1,0:T(8,128)(2,1)}) custom-call(bf16[1040,768]{1,0:T(8,128)(2,1)S(1)} %moments.12.a_ref, bf16[1040,768]{1,0:T(8,128)(2,1)S(1)} %collective-permute-done.15.b_ref, bf16[1040,768]{1,0:T(8,128)(2,1)S(1)} %moments.13.c_ref, bf16[1040,768]{1,0:T(8,128)(2,1)S(1)} %collective-permute-done.16.d_ref, ...), custom_call_target="tpu_custom_call" | custom-call | tf_op jit(solution)/shard_map/add_both_sums/pallas_call | solution.py:383
  173.0 1.8 collective-permute-start.17
  176.2 3.5 %moments.14 = bf16[1040,768]{1,0:T(8,128)(2,1)} custom-call(s32[128]{0:T(128)S(1)} %get-tuple-element.100.order_ref, s32[161]{0:T(256)S(1)} %get-tuple-element.60.start_ref, bf16[2048,768]{1,0:T(8,128)(2,1)S(1)} %copy-done, bf16[128,768]{1,0:T(8,128)(2,1)S(1)} %copy-done.15, bf16[1152,768]{1,0:T(8,128)(2,1)S(1)} %copy-done.2, ...), custom_call_target="tpu_custom_call" | custom-call | flops 805306368 | bytes 3670016 | tf_op jit(solution)/shard_map/moments/pallas_call | solution.py:302
  179.6 1.8 collective-permute-start.19
  190.8 2.3 %moments.15.refs_3_ = bf16[1040,768]{1,0:T(8,128)(2,1)S(1)} custom-call(s32[128]{0:T(128)S(1)} %get-tuple-element.100.order_ref, s32[161]{0:T(256)S(1)} %get-tuple-element.60.start_ref, bf16[2048,768]{1,0:T(8,128)(2,1)S(1)} %copy-done, bf16[128,768]{1,0:T(8,128)(2,1)S(1)} %copy-done.16, bf16[1152,768]{1,0:T(8,128)(2,1)S(1)} %copy-done.3, ...), custom_call_target="tpu_custom_call" | custom-call | flops 805306368 | bytes 3670016 | tf_op jit(solution)/shard_map/moments/pallas_call | solution.py:302
  193.1 24.1 %collective-permute-done.18.refs_2_ = bf16[1040,768]{1,0:T(8,128)(2,1)} collective-permute-done((bf16[1040,768]{1,0:T(8,128)(2,1)}, bf16[1040,768]{1,0:T(8,128)(2,1)}, u32[]{:S(2)}, u32[]{:S(2)}) %collective-permute-start.18) | collective-permute-done | bytes 1597472 | tf_op jit(solution)/shard_map/ppermute | solution.py:505
  217.2 4.7 %results.1 = (f32[1,512]{1,0:T(1,128)}, f32[512,768]{1,0:T(8,128)}, f32[512,768]{1,0:T(8,128)}, f32[16,128]{1,0:T(8,128)}) custom-call(s32[1]{0:T(128)} %bitcast.end_ref, f32[16,128]{1,0:T(8,128)S(1)} %get-tuple-element.71.refs_0_, f32[16,128]{1,0:T(8,128)S(1)} %copy-done.20, bf16[1040,768]{1,0:T(8,128)(2,1)} %collective-permute-done.18.refs_2_, ...), custom_call_target="tpu_custom_call" | custom-call | tf_op jit(solution)/shard_map/results/pallas_call | solution.py:448
  (80 shorter events, 25.2 us)
Async XLA Ops:
  1.6 9.8 %collective-permute-start.1 = (bf16[128,768]{1,0:T(8,128)(2,1)S(1)}, bf16[128,768]{1,0:T(8,128)(2,1)S(1)}, u32[]{:S(2)}, u32[]{:S(2)}) collective-permute-start(bf16[128,768]{1,0:T(8,128)(2,1)S(1)} %slice.3), channel_id=1, source_target_pairs={{0,8},{4,12},{24,16},{28,20},{1,9},{5,13},{25,17},{29,21},{2,10},{... | collective-permute-start | bytes 589832 | tf_op jit(solution)/shard_map/ppermute | solution.py:505
  6.5 4.8 %collective-permute-start = (s32[4,16]{1,0:T(4,128)}, s32[4,16]{1,0:T(4,128)S(1)}, u32[]{:S(2)}, u32[]{:S(2)}) collective-permute-start(s32[4,16]{1,0:T(4,128)} %bitcast.6), channel_id=1, source_target_pairs={{0,8},{4,12},{24,16},{28,20},{1,9},{5,13},{25,17},{29,21},{2,10},{... | collective-permute-start | bytes 776 | tf_op jit(solution)/shard_map/ppermute | solution.py:505
  11.3 45.7 %copy-start.21 = (s32[16,4]{0,1:T(4,128)S(1)}, s32[16,4]{0,1:T(4,128)}, u32[]{:S(2)}) copy-start(s32[16,4]{0,1:T(4,128)} %param.6) | copy-start | bytes 772
  11.4 37.5 %copy-start.14 = (bf16[128,768]{1,0:T(8,128)(2,1)}, bf16[128,768]{1,0:T(8,128)(2,1)S(1)}, u32[]{:S(2)}) copy-start(bf16[128,768]{1,0:T(8,128)(2,1)S(1)} %collective-permute-done.1.x_ref.rest_1_) | copy-start | bytes 589828
  11.4 37.5 %collective-permute-start.2 = (bf16[1,2,528,768]{3,2,1,0:T(8,128)(2,1)S(1)}, bf16[1,2,528,768]{3,2,1,0:T(8,128)(2,1)}, u32[]{:S(2)}, u32[]{:S(2)}) collective-permute-start(bf16[1,2,528,768]{3,2,1,0:T(8,128)(2,1)S(1)} %parameter_shard.1.refs_0_), channel_id=1, source_target_pairs={{0,8},{4,12},{24,16},{28,20},{1,9},{5,13},{25,17},{29,21},{2,10},{... | collective-permute-start | bytes 4866056 | tf_op jit(solution)/shard_map/ppermute | solution.py:505
  16.3 46.8 %collective-permute-start.5 = (bf16[1,2,528,768]{3,2,1,0:T(8,128)(2,1)S(1)}, bf16[1,2,528,768]{3,2,1,0:T(8,128)(2,1)}, u32[]{:S(2)}, u32[]{:S(2)}) collective-permute-start(bf16[1,2,528,768]{3,2,1,0:T(8,128)(2,1)S(1)} %parameter_shard.1.refs_0_), channel_id=1, source_target_pairs={{8,16},{12,20},{16,8},{20,12},{9,17},{13,21},{17,9},{21,13},{10,18... | collective-permute-start | bytes 4866056 | tf_op jit(solution)/shard_map/ppermute | solution.py:505
  21.2 43.6 %collective-permute-start.4 = (bf16[1,2,528,768]{3,2,1,0:T(8,128)(2,1)S(1)}, bf16[1,2,528,768]{3,2,1,0:T(8,128)(2,1)}, u32[]{:S(2)}, u32[]{:S(2)}) collective-permute-start(bf16[1,2,528,768]{3,2,1,0:T(8,128)(2,1)S(1)} %parameter_shard.1.refs_0_), channel_id=1, source_target_pairs={{8,12},{12,8},{16,20},{20,16},{9,13},{13,9},{17,21},{21,17},{10,14... | collective-permute-start | bytes 4866056 | tf_op jit(solution)/shard_map/ppermute | solution.py:505
  48.9 18.5 %collective-permute-start.3 = (bf16[1,2,528,768]{3,2,1,0:T(8,128)(2,1)}, bf16[1,2,528,768]{3,2,1,0:T(8,128)(2,1)}, u32[]{:S(2)}, u32[]{:S(2)}) collective-permute-start(bf16[1,2,528,768]{3,2,1,0:T(8,128)(2,1)} %collective-permute-done.2.refs_2_), channel_id=1, source_target_pairs={{8,16},{12,20},{16,8},{20,12},{9,17},{13,21},{17,9},{21,13},{10,18... | collective-permute-start | bytes 4866056 | tf_op jit(solution)/shard_map/ppermute | solution.py:505
  50.8 42.2 %collective-permute-start.6 = (bf16[1152,768]{1,0:T(8,128)(2,1)}, bf16[1152,768]{1,0:T(8,128)(2,1)S(1)}, u32[]{:S(2)}, u32[]{:S(2)}) collective-permute-start(bf16[1152,768]{1,0:T(8,128)(2,1)} %get-tuple-element.69), channel_id=1, source_target_pairs={{0,8},{4,12},{24,16},{28,20},{1,9},{5,13},{25,17},{29,21},{2,10},{... | collective-permute-start | bytes 5308424 | tf_op jit(solution)/shard_map/ppermute | solution.py:505
  63.1 31.2 %copy-start.23 = (bf16[256,768]{1,0:T(8,128)(2,1)S(1)}, bf16[256,768]{1,0:T(8,128)(2,1)}, u32[]{:S(2)}) copy-start(bf16[256,768]{1,0:T(8,128)(2,1)} %get-tuple-element.81) | copy-start | bytes 1179652
  63.1 35.4 %collective-permute-start.8 = (bf16[1,2,528,768]{3,2,1,0:T(8,128)(2,1)}, bf16[1,2,528,768]{3,2,1,0:T(8,128)(2,1)S(1)}, u32[]{:S(2)}, u32[]{:S(2)}) collective-permute-start(bf16[1,2,528,768]{3,2,1,0:T(8,128)(2,1)} %collective-permute-done.5.refs_3_), channel_id=1, source_target_pairs={{8,12},{12,8},{16,20},{20,16},{9,13},{13,9},{17,21},{21,17},{10,14... | collective-permute-start | bytes 4866056 | tf_op jit(solution)/shard_map/ppermute | solution.py:505
  64.0 34.5 %collective-permute-start.7 = (bf16[1,2,528,768]{3,2,1,0:T(8,128)(2,1)}, bf16[1,2,528,768]{3,2,1,0:T(8,128)(2,1)S(1)}, u32[]{:S(2)}, u32[]{:S(2)}) collective-permute-start(bf16[1,2,528,768]{3,2,1,0:T(8,128)(2,1)} %collective-permute-done.2.refs_2_), channel_id=1, source_target_pairs={{8,12},{12,8},{16,20},{20,16},{9,13},{13,9},{17,21},{21,17},{10,14... | collective-permute-start | bytes 4866056 | tf_op jit(solution)/shard_map/ppermute | solution.py:505
  67.4 31.1 %collective-permute-start.9 = (bf16[1,2,528,768]{3,2,1,0:T(8,128)(2,1)}, bf16[1,2,528,768]{3,2,1,0:T(8,128)(2,1)S(1)}, u32[]{:S(2)}, u32[]{:S(2)}) collective-permute-start(bf16[1,2,528,768]{3,2,1,0:T(8,128)(2,1)} %collective-permute-done.3.refs_1_), channel_id=1, source_target_pairs={{8,12},{12,8},{16,20},{20,16},{9,13},{13,9},{17,21},{21,17},{10,14... | collective-permute-start | bytes 4866056 | tf_op jit(solution)/shard_map/ppermute | solution.py:505
  68.2 54.3 %collective-permute-start.10 = (bf16[512,768]{1,0:T(8,128)(2,1)S(1)}, bf16[512,768]{1,0:T(8,128)(2,1)S(1)}, u32[]{:S(2)}, u32[]{:S(2)}) collective-permute-start(bf16[512,768]{1,0:T(8,128)(2,1)S(1)} %copy-done.22), channel_id=1, source_target_pairs={{0,8},{4,12},{24,16},{28,20},{1,9},{5,13},{25,17},{29,21},{2,10},{... | collective-permute-start | bytes 2359304 | tf_op jit(solution)/shard_map/ppermute | solution.py:505
  94.2 31.8 %collective-permute-start.11 = (bf16[256,768]{1,0:T(8,128)(2,1)S(1)}, bf16[256,768]{1,0:T(8,128)(2,1)S(1)}, u32[]{:S(2)}, u32[]{:S(2)}) collective-permute-start(bf16[256,768]{1,0:T(8,128)(2,1)S(1)} %copy-done.23), channel_id=1, source_target_pairs={{0,8},{4,12},{24,16},{28,20},{1,9},{5,13},{25,17},{29,21},{2,10},{... | collective-permute-start | bytes 1179656 | tf_op jit(solution)/shard_map/ppermute | solution.py:505
  100.9 12.2 %copy-start.15 = (bf16[128,768]{1,0:T(8,128)(2,1)S(1)}, bf16[128,768]{1,0:T(8,128)(2,1)}, u32[]{:S(2)}) copy-start(bf16[128,768]{1,0:T(8,128)(2,1)} %copy-done.14) | copy-start | bytes 589828
  113.1 63.0 %copy-start.4 = (bf16[16,4,128,128]{3,2,1,0:T(8,128)(2,1)}, bf16[16,4,128,128]{3,2,1,0:T(8,128)(2,1)S(1)}, u32[]{:S(2)}) copy-start(bf16[16,4,128,128]{3,2,1,0:T(8,128)(2,1)S(1)} %get-tuple-element.83.rest_5_) | copy-start | bytes 6291460
  114.4 61.7 %copy-start.17 = (bf16[1,4,128,128]{3,2,1,0:T(8,128)(2,1)}, bf16[1,4,128,128]{3,2,1,0:T(8,128)(2,1)S(1)}, u32[]{:S(2)}) copy-start(bf16[1,4,128,128]{3,2,1,0:T(8,128)(2,1)S(1)} %get-tuple-element.84.rest_6_) | copy-start | bytes 393220
  122.5 53.7 %copy-start.6 = (bf16[9,4,128,128]{3,2,1,0:T(8,128)(2,1)}, bf16[9,4,128,128]{3,2,1,0:T(8,128)(2,1)S(1)}, u32[]{:S(2)}) copy-start(bf16[9,4,128,128]{3,2,1,0:T(8,128)(2,1)S(1)} %get-tuple-element.85.rest_7_) | copy-start | bytes 3538948
  122.5 53.7 %copy-start.8 = (bf16[512,768]{1,0:T(8,128)(2,1)}, bf16[512,768]{1,0:T(8,128)(2,1)S(1)}, u32[]{:S(2)}) copy-start(bf16[512,768]{1,0:T(8,128)(2,1)S(1)} %collective-permute-done.10.x_ref.rest_3_) | copy-start | bytes 2359300
  126.0 50.2 %copy-start.10 = (bf16[4,4,128,128]{3,2,1,0:T(8,128)(2,1)}, bf16[4,4,128,128]{3,2,1,0:T(8,128)(2,1)S(1)}, u32[]{:S(2)}) copy-start(bf16[4,4,128,128]{3,2,1,0:T(8,128)(2,1)S(1)} %get-tuple-element.86.rest_8_) | copy-start | bytes 1572868
  128.0 48.2 %copy-start.12 = (bf16[2,4,128,128]{3,2,1,0:T(8,128)(2,1)}, bf16[2,4,128,128]{3,2,1,0:T(8,128)(2,1)S(1)}, u32[]{:S(2)}) copy-start(bf16[2,4,128,128]{3,2,1,0:T(8,128)(2,1)S(1)} %get-tuple-element.87.rest_9_) | copy-start | bytes 786436
  130.0 3.9 %collective-permute-start.12 = (bf16[1040,768]{1,0:T(8,128)(2,1)S(1)}, bf16[1040,768]{1,0:T(8,128)(2,1)S(1)}, u32[]{:S(2)}, u32[]{:S(2)}) collective-permute-start(bf16[1040,768]{1,0:T(8,128)(2,1)S(1)} %moments.8), channel_id=1, source_target_pairs={{8,12},{12,8},{16,20},{20,16},{9,13},{13,9},{17,21},{21,17},{10,14... | collective-permute-start | bytes 4792328 | tf_op jit(solution)/shard_map/ppermute | solution.py:505
  134.4 35.8 %collective-permute-start.14 = (bf16[1040,768]{1,0:T(8,128)(2,1)S(1)}, bf16[1040,768]{1,0:T(8,128)(2,1)S(1)}, u32[]{:S(2)}, u32[]{:S(2)}) collective-permute-start(bf16[1040,768]{1,0:T(8,128)(2,1)S(1)} %add_sums.1), channel_id=1, source_target_pairs={{8,16},{12,20},{16,8},{20,12},{9,17},{13,21},{17,9},{21,13},{10,18... | collective-permute-start | bytes 4792328 | tf_op jit(solution)/shard_map/ppermute | solution.py:505
  140.2 30.0 %collective-permute-start.16 = (bf16[1040,768]{1,0:T(8,128)(2,1)S(1)}, bf16[1040,768]{1,0:T(8,128)(2,1)S(1)}, u32[]{:S(2)}, u32[]{:S(2)}) collective-permute-start(bf16[1040,768]{1,0:T(8,128)(2,1)S(1)} %moments.11), channel_id=1, source_target_pairs={{8,12},{12,8},{16,20},{20,16},{9,13},{13,9},{17,21},{21,17},{10,14... | collective-permute-start | bytes 4792328 | tf_op jit(solution)/shard_map/ppermute | solution.py:505
  141.0 29.3 %collective-permute-start.15 = (bf16[1040,768]{1,0:T(8,128)(2,1)S(1)}, bf16[1040,768]{1,0:T(8,128)(2,1)S(1)}, u32[]{:S(2)}, u32[]{:S(2)}) collective-permute-start(bf16[1040,768]{1,0:T(8,128)(2,1)S(1)} %moments.10), channel_id=1, source_target_pairs={{8,12},{12,8},{16,20},{20,16},{9,13},{13,9},{17,21},{21,17},{10,14... | collective-permute-start | bytes 4792328 | tf_op jit(solution)/shard_map/ppermute | solution.py:505
  141.7 15.9 %collective-permute-start.13 = (f32[16,128]{1,0:T(8,128)S(1)}, f32[16,128]{1,0:T(8,128)S(1)}, u32[]{:S(2)}, u32[]{:S(2)}) collective-permute-start(f32[16,128]{1,0:T(8,128)S(1)} %join_norms.1), channel_id=1, source_target_pairs={{8,0},{12,4},{16,24},{20,28},{9,1},{13,5},{17,25},{21,29},{10,2},{... | collective-permute-start | bytes 24584 | tf_op jit(solution)/shard_map/ppermute | solution.py:505
  157.6 12.6 %copy-start.19 = (f32[16,128]{1,0:T(8,128)}, f32[16,128]{1,0:T(8,128)S(1)}, u32[]{:S(2)}) copy-start(f32[16,128]{1,0:T(8,128)S(1)} %collective-permute-done.13.refs_1_) | copy-start | bytes 24580
  173.0 20.1 %collective-permute-start.17 = (bf16[1040,768]{1,0:T(8,128)(2,1)}, bf16[1040,768]{1,0:T(8,128)(2,1)}, u32[]{:S(2)}, u32[]{:S(2)}) collective-permute-start(bf16[1040,768]{1,0:T(8,128)(2,1)} %get-tuple-element.97), channel_id=1, source_target_pairs={{8,16},{12,20},{16,8},{20,12},{9,17},{13,21},{17,9},{21,13},{10,18... | collective-permute-start | bytes 4792328 | tf_op jit(solution)/shard_map/ppermute | solution.py:505
  174.8 42.4 %collective-permute-start.18 = (bf16[1040,768]{1,0:T(8,128)(2,1)}, bf16[1040,768]{1,0:T(8,128)(2,1)}, u32[]{:S(2)}, u32[]{:S(2)}) collective-permute-start(bf16[1040,768]{1,0:T(8,128)(2,1)} %get-tuple-element.98), channel_id=1, source_target_pairs={{8,0},{12,4},{16,24},{20,28},{9,1},{13,5},{17,25},{21,29},{10,2},{... | collective-permute-start | bytes 4792328 | tf_op jit(solution)/shard_map/ppermute | solution.py:505
  179.6 37.6 %collective-permute-start.19 = (bf16[1040,768]{1,0:T(8,128)(2,1)}, bf16[1040,768]{1,0:T(8,128)(2,1)}, u32[]{:S(2)}, u32[]{:S(2)}) collective-permute-start(bf16[1040,768]{1,0:T(8,128)(2,1)} %moments.14), channel_id=1, source_target_pairs={{8,12},{12,8},{16,20},{20,16},{9,13},{13,9},{17,21},{21,17},{10,14... | collective-permute-start | bytes 4792328 | tf_op jit(solution)/shard_map/ppermute | solution.py:505
  190.8 26.5 %copy-start.20 = (f32[16,128]{1,0:T(8,128)S(1)}, f32[16,128]{1,0:T(8,128)}, u32[]{:S(2)}) copy-start(f32[16,128]{1,0:T(8,128)} %copy-done.19) | copy-start | bytes 24580
  (12 other events, 20.3 us)

commit v14 on v13

--- a/solution.py
+++ b/solution.py
@@ -318,7 +318,7 @@
     )(order, starts, *[in_vmem(r) for r in rows], *[in_vmem(r) for r in resp])
 
 
-CHUNK = 80
+CHUNK = 16
 
 
 def each_chunk(rows, step):
@@ -522,21 +522,20 @@
     where = [chip.reshape(1), core.reshape(1)]
     row_blocks = points.shape[0] // RB
     small = row_blocks // 8
-    cuts = (0, 1, 2 + 4 * small, row_blocks - small, row_blocks)
+    cuts = (0, 1 + 4 * small, row_blocks - 1, row_blocks)
     runs = (row_blocks,) + tuple(b - a for a, b in zip(cuts[:-1], cuts[1:]))
     own_ids = candidates.T
     end_ids = move(own_ids, INWARD)
-    before = move(points[: cuts[1] * RB], INWARD)
     weights = parameter_shard(*parameters)
-    weights_then, end_ids, before = lax.optimization_barrier((weights, end_ids, before))
+    weights_then, end_ids = lax.optimization_barrier((weights, end_ids))
 
     outer = move(weights_then, INWARD)
     across = move(weights, MIDDLE)
-    pieces = cut_rows(after(points, weights_then), [cut * RB for cut in cuts[1:]])
+    pieces = cut_rows(after(points, weights_then), [cut * RB for cut in cuts])
     own_shared = move(after(weights, *pieces), CORES)
     most = move(after(pieces[0], outer), INWARD)
     far = move(outer, MIDDLE)
-    moved = [before, most] + [move(after(piece, far), INWARD) for piece in pieces[1:]]
+    moved = [most] + [move(after(piece, far), INWARD) for piece in pieces[1:]]
     pos, order, starts = pair_lists(
         [own_ids, end_ids], runs, held, 8 * held, lax.axis_size("comp"), line_place, where
     )

time: 225 us -> 222 us (0.987); the launches traced: 222 us -> 222 us
  waiting for transfers between devices: 62.6 us -> 69.4 us
  local copies, waits for them, and re-layouts: 13.9 us -> 9.41 us
  starting transfers between devices: 63.8 us -> 61.4 us
    ppermute x20 -> x19, waiting for transfers between devices: 62.6 us -> 69.4 us  [move(): return lax.ppermute(value, 'dp', pairs)]
    unnamed x48 -> x30, local copies, waits for them, and re-layouts: 12.3 us -> 8.73 us
    ppermute x20 -> x19, starting transfers between devices: 63.8 us -> 61.4 us  [move(): return lax.ppermute(value, 'dp', pairs)]
    pallas_call x5 -> x4, Pallas kernels: 26 us -> 25.5 us  [responsibilities(): pl.pallas_call(functools.partial(density_body, first, count, held), in_sp...]
  transfers between devices with their start and end apart: 20 -> 19, of which waited for: 3 -> 3; matrix products, arithmetic and copies ran while one was open for 0% -> 0% of each run, Pallas kernels for 31% -> 30%
where the time goes in v14:
time: 222 us
  Pallas kernels  80.1 us (36%)
  waiting for transfers between devices  69.4 us (31%)
  starting transfers between devices  61.4 us (28%)
  local copies, waits for them, and re-layouts  9.41 us (4%)
    ppermute x19, waiting for transfers between devices, move(): return lax.ppermute(value, 'dp', pairs)  69.4 us
    ppermute x19, starting transfers between devices, move(): return lax.ppermute(value, 'dp', pairs)  61.4 us
    pallas_call x8, Pallas kernels, moments(): pl.pallas_call(functools.partial(moment_body, tuple(shards), held, runs),...  30.4 us
    pallas_call x4, Pallas kernels, responsibilities(): pl.pallas_call(functools.partial(density_body, first, count, held), in_sp...  25.5 us
    unnamed x30, local copies, waits for them, and re-layouts  8.73 us
    pallas_call x1, Pallas kernels, pair_lists(): pl.pallas_call(functools.partial(list_body, tuple(runs), held, owners, pl...  5.52 us
    pallas_call x1, Pallas kernels, results_of(): pl.pallas_call(functools.partial(result_body, owned), grid=(owned // CB,)...  4.65 us
  transfers between devices with their start and end apart: 19, of which 3 were waited for; matrix products, arithmetic and copies ran while one was open for 0% of the time, Pallas kernels for 30%

profile of v14, /device:TPU:0, one launch (start us, length us, event | category | flops | bytes accessed | tf_op | source)
XLA Modules:
  0.0 221.7 jit_solution(13822640979248567254)
XLA Ops:
  0.6 4.9 %collective-permute-start = (s32[4,16]{1,0:T(4,128)}, s32[4,16]{1,0:T(4,128)S(1)}, u32[]{:S(2)}, u32[]{:S(2)}) collective-permute-start(s32[4,16]{1,0:T(4,128)} %bitcast.6), channel_id=1, source_target_pairs={{0,8},{4,12},{24,16},{28,20},{1,9},{5,13},{25,17},{29,21},{2,10},{... | collective-permute-start | bytes 776 | tf_op jit(solution)/shard_map/ppermute | solution.py:505
  6.3 2.8 %parameter_shard.1.refs_0_ = bf16[1,2,528,768]{3,2,1,0:T(8,128)(2,1)S(1)} custom-call(bf16[512,768]{1,0:T(8,128)(2,1)} %means_hbm.1, bf16[512,768]{1,0:T(8,128)(2,1)} %inv_hbm.1, bf16[1,512]{1,0:T(2,128)(2,1)S(1)} %reshape.32.log_ref), custom_call_target="tpu_custom_call" | custom-call | flops 15728640 | bytes 3145728 | tf_op jit(solution)/shard_map/parameter_shard/pallas_call | solution.py:68
  9.1 3.3 %collective-permute-start.1 = (bf16[1,2,528,768]{3,2,1,0:T(8,128)(2,1)S(1)}, bf16[1,2,528,768]{3,2,1,0:T(8,128)(2,1)}, u32[]{:S(2)}, u32[]{:S(2)}) collective-permute-start(bf16[1,2,528,768]{3,2,1,0:T(8,128)(2,1)S(1)} %parameter_shard.1.refs_0_), channel_id=1, source_target_pairs={{0,8},{4,12},{24,16},{28,20},{1,9},{5,13},{25,17},{29,21},{2,10},{... | collective-permute-start | bytes 4866056 | tf_op jit(solution)/shard_map/ppermute | solution.py:505
  12.4 1.8 collective-permute-start.4
  14.3 3.2 %cut_rows.1 = (bf16[1152,768]{1,0:T(8,128)(2,1)}, bf16[768,768]{1,0:T(8,128)(2,1)}, bf16[128,768]{1,0:T(8,128)(2,1)}) custom-call(bf16[2048,768]{1,0:T(8,128)(2,1)} %rest_0_.15), custom_call_target="tpu_custom_call" | custom-call | tf_op jit(solution)/shard_map/cut_rows/pallas_call | solution.py:113
  17.4 1.8 collective-permute-start.3
  19.3 25.8 %collective-permute-done.1.refs_2_ = bf16[1,2,528,768]{3,2,1,0:T(8,128)(2,1)} collective-permute-done((bf16[1,2,528,768]{3,2,1,0:T(8,128)(2,1)S(1)}, bf16[1,2,528,768]{3,2,1,0:T(8,128)(2,1)}, u32[]{:S(2)}, u32[]{:S(2)}) %collective-permute-start.1) | collective-permute-done | bytes 1622048 | tf_op jit(solution)/shard_map/ppermute | solution.py:505
  45.1 1.9 collective-permute-start.2
  47.0 6.2 %collective-permute-start.5 = (bf16[1152,768]{1,0:T(8,128)(2,1)}, bf16[1152,768]{1,0:T(8,128)(2,1)S(1)}, u32[]{:S(2)}, u32[]{:S(2)}) collective-permute-start(bf16[1152,768]{1,0:T(8,128)(2,1)} %get-tuple-element.65), channel_id=1, source_target_pairs={{0,8},{4,12},{24,16},{28,20},{1,9},{5,13},{25,17},{29,21},{2,10},{... | collective-permute-start | bytes 5308424 | tf_op jit(solution)/shard_map/ppermute | solution.py:505
  53.2 5.5 %pair_lists.1 = (s32[128]{0:T(128)S(1)}, s32[128]{0:T(128)S(1)}, s32[129]{0:T(256)S(1)}) custom-call(s32[1]{0:T(128)} %bitcast.1.rest_0_, s32[1]{0:T(128)} %bitcast.2.rest_1_, s32[4,16]{1,0:T(4,128)S(1)} %bitcast.7, s32[4,16]{1,0:T(4,128)S(1)} %collective-permute-done.rest_3_), custom_call_target="tpu_custom_call" | custom-call | tf_op jit(solution)/shard_map/pair_lists/pallas_call | solution.py:229
  60.5 2.6 %stack_shards.2.refs_0_ = bf16[8,2,528,768]{3,2,1,0:T(8,128)(2,1)S(1)} custom-call(bf16[1,2,528,768]{3,2,1,0:T(8,128)(2,1)S(1)} %parameter_shard.1.refs_0_, bf16[1,2,528,768]{3,2,1,0:T(8,128)(2,1)} %collective-permute-done.3.refs_1_, bf16[1,2,528,768]{3,2,1,0:T(8,128)(2,1)} %collective-permute-done.1.refs_2_, ...), custom_call_target="tpu_custom_call" | custom-call | tf_op jit(solution)/shard_map/stack_shards/pallas_call | solution.py:350
  63.9 25.3 %collective-permute-start.9 = (bf16[768,768]{1,0:T(8,128)(2,1)S(1)}, bf16[768,768]{1,0:T(8,128)(2,1)S(1)}, u32[]{:S(2)}, u32[]{:S(2)}) collective-permute-start(bf16[768,768]{1,0:T(8,128)(2,1)S(1)} %copy-done.13), channel_id=1, source_target_pairs={{0,8},{4,12},{24,16},{28,20},{1,9},{5,13},{25,17},{29,21},{2,10},{... | collective-permute-start | bytes 3538952 | tf_op jit(solution)/shard_map/ppermute | solution.py:505
  90.4 4.2 %collective-permute-start.10 = (bf16[128,768]{1,0:T(8,128)(2,1)S(1)}, bf16[128,768]{1,0:T(8,128)(2,1)S(1)}, u32[]{:S(2)}, u32[]{:S(2)}) collective-permute-start(bf16[128,768]{1,0:T(8,128)(2,1)S(1)} %copy-done.14), channel_id=1, source_target_pairs={{0,8},{4,12},{24,16},{28,20},{1,9},{5,13},{25,17},{29,21},{2,10},{... | collective-permute-start | bytes 589832 | tf_op jit(solution)/shard_map/ppermute | solution.py:505
  94.7 1.6 stack_shards.3.weight_ref
  97.1 12.2 %responsibilities.4 = (bf16[16,4,128,128]{3,2,1,0:T(8,128)(2,1)S(1)}, f32[16,128]{1,0:T(8,128)S(1)}) custom-call(s32[128]{0:T(128)S(1)} %get-tuple-element.73.pos_ref, bf16[2048,768]{1,0:T(8,128)(2,1)S(1)} %copy-done, bf16[8,2,528,768]{3,2,1,0:T(8,128)(2,1)S(1)} %stack_shards.3.weight_ref), custom_call_target="tpu_custom_call" | custom-call | flops 3221225472 | bytes 28311552 | tf_op jit(solution)/shard_map/responsibilities/pallas_call | solution.py:163
  109.3 7.1 %responsibilities.5 = (bf16[9,4,128,128]{3,2,1,0:T(8,128)(2,1)S(1)}, f32[9,128]{1,0:T(8,128)S(1)}) custom-call(s32[128]{0:T(128)S(1)} %get-tuple-element.73.pos_ref, bf16[1152,768]{1,0:T(8,128)(2,1)S(1)} %copy-done.2, bf16[8,2,528,768]{3,2,1,0:T(8,128)(2,1)S(1)} %stack_shards.3.weight_ref), custom_call_target="tpu_custom_call" | custom-call | flops 1811939328 | bytes 15925248 | tf_op jit(solution)/shard_map/responsibilities/pallas_call | solution.py:163
  116.5 4.9 %responsibilities.6 = (bf16[6,4,128,128]{3,2,1,0:T(8,128)(2,1)S(1)}, f32[6,128]{1,0:T(8,128)S(1)}) custom-call(s32[128]{0:T(128)S(1)} %get-tuple-element.73.pos_ref, bf16[768,768]{1,0:T(8,128)(2,1)S(1)} %collective-permute-done.9.x_ref.rest_2_, bf16[8,2,528,768]{3,2,1,0:T(8,128)(2,1)S(1)} %stack_shards.3.weight_ref), custom_call_target="tpu_custom_call" | custom-call | flops 1207959552 | bytes 10616832 | tf_op jit(solution)/shard_map/responsibilities/pallas_call | solution.py:163
  122.7 3.4 %moments.8 = bf16[1040,768]{1,0:T(8,128)(2,1)S(1)} custom-call(s32[128]{0:T(128)S(1)} %get-tuple-element.92.order_ref, s32[129]{0:T(256)S(1)} %get-tuple-element.56.start_ref, bf16[2048,768]{1,0:T(8,128)(2,1)S(1)} %copy-done, bf16[1152,768]{1,0:T(8,128)(2,1)S(1)} %copy-done.2, bf16[768,768]{1,0:T(8,128)(2,1)S(1)} %collective-permute-done.9.x_ref.rest_2_, ...), custom_call_target="tpu_custom_call" | custom-call | flops 805306368 | bytes 3670016 | tf_op jit(solution)/shard_map/moments/pallas_call | solution.py:302
  126.8 1.9 moments.9.refs_0_
  130.3 1.9 moments.10
  132.2 1.9 moments.11
  137.2 3.4 %moments.12.a_ref = bf16[1040,768]{1,0:T(8,128)(2,1)S(1)} custom-call(s32[128]{0:T(128)S(1)} %get-tuple-element.92.order_ref, s32[129]{0:T(256)S(1)} %get-tuple-element.56.start_ref, bf16[2048,768]{1,0:T(8,128)(2,1)S(1)} %copy-done, bf16[1152,768]{1,0:T(8,128)(2,1)S(1)} %copy-done.2, bf16[768,768]{1,0:T(8,128)(2,1)S(1)} %collective-permute-done.9.x_ref.rest_2_, ...), custom_call_target="tpu_custom_call" | custom-call | flops 805306368 | bytes 3670016 | tf_op jit(solution)/shard_map/moments/pallas_call | solution.py:302
  140.6 15.1 %collective-permute-done.12.refs_1_ = f32[16,128]{1,0:T(8,128)S(1)} collective-permute-done((f32[16,128]{1,0:T(8,128)S(1)}, f32[16,128]{1,0:T(8,128)S(1)}, u32[]{:S(2)}, u32[]{:S(2)}) %collective-permute-start.12) | collective-permute-done | bytes 8224 | tf_op jit(solution)/shard_map/ppermute | solution.py:505
  155.6 11.9 %moments.13.c_ref = bf16[1040,768]{1,0:T(8,128)(2,1)S(1)} custom-call(s32[128]{0:T(128)S(1)} %get-tuple-element.92.order_ref, s32[129]{0:T(256)S(1)} %get-tuple-element.56.start_ref, bf16[2048,768]{1,0:T(8,128)(2,1)S(1)} %copy-done, bf16[1152,768]{1,0:T(8,128)(2,1)S(1)} %copy-done.2, bf16[768,768]{1,0:T(8,128)(2,1)S(1)} %collective-permute-done.9.x_ref.rest_2_, ...), custom_call_target="tpu_custom_call" | custom-call | flops 805306368 | bytes 3670016 | tf_op jit(solution)/shard_map/moments/pallas_call | solution.py:302
  167.6 3.1 %add_both_sums.1 = (bf16[1040,768]{1,0:T(8,128)(2,1)}, bf16[1040,768]{1,0:T(8,128)(2,1)}) custom-call(bf16[1040,768]{1,0:T(8,128)(2,1)S(1)} %moments.12.a_ref, bf16[1040,768]{1,0:T(8,128)(2,1)S(1)} %collective-permute-done.14.b_ref, bf16[1040,768]{1,0:T(8,128)(2,1)S(1)} %moments.13.c_ref, bf16[1040,768]{1,0:T(8,128)(2,1)S(1)} %collective-permute-done.15.d_ref, ...), custom_call_target="tpu_custom_call" | custom-call | tf_op jit(solution)/shard_map/add_both_sums/pallas_call | solution.py:383
  170.7 1.8 collective-permute-start.16
  173.9 4.0 %moments.14 = bf16[1040,768]{1,0:T(8,128)(2,1)} custom-call(s32[128]{0:T(128)S(1)} %get-tuple-element.92.order_ref, s32[129]{0:T(256)S(1)} %get-tuple-element.56.start_ref, bf16[2048,768]{1,0:T(8,128)(2,1)S(1)} %copy-done, bf16[1152,768]{1,0:T(8,128)(2,1)S(1)} %copy-done.2, bf16[768,768]{1,0:T(8,128)(2,1)S(1)} %collective-permute-done.9.x_ref.rest_2_, ...), custom_call_target="tpu_custom_call" | custom-call | flops 805306368 | bytes 3670016 | tf_op jit(solution)/shard_map/moments/pallas_call | solution.py:302
  177.9 1.8 collective-permute-start.18
  181.2 1.6 copy-done.5
  186.5 1.9 moments.15.refs_3_
  188.4 28.5 %collective-permute-done.17.refs_2_ = bf16[1040,768]{1,0:T(8,128)(2,1)} collective-permute-done((bf16[1040,768]{1,0:T(8,128)(2,1)}, bf16[1040,768]{1,0:T(8,128)(2,1)}, u32[]{:S(2)}, u32[]{:S(2)}) %collective-permute-start.17) | collective-permute-done | bytes 1597472 | tf_op jit(solution)/shard_map/ppermute | solution.py:505
  216.9 4.7 %results.1 = (f32[1,512]{1,0:T(1,128)}, f32[512,768]{1,0:T(8,128)}, f32[512,768]{1,0:T(8,128)}, f32[16,128]{1,0:T(8,128)}) custom-call(s32[1]{0:T(128)} %bitcast.end_ref, f32[16,128]{1,0:T(8,128)S(1)} %get-tuple-element.67.refs_0_, f32[16,128]{1,0:T(8,128)S(1)} %collective-permute-done.12.refs_1_, bf16[1040,768]{1,0:T(8,128)(2,1)} %collective-permute-done.17.refs_2_, ...), custom_call_target="tpu_custom_call" | custom-call | tf_op jit(solution)/shard_map/results/pallas_call | solution.py:448
  (58 shorter events, 18.1 us)
Async XLA Ops:
  0.6 8.5 %collective-permute-start = (s32[4,16]{1,0:T(4,128)}, s32[4,16]{1,0:T(4,128)S(1)}, u32[]{:S(2)}, u32[]{:S(2)}) collective-permute-start(s32[4,16]{1,0:T(4,128)} %bitcast.6), channel_id=1, source_target_pairs={{0,8},{4,12},{24,16},{28,20},{1,9},{5,13},{25,17},{29,21},{2,10},{... | collective-permute-start | bytes 776 | tf_op jit(solution)/shard_map/ppermute | solution.py:505
  9.1 44.1 %copy-start.12 = (s32[16,4]{0,1:T(4,128)S(1)}, s32[16,4]{0,1:T(4,128)}, u32[]{:S(2)}) copy-start(s32[16,4]{0,1:T(4,128)} %param.6) | copy-start | bytes 772
  9.1 36.0 %collective-permute-start.1 = (bf16[1,2,528,768]{3,2,1,0:T(8,128)(2,1)S(1)}, bf16[1,2,528,768]{3,2,1,0:T(8,128)(2,1)}, u32[]{:S(2)}, u32[]{:S(2)}) collective-permute-start(bf16[1,2,528,768]{3,2,1,0:T(8,128)(2,1)S(1)} %parameter_shard.1.refs_0_), channel_id=1, source_target_pairs={{0,8},{4,12},{24,16},{28,20},{1,9},{5,13},{25,17},{29,21},{2,10},{... | collective-permute-start | bytes 4866056 | tf_op jit(solution)/shard_map/ppermute | solution.py:505
  12.4 46.3 %collective-permute-start.4 = (bf16[1,2,528,768]{3,2,1,0:T(8,128)(2,1)S(1)}, bf16[1,2,528,768]{3,2,1,0:T(8,128)(2,1)}, u32[]{:S(2)}, u32[]{:S(2)}) collective-permute-start(bf16[1,2,528,768]{3,2,1,0:T(8,128)(2,1)S(1)} %parameter_shard.1.refs_0_), channel_id=1, source_target_pairs={{8,16},{12,20},{16,8},{20,12},{9,17},{13,21},{17,9},{21,13},{10,18... | collective-permute-start | bytes 4866056 | tf_op jit(solution)/shard_map/ppermute | solution.py:505
  17.4 43.0 %collective-permute-start.3 = (bf16[1,2,528,768]{3,2,1,0:T(8,128)(2,1)S(1)}, bf16[1,2,528,768]{3,2,1,0:T(8,128)(2,1)}, u32[]{:S(2)}, u32[]{:S(2)}) collective-permute-start(bf16[1,2,528,768]{3,2,1,0:T(8,128)(2,1)S(1)} %parameter_shard.1.refs_0_), channel_id=1, source_target_pairs={{8,12},{12,8},{16,20},{20,16},{9,13},{13,9},{17,21},{21,17},{10,14... | collective-permute-start | bytes 4866056 | tf_op jit(solution)/shard_map/ppermute | solution.py:505
  45.1 18.0 %collective-permute-start.2 = (bf16[1,2,528,768]{3,2,1,0:T(8,128)(2,1)}, bf16[1,2,528,768]{3,2,1,0:T(8,128)(2,1)}, u32[]{:S(2)}, u32[]{:S(2)}) collective-permute-start(bf16[1,2,528,768]{3,2,1,0:T(8,128)(2,1)} %collective-permute-done.1.refs_2_), channel_id=1, source_target_pairs={{8,16},{12,20},{16,8},{20,12},{9,17},{13,21},{17,9},{21,13},{10,18... | collective-permute-start | bytes 4866056 | tf_op jit(solution)/shard_map/ppermute | solution.py:505
  47.0 42.2 %collective-permute-start.5 = (bf16[1152,768]{1,0:T(8,128)(2,1)}, bf16[1152,768]{1,0:T(8,128)(2,1)S(1)}, u32[]{:S(2)}, u32[]{:S(2)}) collective-permute-start(bf16[1152,768]{1,0:T(8,128)(2,1)} %get-tuple-element.65), channel_id=1, source_target_pairs={{0,8},{4,12},{24,16},{28,20},{1,9},{5,13},{25,17},{29,21},{2,10},{... | collective-permute-start | bytes 5308424 | tf_op jit(solution)/shard_map/ppermute | solution.py:505
  58.7 5.1 %copy-start.13 = (bf16[768,768]{1,0:T(8,128)(2,1)S(1)}, bf16[768,768]{1,0:T(8,128)(2,1)}, u32[]{:S(2)}) copy-start(bf16[768,768]{1,0:T(8,128)(2,1)} %get-tuple-element.71) | copy-start | bytes 3538948
  58.8 31.7 %copy-start.14 = (bf16[128,768]{1,0:T(8,128)(2,1)S(1)}, bf16[128,768]{1,0:T(8,128)(2,1)}, u32[]{:S(2)}) copy-start(bf16[128,768]{1,0:T(8,128)(2,1)} %get-tuple-element.74) | copy-start | bytes 589828
  58.8 35.9 %collective-permute-start.7 = (bf16[1,2,528,768]{3,2,1,0:T(8,128)(2,1)}, bf16[1,2,528,768]{3,2,1,0:T(8,128)(2,1)S(1)}, u32[]{:S(2)}, u32[]{:S(2)}) collective-permute-start(bf16[1,2,528,768]{3,2,1,0:T(8,128)(2,1)} %collective-permute-done.4.refs_3_), channel_id=1, source_target_pairs={{8,12},{12,8},{16,20},{20,16},{9,13},{13,9},{17,21},{21,17},{10,14... | collective-permute-start | bytes 4866056 | tf_op jit(solution)/shard_map/ppermute | solution.py:505
  59.7 35.0 %collective-permute-start.6 = (bf16[1,2,528,768]{3,2,1,0:T(8,128)(2,1)}, bf16[1,2,528,768]{3,2,1,0:T(8,128)(2,1)S(1)}, u32[]{:S(2)}, u32[]{:S(2)}) collective-permute-start(bf16[1,2,528,768]{3,2,1,0:T(8,128)(2,1)} %collective-permute-done.1.refs_2_), channel_id=1, source_target_pairs={{8,12},{12,8},{16,20},{20,16},{9,13},{13,9},{17,21},{21,17},{10,14... | collective-permute-start | bytes 4866056 | tf_op jit(solution)/shard_map/ppermute | solution.py:505
  63.1 31.6 %collective-permute-start.8 = (bf16[1,2,528,768]{3,2,1,0:T(8,128)(2,1)}, bf16[1,2,528,768]{3,2,1,0:T(8,128)(2,1)S(1)}, u32[]{:S(2)}, u32[]{:S(2)}) collective-permute-start(bf16[1,2,528,768]{3,2,1,0:T(8,128)(2,1)} %collective-permute-done.2.refs_1_), channel_id=1, source_target_pairs={{8,12},{12,8},{16,20},{20,16},{9,13},{13,9},{17,21},{21,17},{10,14... | collective-permute-start | bytes 4866056 | tf_op jit(solution)/shard_map/ppermute | solution.py:505
  63.9 52.6 %collective-permute-start.9 = (bf16[768,768]{1,0:T(8,128)(2,1)S(1)}, bf16[768,768]{1,0:T(8,128)(2,1)S(1)}, u32[]{:S(2)}, u32[]{:S(2)}) collective-permute-start(bf16[768,768]{1,0:T(8,128)(2,1)S(1)} %copy-done.13), channel_id=1, source_target_pairs={{0,8},{4,12},{24,16},{28,20},{1,9},{5,13},{25,17},{29,21},{2,10},{... | collective-permute-start | bytes 3538952 | tf_op jit(solution)/shard_map/ppermute | solution.py:505
  90.4 31.0 %collective-permute-start.10 = (bf16[128,768]{1,0:T(8,128)(2,1)S(1)}, bf16[128,768]{1,0:T(8,128)(2,1)S(1)}, u32[]{:S(2)}, u32[]{:S(2)}) collective-permute-start(bf16[128,768]{1,0:T(8,128)(2,1)S(1)} %copy-done.14), channel_id=1, source_target_pairs={{0,8},{4,12},{24,16},{28,20},{1,9},{5,13},{25,17},{29,21},{2,10},{... | collective-permute-start | bytes 589832 | tf_op jit(solution)/shard_map/ppermute | solution.py:505
  94.7 2.4 %copy-start = (bf16[2048,768]{1,0:T(8,128)(2,1)S(1)}, bf16[2048,768]{1,0:T(8,128)(2,1)}, u32[]{:S(2)}) copy-start(bf16[2048,768]{1,0:T(8,128)(2,1)} %rest_0_.15) | copy-start | bytes 9437188
  97.1 12.2 %copy-start.2 = (bf16[1152,768]{1,0:T(8,128)(2,1)S(1)}, bf16[1152,768]{1,0:T(8,128)(2,1)}, u32[]{:S(2)}) copy-start(bf16[1152,768]{1,0:T(8,128)(2,1)} %copy-done.1) | copy-start | bytes 5308420
  109.3 64.6 %copy-start.4 = (bf16[16,4,128,128]{3,2,1,0:T(8,128)(2,1)}, bf16[16,4,128,128]{3,2,1,0:T(8,128)(2,1)S(1)}, u32[]{:S(2)}) copy-start(bf16[16,4,128,128]{3,2,1,0:T(8,128)(2,1)S(1)} %get-tuple-element.76.rest_4_) | copy-start | bytes 6291460
  116.4 57.4 %copy-start.8 = (bf16[9,4,128,128]{3,2,1,0:T(8,128)(2,1)}, bf16[9,4,128,128]{3,2,1,0:T(8,128)(2,1)S(1)}, u32[]{:S(2)}) copy-start(bf16[9,4,128,128]{3,2,1,0:T(8,128)(2,1)S(1)} %get-tuple-element.77.rest_5_) | copy-start | bytes 3538948
  116.4 57.4 %copy-start.6 = (bf16[768,768]{1,0:T(8,128)(2,1)}, bf16[768,768]{1,0:T(8,128)(2,1)S(1)}, u32[]{:S(2)}) copy-start(bf16[768,768]{1,0:T(8,128)(2,1)S(1)} %collective-permute-done.9.x_ref.rest_2_) | copy-start | bytes 3538948
  121.4 52.5 %copy-start.10 = (bf16[6,4,128,128]{3,2,1,0:T(8,128)(2,1)}, bf16[6,4,128,128]{3,2,1,0:T(8,128)(2,1)S(1)}, u32[]{:S(2)}) copy-start(bf16[6,4,128,128]{3,2,1,0:T(8,128)(2,1)S(1)} %get-tuple-element.78.rest_6_) | copy-start | bytes 2359300
  126.0 2.7 %collective-permute-start.11 = (bf16[1040,768]{1,0:T(8,128)(2,1)S(1)}, bf16[1040,768]{1,0:T(8,128)(2,1)S(1)}, u32[]{:S(2)}, u32[]{:S(2)}) collective-permute-start(bf16[1040,768]{1,0:T(8,128)(2,1)S(1)} %moments.8), channel_id=1, source_target_pairs={{8,12},{12,8},{16,20},{20,16},{9,13},{13,9},{17,21},{21,17},{10,14... | collective-permute-start | bytes 4792328 | tf_op jit(solution)/shard_map/ppermute | solution.py:505
  129.5 38.1 %collective-permute-start.13 = (bf16[1040,768]{1,0:T(8,128)(2,1)S(1)}, bf16[1040,768]{1,0:T(8,128)(2,1)S(1)}, u32[]{:S(2)}, u32[]{:S(2)}) collective-permute-start(bf16[1040,768]{1,0:T(8,128)(2,1)S(1)} %add_sums.1), channel_id=1, source_target_pairs={{8,16},{12,20},{16,8},{20,12},{9,17},{13,21},{17,9},{21,13},{10,18... | collective-permute-start | bytes 4792328 | tf_op jit(solution)/shard_map/ppermute | solution.py:505
  134.1 33.5 %collective-permute-start.15 = (bf16[1040,768]{1,0:T(8,128)(2,1)S(1)}, bf16[1040,768]{1,0:T(8,128)(2,1)S(1)}, u32[]{:S(2)}, u32[]{:S(2)}) collective-permute-start(bf16[1040,768]{1,0:T(8,128)(2,1)S(1)} %moments.11), channel_id=1, source_target_pairs={{8,12},{12,8},{16,20},{20,16},{9,13},{13,9},{17,21},{21,17},{10,14... | collective-permute-start | bytes 4792328 | tf_op jit(solution)/shard_map/ppermute | solution.py:505
  134.9 32.7 %collective-permute-start.14 = (bf16[1040,768]{1,0:T(8,128)(2,1)S(1)}, bf16[1040,768]{1,0:T(8,128)(2,1)S(1)}, u32[]{:S(2)}, u32[]{:S(2)}) collective-permute-start(bf16[1040,768]{1,0:T(8,128)(2,1)S(1)} %moments.10), channel_id=1, source_target_pairs={{8,12},{12,8},{16,20},{20,16},{9,13},{13,9},{17,21},{21,17},{10,14... | collective-permute-start | bytes 4792328 | tf_op jit(solution)/shard_map/ppermute | solution.py:505
  135.7 19.9 %collective-permute-start.12 = (f32[16,128]{1,0:T(8,128)S(1)}, f32[16,128]{1,0:T(8,128)S(1)}, u32[]{:S(2)}, u32[]{:S(2)}) collective-permute-start(f32[16,128]{1,0:T(8,128)S(1)} %join_norms.1), channel_id=1, source_target_pairs={{8,0},{12,4},{16,24},{20,28},{9,1},{13,5},{17,25},{21,29},{10,2},{... | collective-permute-start | bytes 24584 | tf_op jit(solution)/shard_map/ppermute | solution.py:505
  170.7 17.7 %collective-permute-start.16 = (bf16[1040,768]{1,0:T(8,128)(2,1)}, bf16[1040,768]{1,0:T(8,128)(2,1)}, u32[]{:S(2)}, u32[]{:S(2)}) collective-permute-start(bf16[1040,768]{1,0:T(8,128)(2,1)} %get-tuple-element.89), channel_id=1, source_target_pairs={{8,16},{12,20},{16,8},{20,12},{9,17},{13,21},{17,9},{21,13},{10,18... | collective-permute-start | bytes 4792328 | tf_op jit(solution)/shard_map/ppermute | solution.py:505
  172.6 44.3 %collective-permute-start.17 = (bf16[1040,768]{1,0:T(8,128)(2,1)}, bf16[1040,768]{1,0:T(8,128)(2,1)}, u32[]{:S(2)}, u32[]{:S(2)}) collective-permute-start(bf16[1040,768]{1,0:T(8,128)(2,1)} %get-tuple-element.90), channel_id=1, source_target_pairs={{8,0},{12,4},{16,24},{20,28},{9,1},{13,5},{17,25},{21,29},{10,2},{... | collective-permute-start | bytes 4792328 | tf_op jit(solution)/shard_map/ppermute | solution.py:505
  177.9 39.0 %collective-permute-start.18 = (bf16[1040,768]{1,0:T(8,128)(2,1)}, bf16[1040,768]{1,0:T(8,128)(2,1)}, u32[]{:S(2)}, u32[]{:S(2)}) collective-permute-start(bf16[1040,768]{1,0:T(8,128)(2,1)} %moments.14), channel_id=1, source_target_pairs={{8,12},{12,8},{16,20},{20,16},{9,13},{13,9},{17,21},{21,17},{10,14... | collective-permute-start | bytes 4792328 | tf_op jit(solution)/shard_map/ppermute | solution.py:505
  179.7 1.5 copy-start.3
  181.2 1.6 copy-start.5
  182.8 1.3 copy-start.7
  184.1 1.3 copy-start.9
  (2 other events, 2.3 us)
